TPU v7x, 128 devices: a whole 4x4x4 slice. The times are simulated.
128 devices in a mesh: dp: 32 (over y_lo, x, z), tensor: 4 (over y_hi, core).
Axes of the slice: x: 4, y: 4 (y_hi: 2, y_lo: 2; y = y_hi * 2 + y_lo), z: 4, core: 2. Of those that a mesh axis runs over, the one named last changes fastest.
Arguments:
- tokens: bfloat16 [32, 512, 768], P('dp', 'tensor'), may hold values from -6 to 6
- segments: int32 [32, 512], P('dp'), may hold values from 0 to 1, as said below
- q_weight: bfloat16 [768, 768], P('dp', 'tensor'), may hold values from -0.21875 to 0.21875
- k_weight: bfloat16 [768, 768], P('dp', 'tensor'), may hold values from -0.21875 to 0.21875
- v_weight: bfloat16 [768, 768], P('dp', 'tensor'), may hold values from -0.21875 to 0.21875
- up_weight: bfloat16 [768, 3072], P('dp', 'tensor'), may hold values from -0.21875 to 0.21875
- out_weight: bfloat16 [768, 768], P('dp', 'tensor'), may hold values from -1.75 to 1.75
- down_weight: bfloat16 [768, 3072], P('dp', 'tensor'), may hold values from -0.109375 to 0.109375
- q_bias: float32 [768], P(('dp', 'tensor')), may hold values from -4 to 4
- v_bias: float32 [768], P(('dp', 'tensor')), may hold values from -1.5 to 1.5
- out_bias: float32 [768], P(('dp', 'tensor')), may hold values from -4 to 4
- up_bias: float32 [3072], P(('dp', 'tensor')), may hold values from -6 to 6
- down_bias: float32 [768], P(('dp', 'tensor')), may hold values from -4 to 4
- norm1_gain: float32 [768], P(('dp', 'tensor')), may hold values from 0.5 to 1.5
- norm1_shift: float32 [768], P(('dp', 'tensor')), may hold values from -3 to 3
- norm2_gain: float32 [768], P(('dp', 'tensor')), may hold values from 0.5 to 1.5
- norm2_shift: float32 [768], P(('dp', 'tensor')), may hold values from -3 to 3
- cotangent: bfloat16 [32, 512, 768], P('dp', 'tensor'), may hold values from -6 to 6
Outputs:
- layer_output: bfloat16 [32, 512, 768], P('dp', 'tensor')
- input_grad: float32 [32, 512, 768], P('dp', 'tensor')
- q_weight_grad: float32 [768, 768], P('dp', 'tensor')
- k_weight_grad: float32 [768, 768], P('dp', 'tensor')
- v_weight_grad: float32 [768, 768], P('dp', 'tensor')
- up_weight_grad: float32 [768, 3072], P('dp', 'tensor')
- out_weight_grad: float32 [768, 768], P('dp', 'tensor')
- down_weight_grad: float32 [768, 3072], P('dp', 'tensor')
- q_bias_grad: float32 [768], P(('dp', 'tensor'))
- v_bias_grad: float32 [768], P(('dp', 'tensor'))
- out_bias_grad: float32 [768], P(('dp', 'tensor'))
- up_bias_grad: float32 [3072], P(('dp', 'tensor'))
- down_bias_grad: float32 [768], P(('dp', 'tensor'))
- norm1_gain_grad: float32 [768], P(('dp', 'tensor'))
- norm1_shift_grad: float32 [768], P(('dp', 'tensor'))
- norm2_gain_grad: float32 [768], P(('dp', 'tensor'))
- norm2_shift_grad: float32 [768], P(('dp', 'tensor'))
Inputs may be any that keep to these rules, and one draw needn't show every extreme that they name: `segments`: along each sequence the numbers never fall and begin at 0; tokens with equal numbers in one sequence form one document piece, and attention stays within it. A piece that lies between two others has at least 512 * 200 // 512 tokens.
All inputs are finite; a program needn't handle non-finite values.
Results may differ from a plain program's by a relative error of at most 0.025.
Values may be sent and summed in bfloat16 or wider, within the bound.
No kernel may reach another device: no remote copies, remote signals or barrier semaphores. Data moves between devices by JAX's collectives and lax.ppermute only.
A program may use at most 64 MiB of HBM per device.

v0:
```python
import jax
import jax.numpy as jnp
from jax import lax
from jax.sharding import PartitionSpec as P

HEAD_DIM = 64


NORM_EPSILON = 1e-12
MASKED_SCORE = -1000000000.0
ROOT_HALF = 0.7071067811865476
INV_ROOT_TAU = 0.3989422804014327


def contract(left, right, left_dim, right_dim):
    return lax.dot_general(
        left, right, (((left_dim,), (right_dim,)), ((), ())), preferred_element_type=jnp.float32
    )


def gelu_exact(values):
    return 0.5 * values * (1.0 + lax.erf(values * ROOT_HALF))


def gelu_slope(values):
    return (
        0.5 * (1.0 + lax.erf(values * ROOT_HALF))
        + values * jnp.exp(-0.5 * values * values) * INV_ROOT_TAU
    )


def norm_forward(values, gain, shift):
    center = values - jnp.mean(values, axis=-1, keepdims=True)
    scale_inv = lax.rsqrt(jnp.mean(center * center, axis=-1, keepdims=True) + NORM_EPSILON)
    normed = center * scale_inv
    return (normed * gain + shift, normed, scale_inv)


def norm_backward(upstream, normed, scale_inv, gain):
    scaled = upstream * gain
    inner = scale_inv * (
        scaled
        - jnp.mean(scaled, axis=-1, keepdims=True)
        - normed * jnp.mean(scaled * normed, axis=-1, keepdims=True)
    )
    return (inner, jnp.sum(upstream * normed, axis=(0, 1)), jnp.sum(upstream, axis=(0, 1)))


def head_scores(qkv_rows, same_doc, head_index, head_cols):
    offset = head_index * HEAD_DIM
    query_part = qkv_rows[:, offset : offset + HEAD_DIM]
    key_part = qkv_rows[:, head_cols + offset : head_cols + offset + HEAD_DIM]
    value_part = qkv_rows[:, 2 * head_cols + offset : 2 * head_cols + offset + HEAD_DIM]
    scores = jnp.where(
        same_doc, HEAD_DIM ** (-0.5) * contract(query_part, key_part, 1, 1), MASKED_SCORE
    )
    return (scores, query_part, key_part, value_part)


def attend_forward(qkv_rows, segment_row, head_count, head_cols):
    same_doc = segment_row[:, None] == segment_row[None, :]
    outputs = []
    log_totals = []
    for head_index in range(head_count):
        scores, query_part, key_part, value_part = head_scores(
            qkv_rows, same_doc, head_index, head_cols
        )
        highest = jnp.max(scores, axis=-1, keepdims=True)
        shifted = jnp.exp(scores - highest)
        row_total = jnp.sum(shifted, axis=-1, keepdims=True)
        probs_low = (shifted / row_total).astype(jnp.bfloat16)
        outputs.append(jnp.dot(probs_low, value_part, preferred_element_type=jnp.float32))
        log_totals.append((highest + jnp.log(row_total))[:, 0])
    return (jnp.concatenate(outputs, axis=1).astype(jnp.bfloat16), jnp.stack(log_totals))


def attend_backward(qkv_rows, segment_row, log_totals, grad_rows, head_count, head_cols):
    same_doc = segment_row[:, None] == segment_row[None, :]
    query_grads = []
    key_grads = []
    value_grads = []
    for head_index in range(head_count):
        scores, query_part, key_part, value_part = head_scores(
            qkv_rows, same_doc, head_index, head_cols
        )
        probs = jnp.exp(scores - log_totals[head_index][:, None])
        probs_low = probs.astype(jnp.bfloat16)
        offset = head_index * HEAD_DIM
        grad_head = grad_rows[:, offset : offset + HEAD_DIM]
        value_grads.append(contract(probs_low, grad_head, 0, 0))
        probs_grad = contract(grad_head, value_part, 1, 1)
        scores_grad = probs * (probs_grad - jnp.sum(probs * probs_grad, axis=-1, keepdims=True))
        scores_low = scores_grad.astype(jnp.bfloat16)
        query_grads.append(
            HEAD_DIM ** (-0.5) * jnp.dot(scores_low, key_part, preferred_element_type=jnp.float32)
        )
        key_grads.append(HEAD_DIM ** (-0.5) * contract(scores_low, query_part, 0, 0))
    return jnp.concatenate(query_grads + key_grads + value_grads, axis=1).astype(jnp.bfloat16)


def shards(
    tokens,
    segments,
    q_weight,
    k_weight,
    v_weight,
    up_weight,
    out_weight,
    down_weight,
    q_bias,
    v_bias,
    out_bias,
    up_bias,
    down_bias,
    norm1_gain,
    norm1_shift,
    norm2_gain,
    norm2_shift,
    cotangent,
):
    tensor_size = lax.axis_size("tensor")
    my_index = lax.axis_index("tensor")
    seq_count, local_len, width = tokens.shape
    full_len = local_len * tensor_size
    row_count = seq_count * full_len
    head_cols = q_weight.shape[1]
    hidden_cols = up_weight.shape[1]
    head_count = head_cols // HEAD_DIM
    weights = (
        lax.all_gather(q_weight, "dp", axis=0, tiled=True),
        lax.all_gather(k_weight, "dp", axis=0, tiled=True),
        lax.all_gather(v_weight, "dp", axis=0, tiled=True),
        lax.all_gather(up_weight, "dp", axis=0, tiled=True),
        lax.all_gather(out_weight, "dp", axis=0, tiled=True),
        lax.all_gather(down_weight, "dp", axis=0, tiled=True),
    )
    vectors = (
        lax.all_gather(q_bias, ("dp", "tensor"), axis=0, tiled=True),
        lax.all_gather(v_bias, ("dp", "tensor"), axis=0, tiled=True),
        lax.all_gather(out_bias, ("dp", "tensor"), axis=0, tiled=True),
        lax.all_gather(up_bias, ("dp", "tensor"), axis=0, tiled=True),
        lax.all_gather(down_bias, ("dp", "tensor"), axis=0, tiled=True),
        lax.all_gather(norm1_gain, ("dp", "tensor"), axis=0, tiled=True),
        lax.all_gather(norm1_shift, ("dp", "tensor"), axis=0, tiled=True),
        lax.all_gather(norm2_gain, ("dp", "tensor"), axis=0, tiled=True),
        lax.all_gather(norm2_shift, ("dp", "tensor"), axis=0, tiled=True),
    )
    bias_query = lax.dynamic_slice_in_dim(vectors[0], my_index * head_cols, head_cols)
    bias_value = lax.dynamic_slice_in_dim(vectors[1], my_index * head_cols, head_cols)
    bias_up = lax.dynamic_slice_in_dim(vectors[3], my_index * hidden_cols, hidden_cols)
    bias_out, bias_down = (vectors[2], vectors[4])
    gain_first, shift_first, gain_second, shift_second = (
        vectors[5],
        vectors[6],
        vectors[7],
        vectors[8],
    )
    qkv_weight = jnp.concatenate(weights[:3], axis=1)
    qkv_bias = jnp.concatenate([bias_query, jnp.zeros((head_cols,), jnp.float32), bias_value])
    tokens_full = lax.all_gather(tokens, "tensor", axis=1, tiled=True).reshape(row_count, width)
    qkv_rows = (
        jnp.dot(tokens_full, qkv_weight, preferred_element_type=jnp.float32) + qkv_bias
    ).astype(jnp.bfloat16)
    qkv_seqs = qkv_rows.reshape(seq_count, full_len, 3 * head_cols)
    mixed_seqs, log_totals = lax.map(
        lambda sequence: attend_forward(sequence[0], sequence[1], head_count, head_cols),
        (qkv_seqs, segments),
    )
    mixed_rows = mixed_seqs.reshape(row_count, head_cols)
    attn_part = contract(mixed_rows, weights[4], 1, 1).reshape(seq_count, full_len, width)
    attended = lax.psum_scatter(attn_part, "tensor", scatter_dimension=1, tiled=True)
    first, normed_first, inv_first = norm_forward(
        tokens.astype(jnp.float32) + attended + bias_out, gain_first, shift_first
    )
    hidden_full = lax.all_gather(first.astype(jnp.bfloat16), "tensor", axis=1, tiled=True).reshape(
        row_count, width
    )
    upward = jnp.dot(hidden_full, weights[3], preferred_element_type=jnp.float32) + bias_up
    active = gelu_exact(upward).astype(jnp.bfloat16)
    ffn_part = contract(active, weights[5], 1, 1).reshape(seq_count, full_len, width)
    branch = lax.psum_scatter(ffn_part, "tensor", scatter_dimension=1, tiled=True)
    layer_output, normed_second, inv_second = norm_forward(
        first + branch + bias_down, gain_second, shift_second
    )
    weights = (
        lax.all_gather(q_weight, "dp", axis=0, tiled=True),
        lax.all_gather(k_weight, "dp", axis=0, tiled=True),
        lax.all_gather(v_weight, "dp", axis=0, tiled=True),
        lax.all_gather(up_weight, "dp", axis=0, tiled=True),
        lax.all_gather(out_weight, "dp", axis=0, tiled=True),
        lax.all_gather(down_weight, "dp", axis=0, tiled=True),
    )
    qkv_weight = jnp.concatenate(weights[:3], axis=1)
    second_grad, grad_gain_second, grad_shift_second = norm_backward(
        cotangent.astype(jnp.float32), normed_second, inv_second, gain_second
    )
    branch_low = second_grad.astype(jnp.bfloat16)
    grad_bias_down = jnp.sum(branch_low.astype(jnp.float32), axis=(0, 1))
    branch_full = lax.all_gather(branch_low, "tensor", axis=1, tiled=True).reshape(row_count, width)
    grad_down = contract(branch_full, active, 0, 0)
    active_grad = jnp.dot(branch_full, weights[5], preferred_element_type=jnp.float32)
    upward_grad = (active_grad * gelu_slope(upward)).astype(jnp.bfloat16)
    grad_bias_up = jnp.sum(upward_grad.astype(jnp.float32), axis=0)
    grad_up = contract(hidden_full, upward_grad, 0, 0)
    hidden_part = contract(upward_grad, weights[3], 1, 1).reshape(seq_count, full_len, width)
    hidden_grad = lax.psum_scatter(hidden_part, "tensor", scatter_dimension=1, tiled=True)
    resid_grad, grad_gain_first, grad_shift_first = norm_backward(
        second_grad + hidden_grad, normed_first, inv_first, gain_first
    )
    attended_low = resid_grad.astype(jnp.bfloat16)
    grad_bias_out = jnp.sum(attended_low.astype(jnp.float32), axis=(0, 1))
    attended_full = lax.all_gather(attended_low, "tensor", axis=1, tiled=True).reshape(
        row_count, width
    )
    grad_out = contract(attended_full, mixed_rows, 0, 0)
    mixed_grad = jnp.dot(attended_full, weights[4], preferred_element_type=jnp.float32).astype(
        jnp.bfloat16
    )
    qkv_grad = lax.map(
        lambda sequence: attend_backward(
            sequence[0], sequence[1], sequence[2], sequence[3], head_count, head_cols
        ),
        (qkv_seqs, segments, log_totals, mixed_grad.reshape(seq_count, full_len, head_cols)),
    )
    qkv_grad = qkv_grad.reshape(row_count, 3 * head_cols)
    grad_bias_query = jnp.sum(qkv_grad[:, :head_cols].astype(jnp.float32), axis=0)
    grad_bias_value = jnp.sum(qkv_grad[:, 2 * head_cols :].astype(jnp.float32), axis=0)
    grad_qkv = contract(tokens_full, qkv_grad, 0, 0)
    input_part = contract(qkv_grad, qkv_weight, 1, 1).reshape(seq_count, full_len, width)
    input_grad = resid_grad + lax.psum_scatter(
        input_part.astype(jnp.bfloat16), "tensor", scatter_dimension=1, tiled=True
    ).astype(jnp.float32)
    weight_grads = (
        lax.psum_scatter(
            grad_qkv[:, :head_cols].astype(jnp.bfloat16), "dp", scatter_dimension=0, tiled=True
        ).astype(jnp.float32),
        lax.psum_scatter(
            grad_qkv[:, head_cols : 2 * head_cols].astype(jnp.bfloat16),
            "dp",
            scatter_dimension=0,
            tiled=True,
        ).astype(jnp.float32),
        lax.psum_scatter(
            grad_qkv[:, 2 * head_cols :].astype(jnp.bfloat16), "dp", scatter_dimension=0, tiled=True
        ).astype(jnp.float32),
        lax.psum_scatter(
            grad_up.astype(jnp.bfloat16), "dp", scatter_dimension=0, tiled=True
        ).astype(jnp.float32),
        lax.psum_scatter(
            grad_out.astype(jnp.bfloat16), "dp", scatter_dimension=0, tiled=True
        ).astype(jnp.float32),
        lax.psum_scatter(
            grad_down.astype(jnp.bfloat16), "dp", scatter_dimension=0, tiled=True
        ).astype(jnp.float32),
    )

    def placed(vector, length):
        return lax.dynamic_update_slice_in_dim(
            jnp.zeros((length,), jnp.float32), vector, my_index * vector.shape[0], 0
        )

    vector_grads = (
        lax.psum_scatter(
            placed(grad_bias_query, width), ("dp", "tensor"), scatter_dimension=0, tiled=True
        ),
        lax.psum_scatter(
            placed(grad_bias_value, width), ("dp", "tensor"), scatter_dimension=0, tiled=True
        ),
        lax.psum_scatter(grad_bias_out, ("dp", "tensor"), scatter_dimension=0, tiled=True),
        lax.psum_scatter(
            placed(grad_bias_up, hidden_cols * tensor_size),
            ("dp", "tensor"),
            scatter_dimension=0,
            tiled=True,
        ),
        lax.psum_scatter(grad_bias_down, ("dp", "tensor"), scatter_dimension=0, tiled=True),
        lax.psum_scatter(grad_gain_first, ("dp", "tensor"), scatter_dimension=0, tiled=True),
        lax.psum_scatter(grad_shift_first, ("dp", "tensor"), scatter_dimension=0, tiled=True),
        lax.psum_scatter(grad_gain_second, ("dp", "tensor"), scatter_dimension=0, tiled=True),
        lax.psum_scatter(grad_shift_second, ("dp", "tensor"), scatter_dimension=0, tiled=True),
    )
    return (
        layer_output.astype(jnp.bfloat16),
        input_grad,
        weight_grads[0],
        weight_grads[1],
        weight_grads[2],
        weight_grads[3],
        weight_grads[4],
        weight_grads[5],
        vector_grads[0],
        vector_grads[1],
        vector_grads[2],
        vector_grads[3],
        vector_grads[4],
        vector_grads[5],
        vector_grads[6],
        vector_grads[7],
        vector_grads[8],
    )


def solution(mesh):
    return jax.shard_map(
        shards,
        mesh=mesh,
        in_specs=(
            P("dp", "tensor", None),
            P("dp", None),
            P("dp", "tensor"),
            P("dp", "tensor"),
            P("dp", "tensor"),
            P("dp", "tensor"),
            P("dp", "tensor"),
            P("dp", "tensor"),
            P(("dp", "tensor")),
            P(("dp", "tensor")),
            P(("dp", "tensor")),
            P(("dp", "tensor")),
            P(("dp", "tensor")),
            P(("dp", "tensor")),
            P(("dp", "tensor")),
            P(("dp", "tensor")),
            P(("dp", "tensor")),
            P("dp", "tensor", None),
        ),
        out_specs=(
            P("dp", "tensor", None),
            P("dp", "tensor", None),
            P("dp", "tensor"),
            P("dp", "tensor"),
            P("dp", "tensor"),
            P("dp", "tensor"),
            P("dp", "tensor"),
            P("dp", "tensor"),
            P(("dp", "tensor")),
            P(("dp", "tensor")),
            P(("dp", "tensor")),
            P(("dp", "tensor")),
            P(("dp", "tensor")),
            P(("dp", "tensor")),
            P(("dp", "tensor")),
            P(("dp", "tensor")),
            P(("dp", "tensor")),
        ),
        check_vma=False,
    )
```

profile of v0, /device:TPU:0, one launch (start us, length us, event | category | flops | bytes accessed | tf_op | source)
XLA Modules:
  0.0 1810.2 jit_solution(10851095950138427711)
XLA Ops:
  14.8 69.0 %all-reduce.19 = (f32[768]{0:T(1024)S(1)}, f32[768]{0:T(1024)S(1)}, f32[768]{0:T(1024)S(1)}, f32[768]{0:T(1024)S(1)}, f32[768]{0:T(1024)S(1)}, /*index=5*/f32[3072]{0:T(1024)}, f32[768]{0:T(1024)}, f32[768]{0:T(1024)S(1)}) all-reduce(f32[768]{0:T(1024)S(1)} %dynamic-update-slice.1, ...), channel_id=1, replica_groups=mesh['dp'=32,'tensor'=4] {'dp','tensor'}, use_global_device_ids=true, to_apply=%add.1 | all-reduce | flops 8448 | bytes 67584
  83.9 9.6 all_gather.66
  93.6 79.7 %all_gather.63 = bf16[768,192]{1,0:T(8,128)(2,1)S(1)} all-gather(bf16[24,192]{1,0:T(8,128)(2,1)} %param.20), channel_id=1, replica_groups=mesh['dp'=32,'tensor'=4] {'dp'}, dimensions={0}, use_global_device_ids=true | all-gather | bytes 304128 | tf_op jit(solution)/shard_map/all_gather | solution.py:130
  173.3 77.9 %all_gather.64 = bf16[768,192]{1,0:T(8,128)(2,1)S(1)} all-gather(bf16[24,192]{1,0:T(8,128)(2,1)} %param.21), channel_id=1, replica_groups=mesh['dp'=32,'tensor'=4] {'dp'}, dimensions={0}, use_global_device_ids=true | all-gather | bytes 304128 | tf_op jit(solution)/shard_map/all_gather | solution.py:131
  251.2 79.0 %all_gather.65 = bf16[768,192]{1,0:T(8,128)(2,1)S(1)} all-gather(bf16[24,192]{1,0:T(8,128)(2,1)S(1)} %copy-done.38), channel_id=1, replica_groups=mesh['dp'=32,'tensor'=4] {'dp'}, dimensions={0}, use_global_device_ids=true | all-gather | bytes 304128 | tf_op jit(solution)/shard_map/all_gather | solution.py:132
  335.4 77.7 %all_gather.69 = bf16[768,192]{1,0:T(8,128)(2,1)S(1)} all-gather(bf16[24,192]{1,0:T(8,128)(2,1)S(1)} %copy-done.39), channel_id=1, replica_groups=mesh['dp'=32,'tensor'=4] {'dp'}, dimensions={0}, use_global_device_ids=true | all-gather | bytes 304128 | tf_op jit(solution)/shard_map/all_gather | solution.py:134
  413.1 1.6 convolution_bitcast_fusion
  416.0 1.4 dynamic_slice.27
  417.3 29.4 %reduce-scatter.17.cloned.1.call-done = f32[1,128,768]{2,1,0:T(8,128)} async-done(((f32[1,512,768]{2,1,0:T(8,128)}), f32[1,128,768]{2,1,0:T(8,128)}) %reduce-scatter.17.cloned.1.call-update) | async-done | bytes 393232 | tf_op jit(solution)/shard_map/reduce_scatter | solution.py:171
  446.7 1.2 fusion.83
  448.8 10.2 all_gather.73
  459.0 106.9 %all-gather.3.cloned.1.call-done = bf16[768,768]{1,0:T(8,128)(2,1)} async-done(((bf16[24,768]{1,0:T(8,128)(2,1)}), bf16[768,768]{1,0:T(8,128)(2,1)}) %all-gather.3.cloned.1.call-update) | async-done | bytes 1179664 | tf_op jit(solution)/shard_map/all_gather | solution.py:133
  565.9 3.9 multiply_convert_fusion
  569.7 150.1 %all-gather.5.cloned.1.call-done = bf16[768,768]{1,0:T(8,128)(2,1)} async-done(((bf16[24,768]{1,0:T(8,128)(2,1)}), bf16[768,768]{1,0:T(8,128)(2,1)}) %all-gather.5.cloned.1.call-update) | async-done | bytes 1179664 | tf_op jit(solution)/shard_map/all_gather | solution.py:135
  719.9 3.5 convolution_bitcast_fusion.2
  723.4 35.3 %reduce-scatter.19.cloned.1.call-done = f32[1,128,768]{2,1,0:T(8,128)} async-done(((f32[1,512,768]{2,1,0:T(8,128)}), f32[1,128,768]{2,1,0:T(8,128)}) %reduce-scatter.19.cloned.1.call-update) | async-done | bytes 393232 | tf_op jit(solution)/shard_map/reduce_scatter | solution.py:181
  758.8 1.4 fusion.82
  760.4 1.9 fusion.45
  762.3 1.7 convert_reduce_fusion.2
  764.0 9.9 all_gather.80
  773.9 1.7 convert_reduce_fusion
  775.6 0.9 copy-done.58
  776.5 2.0 convolution_bitcast_fusion.1
  778.6 3.2 convolution_convert_fusion
  783.3 1.3 log_add_fusion.2
  784.5 3.2 convolution_convert_fusion.1
  787.8 25.4 %reduce-scatter.21.cloned.1.call-done = f32[1,128,768]{2,1,0:T(8,128)} async-done(((f32[1,512,768]{2,1,0:T(8,128)}), f32[1,128,768]{2,1,0:T(8,128)}) %reduce-scatter.21.cloned.1.call-update) | async-done | bytes 393232 | tf_op jit(solution)/shard_map/reduce_scatter | solution.py:206
  813.2 2.3 multiply_reduce_fusion.3
  815.5 2.3 convert_reduce_fusion.3
  817.8 9.7 all_gather.81
  833.6 0.9 constant_dynamic-update-slice_fusion.2
  836.0 0.9 copy.41
  836.9 0.9 copy.43
  838.0 0.9 copy.45
  839.0 1.2 convolution_convert_fusion.4
  840.4 3.0 fusion.8
  844.0 132.4 %reduce-scatter.29.cloned.1.call-done = bf16[24,768]{1,0:T(8,128)(2,1)} async-done(((bf16[768,768]{1,0:T(8,128)(2,1)}), bf16[24,768]{1,0:T(8,128)(2,1)}) %reduce-scatter.29.cloned.1.call-update) | async-done | bytes 36880 | tf_op jit(solution)/shard_map/reduce_scatter | solution.py:252
  976.4 1.4 convert_element_type.158
  977.8 158.8 %reduce-scatter.25.cloned.1.call-done = bf16[24,768]{1,0:T(8,128)(2,1)} async-done(((bf16[768,768]{1,0:T(8,128)(2,1)}), bf16[24,768]{1,0:T(8,128)(2,1)}) %reduce-scatter.25.cloned.1.call-update) | async-done | bytes 36880 | tf_op jit(solution)/shard_map/reduce_scatter | solution.py:246
  1136.6 1.4 convert_element_type.154
  1138.8 64.6 %all-reduce.18 = (f32[768]{0:T(1024)S(1)}, f32[768]{0:T(1024)S(1)}, f32[768]{0:T(1024)S(1)}, f32[768]{0:T(1024)S(1)}, f32[3072]{0:T(1024)S(1)}, /*index=5*/f32[7...) all-reduce(f32[768]{0:T(1024)S(1)} %dynamic-update-slice.8, ...), channel_id=1, replica_groups=mesh['dp'=32,'tensor'=4] {'dp','tensor'}, use_global_device_ids=true, to_apply=%add.8 | all-reduce | flops 9984 | bytes 79872
  1209.4 86.6 %reduce-scatter.31.cloned.1.call-done = bf16[24,192]{1,0:T(8,128)(2,1)} async-done(((bf16[768,192]{1,0:T(8,128)(2,1)}), bf16[24,192]{1,0:T(8,128)(2,1)}) %reduce-scatter.31.cloned.1.call-update) | async-done | bytes 9232
  1297.5 157.2 %reduce-scatter.33.cloned.1.call-done = bf16[24,192]{1,0:T(8,128)(2,1)} async-done(((bf16[768,192]{1,0:T(8,128)(2,1)}), bf16[24,192]{1,0:T(8,128)(2,1)}) %reduce-scatter.33.cloned.1.call-update) | async-done | bytes 9232
  1456.3 157.3 %reduce-scatter.35.cloned.1.call-done = bf16[24,192]{1,0:T(8,128)(2,1)} async-done(((bf16[768,192]{1,0:T(8,128)(2,1)}), bf16[24,192]{1,0:T(8,128)(2,1)}) %reduce-scatter.35.cloned.1.call-update) | async-done | bytes 9232
  1615.1 157.3 %reduce-scatter.27.cloned.1.call-done = bf16[24,192]{1,0:T(8,128)(2,1)} async-done(((bf16[768,192]{1,0:T(8,128)(2,1)}), bf16[24,192]{1,0:T(8,128)(2,1)}) %reduce-scatter.27.cloned.1.call-update) | async-done | bytes 9232 | tf_op jit(solution)/shard_map/reduce_scatter | solution.py:249
  1772.4 1.3 convert_element_type.156
  1773.7 27.4 %reduce-scatter.23.cloned.1.call-done = bf16[1,128,768]{2,1,0:T(8,128)(2,1)} async-done(((bf16[1,512,768]{2,1,0:T(8,128)(2,1)}), bf16[1,128,768]{2,1,0:T(8,128)(2,1)}) %reduce-scatter.23.cloned.1.call-update) | async-done | bytes 196624 | tf_op jit(solution)/shard_map/reduce_scatter | solution.py:230
  1801.1 1.7 convert_add_fusion
  (228 shorter events, 35.6 us)
Async XLA Ops:
  8.0 243.1 %copy-start.38 = (bf16[24,192]{1,0:T(8,128)(2,1)S(1)}, bf16[24,192]{1,0:T(8,128)(2,1)}, u32[]{:S(2)}) copy-start(bf16[24,192]{1,0:T(8,128)(2,1)} %param.22) | copy-start | bytes 27652
  8.0 438.7 %reduce-scatter.17.cloned.1.call-start = ((), (), s32[]{:S(2)}) async-start(), calls=%async_computation.10 | async-start | bytes 1966080 | tf_op jit(solution)/shard_map/reduce_scatter | solution.py:171
  93.5 237.6 %copy-start.7 = (bf16[1,512,768]{2,1,0:T(8,128)(2,1)}, bf16[1,512,768]{2,1,0:T(8,128)(2,1)S(1)}, u32[]{:S(2)}) copy-start(bf16[1,512,768]{2,1,0:T(8,128)(2,1)S(1)} %all_gather.66) | copy-start | bytes 2359300
  173.3 157.9 %copy-start.12 = (bf16[768,192]{1,0:T(8,128)(2,1)}, bf16[768,192]{1,0:T(8,128)(2,1)S(1)}, u32[]{:S(2)}) copy-start(bf16[768,192]{1,0:T(8,128)(2,1)S(1)} %all_gather.63) | copy-start | bytes 884740
  251.2 80.0 %copy-start.14 = (bf16[768,192]{1,0:T(8,128)(2,1)}, bf16[768,192]{1,0:T(8,128)(2,1)S(1)}, u32[]{:S(2)}) copy-start(bf16[768,192]{1,0:T(8,128)(2,1)S(1)} %all_gather.64) | copy-start | bytes 884740
  333.1 80.0 %copy-start.22 = (bf16[512,64]{0,1:T(8,128)(2,1)}, bf16[512,64]{0,1:T(8,128)(2,1)S(1)}, u32[]{:S(2)}) copy-start(bf16[512,64]{0,1:T(8,128)(2,1)S(1)} %convolution_convert_fusion.8) | copy-start | bytes 196612
  333.9 79.2 %copy-start.24 = (bf16[512,64]{0,1:T(8,128)(2,1)}, bf16[512,64]{0,1:T(8,128)(2,1)S(1)}, u32[]{:S(2)}) copy-start(bf16[512,64]{0,1:T(8,128)(2,1)S(1)} %convolution_convert_fusion.7) | copy-start | bytes 196612
  335.4 77.7 %copy-start.26 = (bf16[512,64]{0,1:T(8,128)(2,1)}, bf16[512,64]{0,1:T(8,128)(2,1)S(1)}, u32[]{:S(2)}) copy-start(bf16[512,64]{0,1:T(8,128)(2,1)S(1)} %convolution_convert_fusion.6) | copy-start | bytes 196612
  414.7 151.1 %all-gather.3.cloned.1.call-start = ((), (), s32[]{:S(2)}) async-start(), calls=%async_computation.11 | async-start | bytes 1216512 | tf_op jit(solution)/shard_map/all_gather | solution.py:133
  415.3 304.6 %all-gather.5.cloned.1.call-start = ((), (), s32[]{:S(2)}) async-start(), calls=%async_computation.12 | async-start | bytes 1216512 | tf_op jit(solution)/shard_map/all_gather | solution.py:135
  415.9 342.9 %reduce-scatter.19.cloned.1.call-start = ((), (), s32[]{:S(2)}) async-start(), calls=%async_computation.13 | async-start | bytes 1966080 | tf_op jit(solution)/shard_map/reduce_scatter | solution.py:181
  447.9 121.8 %copy-start = (f32[1,128,768]{2,1,0:T(8,128)}, f32[1,128,768]{2,1,0:T(8,128)S(1)}, u32[]{:S(2)}) copy-start(f32[1,128,768]{2,1,0:T(8,128)S(1)} %get-tuple-element.119) | copy-start | bytes 1179652
  447.9 310.8 %copy-start.35 = (f32[128]{0:T(128)}, f32[128]{0:T(128)S(1)}, u32[]{:S(2)}) copy-start(f32[128]{0:T(128)S(1)} %broadcast_multiply_fusion.5) | copy-start | bytes 1540
  723.4 89.8 %reduce-scatter.21.cloned.1.call-start = ((), (), s32[]{:S(2)}) async-start(), calls=%async_computation.14 | async-start | bytes 1966080 | tf_op jit(solution)/shard_map/reduce_scatter | solution.py:206
  760.2 13.7 copy-start.55
  760.2 13.7 copy-start.59
  760.2 13.7 copy-start.36
  760.4 13.5 copy-start.41
  762.3 11.6 copy-start.51
  762.3 11.6 copy-start.52
  778.5 3.3 copy-start.47
  778.5 197.9 %reduce-scatter.29.cloned.1.call-start = ((), (), s32[]{:S(2)}) async-start(), calls=%async_computation.18 | async-start | bytes 1216512 | tf_op jit(solution)/shard_map/reduce_scatter | solution.py:252
  781.8 354.7 %reduce-scatter.25.cloned.1.call-start = ((), (), s32[]{:S(2)}) async-start(), calls=%async_computation.16 | async-start | bytes 1216512 | tf_op jit(solution)/shard_map/reduce_scatter | solution.py:246
  787.7 508.3 %reduce-scatter.31.cloned.1.call-start = ((), (), s32[]{:S(2)}) async-start(), calls=%async_computation.19 | async-start | bytes 405504
  815.5 12.0 copy-start.3
  815.5 12.4 copy-start.11
  836.0 3.0 copy-start.23
  836.0 3.0 copy-start.25
  836.0 3.0 copy-start.27
  836.9 617.9 %reduce-scatter.33.cloned.1.call-start = ((), (), s32[]{:S(2)}) async-start(), calls=%async_computation.20 | async-start | bytes 405504
  837.9 775.7 %reduce-scatter.35.cloned.1.call-start = ((), (), s32[]{:S(2)}) async-start(), calls=%async_computation.21 | async-start | bytes 405504
  838.9 933.5 %reduce-scatter.27.cloned.1.call-start = ((), (), s32[]{:S(2)}) async-start(), calls=%async_computation.17 | async-start | bytes 405504 | tf_op jit(solution)/shard_map/reduce_scatter | solution.py:249
  840.2 3.3 copy-start.57
  840.2 3.5 copy-start.53
  840.2 297.7 %copy-start.18 = (bf16[512,64]{0,1:T(8,128)(2,1)S(1)}, bf16[512,64]{0,1:T(8,128)(2,1)}, u32[]{:S(2)}) copy-start(bf16[512,64]{0,1:T(8,128)(2,1)} %get-tuple-element.146) | copy-start | bytes 196612
  840.2 298.1 %copy-start.19 = (bf16[512,64]{0,1:T(8,128)(2,1)S(1)}, bf16[512,64]{0,1:T(8,128)(2,1)}, u32[]{:S(2)}) copy-start(bf16[512,64]{0,1:T(8,128)(2,1)} %get-tuple-element.140) | copy-start | bytes 196612
  840.3 298.1 %copy-start.20 = (bf16[512,64]{0,1:T(8,128)(2,1)S(1)}, bf16[512,64]{0,1:T(8,128)(2,1)}, u32[]{:S(2)}) copy-start(bf16[512,64]{0,1:T(8,128)(2,1)} %get-tuple-element.142) | copy-start | bytes 196612
  840.3 298.1 %copy-start.21 = (bf16[512,64]{0,1:T(8,128)(2,1)S(1)}, bf16[512,64]{0,1:T(8,128)(2,1)}, u32[]{:S(2)}) copy-start(bf16[512,64]{0,1:T(8,128)(2,1)} %get-tuple-element.144) | copy-start | bytes 196612
  840.3 298.5 %copy-start.29 = (f32[768]{0:T(1024)S(1)}, f32[768]{0:T(1024)}, u32[]{:S(2)}) copy-start(f32[768]{0:T(1024)} %get-tuple-element.86) | copy-start | bytes 9220
  840.3 298.5 %copy-start.30 = (f32[768]{0:T(1024)S(1)}, f32[768]{0:T(1024)}, u32[]{:S(2)}) copy-start(f32[768]{0:T(1024)} %get-tuple-element.91) | copy-start | bytes 9220
  840.3 298.4 %copy-start.31 = (f32[768]{0:T(1024)S(1)}, f32[768]{0:T(1024)}, u32[]{:S(2)}) copy-start(f32[768]{0:T(1024)} %get-tuple-element.110) | copy-start | bytes 9220
  840.3 298.4 %copy-start.32 = (f32[768]{0:T(1024)S(1)}, f32[768]{0:T(1024)}, u32[]{:S(2)}) copy-start(f32[768]{0:T(1024)} %get-tuple-element.84) | copy-start | bytes 9220
  840.3 298.4 %copy-start.33 = (f32[768]{0:T(1024)S(1)}, f32[768]{0:T(1024)}, u32[]{:S(2)}) copy-start(f32[768]{0:T(1024)} %get-tuple-element.89) | copy-start | bytes 9220
  840.3 298.4 %copy-start.34 = (f32[768]{0:T(1024)S(1)}, f32[768]{0:T(1024)}, u32[]{:S(2)}) copy-start(f32[768]{0:T(1024)} %get-tuple-element.112) | copy-start | bytes 9220
  840.3 960.8 %reduce-scatter.23.cloned.1.call-start = ((), (), s32[]{:S(2)}) async-start(), calls=%async_computation.15 | async-start | bytes 983040 | tf_op jit(solution)/shard_map/reduce_scatter | solution.py:230
  843.4 365.2 %copy-start.37 = (f32[128]{0:T(128)S(1)}, f32[128]{0:T(128)}, u32[]{:S(2)}) copy-start(f32[128]{0:T(128)} %copy-done.36) | copy-start | bytes 1540
  843.4 365.2 %copy-start.42 = (f32[128]{0:T(128)S(1)}, f32[128]{0:T(128)}, u32[]{:S(2)}) copy-start(f32[128]{0:T(128)} %copy-done.41) | copy-start | bytes 1540
  843.4 957.7 %copy-start.6 = (f32[1,128,768]{2,1,0:T(8,128)S(1)}, f32[1,128,768]{2,1,0:T(8,128)}, u32[]{:S(2)}) copy-start(f32[1,128,768]{2,1,0:T(8,128)} %get-tuple-element.114) | copy-start | bytes 1179652
  (24 other events, 35.6 us)
Sparse Core Ops, SparseCore 0:
  414.8 31.8 reduce-scatter.16
  723.5 35.2 reduce-scatter.18
  778.6 34.5 reduce-scatter.20
  815.5 160.7 reduce-scatter.28
  978.6 157.9 reduce-scatter.24
  1138.9 157.0 reduce-scatter.30
  1298.4 156.3 reduce-scatter.32
  1457.2 156.3 reduce-scatter.34
  1616.0 156.3 reduce-scatter.26
  1775.1 25.9 reduce-scatter.22
Sparse Core Ops, SparseCore 1:
  416.9 148.9 all-gather.2
  567.5 152.4 all-gather.4
where the time goes:
time: 1810 us
  waiting for transfers between devices  1230 us (68%)
  blocking collectives  487 us (27%)
  matrix products  33.1 us (2%)
  local copies, waits for them, and re-layouts  25.6 us (1%)
  other arithmetic  22.2 us (1%)
    unnamed x15, waiting for transfers between devices  402 us
    reduce_scatter x1, waiting for transfers between devices, shards(): lax.psum_scatter(grad_up.astype(jnp.bfloat16), 'dp', scatter_dimension=0,...  159 us
    reduce_scatter x1, waiting for transfers between devices, shards(): lax.psum_scatter(grad_out.astype(jnp.bfloat16), 'dp', scatter_dimension=0...  157 us
    all_gather x1, waiting for transfers between devices, shards(): lax.all_gather(down_weight, 'dp', axis=0, tiled=True)  150 us
    unnamed x2, blocking collectives  134 us
    reduce_scatter x1, waiting for transfers between devices, shards(): lax.psum_scatter(grad_down.astype(jnp.bfloat16), 'dp', scatter_dimension=...  132 us
    all_gather x1, waiting for transfers between devices, shards(): lax.all_gather(up_weight, 'dp', axis=0, tiled=True)  107 us
    all_gather x1, blocking collectives, shards(): lax.all_gather(q_weight, 'dp', axis=0, tiled=True)  79.7 us
  transfers between devices with their start and end apart: 12, of which 12 were waited for; matrix products, arithmetic and copies ran while one was open for 3% of the time, Pallas kernels for 0%

commit v1 on v0

v1 whole, which is shorter than its diff:
```python
import jax
import jax.numpy as jnp
from jax import lax
from jax.sharding import PartitionSpec as P

HEAD_DIM = 64


NORM_EPSILON = 1e-12
MASKED_SCORE = -1000000000.0
ROOT_HALF = 0.7071067811865476
INV_ROOT_TAU = 0.3989422804014327
LOW = jnp.bfloat16
FULL = jnp.float32


def contract(left, right, left_dim, right_dim):
    return lax.dot_general(
        left, right, (((left_dim,), (right_dim,)), ((), ())), preferred_element_type=jnp.float32
    )


def gelu_exact(values):
    return 0.5 * values * (1.0 + lax.erf(values * ROOT_HALF))


def gelu_slope(values):
    return (
        0.5 * (1.0 + lax.erf(values * ROOT_HALF))
        + values * jnp.exp(-0.5 * values * values) * INV_ROOT_TAU
    )


def norm_forward(values, gain, shift):
    center = values - jnp.mean(values, axis=-1, keepdims=True)
    scale_inv = lax.rsqrt(jnp.mean(center * center, axis=-1, keepdims=True) + NORM_EPSILON)
    normed = center * scale_inv
    return (normed * gain + shift, normed, scale_inv)


def norm_backward(upstream, normed, scale_inv, gain):
    scaled = upstream * gain
    return scale_inv * (
        scaled
        - jnp.mean(scaled, axis=-1, keepdims=True)
        - normed * jnp.mean(scaled * normed, axis=-1, keepdims=True)
    )


def swap(values, mask):
    return lax.ppermute(values, "tensor", [(i, i ^ mask) for i in range(4)])


def after(values, *others):
    return lax.optimization_barrier((values, *others))[0]


def spread(block):
    count = lax.axis_size("dp")
    stacked = jnp.broadcast_to(block[None], (count, *block.shape))
    return lax.all_to_all(stacked, "dp", 0, 0, tiled=True).reshape(-1, block.shape[1])


def gathered_sum(values):
    count = lax.axis_size("dp")
    blocks = values.astype(LOW).reshape(count, values.shape[0] // count, values.shape[1])
    got = lax.all_to_all(blocks, "dp", 0, 0, tiled=True)
    return got


def halves(values):
    high = lax.reduce_precision(values, 8, 7)
    return (high.astype(LOW), (values - high).astype(LOW))


def core_sum(part):
    half = part.shape[0] // 2
    got = swap(part[half:].astype(LOW), 1)
    return part[:half] + got.astype(FULL)


def far_sum(total):
    quarter = total.shape[0] // 2
    sent = total.astype(LOW)
    sent = jnp.concatenate([sent[quarter:], sent[:quarter]], axis=0)
    return swap(sent, 2)


def core_join(rows):
    return jnp.concatenate([rows, swap(rows, 1)], axis=0)


def ordered_segments(segment_row, my_index):
    quarters = segment_row.reshape(4, -1)
    core = my_index % 2 == 1
    quarters = jnp.where(core, quarters[jnp.array([1, 0, 3, 2])], quarters)
    far = my_index // 2 == 1
    quarters = jnp.where(far, quarters[jnp.array([2, 3, 0, 1])], quarters)
    return jnp.concatenate([quarters[0], quarters[2], quarters[1], quarters[3]])


def attend_forward(qkv_rows, same_doc, head_count, head_cols):
    outputs = []
    kept = []
    for head in range(head_count):
        offset = head * HEAD_DIM
        query = qkv_rows[:, offset : offset + HEAD_DIM]
        key = qkv_rows[:, head_cols + offset : head_cols + offset + HEAD_DIM]
        value = qkv_rows[:, 2 * head_cols + offset : 2 * head_cols + offset + HEAD_DIM]
        scores = jnp.where(
            same_doc, HEAD_DIM ** (-0.5) * contract(query, key, 1, 1), MASKED_SCORE
        )
        highest = jnp.max(scores, axis=-1, keepdims=True)
        shifted = jnp.exp(scores - highest)
        row_total = jnp.sum(shifted, axis=-1, keepdims=True)
        probs_low = (shifted / row_total).astype(LOW)
        outputs.append(jnp.dot(probs_low, value, preferred_element_type=FULL))
        kept.append(highest + jnp.log(row_total))
    return (jnp.concatenate(outputs, axis=1).astype(LOW), kept)


def attend_backward(qkv_rows, same_doc, kept, grad_rows, head_count, head_cols):
    query_grads = []
    key_grads = []
    value_grads = []
    for head in range(head_count):
        offset = head * HEAD_DIM
        query = qkv_rows[:, offset : offset + HEAD_DIM]
        key = qkv_rows[:, head_cols + offset : head_cols + offset + HEAD_DIM]
        value = qkv_rows[:, 2 * head_cols + offset : 2 * head_cols + offset + HEAD_DIM]
        scores = jnp.where(
            same_doc, HEAD_DIM ** (-0.5) * contract(query, key, 1, 1), MASKED_SCORE
        )
        probs = jnp.exp(scores - kept[head])
        grad_head = grad_rows[:, offset : offset + HEAD_DIM]
        value_grads.append(contract(probs.astype(LOW), grad_head, 0, 0))
        probs_grad = contract(grad_head, value, 1, 1)
        scores_grad = probs * (probs_grad - jnp.sum(probs * probs_grad, axis=-1, keepdims=True))
        scores_low = scores_grad.astype(LOW)
        query_grads.append(
            HEAD_DIM ** (-0.5) * jnp.dot(scores_low, key, preferred_element_type=FULL)
        )
        key_grads.append(HEAD_DIM ** (-0.5) * contract(scores_low, query, 0, 0))
    return jnp.concatenate(query_grads + key_grads + value_grads, axis=1).astype(LOW)


def shards(
    tokens,
    segments,
    q_weight,
    k_weight,
    v_weight,
    up_weight,
    out_weight,
    down_weight,
    q_bias,
    v_bias,
    out_bias,
    up_bias,
    down_bias,
    norm1_gain,
    norm1_shift,
    norm2_gain,
    norm2_shift,
    cotangent,
):
    my_index = lax.axis_index("tensor")
    local_len, width = tokens.shape[1:]
    head_cols = q_weight.shape[1]
    head_count = head_cols // HEAD_DIM
    tokens = tokens[0]
    cotangent = cotangent[0]

    vector_rows = q_bias.shape[0]
    columns = jnp.stack(
        [q_bias, v_bias, out_bias, down_bias, norm1_gain, norm1_shift, norm2_gain, norm2_shift],
        axis=1,
    )
    columns = jnp.concatenate([columns, up_bias.reshape(vector_rows, 4)], axis=1)
    column_count = columns.shape[1]
    high, low = halves(columns)
    packed = jnp.pad(
        jnp.concatenate([high, low], axis=1), ((0, 2), (0, 128 - 2 * column_count))
    )
    near = [packed] + [swap(packed, mask) for mask in (1, 2, 3)]
    tokens_far = swap(tokens, 2)
    up_full = spread(up_weight)

    near = [block[:vector_rows] for block in near]
    core = my_index % 2 == 1
    near = [
        jnp.where(core, near[1], near[0]),
        jnp.where(core, near[0], near[1]),
        jnp.where(core, near[3], near[2]),
        jnp.where(core, near[2], near[3]),
    ]
    far = my_index // 2 == 1
    near = jnp.concatenate(
        [
            jnp.where(far, near[2], near[0]),
            jnp.where(far, near[3], near[1]),
            jnp.where(far, near[0], near[2]),
            jnp.where(far, near[1], near[3]),
        ],
        axis=0,
    )
    first_block = jnp.concatenate([q_weight, k_weight, v_weight, out_weight, near], axis=1)
    first_block, tokens_pair = lax.optimization_barrier(
        (first_block, jnp.concatenate([tokens, tokens_far], axis=0), up_full)
    )[:2]
    tokens_full = core_join(tokens_pair)
    cotangent_far = swap(after(cotangent, tokens_far), 2)
    first_full = spread(first_block)
    qkv_weight = first_full[:, : 3 * head_cols]
    out_full = first_full[:, 3 * head_cols : 4 * head_cols]
    vectors = first_full[:, 4 * head_cols :].astype(FULL)
    vectors = vectors[:, :column_count] + vectors[:, column_count : 2 * column_count]
    rows = vectors[:, :8].T
    gain_first, shift_first, gain_second, shift_second = rows[4], rows[5], rows[6], rows[7]
    bias_out, bias_down = rows[2], rows[3]
    own = lax.dynamic_slice_in_dim(vectors, my_index * head_cols, head_cols, axis=0)
    bias_up = own[:, 8:12].reshape(-1)
    qkv_bias = jnp.concatenate([own[:, 0], jnp.zeros((head_cols,), FULL), own[:, 1]])

    segment_row = ordered_segments(segments[0], my_index)
    same_doc = segment_row[:, None] == segment_row[None, :]
    qkv_rows = (jnp.dot(tokens_full, qkv_weight, preferred_element_type=FULL) + qkv_bias).astype(
        LOW
    )
    mixed_rows, kept = attend_forward(qkv_rows, same_doc, head_count, head_cols)
    attn_chip = core_sum(contract(mixed_rows, out_full, 1, 1))
    attn_far = far_sum(attn_chip)
    down_full = spread(after(down_weight, attn_chip))
    attn_chip, attn_far, down_full = lax.optimization_barrier((attn_chip, attn_far, down_full))
    first, normed_first, inv_first = norm_forward(
        tokens_pair.astype(FULL) + (attn_chip + attn_far.astype(FULL)) + bias_out,
        gain_first,
        shift_first,
    )
    hidden_full = core_join(first.astype(LOW))
    upward = jnp.dot(hidden_full, up_full, preferred_element_type=FULL) + bias_up
    active = gelu_exact(upward).astype(LOW)
    branch_chip = core_sum(contract(active, down_full, 1, 1))
    branch = branch_chip + far_sum(branch_chip).astype(FULL)
    layer_output, normed_second, inv_second = norm_forward(
        first + branch + bias_down, gain_second, shift_second
    )

    cotangent_pair = jnp.concatenate([cotangent, cotangent_far], axis=0).astype(FULL)
    second_grad = norm_backward(cotangent_pair, normed_second, inv_second, gain_second)
    cotangent_own = cotangent_pair[:local_len]
    grad_gain_second = jnp.sum(cotangent_own * normed_second[:local_len], axis=0)
    grad_shift_second = jnp.sum(cotangent_own, axis=0)
    branch_low = second_grad.astype(LOW)
    grad_bias_down = jnp.sum(branch_low[:local_len].astype(FULL), axis=0)
    branch_full = core_join(branch_low)
    active_grad = jnp.dot(branch_full, down_full, preferred_element_type=FULL)
    upward_grad = (active_grad * gelu_slope(upward)).astype(LOW)
    hidden_chip = core_sum(contract(upward_grad, up_full, 1, 1))
    grad_down = contract(branch_full, active, 0, 0)
    hidden_far = far_sum(hidden_chip)
    down_blocks = gathered_sum(after(grad_down, hidden_chip))
    hidden_chip, hidden_far, down_blocks = lax.optimization_barrier(
        (hidden_chip, hidden_far, down_blocks)
    )
    grad_bias_up = jnp.sum(upward_grad.astype(FULL), axis=0)
    grad_up = contract(hidden_full, upward_grad, 0, 0)
    first_grad = second_grad + (hidden_chip + hidden_far.astype(FULL))
    resid_grad = norm_backward(first_grad, normed_first, inv_first, gain_first)
    first_own = first_grad[:local_len]
    grad_gain_first = jnp.sum(first_own * normed_first[:local_len], axis=0)
    grad_shift_first = jnp.sum(first_own, axis=0)
    attended_low = resid_grad.astype(LOW)
    grad_bias_out = jnp.sum(attended_low[:local_len].astype(FULL), axis=0)
    attended_full = core_join(attended_low)
    mixed_grad = jnp.dot(attended_full, out_full, preferred_element_type=FULL).astype(LOW)
    qkv_grad = attend_backward(qkv_rows, same_doc, kept, mixed_grad, head_count, head_cols)

    grad_bias_query = jnp.sum(qkv_grad[:, :head_cols].astype(FULL), axis=0)
    grad_bias_value = jnp.sum(qkv_grad[:, 2 * head_cols :].astype(FULL), axis=0)
    sharded = jnp.concatenate(
        [grad_bias_query[None], grad_bias_value[None], grad_bias_up.reshape(head_cols, 4).T], axis=0
    )
    sharded = lax.dynamic_update_slice_in_dim(
        jnp.zeros((6, width), FULL), sharded, my_index * head_cols, 1
    )
    vector_sums = jnp.concatenate(
        [
            grad_bias_out[None],
            grad_bias_down[None],
            grad_gain_first[None],
            grad_shift_first[None],
            grad_gain_second[None],
            grad_shift_second[None],
            sharded,
        ],
        axis=0,
    )
    vector_near = [swap(vector_sums, mask) for mask in (1, 2, 3)]
    input_chip = core_sum(contract(qkv_grad, qkv_weight, 1, 1))
    input_far = swap(input_chip[local_len:].astype(LOW), 2)
    up_blocks = gathered_sum(after(grad_up, qkv_grad))
    vector_sums = vector_sums + vector_near[0] + vector_near[1] + vector_near[2]
    grad_qkv = contract(tokens_full, qkv_grad, 0, 0)
    grad_out = contract(attended_full, mixed_rows, 0, 0)
    high, low = halves(vector_sums.T)
    last_block = jnp.concatenate(
        [
            grad_qkv.astype(LOW),
            grad_out.astype(LOW),
            high,
            low,
            jnp.zeros((width, 128 - 2 * column_count), LOW),
        ],
        axis=1,
    )
    last_blocks = gathered_sum(after(last_block, up_blocks))
    input_grad = resid_grad[:local_len] + (input_chip[:local_len] + input_far.astype(FULL))

    down_sum = jnp.sum(down_blocks.astype(FULL), axis=0)
    up_sum = jnp.sum(up_blocks.astype(FULL), axis=0)
    last_sum = jnp.sum(last_blocks.astype(FULL), axis=0)
    columns = last_sum[:, 4 * head_cols :]
    columns = columns[:, :column_count] + columns[:, column_count : 2 * column_count]
    columns = lax.dynamic_slice_in_dim(columns, my_index * vector_rows, vector_rows, axis=0)
    return (
        layer_output[:local_len].astype(LOW)[None],
        input_grad[None],
        last_sum[:, :head_cols],
        last_sum[:, head_cols : 2 * head_cols],
        last_sum[:, 2 * head_cols : 3 * head_cols],
        up_sum,
        last_sum[:, 3 * head_cols : 4 * head_cols],
        down_sum,
        columns[:, 6],
        columns[:, 7],
        columns[:, 0],
        columns[:, 8:12].reshape(-1),
        columns[:, 1],
        columns[:, 2],
        columns[:, 3],
        columns[:, 4],
        columns[:, 5],
    )


def solution(mesh):
    matrix = P("dp", "tensor")
    vector = P(("dp", "tensor"))
    rows = P("dp", "tensor", None)
    return jax.shard_map(
        shards,
        mesh=mesh,
        in_specs=(rows, P("dp", None)) + (matrix,) * 6 + (vector,) * 9 + (rows,),
        out_specs=(rows, rows) + (matrix,) * 6 + (vector,) * 9,
        check_vma=False,
    )
```

time: 1810 us -> 262 us (0.14)
  waiting for transfers between devices: 1230 us -> 115 us
  blocking collectives: 487 us -> 0 us
  starting transfers between devices: 0.5 us -> 67.1 us
    reduce_scatter x7 -> x0, waiting for transfers between devices: 566 us -> none  [the longest x1 159 us: shards(): lax.psum_scatter(grad_up.astype(jnp.bfloat16), 'dp', scatter_dimension=0,...]
    unnamed x15 -> x0, waiting for transfers between devices: 402 us -> none
    all_gather x8 -> x0, blocking collectives: 354 us -> none  [the longest x1 79.7 us: shards(): lax.all_gather(q_weight, 'dp', axis=0, tiled=True)]
    all_gather x2 -> x0, waiting for transfers between devices: 257 us -> none  [the longest x1 150 us: shards(): lax.all_gather(down_weight, 'dp', axis=0, tiled=True)]
    unnamed x2 -> x0, blocking collectives: 134 us -> none
    ppermute x0 -> x20, waiting for transfers between devices: none -> 96 us  [swap(): return lax.ppermute(values, 'tensor', [(i, i ^ mask) for i in range(4)])]
    all_to_all x0 -> x6, starting transfers between devices: none -> 44.6 us  [the longest x3 23.1 us: gathered_sum(): got = lax.all_to_all(blocks, 'dp', 0, 0, tiled=True)]
    ppermute x0 -> x20, starting transfers between devices: none -> 22.4 us  [swap(): return lax.ppermute(values, 'tensor', [(i, i ^ mask) for i in range(4)])]
  transfers between devices with their start and end apart: 12 -> 26, of which waited for: 12 -> 17; matrix products, arithmetic and copies ran while one was open for 3% -> 12% of each run, Pallas kernels for 0% -> 0%
where the time goes in v1:
time: 262 us; the launch traced here: 259 us
  waiting for transfers between devices  115 us (44%)
  starting transfers between devices  67.1 us (26%)
  matrix products  29.3 us (11%)
  local copies, waits for them, and re-layouts  24.5 us (9%)
  other arithmetic  21.2 us (8%)
    ppermute x20, waiting for transfers between devices, swap(): return lax.ppermute(values, 'tensor', [(i, i ^ mask) for i in range(4)])  96 us
    all_to_all x3, starting transfers between devices, gathered_sum(): got = lax.all_to_all(blocks, 'dp', 0, 0, tiled=True)  23.1 us
    ppermute x20, starting transfers between devices, swap(): return lax.ppermute(values, 'tensor', [(i, i ^ mask) for i in range(4)])  22.4 us
    all_to_all x3, starting transfers between devices, spread(): lax.all_to_all(stacked, 'dp', 0, 0, tiled=True).reshape(-1, block.shape[1])  21.6 us
    dot_general x20, matrix products, contract(): lax.dot_general(left, right, (((left_dim,), (right_dim,)), ((), ())), pre...  18 us
    all_to_all x3, waiting for transfers between devices, spread(): lax.all_to_all(stacked, 'dp', 0, 0, tiled=True).reshape(-1, block.shape[1])  17.3 us
  transfers between devices with their start and end apart: 26, of which 17 were waited for; matrix products, arithmetic and copies ran while one was open for 12% of the time, Pallas kernels for 0%

profile of v1, /device:TPU:0, one launch (start us, length us, event | category | flops | bytes accessed | tf_op | source)
XLA Modules:
  0.0 259.0 jit_solution(10186001271912495874)
XLA Ops:
  0.8 1.9 broadcast_in_dim.45
  2.7 9.4 %all-to-all-start = ((bf16[32,24,768]{2,1,0:T(8,128)(2,1)}), bf16[32,24,768]{2,1,0:T(8,128)(2,1)S(1)}, u32[]{:S(2)}, u32[]{:S(2)}) async-start(bf16[32,24,768]{2,1,0:T(8,128)(2,1)} %broadcast_in_dim.45), calls=%async_computation | async-start | bytes 2359296 | tf_op jit(solution)/shard_map/all_to_all | solution.py:61
  13.1 2.1 collective-permute-start
  16.5 2.9 %collective-permute-start.3 = (bf16[128,768]{1,0:T(8,128)(2,1)S(1)}, bf16[128,768]{1,0:T(8,128)(2,1)S(1)}, u32[]{:S(2)}, u32[]{:S(2)}) collective-permute-start(bf16[128,768]{1,0:T(8,128)(2,1)S(1)} %bitcast.70), channel_id=1, source_target_pairs={{0,2},{1,3},{2,0},{3,1},{4,6},{5,7},{6,4},{7,5},{8,10},{9,11},{10,... | collective-permute-start | bytes 589832 | tf_op jit(solution)/shard_map/ppermute | solution.py:51
  19.4 3.9 %collective-permute-done.1 = bf16[8,128]{1,0:T(8,128)(2,1)S(1)} collective-permute-done((bf16[8,128]{1,0:T(8,128)(2,1)S(1)}, bf16[8,128]{1,0:T(8,128)(2,1)S(1)}, u32[]{:S(2)}, u32[]{:S(2)}) %collective-permute-start.1) | collective-permute-done | bytes 2080 | tf_op jit(solution)/shard_map/ppermute | solution.py:51
  23.5 8.8 %collective-permute-done.3 = bf16[128,768]{1,0:T(8,128)(2,1)S(1)} collective-permute-done((bf16[128,768]{1,0:T(8,128)(2,1)S(1)}, bf16[128,768]{1,0:T(8,128)(2,1)S(1)}, u32[]{:S(2)}, u32[]{:S(2)}) %collective-permute-start.3) | collective-permute-done | bytes 196640 | tf_op jit(solution)/shard_map/ppermute | solution.py:51
  33.9 7.5 %all-to-all-start.1 = ((bf16[32,24,896]{2,1,0:T(8,128)(2,1)}), bf16[32,24,896]{2,1,0:T(8,128)(2,1)S(1)}, u32[]{:S(2)}, u32[]{:S(2)}) async-start(bf16[32,24,896]{2,1,0:T(8,128)(2,1)} %broadcast_in_dim.48), calls=%async_computation.1 | async-start | bytes 2752512 | tf_op jit(solution)/shard_map/all_to_all | solution.py:61
  42.7 1.6 collective-permute-done.4
  44.4 17.3 %all-to-all-done.1 = bf16[32,24,896]{2,1,0:T(8,128)(2,1)S(1)} async-done(((bf16[32,24,896]{2,1,0:T(8,128)(2,1)}), bf16[32,24,896]{2,1,0:T(8,128)(2,1)S(1)}, u32[]{:S(2)}, u32[]{:S(2)}) %all-to-all-start.1) | async-done | bytes 1376288 | tf_op jit(solution)/shard_map/all_to_all | solution.py:61
  66.4 1.6 fusion.39
  68.2 1.7 collective-permute-done.5
  72.1 4.7 %all-to-all-start.2 = ((bf16[32,24,768]{2,1,0:T(8,128)(2,1)}), bf16[32,24,768]{2,1,0:T(8,128)(2,1)}, u32[]{:S(2)}, u32[]{:S(2)}) async-start(bf16[32,24,768]{2,1,0:T(8,128)(2,1)} %broadcast_in_dim.98), calls=%async_computation.2 | async-start | bytes 2359296 | tf_op jit(solution)/shard_map/all_to_all | solution.py:61
  78.0 1.9 collective-permute-start.6
  79.9 1.9 slice_reduce_fusion.1
  81.8 18.9 %collective-permute-done.6 = bf16[256,768]{1,0:T(8,128)(2,1)} collective-permute-done((bf16[256,768]{1,0:T(8,128)(2,1)S(1)}, bf16[256,768]{1,0:T(8,128)(2,1)}, u32[]{:S(2)}, u32[]{:S(2)}) %collective-permute-start.6) | collective-permute-done | bytes 393248 | tf_op jit(solution)/shard_map/ppermute | solution.py:51
  100.7 1.5 fusion.89
  105.8 2.4 multiply_convert_fusion
  108.2 2.1 fusion.99
  110.5 1.6 collective-permute-done.8
  112.3 2.0 collective-permute-start.9
  114.2 1.8 collective-permute-start.10
  116.1 9.9 %collective-permute-done.9 = bf16[256,768]{1,0:T(8,128)(2,1)S(1)} collective-permute-done((bf16[256,768]{1,0:T(8,128)(2,1)S(1)}, bf16[256,768]{1,0:T(8,128)(2,1)S(1)}, u32[]{:S(2)}, u32[]{:S(2)}) %collective-permute-start.9) | collective-permute-done | bytes 393248 | tf_op jit(solution)/shard_map/ppermute | solution.py:51
  126.6 2.8 %collective-permute-done.10 = bf16[128,768]{1,0:T(8,128)(2,1)S(1)} collective-permute-done((bf16[128,768]{1,0:T(8,128)(2,1)S(1)}, bf16[128,768]{1,0:T(8,128)(2,1)S(1)}, u32[]{:S(2)}, u32[]{:S(2)}) %collective-permute-start.10) | collective-permute-done | bytes 196640 | tf_op jit(solution)/shard_map/ppermute | solution.py:51
  131.0 1.7 collective-permute-done.11
  132.7 3.0 %convert_reduce_fusion.3 = (f32[768]{0:T(1024)}, bf16[512,768]{1,0:T(8,128)(2,1)S(1)}) fusion(f32[512,768]{1,0:T(8,128)S(1)} %get-tuple-element.113, bf16[768,768]{1,0:T(8,128)(2,1)} %bitcast.16, bf16[256,768]{1,0:T(8,128)(2,1)S(1)} %collective-permute-done.11, bf16[256,768]{1,0:T(8,128)(2,1)S(1)} %fusion.85), kind=kOutput, calls=%fused_computation.15 | convolution fusion | flops 610270464 | bytes 4328448 | tf_op jit(solution)/shard_map/dot_general | solution.py:257
  137.9 1.8 fusion.32
  140.8 8.2 %all-to-all-start.3 = ((bf16[32,24,768]{2,1,0:T(8,128)(2,1)}), bf16[32,24,768]{2,1,0:T(8,128)(2,1)}, u32[]{:S(2)}, u32[]{:S(2)}) async-start(bf16[32,24,768]{2,1,0:T(8,128)(2,1)} %bitcast.69), calls=%async_computation.3 | async-start | bytes 2359296 | tf_op jit(solution)/shard_map/all_to_all | solution.py:67
  150.9 3.0 %collective-permute-start.13 = (bf16[256,768]{1,0:T(8,128)(2,1)S(1)}, bf16[256,768]{1,0:T(8,128)(2,1)}, u32[]{:S(2)}, u32[]{:S(2)}) collective-permute-start(bf16[256,768]{1,0:T(8,128)(2,1)S(1)} %pad_maximum_fusion.13), channel_id=1, source_target_pairs={{0,2},{1,3},{2,0},{3,1},{4,6},{5,7},{6,4},{7,5},{8,10},{9,11},{10,... | collective-permute-start | bytes 1179656 | tf_op jit(solution)/shard_map/ppermute | solution.py:51
  155.1 18.8 %collective-permute-done.13 = bf16[256,768]{1,0:T(8,128)(2,1)} collective-permute-done((bf16[256,768]{1,0:T(8,128)(2,1)S(1)}, bf16[256,768]{1,0:T(8,128)(2,1)}, u32[]{:S(2)}, u32[]{:S(2)}) %collective-permute-start.13) | collective-permute-done | bytes 393248 | tf_op jit(solution)/shard_map/ppermute | solution.py:51
  173.9 2.3 multiply_reduce_fusion.7
  176.2 2.0 fusion.86
  180.2 1.4 reshape.146
  182.6 3.2 %fusion.33 = bf16[768,768]{1,0:T(8,128)(2,1)} fusion(bf16[512,768]{1,0:T(8,128)(2,1)} %copy-done.72, bf16[256,768]{1,0:T(8,128)(2,1)} %collective-permute-done.7, bf16[256,768]{1,0:T(8,128)(2,1)} %get-tuple-element.77), kind=kOutput, calls=%fused_computation.102 | convolution fusion | flops 605552640 | bytes 2752512 | tf_op jit(solution)/shard_map/dot_general | solution.py:18
  185.8 1.8 convolution_convert_fusion.2
  195.6 8.1 %all-to-all-start.4 = ((bf16[32,24,768]{2,1,0:T(8,128)(2,1)}), bf16[32,24,768]{2,1,0:T(8,128)(2,1)}, u32[]{:S(2)}, u32[]{:S(2)}) async-start(bf16[32,24,768]{2,1,0:T(8,128)(2,1)} %bitcast.68), calls=%async_computation.4 | async-start | bytes 2359296 | tf_op jit(solution)/shard_map/all_to_all | solution.py:67
  205.3 1.6 collective-permute-start.18
  206.8 1.5 collective-permute-start.19
  208.4 1.8 convolution_convert_fusion
  210.2 1.3 convolution_convert_fusion.1
  211.5 8.6 %collective-permute-done.18 = f32[12,768]{1,0:T(8,128)S(1)} collective-permute-done((f32[12,768]{1,0:T(8,128)S(1)}, f32[12,768]{1,0:T(8,128)S(1)}, u32[]{:S(2)}, u32[]{:S(2)}) %collective-permute-start.18) | collective-permute-done | bytes 36896 | tf_op jit(solution)/shard_map/ppermute | solution.py:51
  221.0 1.7 all-to-all-done.4
  222.7 1.6 copy.66
  224.3 6.8 %all-to-all-start.5 = ((bf16[32,24,896]{2,1,0:T(8,128)(2,1)}), bf16[32,24,896]{2,1,0:T(8,128)(2,1)S(1)}, u32[]{:S(2)}, u32[]{:S(2)}) async-start(bf16[32,24,896]{2,1,0:T(8,128)(2,1)} %bitcast.60), calls=%async_computation.5 | async-start | bytes 2752512 | tf_op jit(solution)/shard_map/all_to_all | solution.py:67
  232.1 1.7 collective-permute-done.15
  233.9 3.0 %collective-permute-start.16 = (bf16[128,768]{1,0:T(8,128)(2,1)S(1)}, bf16[128,768]{1,0:T(8,128)(2,1)S(1)}, u32[]{:S(2)}, u32[]{:S(2)}) collective-permute-start(bf16[128,768]{1,0:T(8,128)(2,1)S(1)} %slice.530), channel_id=1, source_target_pairs={{0,2},{1,3},{2,0},{3,1},{4,6},{5,7},{6,4},{7,5},{8,10},{9,11},{10,... | collective-permute-start | bytes 589832 | tf_op jit(solution)/shard_map/ppermute | solution.py:51
  237.0 2.1 convert_reduce_fusion.1
  239.0 14.7 %collective-permute-done.16 = bf16[128,768]{1,0:T(8,128)(2,1)S(1)} collective-permute-done((bf16[128,768]{1,0:T(8,128)(2,1)S(1)}, bf16[128,768]{1,0:T(8,128)(2,1)S(1)}, u32[]{:S(2)}, u32[]{:S(2)}) %collective-permute-start.16) | collective-permute-done | bytes 196640 | tf_op jit(solution)/shard_map/ppermute | solution.py:51
  254.5 2.1 convert_reduce_fusion.2
  (292 shorter events, 43.1 us)
Async XLA Ops:
  0.7 11.5 %copy-start.61 = (f32[6]{0:T(128)S(1)}, f32[6]{0:T(128)}, u32[]{:S(2)}) copy-start(f32[6]{0:T(128)} %param.28) | copy-start | bytes 76
  0.7 11.5 %copy-start.62 = (f32[6]{0:T(128)S(1)}, f32[6]{0:T(128)}, u32[]{:S(2)}) copy-start(f32[6]{0:T(128)} %param.29) | copy-start | bytes 76
  0.7 11.6 %copy-start.63 = (f32[6]{0:T(128)S(1)}, f32[6]{0:T(128)}, u32[]{:S(2)}) copy-start(f32[6]{0:T(128)} %param.30) | copy-start | bytes 76
  0.7 11.7 %copy-start.64 = (f32[6]{0:T(128)S(1)}, f32[6]{0:T(128)}, u32[]{:S(2)}) copy-start(f32[6]{0:T(128)} %param.32) | copy-start | bytes 76
  0.7 11.8 %copy-start.65 = (f32[6]{0:T(128)S(1)}, f32[6]{0:T(128)}, u32[]{:S(2)}) copy-start(f32[6]{0:T(128)} %param.33) | copy-start | bytes 76
  0.7 11.9 %copy-start.66 = (f32[6]{0:T(128)S(1)}, f32[6]{0:T(128)}, u32[]{:S(2)}) copy-start(f32[6]{0:T(128)} %param.34) | copy-start | bytes 76
  0.7 12.0 %copy-start.67 = (f32[6]{0:T(128)S(1)}, f32[6]{0:T(128)}, u32[]{:S(2)}) copy-start(f32[6]{0:T(128)} %param.35) | copy-start | bytes 76
  0.7 12.1 %copy-start.68 = (f32[6]{0:T(128)S(1)}, f32[6]{0:T(128)}, u32[]{:S(2)}) copy-start(f32[6]{0:T(128)} %param.36) | copy-start | bytes 76
  0.7 12.1 %copy-start.69 = (f32[24]{0:T(128)S(1)}, f32[24]{0:T(128)}, u32[]{:S(2)}) copy-start(f32[24]{0:T(128)} %param.31) | copy-start | bytes 292
  0.7 15.8 %copy-start.28 = (bf16[1,128,768]{2,1,0:T(8,128)(2,1)S(1)}, bf16[1,128,768]{2,1,0:T(8,128)(2,1)}, u32[]{:S(2)}) copy-start(bf16[1,128,768]{2,1,0:T(8,128)(2,1)} %param.20) | copy-start | bytes 589828
  2.7 20.7 %copy-start.43 = (bf16[24,192]{1,0:T(8,128)(2,1)S(1)}, bf16[24,192]{1,0:T(8,128)(2,1)}, u32[]{:S(2)}) copy-start(bf16[24,192]{1,0:T(8,128)(2,1)} %param.22) | copy-start | bytes 27652
  2.7 20.7 %copy-start.44 = (bf16[24,192]{1,0:T(8,128)(2,1)S(1)}, bf16[24,192]{1,0:T(8,128)(2,1)}, u32[]{:S(2)}) copy-start(bf16[24,192]{1,0:T(8,128)(2,1)} %param.23) | copy-start | bytes 27652
  2.7 20.7 %copy-start.45 = (bf16[24,192]{1,0:T(8,128)(2,1)S(1)}, bf16[24,192]{1,0:T(8,128)(2,1)}, u32[]{:S(2)}) copy-start(bf16[24,192]{1,0:T(8,128)(2,1)} %param.24) | copy-start | bytes 27652
  2.7 20.7 %copy-start.46 = (bf16[24,192]{1,0:T(8,128)(2,1)S(1)}, bf16[24,192]{1,0:T(8,128)(2,1)}, u32[]{:S(2)}) copy-start(bf16[24,192]{1,0:T(8,128)(2,1)} %param.26) | copy-start | bytes 27652
  2.7 29.7 %all-to-all-start = ((bf16[32,24,768]{2,1,0:T(8,128)(2,1)}), bf16[32,24,768]{2,1,0:T(8,128)(2,1)S(1)}, u32[]{:S(2)}, u32[]{:S(2)}) async-start(bf16[32,24,768]{2,1,0:T(8,128)(2,1)} %broadcast_in_dim.45), calls=%async_computation | async-start | bytes 2359296 | tf_op jit(solution)/shard_map/all_to_all | solution.py:61
  13.1 6.3 %collective-permute-start = (bf16[8,128]{1,0:T(8,128)(2,1)S(1)}, bf16[8,128]{1,0:T(8,128)(2,1)S(1)}, u32[]{:S(2)}, u32[]{:S(2)}) collective-permute-start(bf16[8,128]{1,0:T(8,128)(2,1)S(1)} %fusion.76), channel_id=1, source_target_pairs={{0,3},{1,2},{2,1},{3,0},{4,7},{5,6},{6,5},{7,4},{8,11},{9,10},{10,... | collective-permute-start | bytes 6152 | tf_op jit(solution)/shard_map/ppermute | solution.py:51
  15.2 8.1 %collective-permute-start.1 = (bf16[8,128]{1,0:T(8,128)(2,1)S(1)}, bf16[8,128]{1,0:T(8,128)(2,1)S(1)}, u32[]{:S(2)}, u32[]{:S(2)}) collective-permute-start(bf16[8,128]{1,0:T(8,128)(2,1)S(1)} %fusion.76), channel_id=1, source_target_pairs={{0,2},{1,3},{2,0},{3,1},{4,6},{5,7},{6,4},{7,5},{8,10},{9,11},{10,... | collective-permute-start | bytes 6152 | tf_op jit(solution)/shard_map/ppermute | solution.py:51
  16.1 7.2 %collective-permute-start.2 = (bf16[8,128]{1,0:T(8,128)(2,1)S(1)}, bf16[8,128]{1,0:T(8,128)(2,1)S(1)}, u32[]{:S(2)}, u32[]{:S(2)}) collective-permute-start(bf16[8,128]{1,0:T(8,128)(2,1)S(1)} %fusion.76), channel_id=1, source_target_pairs={{0,1},{1,0},{2,3},{3,2},{4,5},{5,4},{6,7},{7,6},{8,9},{9,8},{10,11... | collective-permute-start | bytes 6152 | tf_op jit(solution)/shard_map/ppermute | solution.py:51
  16.5 15.8 %collective-permute-start.3 = (bf16[128,768]{1,0:T(8,128)(2,1)S(1)}, bf16[128,768]{1,0:T(8,128)(2,1)S(1)}, u32[]{:S(2)}, u32[]{:S(2)}) collective-permute-start(bf16[128,768]{1,0:T(8,128)(2,1)S(1)} %bitcast.70), channel_id=1, source_target_pairs={{0,2},{1,3},{2,0},{3,1},{4,6},{5,7},{6,4},{7,5},{8,10},{9,11},{10,... | collective-permute-start | bytes 589832 | tf_op jit(solution)/shard_map/ppermute | solution.py:51
  33.9 27.8 %all-to-all-start.1 = ((bf16[32,24,896]{2,1,0:T(8,128)(2,1)}), bf16[32,24,896]{2,1,0:T(8,128)(2,1)S(1)}, u32[]{:S(2)}, u32[]{:S(2)}) async-start(bf16[32,24,896]{2,1,0:T(8,128)(2,1)} %broadcast_in_dim.48), calls=%async_computation.1 | async-start | bytes 2752512 | tf_op jit(solution)/shard_map/all_to_all | solution.py:61
  42.6 1.8 collective-permute-start.4
  44.4 17.8 %copy-start.27 = (bf16[512,768]{1,0:T(8,128)(2,1)}, bf16[512,768]{1,0:T(8,128)(2,1)S(1)}, u32[]{:S(2)}) copy-start(bf16[512,768]{1,0:T(8,128)(2,1)S(1)} %constant_dynamic-update-slice_fusion) | copy-start | bytes 2359300
  68.1 1.8 collective-permute-start.5
  72.1 28.6 %all-to-all-start.2 = ((bf16[32,24,768]{2,1,0:T(8,128)(2,1)}), bf16[32,24,768]{2,1,0:T(8,128)(2,1)}, u32[]{:S(2)}, u32[]{:S(2)}) async-start(bf16[32,24,768]{2,1,0:T(8,128)(2,1)} %broadcast_in_dim.98), calls=%async_computation.2 | async-start | bytes 2359296 | tf_op jit(solution)/shard_map/all_to_all | solution.py:61
  78.0 22.7 %collective-permute-start.6 = (bf16[256,768]{1,0:T(8,128)(2,1)S(1)}, bf16[256,768]{1,0:T(8,128)(2,1)}, u32[]{:S(2)}, u32[]{:S(2)}) collective-permute-start(bf16[256,768]{1,0:T(8,128)(2,1)S(1)} %pad_maximum_fusion.10), channel_id=1, source_target_pairs={{0,2},{1,3},{2,0},{3,1},{4,6},{5,7},{6,4},{7,5},{8,10},{9,11},{10,... | collective-permute-start | bytes 1179656 | tf_op jit(solution)/shard_map/ppermute | solution.py:51
  103.7 2.1 collective-permute-start.7
  110.3 15.7 %copy-start = (f32[256,768]{1,0:T(8,128)S(1)}, f32[256,768]{1,0:T(8,128)}, u32[]{:S(2)}) copy-start(f32[256,768]{1,0:T(8,128)} %get-tuple-element.78) | copy-start | bytes 2359300
  110.3 1.8 collective-permute-start.8
  112.3 13.7 %collective-permute-start.9 = (bf16[256,768]{1,0:T(8,128)(2,1)S(1)}, bf16[256,768]{1,0:T(8,128)(2,1)S(1)}, u32[]{:S(2)}, u32[]{:S(2)}) collective-permute-start(bf16[256,768]{1,0:T(8,128)(2,1)S(1)} %pad_maximum_fusion.11), channel_id=1, source_target_pairs={{0,2},{1,3},{2,0},{3,1},{4,6},{5,7},{6,4},{7,5},{8,10},{9,11},{10,... | collective-permute-start | bytes 1179656 | tf_op jit(solution)/shard_map/ppermute | solution.py:51
  114.2 15.2 %collective-permute-start.10 = (bf16[128,768]{1,0:T(8,128)(2,1)S(1)}, bf16[128,768]{1,0:T(8,128)(2,1)S(1)}, u32[]{:S(2)}, u32[]{:S(2)}) collective-permute-start(bf16[128,768]{1,0:T(8,128)(2,1)S(1)} %bitcast.61), channel_id=1, source_target_pairs={{0,2},{1,3},{2,0},{3,1},{4,6},{5,7},{6,4},{7,5},{8,10},{9,11},{10,... | collective-permute-start | bytes 589832 | tf_op jit(solution)/shard_map/ppermute | solution.py:51
  130.9 1.8 collective-permute-start.11
  136.6 3.0 %collective-permute-start.12 = (bf16[256,768]{1,0:T(8,128)(2,1)S(1)}, bf16[256,768]{1,0:T(8,128)(2,1)S(1)}, u32[]{:S(2)}, u32[]{:S(2)}) collective-permute-start(bf16[256,768]{1,0:T(8,128)(2,1)S(1)} %slice.527), channel_id=1, source_target_pairs={{0,1},{1,0},{2,3},{3,2},{4,5},{5,4},{6,7},{7,6},{8,9},{9,8},{10,11... | collective-permute-start | bytes 1179656 | tf_op jit(solution)/shard_map/ppermute | solution.py:51
  140.8 33.1 %all-to-all-start.3 = ((bf16[32,24,768]{2,1,0:T(8,128)(2,1)}), bf16[32,24,768]{2,1,0:T(8,128)(2,1)}, u32[]{:S(2)}, u32[]{:S(2)}) async-start(bf16[32,24,768]{2,1,0:T(8,128)(2,1)} %bitcast.69), calls=%async_computation.3 | async-start | bytes 2359296 | tf_op jit(solution)/shard_map/all_to_all | solution.py:67
  150.9 23.0 %collective-permute-start.13 = (bf16[256,768]{1,0:T(8,128)(2,1)S(1)}, bf16[256,768]{1,0:T(8,128)(2,1)}, u32[]{:S(2)}, u32[]{:S(2)}) collective-permute-start(bf16[256,768]{1,0:T(8,128)(2,1)S(1)} %pad_maximum_fusion.13), channel_id=1, source_target_pairs={{0,2},{1,3},{2,0},{3,1},{4,6},{5,7},{6,4},{7,5},{8,10},{9,11},{10,... | collective-permute-start | bytes 1179656 | tf_op jit(solution)/shard_map/ppermute | solution.py:51
  178.2 7.6 %collective-permute-start.14 = (bf16[256,768]{1,0:T(8,128)(2,1)S(1)}, bf16[256,768]{1,0:T(8,128)(2,1)}, u32[]{:S(2)}, u32[]{:S(2)}) collective-permute-start(bf16[256,768]{1,0:T(8,128)(2,1)S(1)} %get-tuple-element.69), channel_id=1, source_target_pairs={{0,1},{1,0},{2,3},{3,2},{4,5},{5,4},{6,7},{7,6},{8,9},{9,8},{10,11... | collective-permute-start | bytes 1179656 | tf_op jit(solution)/shard_map/ppermute | solution.py:51
  194.4 9.3 %copy-start.2 = (f32[256,768]{1,0:T(8,128)S(1)}, f32[256,768]{1,0:T(8,128)}, u32[]{:S(2)}) copy-start(f32[256,768]{1,0:T(8,128)} %get-tuple-element.78) | copy-start | bytes 2359300
  194.4 9.3 %copy-start.8 = (f32[256,768]{1,0:T(8,128)S(1)}, f32[256,768]{1,0:T(8,128)}, u32[]{:S(2)}) copy-start(f32[256,768]{1,0:T(8,128)} %copy-done.7) | copy-start | bytes 2359300
  195.6 8.9 %copy-start.40 = (f32[1,768]{1,0:T(1,128)S(1)}, f32[1,768]{1,0:T(1,128)}, u32[]{:S(2)}) copy-start(f32[1,768]{1,0:T(1,128)} %broadcast_in_dim.102) | copy-start | bytes 9220
  195.6 8.9 %copy-start.41 = (f32[1,768]{1,0:T(1,128)S(1)}, f32[1,768]{1,0:T(1,128)}, u32[]{:S(2)}) copy-start(f32[1,768]{1,0:T(1,128)} %broadcast_in_dim.105) | copy-start | bytes 9220
  195.6 12.8 %copy-start.19 = (bf16[512,576]{0,1:T(8,128)(2,1)S(1)}, bf16[512,576]{0,1:T(8,128)(2,1)}, u32[]{:S(2)}) copy-start(bf16[512,576]{0,1:T(8,128)(2,1)} %copy-done.18) | copy-start | bytes 1769476
  195.6 27.1 %all-to-all-start.4 = ((bf16[32,24,768]{2,1,0:T(8,128)(2,1)}), bf16[32,24,768]{2,1,0:T(8,128)(2,1)}, u32[]{:S(2)}, u32[]{:S(2)}) async-start(bf16[32,24,768]{2,1,0:T(8,128)(2,1)} %bitcast.68), calls=%async_computation.4 | async-start | bytes 2359296 | tf_op jit(solution)/shard_map/all_to_all | solution.py:67
  204.7 6.8 %collective-permute-start.17 = (f32[12,768]{1,0:T(8,128)S(1)}, f32[12,768]{1,0:T(8,128)S(1)}, u32[]{:S(2)}, u32[]{:S(2)}) collective-permute-start(f32[12,768]{1,0:T(8,128)S(1)} %concatenate.88), channel_id=1, source_target_pairs={{0,1},{1,0},{2,3},{3,2},{4,5},{5,4},{6,7},{7,6},{8,9},{9,8},{10,11... | collective-permute-start | bytes 110600 | tf_op jit(solution)/shard_map/ppermute | solution.py:51
  205.3 14.8 %collective-permute-start.18 = (f32[12,768]{1,0:T(8,128)S(1)}, f32[12,768]{1,0:T(8,128)S(1)}, u32[]{:S(2)}, u32[]{:S(2)}) collective-permute-start(f32[12,768]{1,0:T(8,128)S(1)} %concatenate.88), channel_id=1, source_target_pairs={{0,2},{1,3},{2,0},{3,1},{4,6},{5,7},{6,4},{7,5},{8,10},{9,11},{10,... | collective-permute-start | bytes 110600 | tf_op jit(solution)/shard_map/ppermute | solution.py:51
  206.8 13.5 %collective-permute-start.19 = (f32[12,768]{1,0:T(8,128)S(1)}, f32[12,768]{1,0:T(8,128)S(1)}, u32[]{:S(2)}, u32[]{:S(2)}) collective-permute-start(f32[12,768]{1,0:T(8,128)S(1)} %concatenate.88), channel_id=1, source_target_pairs={{0,3},{1,2},{2,1},{3,0},{4,7},{5,6},{6,5},{7,4},{8,11},{9,10},{10,... | collective-permute-start | bytes 110600 | tf_op jit(solution)/shard_map/ppermute | solution.py:51
  224.3 32.3 %all-to-all-start.5 = ((bf16[32,24,896]{2,1,0:T(8,128)(2,1)}), bf16[32,24,896]{2,1,0:T(8,128)(2,1)S(1)}, u32[]{:S(2)}, u32[]{:S(2)}) async-start(bf16[32,24,896]{2,1,0:T(8,128)(2,1)} %bitcast.60), calls=%async_computation.5 | async-start | bytes 2752512 | tf_op jit(solution)/shard_map/all_to_all | solution.py:67
  232.0 21.7 %copy-start.13 = (f32[256,768]{1,0:T(8,128)S(1)}, f32[256,768]{1,0:T(8,128)}, u32[]{:S(2)}) copy-start(f32[256,768]{1,0:T(8,128)} %get-tuple-element.70) | copy-start | bytes 2359300
  232.0 1.8 collective-permute-start.15
  233.9 19.8 %collective-permute-start.16 = (bf16[128,768]{1,0:T(8,128)(2,1)S(1)}, bf16[128,768]{1,0:T(8,128)(2,1)S(1)}, u32[]{:S(2)}, u32[]{:S(2)}) collective-permute-start(bf16[128,768]{1,0:T(8,128)(2,1)S(1)} %slice.530), channel_id=1, source_target_pairs={{0,2},{1,3},{2,0},{3,1},{4,6},{5,7},{6,4},{7,5},{8,10},{9,11},{10,... | collective-permute-start | bytes 589832 | tf_op jit(solution)/shard_map/ppermute | solution.py:51
  (51 other events, 201.1 us)

commit v2 on v1

--- a/solution.py
+++ b/solution.py
@@ -182,9 +182,9 @@
     packed = jnp.pad(
         jnp.concatenate([high, low], axis=1), ((0, 2), (0, 128 - 2 * column_count))
     )
+    first_full = spread(jnp.concatenate([q_weight, k_weight, v_weight, out_weight], axis=1))
     near = [packed] + [swap(packed, mask) for mask in (1, 2, 3)]
     tokens_far = swap(tokens, 2)
-    up_full = spread(up_weight)
 
     near = [block[:vector_rows] for block in near]
     core = my_index % 2 == 1
@@ -204,16 +204,21 @@
         ],
         axis=0,
     )
-    first_block = jnp.concatenate([q_weight, k_weight, v_weight, out_weight, near], axis=1)
-    first_block, tokens_pair = lax.optimization_barrier(
-        (first_block, jnp.concatenate([tokens, tokens_far], axis=0), up_full)
-    )[:2]
+    vectors = spread(near)
+    tokens_pair = jnp.concatenate([tokens, tokens_far], axis=0)
     tokens_full = core_join(tokens_pair)
     cotangent_far = swap(after(cotangent, tokens_far), 2)
-    first_full = spread(first_block)
+    second_full = spread(
+        after(jnp.concatenate([up_weight, down_weight], axis=1), near, tokens_far)
+    )
+    first_full, vectors, tokens_full, cotangent_far = lax.optimization_barrier(
+        (first_full, vectors, tokens_full, cotangent_far)
+    )
+    hidden_cols = up_weight.shape[1]
+    up_full, down_full = second_full[:, :hidden_cols], second_full[:, hidden_cols:]
     qkv_weight = first_full[:, : 3 * head_cols]
     out_full = first_full[:, 3 * head_cols : 4 * head_cols]
-    vectors = first_full[:, 4 * head_cols :].astype(FULL)
+    vectors = vectors.astype(FULL)
     vectors = vectors[:, :column_count] + vectors[:, column_count : 2 * column_count]
     rows = vectors[:, :8].T
     gain_first, shift_first, gain_second, shift_second = rows[4], rows[5], rows[6], rows[7]
@@ -230,8 +235,6 @@
     mixed_rows, kept = attend_forward(qkv_rows, same_doc, head_count, head_cols)
     attn_chip = core_sum(contract(mixed_rows, out_full, 1, 1))
     attn_far = far_sum(attn_chip)
-    down_full = spread(after(down_weight, attn_chip))
-    attn_chip, attn_far, down_full = lax.optimization_barrier((attn_chip, attn_far, down_full))
     first, normed_first, inv_first = norm_forward(
         tokens_pair.astype(FULL) + (attn_chip + attn_far.astype(FULL)) + bias_out,
         gain_first,
@@ -257,14 +260,16 @@
     active_grad = jnp.dot(branch_full, down_full, preferred_element_type=FULL)
     upward_grad = (active_grad * gelu_slope(upward)).astype(LOW)
     hidden_chip = core_sum(contract(upward_grad, up_full, 1, 1))
+    hidden_far = far_sum(hidden_chip)
     grad_down = contract(branch_full, active, 0, 0)
-    hidden_far = far_sum(hidden_chip)
-    down_blocks = gathered_sum(after(grad_down, hidden_chip))
-    hidden_chip, hidden_far, down_blocks = lax.optimization_barrier(
-        (hidden_chip, hidden_far, down_blocks)
-    )
+    grad_up = contract(hidden_full, upward_grad, 0, 0)
     grad_bias_up = jnp.sum(upward_grad.astype(FULL), axis=0)
-    grad_up = contract(hidden_full, upward_grad, 0, 0)
+    pair_blocks = gathered_sum(
+        jnp.concatenate(
+            [after(grad_up, hidden_chip).astype(LOW), after(grad_down, hidden_chip).astype(LOW)],
+            axis=1,
+        )
+    )
     first_grad = second_grad + (hidden_chip + hidden_far.astype(FULL))
     resid_grad = norm_backward(first_grad, normed_first, inv_first, gain_first)
     first_own = first_grad[:local_len]
@@ -299,7 +304,6 @@
     vector_near = [swap(vector_sums, mask) for mask in (1, 2, 3)]
     input_chip = core_sum(contract(qkv_grad, qkv_weight, 1, 1))
     input_far = swap(input_chip[local_len:].astype(LOW), 2)
-    up_blocks = gathered_sum(after(grad_up, qkv_grad))
     vector_sums = vector_sums + vector_near[0] + vector_near[1] + vector_near[2]
     grad_qkv = contract(tokens_full, qkv_grad, 0, 0)
     grad_out = contract(attended_full, mixed_rows, 0, 0)
@@ -314,11 +318,11 @@
         ],
         axis=1,
     )
-    last_blocks = gathered_sum(after(last_block, up_blocks))
+    last_blocks = gathered_sum(last_block)
     input_grad = resid_grad[:local_len] + (input_chip[:local_len] + input_far.astype(FULL))
 
-    down_sum = jnp.sum(down_blocks.astype(FULL), axis=0)
-    up_sum = jnp.sum(up_blocks.astype(FULL), axis=0)
+    pair_sum = jnp.sum(pair_blocks.astype(FULL), axis=0)
+    up_sum, down_sum = pair_sum[:, :hidden_cols], pair_sum[:, hidden_cols:]
     last_sum = jnp.sum(last_blocks.astype(FULL), axis=0)
     columns = last_sum[:, 4 * head_cols :]
     columns = columns[:, :column_count] + columns[:, column_count : 2 * column_count]

time: 262 us -> 267 us (1.019)
  starting transfers between devices: 67.1 us -> 52 us
  waiting for transfers between devices: 115 us -> 129 us
  local copies, waits for them, and re-layouts: 24.5 us -> 35.9 us
  other arithmetic: 21.2 us -> 17.9 us
    all_to_all x3 -> x2, waiting for transfers between devices: 1.7 us -> 16.4 us  [gathered_sum(): got = lax.all_to_all(blocks, 'dp', 0, 0, tiled=True)]
    all_to_all x3, waiting for transfers between devices: 17.3 us -> 5.99 us  [spread(): lax.all_to_all(stacked, 'dp', 0, 0, tiled=True).reshape(-1, block.shape[1])]
    ppermute x20, waiting for transfers between devices: 96 us -> 107 us  [swap(): return lax.ppermute(values, 'tensor', [(i, i ^ mask) for i in range(4)])]
    all_to_all x3 -> x2, starting transfers between devices: 23.1 us -> 14.5 us  [gathered_sum(): got = lax.all_to_all(blocks, 'dp', 0, 0, tiled=True)]
    another operation x8, local copies, waits for them, and re-layouts: 0.74 us -> 5.93 us  [shards(): jnp.stack([q_bias, v_bias, out_bias, down_bias, norm1_gain, norm1_shift,...]
    ppermute x20, starting transfers between devices: 22.4 us -> 17.7 us  [swap(): return lax.ppermute(values, 'tensor', [(i, i ^ mask) for i in range(4)])]
    reduce_sum x2 -> x1, other arithmetic: 4.15 us -> 0.33 us  [shards(): pair_sum = jnp.sum(pair_blocks.astype(FULL), axis=0)]
    concatenate x1 -> x5, other arithmetic: 0.03 us -> 3.52 us  [the longest x1 1.59 us: shards(): jnp.concatenate([after(grad_up, hidden_chip).astype(LOW), after(grad_down...]
  transfers between devices with their start and end apart: 26 -> 25, of which waited for: 17 -> 13; matrix products, arithmetic and copies ran while one was open for 12% -> 14% of each run, Pallas kernels for 0% -> 0%
where the time goes in v2:
time: 267 us; the launch traced here: 264 us
  waiting for transfers between devices  129 us (48%)
  starting transfers between devices  52 us (19%)
  local copies, waits for them, and re-layouts  35.9 us (13%)
  matrix products  27 us (10%)
  other arithmetic  17.9 us (7%)
    ppermute x20, waiting for transfers between devices, swap(): return lax.ppermute(values, 'tensor', [(i, i ^ mask) for i in range(4)])  107 us
    all_to_all x3, starting transfers between devices, spread(): lax.all_to_all(stacked, 'dp', 0, 0, tiled=True).reshape(-1, block.shape[1])  19.8 us
    ppermute x20, starting transfers between devices, swap(): return lax.ppermute(values, 'tensor', [(i, i ^ mask) for i in range(4)])  17.7 us
    dot_general x20, matrix products, contract(): lax.dot_general(left, right, (((left_dim,), (right_dim,)), ((), ())), pre...  17.6 us
    all_to_all x2, waiting for transfers between devices, gathered_sum(): got = lax.all_to_all(blocks, 'dp', 0, 0, tiled=True)  16.4 us
    all_to_all x2, starting transfers between devices, gathered_sum(): got = lax.all_to_all(blocks, 'dp', 0, 0, tiled=True)  14.5 us
    unnamed x124, local copies, waits for them, and re-layouts  6.6 us
    all_to_all x3, waiting for transfers between devices, spread(): lax.all_to_all(stacked, 'dp', 0, 0, tiled=True).reshape(-1, block.shape[1])  5.99 us
  transfers between devices with their start and end apart: 25, of which 13 were waited for; matrix products, arithmetic and copies ran while one was open for 14% of the time, Pallas kernels for 0%

profile of v2, /device:TPU:0, one launch (start us, length us, event | category | flops | bytes accessed | tf_op | source)
XLA Modules:
  0.0 263.9 jit_solution(1793448557996454959)
XLA Ops:
  7.5 3.4 %collective-permute-start.2 = (bf16[8,128]{1,0:T(8,128)(2,1)S(1)}, bf16[8,128]{1,0:T(8,128)(2,1)S(1)}, u32[]{:S(2)}, u32[]{:S(2)}) collective-permute-start(bf16[8,128]{1,0:T(8,128)(2,1)S(1)} %fusion.83), channel_id=1, source_target_pairs={{0,2},{1,3},{2,0},{3,1},{4,6},{5,7},{6,4},{7,5},{8,10},{9,11},{10,... | collective-permute-start | bytes 6152 | tf_op jit(solution)/shard_map/ppermute | solution.py:51
  10.9 1.8 collective-permute-done.2
  12.7 2.7 %collective-permute-done.1 = bf16[8,128]{1,0:T(8,128)(2,1)S(1)} collective-permute-done((bf16[8,128]{1,0:T(8,128)(2,1)S(1)}, bf16[8,128]{1,0:T(8,128)(2,1)S(1)}, u32[]{:S(2)}, u32[]{:S(2)}) %collective-permute-start.1) | collective-permute-done | bytes 2080 | tf_op jit(solution)/shard_map/ppermute | solution.py:51
  16.1 8.3 %all-to-all-start.1 = ((bf16[32,24,128]{2,1,0:T(8,128)(2,1)}), bf16[32,24,128]{2,1,0:T(8,128)(2,1)S(1)}, u32[]{:S(2)}, u32[]{:S(2)}) async-start(bf16[32,24,128]{2,1,0:T(8,128)(2,1)} %broadcast_in_dim.48), calls=%async_computation.1 | async-start | bytes 393216 | tf_op jit(solution)/shard_map/all_to_all | solution.py:61
  24.4 1.9 collective-permute-start
  27.2 6.0 %all-to-all-done.1 = bf16[32,24,128]{2,1,0:T(8,128)(2,1)S(1)} async-done(((bf16[32,24,128]{2,1,0:T(8,128)(2,1)}), bf16[32,24,128]{2,1,0:T(8,128)(2,1)S(1)}, u32[]{:S(2)}, u32[]{:S(2)}) %all-to-all-start.1) | async-done | bytes 196640 | tf_op jit(solution)/shard_map/all_to_all | solution.py:61
  34.3 4.1 %all-to-all-start = ((bf16[32,24,768]{2,1,0:T(8,128)(2,1)}), bf16[32,24,768]{2,1,0:T(8,128)(2,1)S(1)}, u32[]{:S(2)}, u32[]{:S(2)}) async-start(bf16[32,24,768]{2,1,0:T(8,128)(2,1)} %broadcast_in_dim.47), calls=%async_computation | async-start | bytes 2359296 | tf_op jit(solution)/shard_map/all_to_all | solution.py:61
  39.7 1.9 collective-permute-start.5
  42.7 14.3 %collective-permute-done.5 = bf16[128,768]{1,0:T(8,128)(2,1)S(1)} collective-permute-done((bf16[128,768]{1,0:T(8,128)(2,1)S(1)}, bf16[128,768]{1,0:T(8,128)(2,1)S(1)}, u32[]{:S(2)}, u32[]{:S(2)}) %collective-permute-start.5) | collective-permute-done | bytes 196640 | tf_op jit(solution)/shard_map/ppermute | solution.py:51
  62.6 1.6 fusion.46
  64.2 1.2 copy-done.1
  66.2 1.5 broadcast_in_dim.98
  67.8 7.5 %all-to-all-start.2 = ((bf16[32,24,1536]{2,1,0:T(8,128)(2,1)}), bf16[32,24,1536]{2,1,0:T(8,128)(2,1)}, u32[]{:S(2)}, u32[]{:S(2)}) async-start(bf16[32,24,1536]{2,1,0:T(8,128)(2,1)} %broadcast_in_dim.98), calls=%async_computation.2 | async-start | bytes 4718592 | tf_op jit(solution)/shard_map/all_to_all | solution.py:61
  75.3 1.4 fusion.40
  76.7 3.0 %collective-permute-start.7 = (bf16[256,768]{1,0:T(8,128)(2,1)S(1)}, bf16[256,768]{1,0:T(8,128)(2,1)S(1)}, u32[]{:S(2)}, u32[]{:S(2)}) collective-permute-start(bf16[256,768]{1,0:T(8,128)(2,1)S(1)} %pad_maximum_fusion.12), channel_id=1, source_target_pairs={{0,2},{1,3},{2,0},{3,1},{4,6},{5,7},{6,4},{7,5},{8,10},{9,11},{10,... | collective-permute-start | bytes 1179656 | tf_op jit(solution)/shard_map/ppermute | solution.py:51
  79.8 1.5 slice_reduce_fusion.1
  81.3 32.5 %collective-permute-done.7 = bf16[256,768]{1,0:T(8,128)(2,1)S(1)} collective-permute-done((bf16[256,768]{1,0:T(8,128)(2,1)S(1)}, bf16[256,768]{1,0:T(8,128)(2,1)S(1)}, u32[]{:S(2)}, u32[]{:S(2)}) %collective-permute-start.7) | collective-permute-done | bytes 393248 | tf_op jit(solution)/shard_map/ppermute | solution.py:51
  113.8 1.3 fusion.96
  115.3 1.3 fusion.31
  116.6 1.6 dynamic-slice.2
  118.2 1.6 add.194
  119.8 2.4 multiply_convert_fusion
  122.2 2.4 fusion.17
  125.4 1.3 collective-permute-done.9
  127.7 12.3 %collective-permute-done.10 = bf16[256,768]{1,0:T(8,128)(2,1)S(1)} collective-permute-done((bf16[256,768]{1,0:T(8,128)(2,1)S(1)}, bf16[256,768]{1,0:T(8,128)(2,1)S(1)}, u32[]{:S(2)}, u32[]{:S(2)}) %collective-permute-start.10) | collective-permute-done | bytes 393248 | tf_op jit(solution)/shard_map/ppermute | solution.py:51
  141.2 1.7 collective-permute-done.11
  142.9 3.1 %convert_reduce_fusion.2 = (f32[768]{0:T(1024)}, bf16[512,768]{1,0:T(8,128)(2,1)S(1)}) fusion(f32[512,768]{1,0:T(8,128)S(1)} %get-tuple-element.103, bf16[768,1536]{1,0:T(8,128)(2,1)} %bitcast.18, bf16[256,768]{1,0:T(8,128)(2,1)S(1)} %collective-permute-done.11, bf16[256,768]{1,0:T(8,128)(2,1)S(1)} %fusion.92), kind=kOutput, calls=%fused_computation.15 | convolution fusion | flops 610270464 | bytes 4328448 | tf_op jit(solution)/shard_map/dot_general | solution.py:260
  146.9 2.1 fusion.19
  149.2 1.6 collective-permute-done.12
  152.4 11.4 %collective-permute-done.13 = bf16[256,768]{1,0:T(8,128)(2,1)S(1)} collective-permute-done((bf16[256,768]{1,0:T(8,128)(2,1)S(1)}, bf16[256,768]{1,0:T(8,128)(2,1)S(1)}, u32[]{:S(2)}, u32[]{:S(2)}) %collective-permute-start.13) | collective-permute-done | bytes 393248 | tf_op jit(solution)/shard_map/ppermute | solution.py:51
  164.4 1.1 fusion.93
  168.1 1.4 reshape.142
  169.5 1.6 copy.65
  171.1 1.2 slice_reduce_fusion.7
  174.1 1.7 convolution_convert_fusion.2
  183.0 3.0 %collective-permute-start.18 = (f32[12,768]{1,0:T(8,128)S(1)}, f32[12,768]{1,0:T(8,128)S(1)}, u32[]{:S(2)}, u32[]{:S(2)}) collective-permute-start(f32[12,768]{1,0:T(8,128)S(1)} %concatenate.96), channel_id=1, source_target_pairs={{0,2},{1,3},{2,0},{3,1},{4,6},{5,7},{6,4},{7,5},{8,10},{9,11},{10,... | collective-permute-start | bytes 110600 | tf_op jit(solution)/shard_map/ppermute | solution.py:51
  186.0 1.7 convolution_convert_fusion
  187.7 1.3 convolution_convert_fusion.1
  189.8 1.6 copy.66
  191.3 9.8 %all-to-all-start.3 = ((bf16[32,24,896]{2,1,0:T(8,128)(2,1)}), bf16[32,24,896]{2,1,0:T(8,128)(2,1)S(1)}, u32[]{:S(2)}, u32[]{:S(2)}) async-start(bf16[32,24,896]{2,1,0:T(8,128)(2,1)} %bitcast.25), calls=%async_computation.3 | async-start | bytes 2752512 | tf_op jit(solution)/shard_map/all_to_all | solution.py:67
  202.4 1.9 fusion.39
  204.3 1.6 pad_maximum_fusion
  205.9 16.4 %all-to-all-done.3 = bf16[32,24,896]{2,1,0:T(8,128)(2,1)S(1)} async-done(((bf16[32,24,896]{2,1,0:T(8,128)(2,1)}), bf16[32,24,896]{2,1,0:T(8,128)(2,1)S(1)}, u32[]{:S(2)}, u32[]{:S(2)}) %all-to-all-start.3) | async-done | bytes 1376288 | tf_op jit(solution)/shard_map/all_to_all | solution.py:67
  223.4 4.6 %all-to-all-start.4 = ((bf16[32,24,1536]{2,1,0:T(8,128)(2,1)}), bf16[32,24,1536]{2,1,0:T(8,128)(2,1)S(1)}, u32[]{:S(2)}, u32[]{:S(2)}) async-start(bf16[32,24,1536]{2,1,0:T(8,128)(2,1)} %bitcast.26), calls=%async_computation.4 | async-start | bytes 4718592 | tf_op jit(solution)/shard_map/all_to_all | solution.py:67
  228.0 1.9 fusion.25
  230.1 1.7 collective-permute-done.15
  232.8 25.8 %collective-permute-done.16 = bf16[128,768]{1,0:T(8,128)(2,1)S(1)} collective-permute-done((bf16[128,768]{1,0:T(8,128)(2,1)S(1)}, bf16[128,768]{1,0:T(8,128)(2,1)S(1)}, u32[]{:S(2)}, u32[]{:S(2)}) %collective-permute-start.16) | collective-permute-done | bytes 196640 | tf_op jit(solution)/shard_map/ppermute | solution.py:51
  258.7 1.8 fusion.44
  (269 shorter events, 43.6 us)
Async XLA Ops:
  7.5 3.4 %collective-permute-start.3 = (bf16[8,128]{1,0:T(8,128)(2,1)S(1)}, bf16[8,128]{1,0:T(8,128)(2,1)S(1)}, u32[]{:S(2)}, u32[]{:S(2)}) collective-permute-start(bf16[8,128]{1,0:T(8,128)(2,1)S(1)} %fusion.83), channel_id=1, source_target_pairs={{0,1},{1,0},{2,3},{3,2},{4,5},{5,4},{6,7},{7,6},{8,9},{9,8},{10,11... | collective-permute-start | bytes 6152 | tf_op jit(solution)/shard_map/ppermute | solution.py:51
  7.5 5.2 %collective-permute-start.2 = (bf16[8,128]{1,0:T(8,128)(2,1)S(1)}, bf16[8,128]{1,0:T(8,128)(2,1)S(1)}, u32[]{:S(2)}, u32[]{:S(2)}) collective-permute-start(bf16[8,128]{1,0:T(8,128)(2,1)S(1)} %fusion.83), channel_id=1, source_target_pairs={{0,2},{1,3},{2,0},{3,1},{4,6},{5,7},{6,4},{7,5},{8,10},{9,11},{10,... | collective-permute-start | bytes 6152 | tf_op jit(solution)/shard_map/ppermute | solution.py:51
  10.9 4.5 %collective-permute-start.1 = (bf16[8,128]{1,0:T(8,128)(2,1)S(1)}, bf16[8,128]{1,0:T(8,128)(2,1)S(1)}, u32[]{:S(2)}, u32[]{:S(2)}) collective-permute-start(bf16[8,128]{1,0:T(8,128)(2,1)S(1)} %fusion.83), channel_id=1, source_target_pairs={{0,3},{1,2},{2,1},{3,0},{4,7},{5,6},{6,5},{7,4},{8,11},{9,10},{10,... | collective-permute-start | bytes 6152 | tf_op jit(solution)/shard_map/ppermute | solution.py:51
  16.1 17.1 %all-to-all-start.1 = ((bf16[32,24,128]{2,1,0:T(8,128)(2,1)}), bf16[32,24,128]{2,1,0:T(8,128)(2,1)S(1)}, u32[]{:S(2)}, u32[]{:S(2)}) async-start(bf16[32,24,128]{2,1,0:T(8,128)(2,1)} %broadcast_in_dim.48), calls=%async_computation.1 | async-start | bytes 393216 | tf_op jit(solution)/shard_map/all_to_all | solution.py:61
  24.4 15.1 %collective-permute-start = (bf16[128,768]{1,0:T(8,128)(2,1)}, bf16[128,768]{1,0:T(8,128)(2,1)S(1)}, u32[]{:S(2)}, u32[]{:S(2)}) collective-permute-start(bf16[128,768]{1,0:T(8,128)(2,1)} %bitcast.59), channel_id=1, source_target_pairs={{0,2},{1,3},{2,0},{3,1},{4,6},{5,7},{6,4},{7,5},{8,10},{9,11},{10,... | collective-permute-start | bytes 589832 | tf_op jit(solution)/shard_map/ppermute | solution.py:51
  27.2 11.2 %copy-start.54 = (s32[4]{0:T(128)S(1)}, s32[4]{0:T(128)}, u32[]{:S(2)}) copy-start(s32[4]{0:T(128)} %constant.116) | copy-start | bytes 52
  27.2 11.2 %copy-start.55 = (s32[4]{0:T(128)S(1)}, s32[4]{0:T(128)}, u32[]{:S(2)}) copy-start(s32[4]{0:T(128)} %constant.115) | copy-start | bytes 52
  27.2 11.2 %copy-start.22 = (s32[1,512]{1,0:T(1,128)S(1)}, s32[1,512]{1,0:T(1,128)}, u32[]{:S(2)}) copy-start(s32[1,512]{1,0:T(1,128)} %param.21) | copy-start | bytes 6148
  27.2 12.3 %copy-start.11 = (bf16[1,128,768]{2,1,0:T(8,128)(2,1)S(1)}, bf16[1,128,768]{2,1,0:T(8,128)(2,1)}, u32[]{:S(2)}) copy-start(bf16[1,128,768]{2,1,0:T(8,128)(2,1)} %param.20) | copy-start | bytes 589828
  34.3 5.4 %copy-start.8 = (bf16[1,128,768]{2,1,0:T(8,128)(2,1)S(1)}, bf16[1,128,768]{2,1,0:T(8,128)(2,1)}, u32[]{:S(2)}) copy-start(bf16[1,128,768]{2,1,0:T(8,128)(2,1)} %param.37) | copy-start | bytes 589828
  34.3 22.7 %all-to-all-start = ((bf16[32,24,768]{2,1,0:T(8,128)(2,1)}), bf16[32,24,768]{2,1,0:T(8,128)(2,1)S(1)}, u32[]{:S(2)}, u32[]{:S(2)}) async-start(bf16[32,24,768]{2,1,0:T(8,128)(2,1)} %broadcast_in_dim.47), calls=%async_computation | async-start | bytes 2359296 | tf_op jit(solution)/shard_map/all_to_all | solution.py:61
  39.6 17.5 %copy-start.13 = (bf16[128,768]{1,0:T(8,128)(2,1)}, bf16[128,768]{1,0:T(8,128)(2,1)S(1)}, u32[]{:S(2)}) copy-start(bf16[128,768]{1,0:T(8,128)(2,1)S(1)} %collective-permute-done) | copy-start | bytes 589828
  39.6 2.1 collective-permute-start.4
  39.7 17.3 %collective-permute-start.5 = (bf16[128,768]{1,0:T(8,128)(2,1)S(1)}, bf16[128,768]{1,0:T(8,128)(2,1)S(1)}, u32[]{:S(2)}, u32[]{:S(2)}) collective-permute-start(bf16[128,768]{1,0:T(8,128)(2,1)S(1)} %bitcast.54), channel_id=1, source_target_pairs={{0,2},{1,3},{2,0},{3,1},{4,6},{5,7},{6,4},{7,5},{8,10},{9,11},{10,... | collective-permute-start | bytes 589832 | tf_op jit(solution)/shard_map/ppermute | solution.py:51
  42.7 16.0 %copy-start.17 = (bf16[512,768]{1,0:T(8,128)(2,1)}, bf16[512,768]{1,0:T(8,128)(2,1)S(1)}, u32[]{:S(2)}) copy-start(bf16[512,768]{1,0:T(8,128)(2,1)S(1)} %pad_maximum_fusion.1) | copy-start | bytes 2359300
  66.2 9.1 %collective-permute-start.6 = (bf16[256,768]{1,0:T(8,128)(2,1)}, bf16[256,768]{1,0:T(8,128)(2,1)}, u32[]{:S(2)}, u32[]{:S(2)}) collective-permute-start(bf16[256,768]{1,0:T(8,128)(2,1)} %slice.553), channel_id=1, source_target_pairs={{0,1},{1,0},{2,3},{3,2},{4,5},{5,4},{6,7},{7,6},{8,9},{9,8},{10,11... | collective-permute-start | bytes 1179656 | tf_op jit(solution)/shard_map/ppermute | solution.py:51
  67.8 52.1 %all-to-all-start.2 = ((bf16[32,24,1536]{2,1,0:T(8,128)(2,1)}), bf16[32,24,1536]{2,1,0:T(8,128)(2,1)}, u32[]{:S(2)}, u32[]{:S(2)}) async-start(bf16[32,24,1536]{2,1,0:T(8,128)(2,1)} %broadcast_in_dim.98), calls=%async_computation.2 | async-start | bytes 4718592 | tf_op jit(solution)/shard_map/all_to_all | solution.py:61
  75.2 4.5 %copy-start.10 = (f32[768,12]{1,0:T(8,128)S(1)}, f32[768,12]{1,0:T(8,128)}, u32[]{:S(2)}) copy-start(f32[768,12]{1,0:T(8,128)} %copy-done.9) | copy-start | bytes 110596
  76.7 37.0 %copy-start.2 = (f32[512,768]{1,0:T(8,128)S(1)}, f32[512,768]{1,0:T(8,128)}, u32[]{:S(2)}) copy-start(f32[512,768]{1,0:T(8,128)} %copy-done.1) | copy-start | bytes 4718596
  76.7 37.0 %copy-start.12 = (bf16[1,128,768]{2,1,0:T(8,128)(2,1)S(1)}, bf16[1,128,768]{2,1,0:T(8,128)(2,1)}, u32[]{:S(2)}) copy-start(bf16[1,128,768]{2,1,0:T(8,128)(2,1)} %param.20) | copy-start | bytes 589828
  76.7 37.0 %copy-start.14 = (bf16[128,768]{1,0:T(8,128)(2,1)S(1)}, bf16[128,768]{1,0:T(8,128)(2,1)}, u32[]{:S(2)}) copy-start(bf16[128,768]{1,0:T(8,128)(2,1)} %copy-done.13) | copy-start | bytes 589828
  76.7 37.0 %collective-permute-start.7 = (bf16[256,768]{1,0:T(8,128)(2,1)S(1)}, bf16[256,768]{1,0:T(8,128)(2,1)S(1)}, u32[]{:S(2)}, u32[]{:S(2)}) collective-permute-start(bf16[256,768]{1,0:T(8,128)(2,1)S(1)} %pad_maximum_fusion.12), channel_id=1, source_target_pairs={{0,2},{1,3},{2,0},{3,1},{4,6},{5,7},{6,4},{7,5},{8,10},{9,11},{10,... | collective-permute-start | bytes 1179656 | tf_op jit(solution)/shard_map/ppermute | solution.py:51
  116.6 3.2 %collective-permute-start.8 = (bf16[256,768]{1,0:T(8,128)(2,1)}, bf16[256,768]{1,0:T(8,128)(2,1)}, u32[]{:S(2)}, u32[]{:S(2)}) collective-permute-start(bf16[256,768]{1,0:T(8,128)(2,1)} %get-tuple-element.67), channel_id=1, source_target_pairs={{0,1},{1,0},{2,3},{3,2},{4,5},{5,4},{6,7},{7,6},{8,9},{9,8},{10,11... | collective-permute-start | bytes 1179656 | tf_op jit(solution)/shard_map/ppermute | solution.py:51
  124.7 15.3 %copy-start = (f32[256,768]{1,0:T(8,128)S(1)}, f32[256,768]{1,0:T(8,128)}, u32[]{:S(2)}) copy-start(f32[256,768]{1,0:T(8,128)} %get-tuple-element.68) | copy-start | bytes 2359300
  124.7 2.1 collective-permute-start.9
  126.9 13.0 %collective-permute-start.10 = (bf16[256,768]{1,0:T(8,128)(2,1)S(1)}, bf16[256,768]{1,0:T(8,128)(2,1)S(1)}, u32[]{:S(2)}, u32[]{:S(2)}) collective-permute-start(bf16[256,768]{1,0:T(8,128)(2,1)S(1)} %pad_maximum_fusion.13), channel_id=1, source_target_pairs={{0,2},{1,3},{2,0},{3,1},{4,6},{5,7},{6,4},{7,5},{8,10},{9,11},{10,... | collective-permute-start | bytes 1179656 | tf_op jit(solution)/shard_map/ppermute | solution.py:51
  141.0 26.4 %copy-start.15 = (bf16[256,768]{1,0:T(8,128)(2,1)}, bf16[256,768]{1,0:T(8,128)(2,1)S(1)}, u32[]{:S(2)}) copy-start(bf16[256,768]{1,0:T(8,128)(2,1)S(1)} %fusion.92) | copy-start | bytes 1179652
  141.1 1.8 collective-permute-start.11
  149.0 1.8 collective-permute-start.12
  151.0 12.7 %collective-permute-start.13 = (bf16[256,768]{1,0:T(8,128)(2,1)S(1)}, bf16[256,768]{1,0:T(8,128)(2,1)S(1)}, u32[]{:S(2)}, u32[]{:S(2)}) collective-permute-start(bf16[256,768]{1,0:T(8,128)(2,1)S(1)} %pad_maximum_fusion.15), channel_id=1, source_target_pairs={{0,2},{1,3},{2,0},{3,1},{4,6},{5,7},{6,4},{7,5},{8,10},{9,11},{10,... | collective-permute-start | bytes 1179656 | tf_op jit(solution)/shard_map/ppermute | solution.py:51
  165.5 8.6 %collective-permute-start.14 = (bf16[256,768]{1,0:T(8,128)(2,1)S(1)}, bf16[256,768]{1,0:T(8,128)(2,1)}, u32[]{:S(2)}, u32[]{:S(2)}) collective-permute-start(bf16[256,768]{1,0:T(8,128)(2,1)S(1)} %get-tuple-element.59), channel_id=1, source_target_pairs={{0,1},{1,0},{2,3},{3,2},{4,5},{5,4},{6,7},{7,6},{8,9},{9,8},{10,11... | collective-permute-start | bytes 1179656 | tf_op jit(solution)/shard_map/ppermute | solution.py:51
  171.1 4.7 %copy-start.21 = (bf16[512,576]{0,1:T(8,128)(2,1)S(1)}, bf16[512,576]{0,1:T(8,128)(2,1)}, u32[]{:S(2)}) copy-start(bf16[512,576]{0,1:T(8,128)(2,1)} %copy-done.20) | copy-start | bytes 1769476
  179.9 6.1 %copy-start.18 = (bf16[512,768]{1,0:T(8,128)(2,1)S(1)}, bf16[512,768]{1,0:T(8,128)(2,1)}, u32[]{:S(2)}) copy-start(bf16[512,768]{1,0:T(8,128)(2,1)} %copy-done.17) | copy-start | bytes 2359300
  181.4 6.3 %copy-start.24 = (bf16[512,64]{0,1:T(8,128)(2,1)S(1)}, bf16[512,64]{0,1:T(8,128)(2,1)}, u32[]{:S(2)}) copy-start(bf16[512,64]{0,1:T(8,128)(2,1)} %copy-done.23) | copy-start | bytes 196612
  181.4 6.3 %copy-start.26 = (bf16[512,64]{0,1:T(8,128)(2,1)S(1)}, bf16[512,64]{0,1:T(8,128)(2,1)}, u32[]{:S(2)}) copy-start(bf16[512,64]{0,1:T(8,128)(2,1)} %copy-done.25) | copy-start | bytes 196612
  181.4 6.3 %copy-start.28 = (bf16[512,64]{0,1:T(8,128)(2,1)S(1)}, bf16[512,64]{0,1:T(8,128)(2,1)}, u32[]{:S(2)}) copy-start(bf16[512,64]{0,1:T(8,128)(2,1)} %copy-done.27) | copy-start | bytes 196612
  182.2 6.8 %collective-permute-start.19 = (f32[12,768]{1,0:T(8,128)S(1)}, f32[12,768]{1,0:T(8,128)S(1)}, u32[]{:S(2)}, u32[]{:S(2)}) collective-permute-start(f32[12,768]{1,0:T(8,128)S(1)} %concatenate.96), channel_id=1, source_target_pairs={{0,3},{1,2},{2,1},{3,0},{4,7},{5,6},{6,5},{7,4},{8,11},{9,10},{10,... | collective-permute-start | bytes 110600 | tf_op jit(solution)/shard_map/ppermute | solution.py:51
  183.0 6.0 %collective-permute-start.18 = (f32[12,768]{1,0:T(8,128)S(1)}, f32[12,768]{1,0:T(8,128)S(1)}, u32[]{:S(2)}, u32[]{:S(2)}) collective-permute-start(f32[12,768]{1,0:T(8,128)S(1)} %concatenate.96), channel_id=1, source_target_pairs={{0,2},{1,3},{2,0},{3,1},{4,6},{5,7},{6,4},{7,5},{8,10},{9,11},{10,... | collective-permute-start | bytes 110600 | tf_op jit(solution)/shard_map/ppermute | solution.py:51
  186.0 3.1 %collective-permute-start.17 = (f32[12,768]{1,0:T(8,128)S(1)}, f32[12,768]{1,0:T(8,128)S(1)}, u32[]{:S(2)}, u32[]{:S(2)}) collective-permute-start(f32[12,768]{1,0:T(8,128)S(1)} %concatenate.96), channel_id=1, source_target_pairs={{0,1},{1,0},{2,3},{3,2},{4,5},{5,4},{6,7},{7,6},{8,9},{9,8},{10,11... | collective-permute-start | bytes 110600 | tf_op jit(solution)/shard_map/ppermute | solution.py:51
  191.3 9.8 %copy-start.16 = (bf16[256,768]{1,0:T(8,128)(2,1)S(1)}, bf16[256,768]{1,0:T(8,128)(2,1)}, u32[]{:S(2)}) copy-start(bf16[256,768]{1,0:T(8,128)(2,1)} %copy-done.15) | copy-start | bytes 1179652
  191.3 9.9 %copy-start.57 = (bf16[256,768]{1,0:T(8,128)(2,1)S(1)}, bf16[256,768]{1,0:T(8,128)(2,1)}, u32[]{:S(2)}) copy-start(bf16[256,768]{1,0:T(8,128)(2,1)} %copy-done.56) | copy-start | bytes 1179652
  191.3 9.9 %copy-start.59 = (bf16[512,768]{1,0:T(8,128)(2,1)S(1)}, bf16[512,768]{1,0:T(8,128)(2,1)}, u32[]{:S(2)}) copy-start(bf16[512,768]{1,0:T(8,128)(2,1)} %copy-done.58) | copy-start | bytes 2359300
  191.3 30.9 %all-to-all-start.3 = ((bf16[32,24,896]{2,1,0:T(8,128)(2,1)}), bf16[32,24,896]{2,1,0:T(8,128)(2,1)S(1)}, u32[]{:S(2)}, u32[]{:S(2)}) async-start(bf16[32,24,896]{2,1,0:T(8,128)(2,1)} %bitcast.25), calls=%async_computation.3 | async-start | bytes 2752512 | tf_op jit(solution)/shard_map/all_to_all | solution.py:67
  222.3 5.7 %copy-start.4 = (bf16[32,24,768]{2,1,0:T(8,128)(2,1)S(1)}, bf16[32,24,768]{2,1,0:T(8,128)(2,1)}, u32[]{:S(2)}) copy-start(bf16[32,24,768]{2,1,0:T(8,128)(2,1)} %copy-done.3) | copy-start | bytes 3538948
  223.4 39.5 %all-to-all-start.4 = ((bf16[32,24,1536]{2,1,0:T(8,128)(2,1)}), bf16[32,24,1536]{2,1,0:T(8,128)(2,1)S(1)}, u32[]{:S(2)}, u32[]{:S(2)}) async-start(bf16[32,24,1536]{2,1,0:T(8,128)(2,1)} %bitcast.26), calls=%async_computation.4 | async-start | bytes 4718592 | tf_op jit(solution)/shard_map/all_to_all | solution.py:67
  230.0 1.8 collective-permute-start.15
  231.9 26.8 %collective-permute-start.16 = (bf16[128,768]{1,0:T(8,128)(2,1)S(1)}, bf16[128,768]{1,0:T(8,128)(2,1)S(1)}, u32[]{:S(2)}, u32[]{:S(2)}) collective-permute-start(bf16[128,768]{1,0:T(8,128)(2,1)S(1)} %slice.554), channel_id=1, source_target_pairs={{0,2},{1,3},{2,0},{3,1},{4,6},{5,7},{6,4},{7,5},{8,10},{9,11},{10,... | collective-permute-start | bytes 589832 | tf_op jit(solution)/shard_map/ppermute | solution.py:51
  232.8 27.6 %copy-start.6 = (bf16[32,24,896]{2,1,0:T(8,128)(2,1)S(1)}, bf16[32,24,896]{2,1,0:T(8,128)(2,1)}, u32[]{:S(2)}) copy-start(bf16[32,24,896]{2,1,0:T(8,128)(2,1)} %copy-done.5) | copy-start | bytes 4128772
  (39 other events, 67.7 us)

commit v3 on v2

v3 whole, which is shorter than its diff:
```python
import functools

import jax
import jax.numpy as jnp
import numpy as np
from jax import lax
from jax.experimental import pallas as pl
from jax.experimental.pallas import tpu as pltpu
from jax.sharding import PartitionSpec as P

HEAD_DIM = 64
TILE = 128
GROUP = 256


NORM_EPSILON = 1e-12
MASKED_SCORE = -1000000000.0
ROOT_HALF = 0.7071067811865476
INV_ROOT_TAU = 0.3989422804014327
LOW = jnp.bfloat16
FULL = jnp.float32
VMEM_LIMIT = 48 * 1024 * 1024


def contract(left, right, left_dim, right_dim):
    return lax.dot_general(
        left, right, (((left_dim,), (right_dim,)), ((), ())), preferred_element_type=jnp.float32
    )


def gelu_exact(values):
    return 0.5 * values * (1.0 + lax.erf(values * ROOT_HALF))


def gelu_slope(values):
    return (
        0.5 * (1.0 + lax.erf(values * ROOT_HALF))
        + values * jnp.exp(-0.5 * values * values) * INV_ROOT_TAU
    )


def norm_forward(values, gain, shift):
    center = values - jnp.mean(values, axis=-1, keepdims=True)
    scale_inv = lax.rsqrt(jnp.mean(center * center, axis=-1, keepdims=True) + NORM_EPSILON)
    normed = center * scale_inv
    return (normed * gain + shift, normed, scale_inv)


def norm_backward(upstream, normed, scale_inv, gain):
    scaled = upstream * gain
    return scale_inv * (
        scaled
        - jnp.mean(scaled, axis=-1, keepdims=True)
        - normed * jnp.mean(scaled * normed, axis=-1, keepdims=True)
    )


def swap(values, mask):
    return lax.ppermute(values, "tensor", [(i, i ^ mask) for i in range(4)])


def after(values, *others):
    return lax.optimization_barrier((values, *others))[0]


def spread(block):
    count = lax.axis_size("dp")
    stacked = jnp.broadcast_to(block[None], (count, *block.shape))
    return lax.all_to_all(stacked, "dp", 0, 0, tiled=True).reshape(-1, block.shape[1])


def scattered(values):
    count = lax.axis_size("dp")
    blocks = values.reshape(count, values.shape[0] // count, values.shape[1])
    return lax.all_to_all(blocks, "dp", 0, 0, tiled=True)


def halves(values):
    high = lax.reduce_precision(values, 8, 7)
    return (high.astype(LOW), (values - high).astype(LOW))


def core_sum(part):
    half = part.shape[0] // 2
    got = swap(part[half:].astype(LOW), 1)
    return part[:half] + got.astype(FULL)


def far_sum(total):
    quarter = total.shape[0] // 2
    sent = total.astype(LOW)
    sent = jnp.concatenate([sent[quarter:], sent[:quarter]], axis=0)
    return swap(sent, 2)


def core_join(rows):
    return jnp.concatenate([rows, swap(rows, 1)], axis=0)


def ordered_segments(segment_row, my_index):
    quarters = segment_row.reshape(4, -1)
    core = my_index % 2 == 1
    quarters = jnp.where(core, quarters[jnp.array([1, 0, 3, 2])], quarters)
    far = my_index // 2 == 1
    quarters = jnp.where(far, quarters[jnp.array([2, 3, 0, 1])], quarters)
    return jnp.concatenate([quarters[0], quarters[2], quarters[1], quarters[3]])


def call(body, out_shapes, *operands, smem=0):
    specs = [pl.BlockSpec(memory_space=pltpu.SMEM)] * smem
    specs += [pl.BlockSpec(memory_space=pltpu.VMEM)] * (len(operands) - smem)
    return pl.pallas_call(
        body,
        out_shape=[jax.ShapeDtypeStruct(shape, kind) for shape, kind in out_shapes],
        in_specs=specs,
        out_specs=[pl.BlockSpec(memory_space=pltpu.VMEM)] * len(out_shapes),
        compiler_params=pltpu.CompilerParams(vmem_limit_bytes=VMEM_LIMIT),
        cost_estimate=pl.CostEstimate(flops=1000, bytes_accessed=1000, transcendentals=0),
    )(*operands)


def lanes(shape, dim=1):
    return lax.broadcasted_iota(jnp.int32, shape, dim)


def head_tile(head):
    return head // 2


def head_mask(head, shape, dim=1):
    index = lanes(shape, dim)
    return index >= HEAD_DIM if head % 2 else index < HEAD_DIM


def only(values, mask):
    return jnp.where(mask, values, jnp.zeros_like(values))


def packed_out(weight_ref):
    rows = weight_ref.shape[0]
    parts = [
        weight_ref[:, GROUP * i + TILE : GROUP * (i + 1)].astype(FULL) for i in range(3)
    ]
    low = head_mask(0, (rows, TILE))
    first = jnp.where(low, pltpu.roll(parts[0], HEAD_DIM, 1), parts[1])
    second = jnp.where(low, pltpu.roll(parts[2], HEAD_DIM, 1), 0.0)
    return jnp.concatenate([first, second], axis=1).astype(LOW)


def lined_heads(rows):
    first, second = rows[:, :TILE], rows[:, TILE:]
    return [pltpu.roll(first, HEAD_DIM, 1), first, pltpu.roll(second, HEAD_DIM, 1)]


def transposed(values):
    return jnp.transpose(values.astype(FULL))


def expand_matrix(count):
    shape = (count, 4 * count)
    return jnp.where(lanes(shape) // 4 == lanes(shape, 0), 1.0, 0.0).astype(LOW)


def forward_kernel(
    index_ref,
    near_ref,
    other_ref,
    weight_ref,
    segment_ref,
    qkv_ref,
    mixed_ref,
    log_ref,
    send_ref,
    keep_ref,
    vector_ref,
    up_bias_ref,
):
    index = index_ref[0]
    half = near_ref.shape[0]
    columns = 3 * HEAD_DIM
    width = weight_ref.shape[0]
    held = weight_ref[:, 3 * GROUP :].astype(FULL)
    flat = jnp.transpose(held)
    vector_ref[...] = flat[:8] + flat[12:20]
    own = weight_ref[pl.ds(pl.multiple_of(index * columns, 64), columns), 3 * GROUP :].astype(FULL)
    own = jnp.concatenate([own, jnp.zeros((GROUP - columns, TILE), FULL)], axis=0)
    own = jnp.transpose(own)
    expand = expand_matrix(columns)
    wide = jnp.dot(own[:24, :].astype(LOW)[:, :GROUP], jnp.concatenate(
        [expand, jnp.zeros((GROUP - columns, 4 * columns), LOW)], axis=0
    ), preferred_element_type=FULL)
    up_bias = jnp.zeros((1, 4 * columns), FULL)
    place = lanes((1, 4 * columns)) % 4
    for step in range(4):
        row = wide[8 + step : 9 + step] + wide[20 + step : 21 + step]
        up_bias = jnp.where(place == step, row, up_bias)
    up_bias_ref[...] = up_bias
    bias = jnp.concatenate(
        [
            own[0:1] + own[12:13],
            jnp.zeros((1, GROUP), FULL),
            own[1:2] + own[13:14],
        ],
        axis=1,
    )
    keep = lanes((1, 3 * GROUP)) % GROUP < columns
    for at, rows_ref in ((0, near_ref), (half, other_ref)):
        got = jnp.dot(rows_ref[...], weight_ref[:, : 3 * GROUP], preferred_element_type=FULL)
        qkv_ref[at : at + half, :] = jnp.where(keep, got + bias, 0.0).astype(LOW)

    length = 2 * half
    row_segments = segment_ref[...]
    column_segments = jnp.transpose(
        jnp.broadcast_to(row_segments.astype(FULL), (TILE, length))
    )[:, :1].astype(jnp.int32)
    same = column_segments == row_segments
    mixed_tiles = [None, None]
    for head in range(3):
        at = TILE * head_tile(head)
        mask = head_mask(head, (length, TILE))
        key = only(qkv_ref[:, GROUP + at : GROUP + at + TILE], mask) * jnp.asarray(0.125, LOW)
        scores = contract(key, qkv_ref[:, at : at + TILE], 1, 1)
        scores = jnp.where(same, scores, MASKED_SCORE)
        highest = jnp.max(scores, axis=0, keepdims=True)
        shifted = jnp.exp(scores - highest)
        total = jnp.sum(shifted, axis=0, keepdims=True)
        probs = (shifted * (1.0 / total)).astype(LOW)
        log_ref[head : head + 1, :] = highest + jnp.log(total)
        value = only(qkv_ref[:, 2 * GROUP + at : 2 * GROUP + at + TILE], mask)
        got = jnp.dot(transposed(value).astype(LOW), probs, preferred_element_type=FULL)
        tile = head_tile(head)
        mixed_tiles[tile] = got if mixed_tiles[tile] is None else mixed_tiles[tile] + got
    log_ref[3:, :] = jnp.zeros((5, length), FULL)
    for tile in range(2):
        mixed_ref[:, TILE * tile : TILE * (tile + 1)] = jnp.transpose(mixed_tiles[tile]).astype(LOW)
    out = packed_out(weight_ref)
    keep_ref[...] = contract(mixed_ref[:half, :], out, 1, 1)
    send_ref[...] = contract(mixed_ref[half:, :], out, 1, 1).astype(LOW)


def backward_kernel(
    index_ref,
    near_ref,
    other_ref,
    qkv_ref,
    log_ref,
    weight_ref,
    segment_ref,
    sums_ref,
    up_sum_ref,
    grad_ref,
    send_ref,
    keep_ref,
    vector_ref,
    mixed_grad,
    key_grad,
    value_grad,
    columns_held,
):
    index = index_ref[0]
    half = near_ref.shape[0]
    length = 2 * half
    columns = 3 * HEAD_DIM
    out = packed_out(weight_ref)
    mixed_grad[:half, :] = jnp.dot(near_ref[...], out, preferred_element_type=FULL).astype(LOW)
    mixed_grad[half:, :] = jnp.dot(other_ref[...], out, preferred_element_type=FULL).astype(LOW)
    row_segments = segment_ref[...]
    column_segments = jnp.transpose(
        jnp.broadcast_to(row_segments.astype(FULL), (TILE, length))
    )[:, :1].astype(jnp.int32)
    same = column_segments == row_segments
    sums = []
    for tile in range(2):
        at = TILE * tile
        query_grad = jnp.zeros((TILE, length), FULL)
        for head in (0, 1) if tile == 0 else (2,):
            mask = head_mask(head, (length, TILE))
            scale = jnp.asarray(0.125, LOW)
            key = only(qkv_ref[:, GROUP + at : GROUP + at + TILE], mask) * scale
            query = only(qkv_ref[:, at : at + TILE], mask)
            value = only(qkv_ref[:, 2 * GROUP + at : 2 * GROUP + at + TILE], mask)
            grad = only(mixed_grad[:, at : at + TILE], mask)
            scores = contract(key, query, 1, 1)
            probs = jnp.exp(
                jnp.where(same, scores, MASKED_SCORE) - log_ref[head : head + 1, :]
            )
            probs_grad = contract(value, grad, 1, 1)
            inner = jnp.sum(probs * probs_grad, axis=0, keepdims=True)
            scores_grad = (probs * (probs_grad - inner)).astype(LOW)
            got = jnp.dot(probs.astype(LOW), grad, preferred_element_type=FULL)
            got_key = jnp.dot(scores_grad, query * scale, preferred_element_type=FULL)
            if head % 2 == 0:
                value_grad[...] = got
                key_grad[...] = got_key
            else:
                value_grad[...] += got
                key_grad[...] += got_key
            query_grad += jnp.dot(
                transposed(key).astype(LOW), scores_grad, preferred_element_type=FULL
            )
        query_low = jnp.transpose(query_grad).astype(LOW)
        value_low = value_grad[...].astype(LOW)
        grad_ref[:, at : at + TILE] = query_low
        grad_ref[:, GROUP + at : GROUP + at + TILE] = key_grad[...].astype(LOW)
        grad_ref[:, 2 * GROUP + at : 2 * GROUP + at + TILE] = value_low
        sums.append(
            (
                jnp.sum(query_low.astype(FULL), axis=0, keepdims=True),
                jnp.sum(value_low.astype(FULL), axis=0, keepdims=True),
            )
        )
    wide = weight_ref[:, : 3 * GROUP]
    keep_ref[...] = contract(grad_ref[:half, :], wide, 1, 1)
    send_ref[...] = contract(grad_ref[half:, :], wide, 1, 1).astype(LOW)

    up_row = up_sum_ref[...]
    place = lanes((8, 4 * columns))
    spaced = jnp.where(place % 4 == lanes((8, 4 * columns), 0), up_row, 0.0)
    high = spaced.astype(LOW)
    low = (spaced - high.astype(FULL)).astype(LOW)
    expand = expand_matrix(columns)
    up_rows = contract(high, expand, 1, 1) + contract(low, expand, 1, 1)
    up_rows = jnp.concatenate([up_rows, jnp.zeros((8, GROUP - columns), FULL)], axis=1)
    query_sum = jnp.concatenate([sums[0][0], sums[1][0]], axis=1)
    value_sum = jnp.concatenate([sums[0][1], sums[1][1]], axis=1)
    at_row = lanes((8, GROUP), 0)
    late = jnp.where(at_row == 6, query_sum, jnp.where(at_row == 7, value_sum, 0.0))
    stacked = jnp.concatenate([late, up_rows, jnp.zeros((TILE - 16, GROUP), FULL)], axis=0)
    columns_held[...] = jnp.zeros_like(columns_held)
    columns_held[pl.ds(pl.multiple_of(index * columns, 64), columns), :] = jnp.transpose(stacked)[
        :columns
    ]
    placed = jnp.transpose(columns_held[...])[:16]
    given = sums_ref[...]
    vector_ref[:8, :] = placed[:8] + given
    vector_ref[8:, :] = placed[8:]


def weights_kernel(tokens_near, tokens_other, near_ref, other_ref, grad_ref, mixed_ref, out_ref):
    half = near_ref.shape[0]
    width = near_ref.shape[1]
    got = contract(tokens_near[...], grad_ref[:half, :], 0, 0) + contract(
        tokens_other[...], grad_ref[half:, :], 0, 0
    )
    out_grad = contract(near_ref[...], mixed_ref[:half, :], 0, 0) + contract(
        other_ref[...], mixed_ref[half:, :], 0, 0
    )
    high = head_mask(1, (width, TILE))
    for part, lined in enumerate(lined_heads(out_grad)):
        at = GROUP * part
        out_ref[:, at : at + TILE] = got[:, at : at + TILE].astype(LOW)
        out_ref[:, at + TILE : at + GROUP] = jnp.where(
            high, lined, got[:, at + TILE : at + GROUP]
        ).astype(LOW)
    out_ref[:, 3 * GROUP :] = jnp.zeros((width, TILE), LOW)


def packing(vector_rows):
    place = np.arange(12 * vector_rows)
    many = 8 * vector_rows
    row = np.where(place < many, place % vector_rows, (place - many) // 4)
    column = np.where(place < many, place // vector_rows, 8 + (place - many) % 4)
    rows = (row[None, :] == np.arange(vector_rows)[:, None]).astype(np.float32)
    columns = (column[:, None] == np.arange(12)[None, :]).astype(np.float32)
    return (rows, columns)


def shards(
    tokens,
    segments,
    q_weight,
    k_weight,
    v_weight,
    up_weight,
    out_weight,
    down_weight,
    q_bias,
    v_bias,
    out_bias,
    up_bias,
    down_bias,
    norm1_gain,
    norm1_shift,
    norm2_gain,
    norm2_shift,
    cotangent,
):
    my_index = lax.axis_index("tensor")
    local_len, width = tokens.shape[1:]
    half = 2 * local_len
    length = 4 * local_len
    head_cols = q_weight.shape[1]
    hidden_cols = up_weight.shape[1]
    tokens = tokens[0]
    cotangent = cotangent[0]
    index = my_index.reshape(1)

    vector_rows = q_bias.shape[0]
    row_place, column_place = packing(vector_rows)
    flat = jnp.concatenate(
        [
            q_bias,
            v_bias,
            out_bias,
            down_bias,
            norm1_gain,
            norm1_shift,
            norm2_gain,
            norm2_shift,
            up_bias,
        ]
    )
    high, low = halves(flat)
    spaced = jnp.concatenate([high * row_place.astype(LOW), low * row_place.astype(LOW)], axis=1)
    spaced = jnp.pad(spaced, ((0, 2), (0, 0)))
    select = np.zeros((2 * flat.shape[0], TILE), np.float32)
    select[: flat.shape[0], :12] = column_place
    select[flat.shape[0] :, 12:24] = column_place
    packed = jnp.dot(spaced, select.astype(LOW), preferred_element_type=FULL).astype(LOW)
    near = [packed] + [swap(packed, mask) for mask in (1, 2, 3)]
    tokens_far = swap(tokens, 2)
    near = [block[:vector_rows] for block in near]
    core = my_index % 2 == 1
    near = [
        jnp.where(core, near[1], near[0]),
        jnp.where(core, near[0], near[1]),
        jnp.where(core, near[3], near[2]),
        jnp.where(core, near[2], near[3]),
    ]
    far = my_index // 2 == 1
    near = jnp.concatenate(
        [
            jnp.where(far, near[2], near[0]),
            jnp.where(far, near[3], near[1]),
            jnp.where(far, near[0], near[2]),
            jnp.where(far, near[1], near[3]),
        ],
        axis=0,
    )
    pads = [out_weight[:, HEAD_DIM * i : HEAD_DIM * (i + 1)] for i in range(3)]
    first_block = jnp.concatenate(
        [q_weight, pads[0], k_weight, pads[1], v_weight, pads[2], near], axis=1
    )
    first_full = spread(first_block)
    tokens_pair = jnp.concatenate([tokens, tokens_far], axis=0)
    tokens_core = swap(tokens_pair, 1)
    cotangent_far = swap(after(cotangent, tokens_far), 2)
    segment_row = ordered_segments(segments[0], my_index)[None]
    second_block = jnp.concatenate([up_weight, down_weight], axis=1)
    first_full, second_block, tokens_core, cotangent_far, segment_row = lax.optimization_barrier(
        (first_full, second_block, tokens_core, cotangent_far, segment_row)
    )
    second_full = spread(second_block)
    up_full, down_full = second_full[:, :hidden_cols], second_full[:, hidden_cols:]

    qkv_rows, mixed_rows, log_totals, attn_send, attn_keep, rows, bias_up = call(
        forward_kernel,
        [
            ((length, 3 * GROUP), LOW),
            ((length, GROUP), LOW),
            ((8, length), FULL),
            ((half, width), LOW),
            ((half, width), FULL),
            ((8, width), FULL),
            ((1, hidden_cols), FULL),
        ],
        index,
        tokens_pair,
        tokens_core,
        first_full,
        segment_row,
        smem=1,
    )
    gain_first, shift_first, gain_second, shift_second = rows[4], rows[5], rows[6], rows[7]
    bias_out, bias_down = rows[2], rows[3]
    attn_chip = attn_keep + swap(attn_send, 1).astype(FULL)
    attn_far = far_sum(attn_chip)
    first, normed_first, inv_first = norm_forward(
        tokens_pair.astype(FULL) + (attn_chip + attn_far.astype(FULL)) + bias_out,
        gain_first,
        shift_first,
    )
    hidden_full = core_join(first.astype(LOW))
    upward = jnp.dot(hidden_full, up_full, preferred_element_type=FULL) + bias_up
    active = gelu_exact(upward).astype(LOW)
    branch_chip = core_sum(contract(active, down_full, 1, 1))
    branch = branch_chip + far_sum(branch_chip).astype(FULL)
    layer_output, normed_second, inv_second = norm_forward(
        first + branch + bias_down, gain_second, shift_second
    )

    cotangent_pair = jnp.concatenate([cotangent, cotangent_far], axis=0).astype(FULL)
    second_grad = norm_backward(cotangent_pair, normed_second, inv_second, gain_second)
    cotangent_own = cotangent_pair[:local_len]
    grad_gain_second = jnp.sum(cotangent_own * normed_second[:local_len], axis=0)
    grad_shift_second = jnp.sum(cotangent_own, axis=0)
    branch_low = second_grad.astype(LOW)
    grad_bias_down = jnp.sum(branch_low[:local_len].astype(FULL), axis=0)
    branch_full = core_join(branch_low)
    active_grad = jnp.dot(branch_full, down_full, preferred_element_type=FULL)
    upward_grad = (active_grad * gelu_slope(upward)).astype(LOW)
    hidden_chip = core_sum(contract(upward_grad, up_full, 1, 1))
    hidden_far = far_sum(hidden_chip)
    grad_down = contract(branch_full, active, 0, 0)
    grad_up = contract(hidden_full, upward_grad, 0, 0)
    grad_bias_up = jnp.sum(upward_grad.astype(FULL), axis=0)
    pair_blocks = scattered(
        jnp.concatenate(
            [after(grad_up, hidden_chip).astype(LOW), after(grad_down, hidden_chip).astype(LOW)],
            axis=1,
        )
    )
    first_grad = second_grad + (hidden_chip + hidden_far.astype(FULL))
    resid_grad = norm_backward(first_grad, normed_first, inv_first, gain_first)
    first_own = first_grad[:local_len]
    grad_gain_first = jnp.sum(first_own * normed_first[:local_len], axis=0)
    grad_shift_first = jnp.sum(first_own, axis=0)
    attended_low = resid_grad.astype(LOW)
    grad_bias_out = jnp.sum(attended_low[:local_len].astype(FULL), axis=0)
    attended_core = swap(attended_low, 1)
    zero_row = jnp.zeros((width,), FULL)
    given = jnp.stack(
        [
            grad_bias_out,
            grad_bias_down,
            grad_gain_first,
            grad_shift_first,
            grad_gain_second,
            grad_shift_second,
            zero_row,
            zero_row,
        ]
    )
    qkv_grad, input_send, input_keep, vector_sums = pl.pallas_call(
        backward_kernel,
        out_shape=[
            jax.ShapeDtypeStruct((length, 3 * GROUP), LOW),
            jax.ShapeDtypeStruct((half, width), LOW),
            jax.ShapeDtypeStruct((half, width), FULL),
            jax.ShapeDtypeStruct((16, width), FULL),
        ],
        in_specs=[pl.BlockSpec(memory_space=pltpu.SMEM)]
        + [pl.BlockSpec(memory_space=pltpu.VMEM)] * 8,
        out_specs=[pl.BlockSpec(memory_space=pltpu.VMEM)] * 4,
        scratch_shapes=[
            pltpu.VMEM((length, GROUP), LOW),
            pltpu.VMEM((length, TILE), FULL),
            pltpu.VMEM((length, TILE), FULL),
            pltpu.VMEM((width, TILE), FULL),
        ],
        compiler_params=pltpu.CompilerParams(vmem_limit_bytes=VMEM_LIMIT),
        cost_estimate=pl.CostEstimate(flops=1000, bytes_accessed=1000, transcendentals=0),
    )(
        index,
        attended_low,
        attended_core,
        qkv_rows,
        log_totals,
        first_full,
        segment_row,
        given,
        grad_bias_up[None],
    )
    vector_near = [swap(vector_sums, mask) for mask in (1, 2, 3)]
    input_got = swap(input_send, 1)
    (last_block,) = call(
        weights_kernel,
        [((width, 3 * GROUP + TILE), LOW)],
        tokens_pair,
        tokens_core,
        attended_low,
        attended_core,
        qkv_grad,
        mixed_rows,
    )
    vector_sums = vector_sums + vector_near[0] + vector_near[1] + vector_near[2]
    high, low = halves(vector_sums[:12].T)
    last_block = lax.dynamic_update_slice(
        last_block, jnp.concatenate([high, low], axis=1), (0, 3 * GROUP)
    )
    input_chip = input_keep + input_got.astype(FULL)
    input_far = swap(input_chip[local_len:].astype(LOW), 2)
    last_blocks = scattered(after(last_block, input_chip))
    input_grad = resid_grad[:local_len] + (input_chip[:local_len] + input_far.astype(FULL))

    pair_sum = jnp.sum(pair_blocks.astype(FULL), axis=0)
    up_sum, down_sum = pair_sum[:, :hidden_cols], pair_sum[:, hidden_cols:]
    last_sum = jnp.sum(last_blocks.astype(FULL), axis=0)
    columns = last_sum[:, 3 * GROUP :]
    columns = columns[:, :12] + columns[:, 12:24]
    columns = lax.dynamic_slice_in_dim(columns, my_index * vector_rows, vector_rows, axis=0)
    return (
        layer_output[:local_len].astype(LOW)[None],
        input_grad[None],
        last_sum[:, :head_cols],
        last_sum[:, GROUP : GROUP + head_cols],
        last_sum[:, 2 * GROUP : 2 * GROUP + head_cols],
        up_sum,
        jnp.concatenate(
            [last_sum[:, GROUP * i + head_cols : GROUP * (i + 1)] for i in range(3)], axis=1
        ),
        down_sum,
        columns[:, 6],
        columns[:, 7],
        columns[:, 0],
        columns[:, 8:12].reshape(-1),
        columns[:, 1],
        columns[:, 2],
        columns[:, 3],
        columns[:, 4],
        columns[:, 5],
    )


def solution(mesh):
    matrix = P("dp", "tensor")
    vector = P(("dp", "tensor"))
    rows = P("dp", "tensor", None)
    return jax.shard_map(
        shards,
        mesh=mesh,
        in_specs=(rows, P("dp", None)) + (matrix,) * 6 + (vector,) * 9 + (rows,),
        out_specs=(rows, rows) + (matrix,) * 6 + (vector,) * 9,
        check_vma=False,
    )
```

time: 267 us -> 219 us (0.82)
  waiting for transfers between devices: 129 us -> 100 us
  local copies, waits for them, and re-layouts: 35.9 us -> 18.3 us
  matrix products: 27 us -> 12.6 us
  Pallas kernels: 0 us -> 10.1 us
  starting transfers between devices: 52 us -> 55.6 us
    all_to_all x2, waiting for transfers between devices: 16.4 us -> 0.01 us  [scattered(): return lax.all_to_all(blocks, 'dp', 0, 0, tiled=True)]
    dot_general x20 -> x4, matrix products: 17.6 us -> 6.89 us  [contract(): lax.dot_general(left, right, (((left_dim,), (right_dim,)), ((), ())), pre...]
    pallas_call x0 -> x3, Pallas kernels: none -> 10.1 us  [the longest x2 5.75 us: call(): pl.pallas_call(body, out_shape=[jax.ShapeDtypeStruct(shape, kind) for sha...]
    ppermute x20, waiting for transfers between devices: 107 us -> 100 us  [swap(): return lax.ppermute(values, 'tensor', [(i, i ^ mask) for i in range(4)])]
    all_to_all x3 -> x2, waiting for transfers between devices: 5.99 us -> 0.01 us  [spread(): lax.all_to_all(stacked, 'dp', 0, 0, tiled=True).reshape(-1, block.shape[1])]
    all_to_all x2, starting transfers between devices: 14.5 us -> 20.4 us  [scattered(): return lax.all_to_all(blocks, 'dp', 0, 0, tiled=True)]
    another operation x8, local copies, waits for them, and re-layouts: 5.93 us -> 0.07 us  [shards(): jnp.stack([grad_bias_out, grad_bias_down, grad_gain_first, grad_shift_fir...]
    all_to_all x3 -> x2, starting transfers between devices: 19.8 us -> 16 us  [spread(): lax.all_to_all(stacked, 'dp', 0, 0, tiled=True).reshape(-1, block.shape[1])]
  transfers between devices with their start and end apart: 25 -> 24, of which waited for: 13 -> 10; matrix products, arithmetic and copies ran while one was open for 14% -> 12% of each run, Pallas kernels for 0% -> 3%
where the time goes in v3:
time: 219 us; the launch traced here: 217 us
  waiting for transfers between devices  100 us (46%)
  starting transfers between devices  55.6 us (25%)
  other arithmetic  18.7 us (9%)
  local copies, waits for them, and re-layouts  18.3 us (8%)
  matrix products  12.6 us (6%)
  Pallas kernels  10.1 us (5%)
    ppermute x20, waiting for transfers between devices, swap(): return lax.ppermute(values, 'tensor', [(i, i ^ mask) for i in range(4)])  100 us
    all_to_all x2, starting transfers between devices, scattered(): return lax.all_to_all(blocks, 'dp', 0, 0, tiled=True)  20.4 us
    ppermute x20, starting transfers between devices, swap(): return lax.ppermute(values, 'tensor', [(i, i ^ mask) for i in range(4)])  19.1 us
    all_to_all x2, starting transfers between devices, spread(): lax.all_to_all(stacked, 'dp', 0, 0, tiled=True).reshape(-1, block.shape[1])  16 us
    dot_general x4, matrix products, contract(): lax.dot_general(left, right, (((left_dim,), (right_dim,)), ((), ())), pre...  6.89 us
    unnamed x42, local copies, waits for them, and re-layouts  5.76 us
    pallas_call x2, Pallas kernels, call(): pl.pallas_call(body, out_shape=[jax.ShapeDtypeStruct(shape, kind) for sha...  5.75 us
    pallas_call x1, Pallas kernels, shards(): pl.pallas_call(backward_kernel, out_shape=[jax.ShapeDtypeStruct((length,...  4.39 us
  transfers between devices with their start and end apart: 24, of which 10 were waited for; matrix products, arithmetic and copies ran while one was open for 12% of the time, Pallas kernels for 3%

profile of v3, /device:TPU:0, one launch (start us, length us, event | category | flops | bytes accessed | tf_op | source)
XLA Modules:
  0.0 216.8 jit_solution(7548324261576188829)
XLA Ops:
  0.7 0.9 concatenate.59
  2.2 1.0 convolution_convert_fusion
  3.2 2.7 %collective-permute-start.1 = (bf16[8,128]{1,0:T(8,128)(2,1)S(1)}, bf16[8,128]{1,0:T(8,128)(2,1)S(1)}, u32[]{:S(2)}, u32[]{:S(2)}) collective-permute-start(bf16[8,128]{1,0:T(8,128)(2,1)S(1)} %convolution_convert_fusion), channel_id=1, source_target_pairs={{0,3},{1,2},{2,1},{3,0},{4,7},{5,6},{6,5},{7,4},{8,11},{9,10},{10,... | collective-permute-start | bytes 6152 | tf_op jit(solution)/shard_map/ppermute | solution.py:59
  6.6 3.2 %collective-permute-start = (bf16[128,768]{1,0:T(8,128)(2,1)}, bf16[128,768]{1,0:T(8,128)(2,1)S(1)}, u32[]{:S(2)}, u32[]{:S(2)}) collective-permute-start(bf16[128,768]{1,0:T(8,128)(2,1)} %bitcast.39), channel_id=1, source_target_pairs={{0,2},{1,3},{2,0},{3,1},{4,6},{5,7},{6,4},{7,5},{8,10},{9,11},{10,... | collective-permute-start | bytes 589832 | tf_op jit(solution)/shard_map/ppermute | solution.py:59
  9.8 0.8 fusion.54
  11.0 0.8 concatenate.62
  11.8 1.2 broadcast_in_dim.16
  13.1 8.4 %all-to-all-start = ((bf16[32,24,896]{2,1,0:T(8,128)(2,1)}), bf16[32,24,896]{2,1,0:T(8,128)(2,1)S(1)}, u32[]{:S(2)}, u32[]{:S(2)}) async-start(bf16[32,24,896]{2,1,0:T(8,128)(2,1)} %broadcast_in_dim.16), calls=%async_computation | async-start | bytes 2752512 | tf_op jit(solution)/shard_map/all_to_all | solution.py:69
  23.6 1.9 collective-permute-start.5
  25.5 16.9 %collective-permute-done.5 = bf16[128,768]{1,0:T(8,128)(2,1)S(1)} collective-permute-done((bf16[128,768]{1,0:T(8,128)(2,1)S(1)}, bf16[128,768]{1,0:T(8,128)(2,1)S(1)}, u32[]{:S(2)}, u32[]{:S(2)}) %collective-permute-start.5) | collective-permute-done | bytes 196640 | tf_op jit(solution)/shard_map/ppermute | solution.py:59
  42.4 3.5 %shard_map.350 = (bf16[512,768]{1,0:T(8,128)(2,1)S(1)}, bf16[512,256]{1,0:T(8,128)(2,1)S(1)}, f32[8,512]{1,0:T(8,128)S(1)}, bf16[256,768]{1,0:T(8,128)(2,1)}, f3...) custom-call(s32[1]{0:T(128)} %bitcast.1.index_ref, ...), custom_call_target="tpu_custom_call" | custom-call | flops 1000 | bytes 1000 | tf_op jit(solution)/shard_map/pallas_call | solution.py:112
  45.9 0.9 copy-done
  47.5 1.5 broadcast_in_dim.20
  49.1 7.6 %all-to-all-start.1 = ((bf16[32,24,1536]{2,1,0:T(8,128)(2,1)}), bf16[32,24,1536]{2,1,0:T(8,128)(2,1)}, u32[]{:S(2)}, u32[]{:S(2)}) async-start(bf16[32,24,1536]{2,1,0:T(8,128)(2,1)} %broadcast_in_dim.20), calls=%async_computation.1 | async-start | bytes 4718592 | tf_op jit(solution)/shard_map/all_to_all | solution.py:69
  56.7 1.1 fusion.13
  57.9 3.0 %collective-permute-start.7 = (bf16[256,768]{1,0:T(8,128)(2,1)S(1)}, bf16[256,768]{1,0:T(8,128)(2,1)S(1)}, u32[]{:S(2)}, u32[]{:S(2)}) collective-permute-start(bf16[256,768]{1,0:T(8,128)(2,1)S(1)} %pad_maximum_fusion.8), channel_id=1, source_target_pairs={{0,2},{1,3},{2,0},{3,1},{4,6},{5,7},{6,4},{7,5},{8,10},{9,11},{10,... | collective-permute-start | bytes 1179656 | tf_op jit(solution)/shard_map/ppermute | solution.py:59
  61.0 34.2 %collective-permute-done.7 = bf16[256,768]{1,0:T(8,128)(2,1)S(1)} collective-permute-done((bf16[256,768]{1,0:T(8,128)(2,1)S(1)}, bf16[256,768]{1,0:T(8,128)(2,1)S(1)}, u32[]{:S(2)}, u32[]{:S(2)}) %collective-permute-start.7) | collective-permute-done | bytes 393248 | tf_op jit(solution)/shard_map/ppermute | solution.py:59
  95.2 1.3 fusion.46
  96.8 1.0 fusion.12
  97.8 2.0 collective-permute-done.8
  99.8 2.4 %multiply_convert_fusion = (bf16[512,768]{1,0:T(8,128)(2,1)S(1)}, f32[512,768]{1,0:T(8,128)S(1)}) fusion(f32[768]{0:T(1024)S(1)} %reduce.3, bf16[768,1536]{1,0:T(8,128)(2,1)} %bitcast.10, bf16[256,768]{1,0:T(8,128)(2,1)} %collective-permute-done.8, bf16[256,768]{1,0:T(8,128)(2,1)} %get-tuple-element.89), kind=kOutput, calls=%fused_computation.13 | convolution fusion | flops 607911936 | bytes 4328448 | tf_op jit(solution)/shard_map/dot_general | solution.py:484
  102.2 2.1 fusion.7
  104.6 1.6 collective-permute-done.9
  107.0 12.0 %collective-permute-done.10 = bf16[256,768]{1,0:T(8,128)(2,1)S(1)} collective-permute-done((bf16[256,768]{1,0:T(8,128)(2,1)S(1)}, bf16[256,768]{1,0:T(8,128)(2,1)S(1)}, u32[]{:S(2)}, u32[]{:S(2)}) %collective-permute-start.10) | collective-permute-done | bytes 393248 | tf_op jit(solution)/shard_map/ppermute | solution.py:59
  119.9 0.9 copy-done.7
  121.4 0.9 fusion.40
  123.1 2.4 %convert_reduce_fusion.2 = (f32[768]{0:T(1024)S(1)}, bf16[512,768]{1,0:T(8,128)(2,1)S(1)}) fusion(f32[512,768]{1,0:T(8,128)S(1)} %get-tuple-element.126, bf16[768,1536]{1,0:T(8,128)(2,1)} %bitcast.10, bf16[256,768]{1,0:T(8,128)(2,1)S(1)} %collective-permute-done.11, bf16[256,768]{1,0:T(8,128)(2,1)S(1)} %fusion.41), kind=kOutput, calls=%fused_computation.12 | convolution fusion | flops 610270464 | bytes 4328448 | tf_op jit(solution)/shard_map/dot_general | solution.py:500
  125.4 2.1 fusion.9
  127.8 1.9 fusion.15
  129.8 1.0 fusion.44
  133.0 1.6 pad_maximum_fusion
  134.6 9.7 %all-to-all-start.3 = ((bf16[32,24,1536]{2,1,0:T(8,128)(2,1)}), bf16[32,24,1536]{2,1,0:T(8,128)(2,1)}, u32[]{:S(2)}, u32[]{:S(2)}) async-start(bf16[32,24,1536]{2,1,0:T(8,128)(2,1)} %bitcast.33), calls=%async_computation.3 | async-start | bytes 4718592 | tf_op jit(solution)/shard_map/all_to_all | solution.py:75
  144.8 2.0 multiply_reduce_fusion.4
  146.8 1.1 fusion.43
  149.2 1.1 slice_reduce_fusion.1
  150.4 1.1 copy-done.1
  151.6 4.4 %shard_map.351 = (bf16[512,768]{1,0:T(8,128)(2,1)S(1)}, bf16[256,768]{1,0:T(8,128)(2,1)}, f32[256,768]{1,0:T(8,128)S(1)}, f32[16,768]{1,0:T(8,128)S(1)}) custom-call(s32[1]{0:T(128)} %bitcast.1.index_ref, bf16[256,768]{1,0:T(8,128)(2,1)S(1)} %get-tuple-element.81.near_ref, bf16[256,768]{1,0:T(8,128)(2,1)S(1)} %collective-permute-done.14.other_ref, ...), custom_call_target="tpu_custom_call" | custom-call | flops 1000 | bytes 1000 | tf_op jit(solution)/shard_map/pallas_call | solution.py:534
  156.0 0.9 copy-done.2
  156.9 2.4 %collective-permute-start.18 = (f32[16,768]{1,0:T(8,128)S(1)}, f32[16,768]{1,0:T(8,128)S(1)}, u32[]{:S(2)}, u32[]{:S(2)}) collective-permute-start(f32[16,768]{1,0:T(8,128)S(1)} %get-tuple-element.53), channel_id=1, source_target_pairs={{0,2},{1,3},{2,0},{3,1},{4,6},{5,7},{6,4},{7,5},{8,10},{9,11},{10,... | collective-permute-start | bytes 147464 | tf_op jit(solution)/shard_map/ppermute | solution.py:59
  159.3 0.9 collective-permute-start.19
  160.5 2.2 %shard_map.352 = bf16[768,896]{1,0:T(8,128)(2,1)} custom-call(bf16[256,768]{1,0:T(8,128)(2,1)S(1)} %pad_maximum_fusion.7.near_ref.tokens_near, bf16[256,768]{1,0:T(8,128)(2,1)S(1)} %collective-permute-done.4.other_ref.tokens_other, bf16[256,768]{1,0:T(8,128)(2,1)S(1)} %get-tuple-element.81.near_ref, bf16[256,768]{1,0:T(8,128)(2,1)S(1)} %collective-permute-done.14.other_ref, ...), custom_call_target="tpu_custom_call" | custom-call | flops 1000 | bytes 1000 | tf_op jit(solution)/shard_map/pallas_call | solution.py:112
  162.7 12.3 %collective-permute-done.18 = f32[16,768]{1,0:T(8,128)S(1)} collective-permute-done((f32[16,768]{1,0:T(8,128)S(1)}, f32[16,768]{1,0:T(8,128)S(1)}, u32[]{:S(2)}, u32[]{:S(2)}) %collective-permute-start.18) | collective-permute-done | bytes 49184 | tf_op jit(solution)/shard_map/ppermute | solution.py:59
  175.3 2.7 %dynamic_update_slice.3 = bf16[768,896]{1,0:T(8,128)(2,1)} dynamic-update-slice(bf16[768,896]{1,0:T(8,128)(2,1)} %shard_map.352, bf16[768,24]{1,0:T(8,128)(2,1)S(1)} %copy.44, s32[]{:T(128)} %constant.62.clone.1, s32[]{:T(128)} %constant.75.clone.1) | dynamic-update-slice | bytes 73732 | tf_op jit(solution)/shard_map/dynamic_update_slice | solution.py:578
  178.1 10.8 %all-to-all-start.2 = ((bf16[32,24,896]{2,1,0:T(8,128)(2,1)}), bf16[32,24,896]{2,1,0:T(8,128)(2,1)S(1)}, u32[]{:S(2)}, u32[]{:S(2)}) async-start(bf16[32,24,896]{2,1,0:T(8,128)(2,1)} %bitcast.14), calls=%async_computation.2 | async-start | bytes 2752512 | tf_op jit(solution)/shard_map/all_to_all | solution.py:75
  188.9 1.8 collective-permute-start.16
  190.7 19.5 %collective-permute-done.16 = bf16[128,768]{1,0:T(8,128)(2,1)S(1)} collective-permute-done((bf16[128,768]{1,0:T(8,128)(2,1)S(1)}, bf16[128,768]{1,0:T(8,128)(2,1)S(1)}, u32[]{:S(2)}, u32[]{:S(2)}) %collective-permute-start.16) | collective-permute-done | bytes 196640 | tf_op jit(solution)/shard_map/ppermute | solution.py:59
  211.0 2.0 convert_reduce_fusion
  214.0 0.8 slice_reduce_fusion.2
  (134 shorter events, 16.9 us)
Async XLA Ops:
  3.2 7.5 %collective-permute-start.1 = (bf16[8,128]{1,0:T(8,128)(2,1)S(1)}, bf16[8,128]{1,0:T(8,128)(2,1)S(1)}, u32[]{:S(2)}, u32[]{:S(2)}) collective-permute-start(bf16[8,128]{1,0:T(8,128)(2,1)S(1)} %convolution_convert_fusion), channel_id=1, source_target_pairs={{0,3},{1,2},{2,1},{3,0},{4,7},{5,6},{6,5},{7,4},{8,11},{9,10},{10,... | collective-permute-start | bytes 6152 | tf_op jit(solution)/shard_map/ppermute | solution.py:59
  5.9 5.1 %collective-permute-start.2 = (bf16[8,128]{1,0:T(8,128)(2,1)S(1)}, bf16[8,128]{1,0:T(8,128)(2,1)S(1)}, u32[]{:S(2)}, u32[]{:S(2)}) collective-permute-start(bf16[8,128]{1,0:T(8,128)(2,1)S(1)} %convolution_convert_fusion), channel_id=1, source_target_pairs={{0,2},{1,3},{2,0},{3,1},{4,6},{5,7},{6,4},{7,5},{8,10},{9,11},{10,... | collective-permute-start | bytes 6152 | tf_op jit(solution)/shard_map/ppermute | solution.py:59
  6.5 4.5 %collective-permute-start.3 = (bf16[8,128]{1,0:T(8,128)(2,1)S(1)}, bf16[8,128]{1,0:T(8,128)(2,1)S(1)}, u32[]{:S(2)}, u32[]{:S(2)}) collective-permute-start(bf16[8,128]{1,0:T(8,128)(2,1)S(1)} %convolution_convert_fusion), channel_id=1, source_target_pairs={{0,1},{1,0},{2,3},{3,2},{4,5},{5,4},{6,7},{7,6},{8,9},{9,8},{10,11... | collective-permute-start | bytes 6152 | tf_op jit(solution)/shard_map/ppermute | solution.py:59
  6.6 16.1 %collective-permute-start = (bf16[128,768]{1,0:T(8,128)(2,1)}, bf16[128,768]{1,0:T(8,128)(2,1)S(1)}, u32[]{:S(2)}, u32[]{:S(2)}) collective-permute-start(bf16[128,768]{1,0:T(8,128)(2,1)} %bitcast.39), channel_id=1, source_target_pairs={{0,2},{1,3},{2,0},{3,1},{4,6},{5,7},{6,4},{7,5},{8,10},{9,11},{10,... | collective-permute-start | bytes 589832 | tf_op jit(solution)/shard_map/ppermute | solution.py:59
  13.0 8.5 %copy-start.20 = (s32[4]{0:T(128)S(1)}, s32[4]{0:T(128)}, u32[]{:S(2)}) copy-start(s32[4]{0:T(128)} %constant.110) | copy-start | bytes 52
  13.0 8.5 %copy-start.16 = (s32[1,512]{1,0:T(1,128)S(1)}, s32[1,512]{1,0:T(1,128)}, u32[]{:S(2)}) copy-start(s32[1,512]{1,0:T(1,128)} %param.24) | copy-start | bytes 6148
  13.0 9.1 %copy-start.19 = (s32[4]{0:T(128)S(1)}, s32[4]{0:T(128)}, u32[]{:S(2)}) copy-start(s32[4]{0:T(128)} %constant.111) | copy-start | bytes 52
  13.0 10.4 %copy-start.12 = (bf16[1,128,768]{2,1,0:T(8,128)(2,1)S(1)}, bf16[1,128,768]{2,1,0:T(8,128)(2,1)}, u32[]{:S(2)}) copy-start(bf16[1,128,768]{2,1,0:T(8,128)(2,1)} %param.23) | copy-start | bytes 589828
  13.0 10.5 %copy-start.9 = (bf16[1,128,768]{2,1,0:T(8,128)(2,1)S(1)}, bf16[1,128,768]{2,1,0:T(8,128)(2,1)}, u32[]{:S(2)}) copy-start(bf16[1,128,768]{2,1,0:T(8,128)(2,1)} %param.40) | copy-start | bytes 589828
  13.1 12.4 %copy-start.17 = (bf16[24,768]{1,0:T(8,128)(2,1)S(1)}, bf16[24,768]{1,0:T(8,128)(2,1)}, u32[]{:S(2)}) copy-start(bf16[24,768]{1,0:T(8,128)(2,1)} %param.30) | copy-start | bytes 110596
  13.1 12.4 %copy-start.18 = (bf16[24,768]{1,0:T(8,128)(2,1)S(1)}, bf16[24,768]{1,0:T(8,128)(2,1)}, u32[]{:S(2)}) copy-start(bf16[24,768]{1,0:T(8,128)(2,1)} %param.28) | copy-start | bytes 110596
  13.1 29.3 %all-to-all-start = ((bf16[32,24,896]{2,1,0:T(8,128)(2,1)}), bf16[32,24,896]{2,1,0:T(8,128)(2,1)S(1)}, u32[]{:S(2)}, u32[]{:S(2)}) async-start(bf16[32,24,896]{2,1,0:T(8,128)(2,1)} %broadcast_in_dim.16), calls=%async_computation | async-start | bytes 2752512 | tf_op jit(solution)/shard_map/all_to_all | solution.py:69
  22.7 0.7 copy-start.14
  23.4 19.0 %collective-permute-start.4 = (bf16[256,768]{1,0:T(8,128)(2,1)S(1)}, bf16[256,768]{1,0:T(8,128)(2,1)S(1)}, u32[]{:S(2)}, u32[]{:S(2)}) collective-permute-start(bf16[256,768]{1,0:T(8,128)(2,1)S(1)} %pad_maximum_fusion.7.near_ref.tokens_near), channel_id=1, source_target_pairs={{0,1},{1,0},{2,3},{3,2},{4,5},{5,4},{6,7},{7,6},{8,9},{9,8},{10,11... | collective-permute-start | bytes 1179656 | tf_op jit(solution)/shard_map/ppermute | solution.py:59
  23.6 18.8 %collective-permute-start.5 = (bf16[128,768]{1,0:T(8,128)(2,1)S(1)}, bf16[128,768]{1,0:T(8,128)(2,1)S(1)}, u32[]{:S(2)}, u32[]{:S(2)}) collective-permute-start(bf16[128,768]{1,0:T(8,128)(2,1)S(1)} %bitcast.34), channel_id=1, source_target_pairs={{0,2},{1,3},{2,0},{3,1},{4,6},{5,7},{6,4},{7,5},{8,10},{9,11},{10,... | collective-permute-start | bytes 589832 | tf_op jit(solution)/shard_map/ppermute | solution.py:59
  45.9 0.9 copy-start
  46.8 0.7 copy-start.4
  47.5 9.2 %collective-permute-start.6 = (bf16[256,768]{1,0:T(8,128)(2,1)}, bf16[256,768]{1,0:T(8,128)(2,1)}, u32[]{:S(2)}, u32[]{:S(2)}) collective-permute-start(bf16[256,768]{1,0:T(8,128)(2,1)} %get-tuple-element.42), channel_id=1, source_target_pairs={{0,1},{1,0},{2,3},{3,2},{4,5},{5,4},{6,7},{7,6},{8,9},{9,8},{10,11... | collective-permute-start | bytes 1179656 | tf_op jit(solution)/shard_map/ppermute | solution.py:59
  49.1 50.7 %all-to-all-start.1 = ((bf16[32,24,1536]{2,1,0:T(8,128)(2,1)}), bf16[32,24,1536]{2,1,0:T(8,128)(2,1)}, u32[]{:S(2)}, u32[]{:S(2)}) async-start(bf16[32,24,1536]{2,1,0:T(8,128)(2,1)} %broadcast_in_dim.20), calls=%async_computation.1 | async-start | bytes 4718592 | tf_op jit(solution)/shard_map/all_to_all | solution.py:69
  56.7 38.5 %copy-start.13 = (bf16[1,128,768]{2,1,0:T(8,128)(2,1)S(1)}, bf16[1,128,768]{2,1,0:T(8,128)(2,1)}, u32[]{:S(2)}) copy-start(bf16[1,128,768]{2,1,0:T(8,128)(2,1)} %param.23) | copy-start | bytes 589828
  56.7 38.5 %copy-start.15 = (bf16[128,768]{1,0:T(8,128)(2,1)S(1)}, bf16[128,768]{1,0:T(8,128)(2,1)}, u32[]{:S(2)}) copy-start(bf16[128,768]{1,0:T(8,128)(2,1)} %copy-done.14) | copy-start | bytes 589828
  57.9 37.3 %collective-permute-start.7 = (bf16[256,768]{1,0:T(8,128)(2,1)S(1)}, bf16[256,768]{1,0:T(8,128)(2,1)S(1)}, u32[]{:S(2)}, u32[]{:S(2)}) collective-permute-start(bf16[256,768]{1,0:T(8,128)(2,1)S(1)} %pad_maximum_fusion.8), channel_id=1, source_target_pairs={{0,2},{1,3},{2,0},{3,1},{4,6},{5,7},{6,4},{7,5},{8,10},{9,11},{10,... | collective-permute-start | bytes 1179656 | tf_op jit(solution)/shard_map/ppermute | solution.py:59
  97.7 49.1 %copy-start.6 = (f32[256,768]{1,0:T(8,128)}, f32[256,768]{1,0:T(8,128)S(1)}, u32[]{:S(2)}) copy-start(f32[256,768]{1,0:T(8,128)S(1)} %get-tuple-element.90) | copy-start | bytes 2359300
  97.7 2.1 collective-permute-start.8
  104.3 1.8 collective-permute-start.9
  106.3 12.7 %collective-permute-start.10 = (bf16[256,768]{1,0:T(8,128)(2,1)S(1)}, bf16[256,768]{1,0:T(8,128)(2,1)S(1)}, u32[]{:S(2)}, u32[]{:S(2)}) collective-permute-start(bf16[256,768]{1,0:T(8,128)(2,1)S(1)} %pad_maximum_fusion.9), channel_id=1, source_target_pairs={{0,2},{1,3},{2,0},{3,1},{4,6},{5,7},{6,4},{7,5},{8,10},{9,11},{10,... | collective-permute-start | bytes 1179656 | tf_op jit(solution)/shard_map/ppermute | solution.py:59
  119.9 0.9 copy-start.7
  121.1 2.0 collective-permute-start.11
  127.6 2.2 %collective-permute-start.12 = (bf16[256,768]{1,0:T(8,128)(2,1)S(1)}, bf16[256,768]{1,0:T(8,128)(2,1)S(1)}, u32[]{:S(2)}, u32[]{:S(2)}) collective-permute-start(bf16[256,768]{1,0:T(8,128)(2,1)S(1)} %slice.387), channel_id=1, source_target_pairs={{0,1},{1,0},{2,3},{3,2},{4,5},{5,4},{6,7},{7,6},{8,9},{9,8},{10,11... | collective-permute-start | bytes 1179656 | tf_op jit(solution)/shard_map/ppermute | solution.py:59
  131.6 13.2 %collective-permute-start.13 = (bf16[256,768]{1,0:T(8,128)(2,1)}, bf16[256,768]{1,0:T(8,128)(2,1)}, u32[]{:S(2)}, u32[]{:S(2)}) collective-permute-start(bf16[256,768]{1,0:T(8,128)(2,1)} %pad_maximum_fusion.11), channel_id=1, source_target_pairs={{0,2},{1,3},{2,0},{3,1},{4,6},{5,7},{6,4},{7,5},{8,10},{9,11},{10,... | collective-permute-start | bytes 1179656 | tf_op jit(solution)/shard_map/ppermute | solution.py:59
  134.6 43.5 %all-to-all-start.3 = ((bf16[32,24,1536]{2,1,0:T(8,128)(2,1)}), bf16[32,24,1536]{2,1,0:T(8,128)(2,1)}, u32[]{:S(2)}, u32[]{:S(2)}) async-start(bf16[32,24,1536]{2,1,0:T(8,128)(2,1)} %bitcast.33), calls=%async_computation.3 | async-start | bytes 4718592 | tf_op jit(solution)/shard_map/all_to_all | solution.py:75
  146.8 1.2 copy-start.8
  146.8 1.7 copy-start.10
  148.0 2.5 %collective-permute-start.14 = (bf16[256,768]{1,0:T(8,128)(2,1)S(1)}, bf16[256,768]{1,0:T(8,128)(2,1)S(1)}, u32[]{:S(2)}, u32[]{:S(2)}) collective-permute-start(bf16[256,768]{1,0:T(8,128)(2,1)S(1)} %get-tuple-element.81.near_ref), channel_id=1, source_target_pairs={{0,1},{1,0},{2,3},{3,2},{4,5},{5,4},{6,7},{7,6},{8,9},{9,8},{10,11... | collective-permute-start | bytes 1179656 | tf_op jit(solution)/shard_map/ppermute | solution.py:59
  150.3 10.2 %copy-start.5 = (bf16[512,256]{1,0:T(8,128)(2,1)S(1)}, bf16[512,256]{1,0:T(8,128)(2,1)}, u32[]{:S(2)}) copy-start(bf16[512,256]{1,0:T(8,128)(2,1)} %copy-done.4) | copy-start | bytes 786436
  150.4 1.1 copy-start.1
  156.0 0.9 copy-start.2
  156.8 5.9 %collective-permute-start.17 = (f32[16,768]{1,0:T(8,128)S(1)}, f32[16,768]{1,0:T(8,128)S(1)}, u32[]{:S(2)}, u32[]{:S(2)}) collective-permute-start(f32[16,768]{1,0:T(8,128)S(1)} %get-tuple-element.53), channel_id=1, source_target_pairs={{0,1},{1,0},{2,3},{3,2},{4,5},{5,4},{6,7},{7,6},{8,9},{9,8},{10,11... | collective-permute-start | bytes 147464 | tf_op jit(solution)/shard_map/ppermute | solution.py:59
  156.9 18.2 %collective-permute-start.18 = (f32[16,768]{1,0:T(8,128)S(1)}, f32[16,768]{1,0:T(8,128)S(1)}, u32[]{:S(2)}, u32[]{:S(2)}) collective-permute-start(f32[16,768]{1,0:T(8,128)S(1)} %get-tuple-element.53), channel_id=1, source_target_pairs={{0,2},{1,3},{2,0},{3,1},{4,6},{5,7},{6,4},{7,5},{8,10},{9,11},{10,... | collective-permute-start | bytes 147464 | tf_op jit(solution)/shard_map/ppermute | solution.py:59
  159.3 15.8 %collective-permute-start.19 = (f32[16,768]{1,0:T(8,128)S(1)}, f32[16,768]{1,0:T(8,128)S(1)}, u32[]{:S(2)}, u32[]{:S(2)}) collective-permute-start(f32[16,768]{1,0:T(8,128)S(1)} %get-tuple-element.53), channel_id=1, source_target_pairs={{0,3},{1,2},{2,1},{3,0},{4,7},{5,6},{6,5},{7,4},{8,11},{9,10},{10,... | collective-permute-start | bytes 147464 | tf_op jit(solution)/shard_map/ppermute | solution.py:59
  160.2 17.8 %collective-permute-start.15 = (bf16[256,768]{1,0:T(8,128)(2,1)}, bf16[256,768]{1,0:T(8,128)(2,1)S(1)}, u32[]{:S(2)}, u32[]{:S(2)}) collective-permute-start(bf16[256,768]{1,0:T(8,128)(2,1)} %get-tuple-element.50), channel_id=1, source_target_pairs={{0,1},{1,0},{2,3},{3,2},{4,5},{5,4},{6,7},{7,6},{8,9},{9,8},{10,11... | collective-permute-start | bytes 1179656 | tf_op jit(solution)/shard_map/ppermute | solution.py:59
  160.5 17.5 %copy-start.3 = (f32[256,768]{1,0:T(8,128)S(1)}, f32[256,768]{1,0:T(8,128)}, u32[]{:S(2)}) copy-start(f32[256,768]{1,0:T(8,128)} %copy-done.2) | copy-start | bytes 2359300
  178.1 32.1 %copy-start.11 = (f32[256,768]{1,0:T(8,128)S(1)}, f32[256,768]{1,0:T(8,128)}, u32[]{:S(2)}) copy-start(f32[256,768]{1,0:T(8,128)} %get-tuple-element.82) | copy-start | bytes 2359300
  178.1 35.6 %all-to-all-start.2 = ((bf16[32,24,896]{2,1,0:T(8,128)(2,1)}), bf16[32,24,896]{2,1,0:T(8,128)(2,1)S(1)}, u32[]{:S(2)}, u32[]{:S(2)}) async-start(bf16[32,24,896]{2,1,0:T(8,128)(2,1)} %bitcast.14), calls=%async_computation.2 | async-start | bytes 2752512 | tf_op jit(solution)/shard_map/all_to_all | solution.py:75
  188.9 21.3 %collective-permute-start.16 = (bf16[128,768]{1,0:T(8,128)(2,1)S(1)}, bf16[128,768]{1,0:T(8,128)(2,1)S(1)}, u32[]{:S(2)}, u32[]{:S(2)}) collective-permute-start(bf16[128,768]{1,0:T(8,128)(2,1)S(1)} %slice.389), channel_id=1, source_target_pairs={{0,2},{1,3},{2,0},{3,1},{4,6},{5,7},{6,4},{7,5},{8,10},{9,11},{10,... | collective-permute-start | bytes 589832 | tf_op jit(solution)/shard_map/ppermute | solution.py:59

commit v4 on v3

--- a/solution.py
+++ b/solution.py
@@ -2,7 +2,6 @@
 
 import jax
 import jax.numpy as jnp
-import numpy as np
 from jax import lax
 from jax.experimental import pallas as pl
 from jax.experimental.pallas import tpu as pltpu
@@ -28,33 +27,6 @@
     )
 
 
-def gelu_exact(values):
-    return 0.5 * values * (1.0 + lax.erf(values * ROOT_HALF))
-
-
-def gelu_slope(values):
-    return (
-        0.5 * (1.0 + lax.erf(values * ROOT_HALF))
-        + values * jnp.exp(-0.5 * values * values) * INV_ROOT_TAU
-    )
-
-
-def norm_forward(values, gain, shift):
-    center = values - jnp.mean(values, axis=-1, keepdims=True)
-    scale_inv = lax.rsqrt(jnp.mean(center * center, axis=-1, keepdims=True) + NORM_EPSILON)
-    normed = center * scale_inv
-    return (normed * gain + shift, normed, scale_inv)
-
-
-def norm_backward(upstream, normed, scale_inv, gain):
-    scaled = upstream * gain
-    return scale_inv * (
-        scaled
-        - jnp.mean(scaled, axis=-1, keepdims=True)
-        - normed * jnp.mean(scaled * normed, axis=-1, keepdims=True)
-    )
-
-
 def swap(values, mask):
     return lax.ppermute(values, "tensor", [(i, i ^ mask) for i in range(4)])
 
@@ -63,27 +35,28 @@
     return lax.optimization_barrier((values, *others))[0]
 
 
-def spread(block):
+def spread(stacked):
+    return lax.all_to_all(stacked, "dp", 0, 0, tiled=True)
+
+
+def plane_groups():
+    count = lax.axis_size("dp") // 2
+    return [list(range(count)), list(range(count, 2 * count))]
+
+
+def plane(stacked):
+    return lax.all_to_all(stacked, "dp", 0, 0, tiled=True, axis_index_groups=plane_groups())
+
+
+def side(values):
     count = lax.axis_size("dp")
-    stacked = jnp.broadcast_to(block[None], (count, *block.shape))
-    return lax.all_to_all(stacked, "dp", 0, 0, tiled=True).reshape(-1, block.shape[1])
-
-
-def scattered(values):
-    count = lax.axis_size("dp")
-    blocks = values.reshape(count, values.shape[0] // count, values.shape[1])
-    return lax.all_to_all(blocks, "dp", 0, 0, tiled=True)
+    pairs = [(i, (i + count // 2) % count) for i in range(count)]
+    return lax.ppermute(values, "dp", pairs)
 
 
 def halves(values):
     high = lax.reduce_precision(values, 8, 7)
     return (high.astype(LOW), (values - high).astype(LOW))
-
-
-def core_sum(part):
-    half = part.shape[0] // 2
-    got = swap(part[half:].astype(LOW), 1)
-    return part[:half] + got.astype(FULL)
 
 
 def far_sum(total):
@@ -91,10 +64,6 @@
     sent = total.astype(LOW)
     sent = jnp.concatenate([sent[quarter:], sent[:quarter]], axis=0)
     return swap(sent, 2)
-
-
-def core_join(rows):
-    return jnp.concatenate([rows, swap(rows, 1)], axis=0)
 
 
 def ordered_segments(segment_row, my_index):
@@ -106,7 +75,7 @@
     return jnp.concatenate([quarters[0], quarters[2], quarters[1], quarters[3]])
 
 
-def call(body, out_shapes, *operands, smem=0):
+def call(body, out_shapes, *operands, smem=0, scratch=()):
     specs = [pl.BlockSpec(memory_space=pltpu.SMEM)] * smem
     specs += [pl.BlockSpec(memory_space=pltpu.VMEM)] * (len(operands) - smem)
     return pl.pallas_call(
@@ -114,6 +83,7 @@
         out_shape=[jax.ShapeDtypeStruct(shape, kind) for shape, kind in out_shapes],
         in_specs=specs,
         out_specs=[pl.BlockSpec(memory_space=pltpu.VMEM)] * len(out_shapes),
+        scratch_shapes=list(scratch),
         compiler_params=pltpu.CompilerParams(vmem_limit_bytes=VMEM_LIMIT),
         cost_estimate=pl.CostEstimate(flops=1000, bytes_accessed=1000, transcendentals=0),
     )(*operands)
@@ -355,14 +325,302 @@
     out_ref[:, 3 * GROUP :] = jnp.zeros((width, TILE), LOW)
 
 
-def packing(vector_rows):
-    place = np.arange(12 * vector_rows)
+def place_of(vector_rows, shape, dim):
+    place = lanes(shape, dim)
     many = 8 * vector_rows
-    row = np.where(place < many, place % vector_rows, (place - many) // 4)
-    column = np.where(place < many, place // vector_rows, 8 + (place - many) % 4)
-    rows = (row[None, :] == np.arange(vector_rows)[:, None]).astype(np.float32)
-    columns = (column[:, None] == np.arange(12)[None, :]).astype(np.float32)
-    return (rows, columns)
+    row = jnp.where(place < many, place % vector_rows, (place - many) // 4)
+    column = jnp.where(place < many, place // vector_rows, 8 + (place - many) % 4)
+    return (row, jnp.where(place < many + 4 * vector_rows, column, 1000))
+
+
+def first_block_kernel(
+    index_ref, own_ref, core_ref, far_ref, both_ref, q_ref, k_ref, v_ref, out_ref, block_ref
+):
+    index = index_ref[0]
+    rows = q_ref.shape[0]
+    vector_rows = rows // 4
+    shape = (rows, own_ref.shape[1])
+    row_at = lanes(shape, 0)
+    near = [own_ref[...], core_ref[...], far_ref[...], both_ref[...]]
+    spread_rows = jnp.zeros(shape, FULL)
+    for at in range(4):
+        row = near[3]
+        for mask in (2, 1, 0):
+            row = jnp.where((index ^ mask) == at, near[mask], row)
+        spread_rows = jnp.where(row_at // vector_rows == at, row, spread_rows)
+    place_row, _ = place_of(vector_rows, shape, 1)
+    spread_rows = jnp.where(place_row == row_at % vector_rows, spread_rows, 0.0)
+    high = spread_rows.astype(LOW)
+    low = (spread_rows - high.astype(FULL)).astype(LOW)
+    shape = (shape[1], TILE)
+    _, place_column = place_of(vector_rows, shape, 0)
+    columns = lanes(shape)
+    first = jnp.where(place_column == columns, 1.0, 0.0).astype(LOW)
+    second = jnp.where(place_column + 12 == columns, 1.0, 0.0).astype(LOW)
+    packed = jnp.dot(high, first, preferred_element_type=FULL) + jnp.dot(
+        low, second, preferred_element_type=FULL
+    )
+    out = out_ref[...].astype(FULL)
+    block = jnp.concatenate(
+        [
+            q_ref[...].astype(FULL),
+            out[:, :HEAD_DIM],
+            k_ref[...].astype(FULL),
+            out[:, HEAD_DIM : 2 * HEAD_DIM],
+            v_ref[...].astype(FULL),
+            out[:, 2 * HEAD_DIM :],
+            packed,
+        ],
+        axis=1,
+    ).astype(LOW)
+    for at in range(block_ref.shape[0]):
+        block_ref[at] = block
+
+
+def second_block_kernel(index_ref, own_ref, other_ref, block_ref):
+    lower = index_ref[0] == 0
+    own = own_ref[...].astype(FULL)
+    other = other_ref[...].astype(FULL)
+    block = jnp.concatenate(
+        [jnp.where(lower, own, other), jnp.where(lower, other, own)], axis=0
+    ).astype(LOW)
+    for at in range(block_ref.shape[0]):
+        block_ref[at] = block
+
+
+def moments(values, gain, shift):
+    center = values - jnp.mean(values, axis=-1, keepdims=True)
+    scale_inv = lax.rsqrt(jnp.mean(center * center, axis=-1, keepdims=True) + NORM_EPSILON)
+    normed = center * scale_inv
+    return (normed * gain + shift, normed, scale_inv)
+
+
+def norm_backward(upstream, normed, scale_inv, gain):
+    scaled = upstream * gain
+    return scale_inv * (
+        scaled
+        - jnp.mean(scaled, axis=-1, keepdims=True)
+        - normed * jnp.mean(scaled * normed, axis=-1, keepdims=True)
+    )
+
+
+def blocks_of(rows, size=64):
+    return [(at, at + size) for at in range(0, rows, size)]
+
+
+def first_norm_kernel(
+    tokens_ref, chip_ref, far_ref, rows_ref, first_ref, low_ref, normed_ref, scale_ref
+):
+    for at, to in blocks_of(tokens_ref.shape[0]):
+        values = (
+            tokens_ref[at:to].astype(FULL)
+            + (chip_ref[at:to] + far_ref[at:to].astype(FULL))
+            + rows_ref[2:3]
+        )
+        first, normed, scale_inv = moments(values, rows_ref[4:5], rows_ref[5:6])
+        first_ref[at:to] = first
+        low_ref[at:to] = first.astype(LOW)
+        normed_ref[at:to] = normed
+        scale_ref[at:to] = jnp.broadcast_to(scale_inv, (to - at, TILE))
+
+
+def feed_kernel(
+    near_ref,
+    other_ref,
+    blocks_ref,
+    bias_ref,
+    active_ref,
+    slope_ref,
+    keep_ref,
+    send_ref,
+    up_ref,
+    down_ref,
+):
+    count, rows, wide = blocks_ref.shape
+    rows = rows // 2
+    hidden = wide // 2
+    group = 1 if rows % 16 == 0 else 2
+    for lower in range(2):
+        for at in range(0, count, group):
+            got = jnp.concatenate(
+                [
+                    blocks_ref[at + i].astype(FULL)[rows * lower : rows * (lower + 1)]
+                    for i in range(group)
+                ],
+                axis=0,
+            ).astype(LOW)
+            to = (lower * count + at) * rows
+            up_ref[to : to + group * rows] = got[:, :hidden]
+            down_ref[to : to + group * rows] = got[:, hidden:]
+    half = near_ref.shape[0]
+    size = half // 2
+    for base, rows_ref in ((half, other_ref), (0, near_ref)):
+        for at, to in blocks_of(half, size):
+            upward = (
+                jnp.dot(rows_ref[at:to], up_ref[...], preferred_element_type=FULL) + bias_ref[...]
+            )
+            for low, high in blocks_of(size, 32):
+                part = upward[low:high]
+                gate = 0.5 * (1.0 + lax.erf(part * ROOT_HALF))
+                active_ref[base + at + low : base + at + high] = (part * gate).astype(LOW)
+                slope_ref[base + at + low : base + at + high] = (
+                    gate + part * jnp.exp(-0.5 * part * part) * INV_ROOT_TAU
+                )
+            got = contract(active_ref[base + at : base + to], down_ref[...], 1, 1)
+            if base:
+                send_ref[at:to] = got.astype(LOW)
+            else:
+                keep_ref[at:to] = got
+
+
+def second_norm_kernel(
+    first_ref,
+    chip_ref,
+    far_ref,
+    rows_ref,
+    cotangent_ref,
+    cotangent_far_ref,
+    output_ref,
+    grad_ref,
+    low_ref,
+    sums_ref,
+):
+    own = output_ref.shape[0]
+    sums = [jnp.zeros((1, first_ref.shape[1]), FULL) for _ in range(3)]
+    for at, to in blocks_of(first_ref.shape[0]):
+        values = first_ref[at:to] + (chip_ref[at:to] + far_ref[at:to].astype(FULL)) + rows_ref[3:4]
+        output, normed, scale_inv = moments(values, rows_ref[6:7], rows_ref[7:8])
+        if to <= own:
+            upstream = cotangent_ref[at:to].astype(FULL)
+            output_ref[at:to] = output.astype(LOW)
+        else:
+            upstream = cotangent_far_ref[at - own : to - own].astype(FULL)
+        grad = norm_backward(upstream, normed, scale_inv, rows_ref[6:7])
+        grad_ref[at:to] = grad
+        low = grad.astype(LOW)
+        low_ref[at:to] = low
+        if to <= own:
+            for i, part in enumerate((low.astype(FULL), upstream * normed, upstream)):
+                sums[i] += jnp.sum(part, axis=0, keepdims=True)
+    sums_ref[...] = jnp.concatenate(sums + [jnp.zeros((5, sums[0].shape[1]), FULL)], axis=0)
+
+
+def feed_backward_kernel(
+    near_ref, other_ref, up_ref, down_ref, slope_ref, grad_ref, keep_ref, send_ref, sum_ref
+):
+    half = near_ref.shape[0]
+    size = half // 2
+    total = jnp.zeros((1, up_ref.shape[1]), FULL)
+    for base, rows_ref in ((half, other_ref), (0, near_ref)):
+        for at, to in blocks_of(half, size):
+            grad = jnp.dot(rows_ref[at:to], down_ref[...], preferred_element_type=FULL)
+            for low, high in blocks_of(size, 32):
+                place = slice(base + at + low, base + at + high)
+                part = (grad[low:high] * slope_ref[place]).astype(LOW)
+                grad_ref[place] = part
+                total += jnp.sum(part.astype(FULL), axis=0, keepdims=True)
+            got = contract(grad_ref[base + at : base + to], up_ref[...], 1, 1)
+            if base:
+                send_ref[at:to] = got.astype(LOW)
+            else:
+                keep_ref[at:to] = got
+    sum_ref[...] = total
+
+
+def feed_weights_kernel(
+    hidden_near, hidden_other, branch_near, branch_other, active_ref, grad_ref, out_ref
+):
+    half = hidden_near.shape[0]
+    count, rows, wide = out_ref.shape
+    rows = rows // 2
+    hidden = wide // 2
+    for place, near, other, right in (
+        (0, hidden_near, hidden_other, grad_ref),
+        (hidden, branch_near, branch_other, active_ref),
+    ):
+        got = contract(near[...], right[:half], 0, 0) + contract(other[...], right[half:], 0, 0)
+        for at in range(count):
+            out_ref[at, :, place : place + hidden] = jnp.concatenate(
+                [got[at * rows : (at + 1) * rows], got[(count + at) * rows :][:rows]], axis=0
+            ).astype(LOW)
+
+
+def first_norm_backward_kernel(
+    second_ref,
+    chip_ref,
+    far_ref,
+    normed_ref,
+    scale_ref,
+    rows_ref,
+    second_sums_ref,
+    grad_ref,
+    low_ref,
+    sums_ref,
+):
+    own = grad_ref.shape[0]
+    sums = [jnp.zeros((1, second_ref.shape[1]), FULL) for _ in range(3)]
+    for at, to in blocks_of(second_ref.shape[0]):
+        upstream = second_ref[at:to] + (chip_ref[at:to] + far_ref[at:to].astype(FULL))
+        normed = normed_ref[at:to]
+        grad = norm_backward(upstream, normed, scale_ref[at:to, :1], rows_ref[4:5])
+        low = grad.astype(LOW)
+        low_ref[at:to] = low
+        if to <= own:
+            grad_ref[at:to] = grad
+            for i, part in enumerate((low.astype(FULL), upstream * normed, upstream)):
+                sums[i] += jnp.sum(part, axis=0, keepdims=True)
+    given = second_sums_ref[...]
+    sums_ref[...] = jnp.concatenate(
+        [
+            sums[0],
+            given[0:1],
+            sums[1],
+            sums[2],
+            given[1:3],
+            jnp.zeros((2, sums[0].shape[1]), FULL),
+        ],
+        axis=0,
+    )
+
+
+def plane_sum_kernel(index_ref, blocks_ref, keep_ref, send_ref):
+    rows = keep_ref.shape[0]
+    total = blocks_ref[0].astype(FULL)
+    for at in range(1, blocks_ref.shape[0]):
+        total += blocks_ref[at].astype(FULL)
+    lower = index_ref[0] == 0
+    keep_ref[...] = jnp.where(lower, total[:rows], total[rows:])
+    send_ref[...] = jnp.where(lower, total[rows:], total[:rows])
+
+
+def last_sum_kernel(index_ref, blocks_ref, q_ref, k_ref, v_ref, out_ref, vector_ref):
+    index = index_ref[0]
+    rows = q_ref.shape[0]
+    vector_rows = rows // 4
+    columns = q_ref.shape[1]
+    total = blocks_ref[0].astype(FULL)
+    for at in range(1, blocks_ref.shape[0]):
+        total += blocks_ref[at].astype(FULL)
+    q_ref[...] = total[:, :columns]
+    k_ref[...] = total[:, GROUP : GROUP + columns]
+    v_ref[...] = total[:, 2 * GROUP : 2 * GROUP + columns]
+    out_ref[...] = jnp.concatenate(
+        [total[:, GROUP * i + columns : GROUP * (i + 1)] for i in range(3)], axis=1
+    )
+    packed = total[:, 3 * GROUP :]
+    packed = packed + pltpu.roll(packed, TILE - 12, 1)
+    wide = vector_ref.shape[1]
+    _, place_column = place_of(vector_rows, (TILE, wide), 1)
+    select = jnp.where(place_column == lanes((TILE, wide), 0), 1.0, 0.0).astype(LOW)
+    line = jnp.zeros((rows, wide), FULL)
+    left = packed
+    for _ in range(3):
+        part = left.astype(LOW)
+        left = left - part.astype(FULL)
+        line += jnp.dot(part, select, preferred_element_type=FULL)
+    place_row, _ = place_of(vector_rows, (rows, wide), 1)
+    keep = place_row + index * vector_rows == lanes((rows, wide), 0)
+    vector_ref[...] = jnp.sum(jnp.where(keep, line, 0.0), axis=0, keepdims=True)
 
 
 def shards(
@@ -386,18 +644,20 @@
     cotangent,
 ):
     my_index = lax.axis_index("tensor")
+    dp_count = lax.axis_size("dp")
     local_len, width = tokens.shape[1:]
     half = 2 * local_len
     length = 4 * local_len
-    head_cols = q_weight.shape[1]
+    shard_rows, head_cols = q_weight.shape
     hidden_cols = up_weight.shape[1]
     tokens = tokens[0]
     cotangent = cotangent[0]
     index = my_index.reshape(1)
+    side_index = (lax.axis_index("dp") // (dp_count // 2)).reshape(1)
 
     vector_rows = q_bias.shape[0]
-    row_place, column_place = packing(vector_rows)
-    flat = jnp.concatenate(
+    line_size = -(-12 * vector_rows // TILE) * TILE
+    line = jnp.concatenate(
         [
             q_bias,
             v_bias,
@@ -408,50 +668,41 @@
             norm2_gain,
             norm2_shift,
             up_bias,
+            jnp.zeros((line_size - 12 * vector_rows,), FULL),
         ]
-    )
-    high, low = halves(flat)
-    spaced = jnp.concatenate([high * row_place.astype(LOW), low * row_place.astype(LOW)], axis=1)
-    spaced = jnp.pad(spaced, ((0, 2), (0, 0)))
-    select = np.zeros((2 * flat.shape[0], TILE), np.float32)
-    select[: flat.shape[0], :12] = column_place
-    select[flat.shape[0] :, 12:24] = column_place
-    packed = jnp.dot(spaced, select.astype(LOW), preferred_element_type=FULL).astype(LOW)
-    near = [packed] + [swap(packed, mask) for mask in (1, 2, 3)]
+    )[None]
+    lines = [line] + [swap(line, mask) for mask in (1, 2, 3)]
     tokens_far = swap(tokens, 2)
-    near = [block[:vector_rows] for block in near]
-    core = my_index % 2 == 1
-    near = [
-        jnp.where(core, near[1], near[0]),
-        jnp.where(core, near[0], near[1]),
-        jnp.where(core, near[3], near[2]),
-        jnp.where(core, near[2], near[3]),
-    ]
-    far = my_index // 2 == 1
-    near = jnp.concatenate(
-        [
-            jnp.where(far, near[2], near[0]),
-            jnp.where(far, near[3], near[1]),
-            jnp.where(far, near[0], near[2]),
-            jnp.where(far, near[1], near[3]),
-        ],
-        axis=0,
-    )
-    pads = [out_weight[:, HEAD_DIM * i : HEAD_DIM * (i + 1)] for i in range(3)]
-    first_block = jnp.concatenate(
-        [q_weight, pads[0], k_weight, pads[1], v_weight, pads[2], near], axis=1
-    )
-    first_full = spread(first_block)
+    second_own = jnp.concatenate([up_weight, down_weight], axis=1)
+    second_side = side(second_own)
+    (first_block,) = call(
+        first_block_kernel,
+        [((dp_count, shard_rows, 3 * GROUP + TILE), LOW)],
+        index,
+        *lines,
+        q_weight,
+        k_weight,
+        v_weight,
+        out_weight,
+        smem=1,
+    )
+    first_full = spread(first_block).reshape(width, -1)
     tokens_pair = jnp.concatenate([tokens, tokens_far], axis=0)
     tokens_core = swap(tokens_pair, 1)
     cotangent_far = swap(after(cotangent, tokens_far), 2)
     segment_row = ordered_segments(segments[0], my_index)[None]
-    second_block = jnp.concatenate([up_weight, down_weight], axis=1)
+    (second_block,) = call(
+        second_block_kernel,
+        [((dp_count // 2, 2 * shard_rows, 2 * hidden_cols), LOW)],
+        side_index,
+        second_own,
+        second_side,
+        smem=1,
+    )
     first_full, second_block, tokens_core, cotangent_far, segment_row = lax.optimization_barrier(
         (first_full, second_block, tokens_core, cotangent_far, segment_row)
     )
-    second_full = spread(second_block)
-    up_full, down_full = second_full[:, :hidden_cols], second_full[:, hidden_cols:]
+    second_full = plane(second_block)
 
     qkv_rows, mixed_rows, log_totals, attn_send, attn_keep, rows, bias_up = call(
         forward_kernel,
@@ -471,86 +722,90 @@
         segment_row,
         smem=1,
     )
-    gain_first, shift_first, gain_second, shift_second = rows[4], rows[5], rows[6], rows[7]
-    bias_out, bias_down = rows[2], rows[3]
     attn_chip = attn_keep + swap(attn_send, 1).astype(FULL)
-    attn_far = far_sum(attn_chip)
-    first, normed_first, inv_first = norm_forward(
-        tokens_pair.astype(FULL) + (attn_chip + attn_far.astype(FULL)) + bias_out,
-        gain_first,
-        shift_first,
-    )
-    hidden_full = core_join(first.astype(LOW))
-    upward = jnp.dot(hidden_full, up_full, preferred_element_type=FULL) + bias_up
-    active = gelu_exact(upward).astype(LOW)
-    branch_chip = core_sum(contract(active, down_full, 1, 1))
-    branch = branch_chip + far_sum(branch_chip).astype(FULL)
-    layer_output, normed_second, inv_second = norm_forward(
-        first + branch + bias_down, gain_second, shift_second
-    )
-
-    cotangent_pair = jnp.concatenate([cotangent, cotangent_far], axis=0).astype(FULL)
-    second_grad = norm_backward(cotangent_pair, normed_second, inv_second, gain_second)
-    cotangent_own = cotangent_pair[:local_len]
-    grad_gain_second = jnp.sum(cotangent_own * normed_second[:local_len], axis=0)
-    grad_shift_second = jnp.sum(cotangent_own, axis=0)
-    branch_low = second_grad.astype(LOW)
-    grad_bias_down = jnp.sum(branch_low[:local_len].astype(FULL), axis=0)
-    branch_full = core_join(branch_low)
-    active_grad = jnp.dot(branch_full, down_full, preferred_element_type=FULL)
-    upward_grad = (active_grad * gelu_slope(upward)).astype(LOW)
-    hidden_chip = core_sum(contract(upward_grad, up_full, 1, 1))
+    first, hidden_low, normed_first, inv_first = call(
+        first_norm_kernel,
+        [((half, width), FULL), ((half, width), LOW), ((half, width), FULL), ((half, TILE), FULL)],
+        tokens_pair,
+        attn_chip,
+        far_sum(attn_chip),
+        rows,
+    )
+    hidden_core = swap(hidden_low, 1)
+    active, slope, branch_keep, branch_send, up_full, down_full = call(
+        feed_kernel,
+        [
+            ((length, hidden_cols), LOW),
+            ((length, hidden_cols), FULL),
+            ((half, width), FULL),
+            ((half, width), LOW),
+            ((width, hidden_cols), LOW),
+            ((width, hidden_cols), LOW),
+        ],
+        hidden_low,
+        hidden_core,
+        second_full,
+        bias_up,
+    )
+    branch_chip = branch_keep + swap(branch_send, 1).astype(FULL)
+    layer_output, second_grad, branch_low, second_sums = call(
+        second_norm_kernel,
+        [((local_len, width), LOW), ((half, width), FULL), ((half, width), LOW), ((8, width), FULL)],
+        first,
+        branch_chip,
+        far_sum(branch_chip),
+        rows,
+        cotangent,
+        cotangent_far,
+    )
+    branch_core = swap(branch_low, 1)
+    upward_grad, hidden_keep, hidden_send, up_sum = call(
+        feed_backward_kernel,
+        [
+            ((length, hidden_cols), LOW),
+            ((half, width), FULL),
+            ((half, width), LOW),
+            ((1, hidden_cols), FULL),
+        ],
+        branch_low,
+        branch_core,
+        up_full,
+        down_full,
+        slope,
+    )
+    hidden_chip = hidden_keep + swap(hidden_send, 1).astype(FULL)
     hidden_far = far_sum(hidden_chip)
-    grad_down = contract(branch_full, active, 0, 0)
-    grad_up = contract(hidden_full, upward_grad, 0, 0)
-    grad_bias_up = jnp.sum(upward_grad.astype(FULL), axis=0)
-    pair_blocks = scattered(
-        jnp.concatenate(
-            [after(grad_up, hidden_chip).astype(LOW), after(grad_down, hidden_chip).astype(LOW)],
-            axis=1,
-        )
-    )
-    first_grad = second_grad + (hidden_chip + hidden_far.astype(FULL))
-    resid_grad = norm_backward(first_grad, normed_first, inv_first, gain_first)
-    first_own = first_grad[:local_len]
-    grad_gain_first = jnp.sum(first_own * normed_first[:local_len], axis=0)
-    grad_shift_first = jnp.sum(first_own, axis=0)
-    attended_low = resid_grad.astype(LOW)
-    grad_bias_out = jnp.sum(attended_low[:local_len].astype(FULL), axis=0)
+    (pair_block,) = call(
+        feed_weights_kernel,
+        [((dp_count // 2, 2 * shard_rows, 2 * hidden_cols), LOW)],
+        hidden_low,
+        hidden_core,
+        branch_low,
+        branch_core,
+        active,
+        upward_grad,
+    )
+    pair_blocks = plane(after(pair_block, hidden_chip))
+    resid_grad, attended_low, given = call(
+        first_norm_backward_kernel,
+        [((local_len, width), FULL), ((half, width), LOW), ((8, width), FULL)],
+        second_grad,
+        hidden_chip,
+        hidden_far,
+        normed_first,
+        inv_first,
+        rows,
+        second_sums,
+    )
     attended_core = swap(attended_low, 1)
-    zero_row = jnp.zeros((width,), FULL)
-    given = jnp.stack(
+    qkv_grad, input_send, input_keep, vector_sums = call(
+        backward_kernel,
         [
-            grad_bias_out,
-            grad_bias_down,
-            grad_gain_first,
-            grad_shift_first,
-            grad_gain_second,
-            grad_shift_second,
-            zero_row,
-            zero_row,
-        ]
-    )
-    qkv_grad, input_send, input_keep, vector_sums = pl.pallas_call(
-        backward_kernel,
-        out_shape=[
-            jax.ShapeDtypeStruct((length, 3 * GROUP), LOW),
-            jax.ShapeDtypeStruct((half, width), LOW),
-            jax.ShapeDtypeStruct((half, width), FULL),
-            jax.ShapeDtypeStruct((16, width), FULL),
+            ((length, 3 * GROUP), LOW),
+            ((half, width), LOW),
+            ((half, width), FULL),
+            ((16, width), FULL),
         ],
-        in_specs=[pl.BlockSpec(memory_space=pltpu.SMEM)]
-        + [pl.BlockSpec(memory_space=pltpu.VMEM)] * 8,
-        out_specs=[pl.BlockSpec(memory_space=pltpu.VMEM)] * 4,
-        scratch_shapes=[
-            pltpu.VMEM((length, GROUP), LOW),
-            pltpu.VMEM((length, TILE), FULL),
-            pltpu.VMEM((length, TILE), FULL),
-            pltpu.VMEM((width, TILE), FULL),
-        ],
-        compiler_params=pltpu.CompilerParams(vmem_limit_bytes=VMEM_LIMIT),
-        cost_estimate=pl.CostEstimate(flops=1000, bytes_accessed=1000, transcendentals=0),
-    )(
         index,
         attended_low,
         attended_core,
@@ -559,7 +814,14 @@
         first_full,
         segment_row,
         given,
-        grad_bias_up[None],
+        up_sum,
+        smem=1,
+        scratch=[
+            pltpu.VMEM((length, GROUP), LOW),
+            pltpu.VMEM((length, TILE), FULL),
+            pltpu.VMEM((length, TILE), FULL),
+            pltpu.VMEM((width, TILE), FULL),
+        ],
     )
     vector_near = [swap(vector_sums, mask) for mask in (1, 2, 3)]
     input_got = swap(input_send, 1)
@@ -580,35 +842,46 @@
     )
     input_chip = input_keep + input_got.astype(FULL)
     input_far = swap(input_chip[local_len:].astype(LOW), 2)
-    last_blocks = scattered(after(last_block, input_chip))
-    input_grad = resid_grad[:local_len] + (input_chip[:local_len] + input_far.astype(FULL))
-
-    pair_sum = jnp.sum(pair_blocks.astype(FULL), axis=0)
-    up_sum, down_sum = pair_sum[:, :hidden_cols], pair_sum[:, hidden_cols:]
-    last_sum = jnp.sum(last_blocks.astype(FULL), axis=0)
-    columns = last_sum[:, 3 * GROUP :]
-    columns = columns[:, :12] + columns[:, 12:24]
-    columns = lax.dynamic_slice_in_dim(columns, my_index * vector_rows, vector_rows, axis=0)
+    last_blocks = spread(
+        after(last_block, input_chip).reshape(dp_count, shard_rows, 3 * GROUP + TILE)
+    )
+    input_grad = resid_grad + (input_chip[:local_len] + input_far.astype(FULL))
+
+    pair_keep, pair_send = call(
+        plane_sum_kernel,
+        [((shard_rows, 2 * hidden_cols), FULL)] * 2,
+        side_index,
+        pair_blocks,
+        smem=1,
+    )
+    pair_sum = pair_keep + side(pair_send)
+    q_grad, k_grad, v_grad, out_grad, line = call(
+        last_sum_kernel,
+        [((shard_rows, head_cols), FULL)] * 4 + [((1, line_size), FULL)],
+        index,
+        last_blocks,
+        smem=1,
+    )
+    line = line[0]
+    vectors = [line[vector_rows * i : vector_rows * (i + 1)] for i in range(8)]
     return (
-        layer_output[:local_len].astype(LOW)[None],
+        layer_output[None],
         input_grad[None],
-        last_sum[:, :head_cols],
-        last_sum[:, GROUP : GROUP + head_cols],
-        last_sum[:, 2 * GROUP : 2 * GROUP + head_cols],
-        up_sum,
-        jnp.concatenate(
-            [last_sum[:, GROUP * i + head_cols : GROUP * (i + 1)] for i in range(3)], axis=1
-        ),
-        down_sum,
-        columns[:, 6],
-        columns[:, 7],
-        columns[:, 0],
-        columns[:, 8:12].reshape(-1),
-        columns[:, 1],
-        columns[:, 2],
-        columns[:, 3],
-        columns[:, 4],
-        columns[:, 5],
+        q_grad,
+        k_grad,
+        v_grad,
+        pair_sum[:, :hidden_cols],
+        out_grad,
+        pair_sum[:, hidden_cols:],
+        vectors[6],
+        vectors[7],
+        vectors[0],
+        line[8 * vector_rows : 12 * vector_rows],
+        vectors[1],
+        vectors[2],
+        vectors[3],
+        vectors[4],
+        vectors[5],
     )
 
 

time: 219 us -> 196 us (0.89)
  other arithmetic: 18.7 us -> 2.34 us
  Pallas kernels: 10.1 us -> 25.9 us
  matrix products: 12.6 us -> 0 us
  starting transfers between devices: 55.6 us -> 49.7 us
  local copies, waits for them, and re-layouts: 18.3 us -> 15 us
    pallas_call x2 -> x13, Pallas kernels: 5.75 us -> 25.9 us  [call(): pl.pallas_call(body, out_shape=[jax.ShapeDtypeStruct(shape, kind) for sha...]
    all_to_all x4, waiting for transfers between devices: 0.01 us -> 14.1 us  [the longest x2 14.1 us: plane(): lax.all_to_all(stacked, 'dp', 0, 0, tiled=True, axis_index_groups=plane_g...]
    ppermute x20, waiting for transfers between devices: 100 us -> 87.4 us  [swap(): return lax.ppermute(values, 'tensor', [(i, i ^ mask) for i in range(4)])]
    dot_general x7 -> x0, matrix products: 12.6 us -> none  [the longest x4 6.89 us: contract(): lax.dot_general(left, right, (((left_dim,), (right_dim,)), ((), ())), pre...]
    all_to_all x4, starting transfers between devices: 36.4 us -> 27 us  [the longest x2 15.6 us: spread(): return lax.all_to_all(stacked, 'dp', 0, 0, tiled=True)]
    reduce_sum x12 -> x0, other arithmetic: 8.5 us -> none  [the longest x2 2.31 us: norm_backward(): jnp.mean(scaled, axis=-1, keepdims=True)]
    pallas_call x1 -> x0, Pallas kernels: 4.39 us -> none  [shards(): pl.pallas_call(backward_kernel, out_shape=[jax.ShapeDtypeStruct((length,...]
    convert_element_type x4 -> x0, other arithmetic: 3.23 us -> none  [the longest x1 1.12 us: shards(): attended_low = resid_grad.astype(LOW)]
  transfers between devices with their start and end apart: 24 -> 26, of which waited for: 10 -> 17; matrix products, arithmetic and copies ran while one was open for 12% -> 4% of each run, Pallas kernels for 3% -> 7%
where the time goes in v4:
time: 196 us; the launch traced here: 195 us
  waiting for transfers between devices  101 us (52%)
  starting transfers between devices  49.7 us (25%)
  Pallas kernels  25.9 us (13%)
  local copies, waits for them, and re-layouts  15 us (8%)
  other arithmetic  2.34 us (1%)
    ppermute x20, waiting for transfers between devices, swap(): return lax.ppermute(values, 'tensor', [(i, i ^ mask) for i in range(4)])  87.4 us
    pallas_call x13, Pallas kernels, call(): pl.pallas_call(body, out_shape=[jax.ShapeDtypeStruct(shape, kind) for sha...  25.9 us
    ppermute x20, starting transfers between devices, swap(): return lax.ppermute(values, 'tensor', [(i, i ^ mask) for i in range(4)])  19.5 us
    all_to_all x2, starting transfers between devices, spread(): return lax.all_to_all(stacked, 'dp', 0, 0, tiled=True)  15.6 us
    all_to_all x2, waiting for transfers between devices, plane(): lax.all_to_all(stacked, 'dp', 0, 0, tiled=True, axis_index_groups=plane_g...  14.1 us
    all_to_all x2, starting transfers between devices, plane(): lax.all_to_all(stacked, 'dp', 0, 0, tiled=True, axis_index_groups=plane_g...  11.4 us
    unnamed x47, local copies, waits for them, and re-layouts  8.14 us
  transfers between devices with their start and end apart: 26, of which 17 were waited for; matrix products, arithmetic and copies ran while one was open for 4% of the time, Pallas kernels for 7%

profile of v4, /device:TPU:0, one launch (start us, length us, event | category | flops | bytes accessed | tf_op | source)
XLA Modules:
  0.0 195.4 jit_solution(5235685812803203059)
XLA Ops:
  0.7 0.9 concatenate.25
  1.5 2.8 %collective-permute-start.3 = (f32[1,128]{1,0:T(1,128)S(1)}, f32[1,128]{1,0:T(1,128)S(1)}, u32[]{:S(2)}, u32[]{:S(2)}) collective-permute-start(f32[1,128]{1,0:T(1,128)S(1)} %bitcast.47), channel_id=1, source_target_pairs={{0,3},{1,2},{2,1},{3,0},{4,7},{5,6},{6,5},{7,4},{8,11},{9,10},{10,... | collective-permute-start | bytes 1544 | tf_op jit(solution)/shard_map/ppermute | solution.py:31
  5.0 1.1 collective-permute-done.3.both_ref
  6.0 3.3 %collective-permute-done.2.far_ref = f32[1,128]{1,0:T(1,128)S(1)} collective-permute-done((f32[1,128]{1,0:T(1,128)S(1)}, f32[1,128]{1,0:T(1,128)S(1)}, u32[]{:S(2)}, u32[]{:S(2)}) %collective-permute-start.2) | collective-permute-done | bytes 544 | tf_op jit(solution)/shard_map/ppermute | solution.py:31
  12.2 1.3 shard_map.323
  13.5 8.4 %all-to-all-start = ((bf16[32,24,896]{2,1,0:T(8,128)(2,1)}), bf16[32,24,896]{2,1,0:T(8,128)(2,1)S(1)}, u32[]{:S(2)}, u32[]{:S(2)}) async-start(bf16[32,24,896]{2,1,0:T(8,128)(2,1)} %shard_map.323), calls=%async_computation | async-start | bytes 2752512 | tf_op jit(solution)/shard_map/all_to_all | solution.py:39
  22.0 1.9 collective-permute-start.4
  23.9 1.8 collective-permute-start
  26.9 17.6 %collective-permute-done = bf16[128,768]{1,0:T(8,128)(2,1)S(1)} collective-permute-done((bf16[128,768]{1,0:T(8,128)(2,1)S(1)}, bf16[128,768]{1,0:T(8,128)(2,1)S(1)}, u32[]{:S(2)}, u32[]{:S(2)}) %collective-permute-start) | collective-permute-done | bytes 196640 | tf_op jit(solution)/shard_map/ppermute | solution.py:31
  44.6 1.8 collective-permute-start.6
  46.6 1.4 copy-done
  48.0 5.4 %collective-permute-done.6.cotangent_far_ref = bf16[128,768]{1,0:T(8,128)(2,1)S(1)} collective-permute-done((bf16[128,768]{1,0:T(8,128)(2,1)S(1)}, bf16[128,768]{1,0:T(8,128)(2,1)S(1)}, u32[]{:S(2)}, u32[]{:S(2)}) %collective-permute-start.6) | collective-permute-done | bytes 196640 | tf_op jit(solution)/shard_map/ppermute | solution.py:31
  53.4 6.9 %all-to-all-start.1 = ((bf16[16,48,1536]{2,1,0:T(8,128)(2,1)}), bf16[16,48,1536]{2,1,0:T(8,128)(2,1)}, u32[]{:S(2)}, u32[]{:S(2)}) async-start(bf16[16,48,1536]{2,1,0:T(8,128)(2,1)} %copy-done), calls=%async_computation.1 | async-start | bytes 4718592 | tf_op jit(solution)/shard_map/all_to_all | solution.py:48
  60.3 2.8 %shard_map.325 = (bf16[512,768]{1,0:T(8,128)(2,1)S(1)}, bf16[512,256]{1,0:T(8,128)(2,1)S(1)}, f32[8,512]{1,0:T(8,128)S(1)}, bf16[256,768]{1,0:T(8,128)(2,1)S(1)}...) custom-call(s32[1]{0:T(128)} %bitcast.1.index_ref, ...), custom_call_target="tpu_custom_call" | custom-call | flops 1000 | bytes 1000 | tf_op jit(solution)/shard_map/pallas_call | solution.py:81
  63.1 0.9 copy-done.2
  64.0 1.7 collective-permute-done.7
  65.9 1.8 collective-permute-start.8
  67.7 11.0 %collective-permute-done.8.far_ref = bf16[256,768]{1,0:T(8,128)(2,1)S(1)} collective-permute-done((bf16[256,768]{1,0:T(8,128)(2,1)S(1)}, bf16[256,768]{1,0:T(8,128)(2,1)S(1)}, u32[]{:S(2)}, u32[]{:S(2)}) %collective-permute-start.8) | collective-permute-done | bytes 393248 | tf_op jit(solution)/shard_map/ppermute | solution.py:31
  79.1 0.9 copy-done.4
  80.0 0.9 copy-done.8
  80.8 1.7 collective-permute-done.9.other_ref.hidden_other
  82.6 11.1 %all-to-all-done.1.blocks_ref = bf16[16,48,1536]{2,1,0:T(8,128)(2,1)} async-done(((bf16[16,48,1536]{2,1,0:T(8,128)(2,1)}), bf16[16,48,1536]{2,1,0:T(8,128)(2,1)}, u32[]{:S(2)}, u32[]{:S(2)}) %all-to-all-start.1) | async-done | bytes 2359328 | tf_op jit(solution)/shard_map/all_to_all | solution.py:48
  93.7 5.0 %shard_map.327 = (bf16[512,768]{1,0:T(8,128)(2,1)S(1)}, f32[512,768]{1,0:T(8,128)}, f32[256,768]{1,0:T(8,128)S(1)}, bf16[256,768]{1,0:T(8,128)(2,1)S(1)}, bf16[7...) custom-call(bf16[256,768]{1,0:T(8,128)(2,1)S(1)} %get-tuple-element.72.near_ref.hidden_near, ...), custom_call_target="tpu_custom_call" | custom-call | flops 1000 | bytes 1000 | tf_op jit(solution)/shard_map/pallas_call | solution.py:81
  98.8 1.7 collective-permute-done.10
  100.7 1.8 collective-permute-start.11
  102.4 11.0 %collective-permute-done.11.far_ref = bf16[256,768]{1,0:T(8,128)(2,1)S(1)} collective-permute-done((bf16[256,768]{1,0:T(8,128)(2,1)S(1)}, bf16[256,768]{1,0:T(8,128)(2,1)S(1)}, u32[]{:S(2)}, u32[]{:S(2)}) %collective-permute-start.11) | collective-permute-done | bytes 393248 | tf_op jit(solution)/shard_map/ppermute | solution.py:31
  113.4 1.1 shard_map.328
  114.5 1.7 collective-permute-done.12.other_ref.branch_other
  116.3 3.6 %shard_map.329 = (bf16[512,768]{1,0:T(8,128)(2,1)S(1)}, f32[256,768]{1,0:T(8,128)S(1)}, bf16[256,768]{1,0:T(8,128)(2,1)S(1)}, f32[1,768]{1,0:T(1,128)S(1)}) custom-call(bf16[256,768]{1,0:T(8,128)(2,1)S(1)} %get-tuple-element.80.near_ref.branch_near, bf16[256,768]{1,0:T(8,128)(2,1)S(1)} %collective-permute-done.12.other_ref.branch_other, ...), custom_call_target="tpu_custom_call" | custom-call | flops 1000 | bytes 1000 | tf_op jit(solution)/shard_map/pallas_call | solution.py:81
  120.1 1.4 shard_map.334
  121.8 1.2 copy-done.1
  123.0 4.5 %all-to-all-start.3 = ((bf16[16,48,1536]{2,1,0:T(8,128)(2,1)}), bf16[16,48,1536]{2,1,0:T(8,128)(2,1)}, u32[]{:S(2)}, u32[]{:S(2)}) async-start(bf16[16,48,1536]{2,1,0:T(8,128)(2,1)} %copy-done.1), calls=%async_computation.3 | async-start | bytes 4718592 | tf_op jit(solution)/shard_map/all_to_all | solution.py:48
  127.5 1.8 collective-permute-start.14
  129.3 11.2 %collective-permute-done.14.far_ref = bf16[256,768]{1,0:T(8,128)(2,1)S(1)} collective-permute-done((bf16[256,768]{1,0:T(8,128)(2,1)S(1)}, bf16[256,768]{1,0:T(8,128)(2,1)S(1)}, u32[]{:S(2)}, u32[]{:S(2)}) %collective-permute-start.14) | collective-permute-done | bytes 393248 | tf_op jit(solution)/shard_map/ppermute | solution.py:31
  141.1 1.7 collective-permute-done.15.other_ref
  142.8 4.4 %shard_map.331 = (bf16[512,768]{1,0:T(8,128)(2,1)S(1)}, bf16[256,768]{1,0:T(8,128)(2,1)}, f32[256,768]{1,0:T(8,128)S(1)}, f32[16,768]{1,0:T(8,128)S(1)}) custom-call(s32[1]{0:T(128)} %bitcast.1.index_ref, bf16[256,768]{1,0:T(8,128)(2,1)S(1)} %get-tuple-element.90.near_ref, bf16[256,768]{1,0:T(8,128)(2,1)S(1)} %collective-permute-done.15.other_ref, ...), custom_call_target="tpu_custom_call" | custom-call | flops 1000 | bytes 1000 | tf_op jit(solution)/shard_map/pallas_call | solution.py:81
  147.2 1.4 collective-permute-start.20
  148.7 1.9 collective-permute-start.19
  151.0 2.2 %shard_map.332 = bf16[768,896]{1,0:T(8,128)(2,1)} custom-call(bf16[256,768]{1,0:T(8,128)(2,1)S(1)} %pad_maximum_fusion.near_ref.tokens_ref.tokens_near, bf16[256,768]{1,0:T(8,128)(2,1)S(1)} %collective-permute-done.5.other_ref.tokens_other, bf16[256,768]{1,0:T(8,128)(2,1)S(1)} %get-tuple-element.90.near_ref, ...), custom_call_target="tpu_custom_call" | custom-call | flops 1000 | bytes 1000 | tf_op jit(solution)/shard_map/pallas_call | solution.py:81
  153.3 1.0 collective-permute-done.19
  154.5 2.7 %dynamic_update_slice.3 = bf16[768,896]{1,0:T(8,128)(2,1)} dynamic-update-slice(bf16[768,896]{1,0:T(8,128)(2,1)} %shard_map.332, bf16[768,24]{1,0:T(8,128)(2,1)S(1)} %copy.41, s32[]{:T(128)} %constant.50.clone.1, s32[]{:T(128)} %constant.55.clone.1) | dynamic-update-slice | bytes 73732 | tf_op jit(solution)/shard_map/dynamic_update_slice | solution.py:840
  157.2 1.1 convert_add_fusion
  158.3 2.9 %all-to-all-done.3.blocks_ref = bf16[16,48,1536]{2,1,0:T(8,128)(2,1)} async-done(((bf16[16,48,1536]{2,1,0:T(8,128)(2,1)}), bf16[16,48,1536]{2,1,0:T(8,128)(2,1)}, u32[]{:S(2)}, u32[]{:S(2)}) %all-to-all-start.3) | async-done | bytes 2359328 | tf_op jit(solution)/shard_map/all_to_all | solution.py:48
  161.2 7.1 %all-to-all-start.2 = ((bf16[32,24,896]{2,1,0:T(8,128)(2,1)}), bf16[32,24,896]{2,1,0:T(8,128)(2,1)S(1)}, u32[]{:S(2)}, u32[]{:S(2)}) async-start(bf16[32,24,896]{2,1,0:T(8,128)(2,1)} %bitcast.15), calls=%async_computation.2 | async-start | bytes 2752512 | tf_op jit(solution)/shard_map/all_to_all | solution.py:39
  168.4 3.0 %collective-permute-start.17 = (bf16[128,768]{1,0:T(8,128)(2,1)S(1)}, bf16[128,768]{1,0:T(8,128)(2,1)S(1)}, u32[]{:S(2)}, u32[]{:S(2)}) collective-permute-start(bf16[128,768]{1,0:T(8,128)(2,1)S(1)} %slice.180), channel_id=1, source_target_pairs={{0,2},{1,3},{2,0},{3,1},{4,6},{5,7},{6,4},{7,5},{8,10},{9,11},{10,... | collective-permute-start | bytes 589832 | tf_op jit(solution)/shard_map/ppermute | solution.py:31
  171.4 2.0 %shard_map.335 = (f32[24,1536]{1,0:T(8,128)S(1)}, f32[24,1536]{1,0:T(8,128)S(1)}) custom-call(s32[1]{0:T(128)} %bitcast.4.index_ref, bf16[16,48,1536]{2,1,0:T(8,128)(2,1)} %all-to-all-done.3.blocks_ref), custom_call_target="tpu_custom_call" | custom-call | flops 1000 | bytes 1000 | tf_op jit(solution)/shard_map/pallas_call | solution.py:81
  173.3 1.3 collective-permute-start.21
  174.6 17.2 %collective-permute-done.17 = bf16[128,768]{1,0:T(8,128)(2,1)S(1)} collective-permute-done((bf16[128,768]{1,0:T(8,128)(2,1)S(1)}, bf16[128,768]{1,0:T(8,128)(2,1)S(1)}, u32[]{:S(2)}, u32[]{:S(2)}) %collective-permute-start.17) | collective-permute-done | bytes 196640 | tf_op jit(solution)/shard_map/ppermute | solution.py:31
  (96 shorter events, 11.2 us)
Async XLA Ops:
  1.5 4.5 %collective-permute-start.3 = (f32[1,128]{1,0:T(1,128)S(1)}, f32[1,128]{1,0:T(1,128)S(1)}, u32[]{:S(2)}, u32[]{:S(2)}) collective-permute-start(f32[1,128]{1,0:T(1,128)S(1)} %bitcast.47), channel_id=1, source_target_pairs={{0,3},{1,2},{2,1},{3,0},{4,7},{5,6},{6,5},{7,4},{8,11},{9,10},{10,... | collective-permute-start | bytes 1544 | tf_op jit(solution)/shard_map/ppermute | solution.py:31
  4.3 5.0 %collective-permute-start.2 = (f32[1,128]{1,0:T(1,128)S(1)}, f32[1,128]{1,0:T(1,128)S(1)}, u32[]{:S(2)}, u32[]{:S(2)}) collective-permute-start(f32[1,128]{1,0:T(1,128)S(1)} %bitcast.48), channel_id=1, source_target_pairs={{0,2},{1,3},{2,0},{3,1},{4,6},{5,7},{6,4},{7,5},{8,10},{9,11},{10,... | collective-permute-start | bytes 1544 | tf_op jit(solution)/shard_map/ppermute | solution.py:31
  4.9 4.4 %collective-permute-start.1 = (f32[1,128]{1,0:T(1,128)S(1)}, f32[1,128]{1,0:T(1,128)S(1)}, u32[]{:S(2)}, u32[]{:S(2)}) collective-permute-start(f32[1,128]{1,0:T(1,128)S(1)} %bitcast.49), channel_id=1, source_target_pairs={{0,1},{1,0},{2,3},{3,2},{4,5},{5,4},{6,7},{7,6},{8,9},{9,8},{10,11... | collective-permute-start | bytes 1544 | tf_op jit(solution)/shard_map/ppermute | solution.py:31
  9.3 0.7 copy-start.13
  10.1 0.7 copy-start.14
  10.8 0.7 copy-start.15
  13.5 8.5 %copy-start.19 = (bf16[24,768]{1,0:T(8,128)(2,1)S(1)}, bf16[24,768]{1,0:T(8,128)(2,1)}, u32[]{:S(2)}) copy-start(bf16[24,768]{1,0:T(8,128)(2,1)} %param.25) | copy-start | bytes 110596
  13.5 8.5 %copy-start.20 = (bf16[24,768]{1,0:T(8,128)(2,1)S(1)}, bf16[24,768]{1,0:T(8,128)(2,1)}, u32[]{:S(2)}) copy-start(bf16[24,768]{1,0:T(8,128)(2,1)} %param.27) | copy-start | bytes 110596
  13.5 10.4 %copy-start.17 = (bf16[1,128,768]{2,1,0:T(8,128)(2,1)S(1)}, bf16[1,128,768]{2,1,0:T(8,128)(2,1)}, u32[]{:S(2)}) copy-start(bf16[1,128,768]{2,1,0:T(8,128)(2,1)} %param.20) | copy-start | bytes 589828
  13.5 12.2 %copy-start.21 = (s32[4]{0:T(128)S(1)}, s32[4]{0:T(128)}, u32[]{:S(2)}) copy-start(s32[4]{0:T(128)} %constant.85) | copy-start | bytes 52
  13.5 12.2 %copy-start.22 = (s32[4]{0:T(128)S(1)}, s32[4]{0:T(128)}, u32[]{:S(2)}) copy-start(s32[4]{0:T(128)} %constant.84) | copy-start | bytes 52
  13.5 12.2 %copy-start.18 = (s32[1,512]{1,0:T(1,128)S(1)}, s32[1,512]{1,0:T(1,128)}, u32[]{:S(2)}) copy-start(s32[1,512]{1,0:T(1,128)} %param.21) | copy-start | bytes 6148
  13.5 31.1 %copy-start.12 = (bf16[1,128,768]{2,1,0:T(8,128)(2,1)S(1)}, bf16[1,128,768]{2,1,0:T(8,128)(2,1)}, u32[]{:S(2)}) copy-start(bf16[1,128,768]{2,1,0:T(8,128)(2,1)} %param.37) | copy-start | bytes 589828
  13.5 39.9 %all-to-all-start = ((bf16[32,24,896]{2,1,0:T(8,128)(2,1)}), bf16[32,24,896]{2,1,0:T(8,128)(2,1)S(1)}, u32[]{:S(2)}, u32[]{:S(2)}) async-start(bf16[32,24,896]{2,1,0:T(8,128)(2,1)} %shard_map.323), calls=%async_computation | async-start | bytes 2752512 | tf_op jit(solution)/shard_map/all_to_all | solution.py:39
  22.0 24.4 %collective-permute-start.4 = (bf16[24,1536]{1,0:T(8,128)(2,1)S(1)}, bf16[24,1536]{1,0:T(8,128)(2,1)S(1)}, u32[]{:S(2)}, u32[]{:S(2)}) collective-permute-start(bf16[24,1536]{1,0:T(8,128)(2,1)S(1)} %constant_dynamic-update-slice_fusion.own_ref), channel_id=1, source_target_pairs={{0,64},{4,68},{8,72},{12,76},{16,80},{20,84},{24,88},{28,92},{32,9... | collective-permute-start | bytes 221192 | tf_op jit(solution)/shard_map/ppermute | solution.py:54
  23.9 20.5 %collective-permute-start = (bf16[128,768]{1,0:T(8,128)(2,1)S(1)}, bf16[128,768]{1,0:T(8,128)(2,1)S(1)}, u32[]{:S(2)}, u32[]{:S(2)}) collective-permute-start(bf16[128,768]{1,0:T(8,128)(2,1)S(1)} %bitcast.51), channel_id=1, source_target_pairs={{0,2},{1,3},{2,0},{3,1},{4,6},{5,7},{6,4},{7,5},{8,10},{9,11},{10,... | collective-permute-start | bytes 589832 | tf_op jit(solution)/shard_map/ppermute | solution.py:31
  44.4 8.9 %collective-permute-start.5 = (bf16[256,768]{1,0:T(8,128)(2,1)S(1)}, bf16[256,768]{1,0:T(8,128)(2,1)S(1)}, u32[]{:S(2)}, u32[]{:S(2)}) collective-permute-start(bf16[256,768]{1,0:T(8,128)(2,1)S(1)} %pad_maximum_fusion.near_ref.tokens_ref.tokens_near), channel_id=1, source_target_pairs={{0,1},{1,0},{2,3},{3,2},{4,5},{5,4},{6,7},{7,6},{8,9},{9,8},{10,11... | collective-permute-start | bytes 1179656 | tf_op jit(solution)/shard_map/ppermute | solution.py:31
  44.6 8.8 %collective-permute-start.6 = (bf16[128,768]{1,0:T(8,128)(2,1)S(1)}, bf16[128,768]{1,0:T(8,128)(2,1)S(1)}, u32[]{:S(2)}, u32[]{:S(2)}) collective-permute-start(bf16[128,768]{1,0:T(8,128)(2,1)S(1)} %bitcast.43), channel_id=1, source_target_pairs={{0,2},{1,3},{2,0},{3,1},{4,6},{5,7},{6,4},{7,5},{8,10},{9,11},{10,... | collective-permute-start | bytes 589832 | tf_op jit(solution)/shard_map/ppermute | solution.py:31
  46.6 1.4 copy-start
  53.4 40.3 %all-to-all-start.1 = ((bf16[16,48,1536]{2,1,0:T(8,128)(2,1)}), bf16[16,48,1536]{2,1,0:T(8,128)(2,1)}, u32[]{:S(2)}, u32[]{:S(2)}) async-start(bf16[16,48,1536]{2,1,0:T(8,128)(2,1)} %copy-done), calls=%async_computation.1 | async-start | bytes 4718592 | tf_op jit(solution)/shard_map/all_to_all | solution.py:48
  63.1 0.9 copy-start.2
  64.0 1.9 copy-start.10
  64.0 1.7 collective-permute-start.7
  65.9 12.7 %collective-permute-start.8 = (bf16[256,768]{1,0:T(8,128)(2,1)S(1)}, bf16[256,768]{1,0:T(8,128)(2,1)S(1)}, u32[]{:S(2)}, u32[]{:S(2)}) collective-permute-start(bf16[256,768]{1,0:T(8,128)(2,1)S(1)} %pad_maximum_fusion.1), channel_id=1, source_target_pairs={{0,2},{1,3},{2,0},{3,1},{4,6},{5,7},{6,4},{7,5},{8,10},{9,11},{10,... | collective-permute-start | bytes 1179656 | tf_op jit(solution)/shard_map/ppermute | solution.py:31
  79.1 0.9 copy-start.4
  80.0 0.9 copy-start.8
  80.8 1.7 collective-permute-start.9
  98.8 1.7 collective-permute-start.10
  100.6 12.8 %copy-start.9 = (f32[256,768]{1,0:T(8,128)S(1)}, f32[256,768]{1,0:T(8,128)}, u32[]{:S(2)}) copy-start(f32[256,768]{1,0:T(8,128)} %copy-done.8) | copy-start | bytes 2359300
  100.7 12.7 %collective-permute-start.11 = (bf16[256,768]{1,0:T(8,128)(2,1)S(1)}, bf16[256,768]{1,0:T(8,128)(2,1)S(1)}, u32[]{:S(2)}, u32[]{:S(2)}) collective-permute-start(bf16[256,768]{1,0:T(8,128)(2,1)S(1)} %pad_maximum_fusion.2), channel_id=1, source_target_pairs={{0,2},{1,3},{2,0},{3,1},{4,6},{5,7},{6,4},{7,5},{8,10},{9,11},{10,... | collective-permute-start | bytes 1179656 | tf_op jit(solution)/shard_map/ppermute | solution.py:31
  114.5 5.3 %copy-start.6 = (f32[256,768]{1,0:T(8,128)}, f32[256,768]{1,0:T(8,128)S(1)}, u32[]{:S(2)}) copy-start(f32[256,768]{1,0:T(8,128)S(1)} %get-tuple-element.79.second_ref) | copy-start | bytes 2359300
  114.5 1.7 collective-permute-start.12
  119.9 1.8 collective-permute-start.13
  121.5 1.4 copy-start.1
  123.0 38.2 %all-to-all-start.3 = ((bf16[16,48,1536]{2,1,0:T(8,128)(2,1)}), bf16[16,48,1536]{2,1,0:T(8,128)(2,1)}, u32[]{:S(2)}, u32[]{:S(2)}) async-start(bf16[16,48,1536]{2,1,0:T(8,128)(2,1)} %copy-done.1), calls=%async_computation.3 | async-start | bytes 4718592 | tf_op jit(solution)/shard_map/all_to_all | solution.py:48
  127.4 13.1 %copy-start.5 = (f32[256,768]{1,0:T(8,128)S(1)}, f32[256,768]{1,0:T(8,128)}, u32[]{:S(2)}) copy-start(f32[256,768]{1,0:T(8,128)} %copy-done.4) | copy-start | bytes 2359300
  127.4 13.1 %copy-start.7 = (f32[256,768]{1,0:T(8,128)S(1)}, f32[256,768]{1,0:T(8,128)}, u32[]{:S(2)}) copy-start(f32[256,768]{1,0:T(8,128)} %copy-done.6) | copy-start | bytes 2359300
  127.5 13.0 %collective-permute-start.14 = (bf16[256,768]{1,0:T(8,128)(2,1)S(1)}, bf16[256,768]{1,0:T(8,128)(2,1)S(1)}, u32[]{:S(2)}, u32[]{:S(2)}) collective-permute-start(bf16[256,768]{1,0:T(8,128)(2,1)S(1)} %pad_maximum_fusion.3), channel_id=1, source_target_pairs={{0,2},{1,3},{2,0},{3,1},{4,6},{5,7},{6,4},{7,5},{8,10},{9,11},{10,... | collective-permute-start | bytes 1179656 | tf_op jit(solution)/shard_map/ppermute | solution.py:31
  140.5 2.3 %copy-start.3 = (bf16[512,768]{1,0:T(8,128)(2,1)S(1)}, bf16[512,768]{1,0:T(8,128)(2,1)}, u32[]{:S(2)}) copy-start(bf16[512,768]{1,0:T(8,128)(2,1)} %copy-done.2) | copy-start | bytes 2359300
  141.0 1.8 collective-permute-start.15
  142.8 8.2 %copy-start.11 = (bf16[512,256]{1,0:T(8,128)(2,1)S(1)}, bf16[512,256]{1,0:T(8,128)(2,1)}, u32[]{:S(2)}) copy-start(bf16[512,256]{1,0:T(8,128)(2,1)} %copy-done.10) | copy-start | bytes 786436
  147.2 6.0 %collective-permute-start.20 = (f32[16,768]{1,0:T(8,128)S(1)}, f32[16,768]{1,0:T(8,128)S(1)}, u32[]{:S(2)}, u32[]{:S(2)}) collective-permute-start(f32[16,768]{1,0:T(8,128)S(1)} %get-tuple-element.99), channel_id=1, source_target_pairs={{0,3},{1,2},{2,1},{3,0},{4,7},{5,6},{6,5},{7,4},{8,11},{9,10},{10,... | collective-permute-start | bytes 147464 | tf_op jit(solution)/shard_map/ppermute | solution.py:31
  148.7 5.6 %collective-permute-start.19 = (f32[16,768]{1,0:T(8,128)S(1)}, f32[16,768]{1,0:T(8,128)S(1)}, u32[]{:S(2)}, u32[]{:S(2)}) collective-permute-start(f32[16,768]{1,0:T(8,128)S(1)} %get-tuple-element.99), channel_id=1, source_target_pairs={{0,2},{1,3},{2,0},{3,1},{4,6},{5,7},{6,4},{7,5},{8,10},{9,11},{10,... | collective-permute-start | bytes 147464 | tf_op jit(solution)/shard_map/ppermute | solution.py:31
  150.5 3.8 %collective-permute-start.18 = (f32[16,768]{1,0:T(8,128)S(1)}, f32[16,768]{1,0:T(8,128)S(1)}, u32[]{:S(2)}, u32[]{:S(2)}) collective-permute-start(f32[16,768]{1,0:T(8,128)S(1)} %get-tuple-element.99), channel_id=1, source_target_pairs={{0,1},{1,0},{2,3},{3,2},{4,5},{5,4},{6,7},{7,6},{8,9},{9,8},{10,11... | collective-permute-start | bytes 147464 | tf_op jit(solution)/shard_map/ppermute | solution.py:31
  150.6 6.6 %collective-permute-start.16 = (bf16[256,768]{1,0:T(8,128)(2,1)}, bf16[256,768]{1,0:T(8,128)(2,1)}, u32[]{:S(2)}, u32[]{:S(2)}) collective-permute-start(bf16[256,768]{1,0:T(8,128)(2,1)} %get-tuple-element.96), channel_id=1, source_target_pairs={{0,1},{1,0},{2,3},{3,2},{4,5},{5,4},{6,7},{7,6},{8,9},{9,8},{10,11... | collective-permute-start | bytes 1179656 | tf_op jit(solution)/shard_map/ppermute | solution.py:31
  161.2 32.1 %all-to-all-start.2 = ((bf16[32,24,896]{2,1,0:T(8,128)(2,1)}), bf16[32,24,896]{2,1,0:T(8,128)(2,1)S(1)}, u32[]{:S(2)}, u32[]{:S(2)}) async-start(bf16[32,24,896]{2,1,0:T(8,128)(2,1)} %bitcast.15), calls=%async_computation.2 | async-start | bytes 2752512 | tf_op jit(solution)/shard_map/all_to_all | solution.py:39
  168.4 23.4 %collective-permute-start.17 = (bf16[128,768]{1,0:T(8,128)(2,1)S(1)}, bf16[128,768]{1,0:T(8,128)(2,1)S(1)}, u32[]{:S(2)}, u32[]{:S(2)}) collective-permute-start(bf16[128,768]{1,0:T(8,128)(2,1)S(1)} %slice.180), channel_id=1, source_target_pairs={{0,2},{1,3},{2,0},{3,1},{4,6},{5,7},{6,4},{7,5},{8,10},{9,11},{10,... | collective-permute-start | bytes 589832 | tf_op jit(solution)/shard_map/ppermute | solution.py:31
  173.3 19.3 %collective-permute-start.21 = (f32[24,1536]{1,0:T(8,128)S(1)}, f32[24,1536]{1,0:T(8,128)S(1)}, u32[]{:S(2)}, u32[]{:S(2)}) collective-permute-start(f32[24,1536]{1,0:T(8,128)S(1)} %get-tuple-element.108), channel_id=1, source_target_pairs={{0,64},{4,68},{8,72},{12,76},{16,80},{20,84},{24,88},{28,92},{32,9... | collective-permute-start | bytes 442376 | tf_op jit(solution)/shard_map/ppermute | solution.py:54
  (1 other events, 0.7 us)

commit v5 on v4

--- a/solution.py
+++ b/solution.py
@@ -59,11 +59,10 @@
     return (high.astype(LOW), (values - high).astype(LOW))
 
 
-def far_sum(total):
+def far_pack(total):
     quarter = total.shape[0] // 2
     sent = total.astype(LOW)
-    sent = jnp.concatenate([sent[quarter:], sent[:quarter]], axis=0)
-    return swap(sent, 2)
+    return jnp.concatenate([sent[quarter:], sent[:quarter]], axis=0)
 
 
 def ordered_segments(segment_row, my_index):
@@ -75,14 +74,24 @@
     return jnp.concatenate([quarters[0], quarters[2], quarters[1], quarters[3]])
 
 
-def call(body, out_shapes, *operands, smem=0, scratch=()):
+def call(body, out_shapes, *operands, smem=0, scratch=(), away=(), far=(), aliases=None):
     specs = [pl.BlockSpec(memory_space=pltpu.SMEM)] * smem
-    specs += [pl.BlockSpec(memory_space=pltpu.VMEM)] * (len(operands) - smem)
+    specs += [
+        pl.BlockSpec(memory_space=pltpu.HBM if i in far else pltpu.VMEM)
+        for i in range(smem, len(operands))
+    ]
     return pl.pallas_call(
         body,
-        out_shape=[jax.ShapeDtypeStruct(shape, kind) for shape, kind in out_shapes],
+        out_shape=[
+            pltpu.HBM(shape, kind) if i in away else jax.ShapeDtypeStruct(shape, kind)
+            for i, (shape, kind) in enumerate(out_shapes)
+        ],
         in_specs=specs,
-        out_specs=[pl.BlockSpec(memory_space=pltpu.VMEM)] * len(out_shapes),
+        out_specs=[
+            pl.BlockSpec(memory_space=pltpu.HBM if i in away else pltpu.VMEM)
+            for i in range(len(out_shapes))
+        ],
+        input_output_aliases=aliases or {},
         scratch_shapes=list(scratch),
         compiler_params=pltpu.CompilerParams(vmem_limit_bytes=VMEM_LIMIT),
         cost_estimate=pl.CostEstimate(flops=1000, bytes_accessed=1000, transcendentals=0),
@@ -137,13 +146,15 @@
     other_ref,
     weight_ref,
     segment_ref,
-    qkv_ref,
+    qkv_out,
     mixed_ref,
     log_ref,
     send_ref,
     keep_ref,
     vector_ref,
     up_bias_ref,
+    qkv_ref,
+    qkv_sem,
 ):
     index = index_ref[0]
     half = near_ref.shape[0]
@@ -177,6 +188,8 @@
     for at, rows_ref in ((0, near_ref), (half, other_ref)):
         got = jnp.dot(rows_ref[...], weight_ref[:, : 3 * GROUP], preferred_element_type=FULL)
         qkv_ref[at : at + half, :] = jnp.where(keep, got + bias, 0.0).astype(LOW)
+    qkv_copy = pltpu.make_async_copy(qkv_ref, qkv_out, qkv_sem)
+    qkv_copy.start()
 
     length = 2 * half
     row_segments = segment_ref[...]
@@ -206,6 +219,7 @@
     out = packed_out(weight_ref)
     keep_ref[...] = contract(mixed_ref[:half, :], out, 1, 1)
     send_ref[...] = contract(mixed_ref[half:, :], out, 1, 1).astype(LOW)
+    qkv_copy.wait()
 
 
 def backward_kernel(
@@ -218,6 +232,7 @@
     segment_ref,
     sums_ref,
     up_sum_ref,
+    up_sum_other_ref,
     grad_ref,
     send_ref,
     keep_ref,
@@ -283,7 +298,7 @@
     keep_ref[...] = contract(grad_ref[:half, :], wide, 1, 1)
     send_ref[...] = contract(grad_ref[half:, :], wide, 1, 1).astype(LOW)
 
-    up_row = up_sum_ref[...]
+    up_row = up_sum_ref[...] + up_sum_other_ref[...]
     place = lanes((8, 4 * columns))
     spaced = jnp.where(place % 4 == lanes((8, 4 * columns), 0), up_row, 0.0)
     high = spaced.astype(LOW)
@@ -306,7 +321,9 @@
     vector_ref[8:, :] = placed[8:]
 
 
-def weights_kernel(tokens_near, tokens_other, near_ref, other_ref, grad_ref, mixed_ref, out_ref):
+def weights_kernel(
+    tokens_near, tokens_other, near_ref, other_ref, grad_ref, mixed_ref, out, out_ref, sem
+):
     half = near_ref.shape[0]
     width = near_ref.shape[1]
     got = contract(tokens_near[...], grad_ref[:half, :], 0, 0) + contract(
@@ -322,7 +339,22 @@
         out_ref[:, at + TILE : at + GROUP] = jnp.where(
             high, lined, got[:, at + TILE : at + GROUP]
         ).astype(LOW)
-    out_ref[:, 3 * GROUP :] = jnp.zeros((width, TILE), LOW)
+    copy = pltpu.make_async_copy(out_ref, out.at[:, : 3 * GROUP], sem)
+    copy.start()
+    copy.wait()
+
+
+def vectors_kernel(block_ref, own_ref, core_ref, far_ref, both_ref, out_ref, held, sem):
+    total = own_ref[...] + core_ref[...] + (far_ref[...] + both_ref[...])
+    total = total[:12]
+    high = total.astype(LOW).astype(FULL)
+    rows = jnp.concatenate(
+        [high, total - high, jnp.zeros((TILE - 24, total.shape[1]), FULL)], axis=0
+    )
+    held[...] = jnp.transpose(rows).astype(LOW)
+    copy = pltpu.make_async_copy(held, out_ref.at[:, 3 * GROUP :], sem)
+    copy.start()
+    copy.wait()
 
 
 def place_of(vector_rows, shape, dim):
@@ -334,10 +366,11 @@
 
 
 def first_block_kernel(
-    index_ref, own_ref, core_ref, far_ref, both_ref, q_ref, k_ref, v_ref, out_ref, block_ref
+    index_ref, own_ref, core_ref, far_ref, both_ref, weight_ref, block_ref
 ):
     index = index_ref[0]
-    rows = q_ref.shape[0]
+    rows = weight_ref.shape[0]
+    columns_each = weight_ref.shape[1] // 4
     vector_rows = rows // 4
     shape = (rows, own_ref.shape[1])
     row_at = lanes(shape, 0)
@@ -360,14 +393,17 @@
     packed = jnp.dot(high, first, preferred_element_type=FULL) + jnp.dot(
         low, second, preferred_element_type=FULL
     )
-    out = out_ref[...].astype(FULL)
+    weight = weight_ref[...].astype(FULL)
+    q_part, k_part, v_part, out = [
+        weight[:, columns_each * i : columns_each * (i + 1)] for i in range(4)
+    ]
     block = jnp.concatenate(
         [
-            q_ref[...].astype(FULL),
+            q_part,
             out[:, :HEAD_DIM],
-            k_ref[...].astype(FULL),
+            k_part,
             out[:, HEAD_DIM : 2 * HEAD_DIM],
-            v_ref[...].astype(FULL),
+            v_part,
             out[:, 2 * HEAD_DIM :],
             packed,
         ],
@@ -408,33 +444,35 @@
     return [(at, at + size) for at in range(0, rows, size)]
 
 
-def first_norm_kernel(
-    tokens_ref, chip_ref, far_ref, rows_ref, first_ref, low_ref, normed_ref, scale_ref
-):
-    for at, to in blocks_of(tokens_ref.shape[0]):
+def first_norm_kernel(tokens_ref, chip_ref, far_ref, rows_ref, low_ref, scale_ref):
+    for at, to in blocks_of(tokens_ref.shape[0], TILE):
         values = (
             tokens_ref[at:to].astype(FULL)
             + (chip_ref[at:to] + far_ref[at:to].astype(FULL))
             + rows_ref[2:3]
         )
-        first, normed, scale_inv = moments(values, rows_ref[4:5], rows_ref[5:6])
-        first_ref[at:to] = first
+        first, _, scale_inv = moments(values, rows_ref[4:5], rows_ref[5:6])
         low_ref[at:to] = first.astype(LOW)
-        normed_ref[at:to] = normed
-        scale_ref[at:to] = jnp.broadcast_to(scale_inv, (to - at, TILE))
-
-
-def feed_kernel(
-    near_ref,
-    other_ref,
-    blocks_ref,
-    bias_ref,
-    active_ref,
-    slope_ref,
-    keep_ref,
-    send_ref,
-    up_ref,
-    down_ref,
+        scale_ref[:, at:to] = jnp.transpose(jnp.broadcast_to(scale_inv, (TILE, TILE)))[:8]
+
+
+def feed_rows(rows_ref, up, down, bias_ref, active_ref, slope_ref, part_ref):
+    size = rows_ref.shape[0] // 2
+    for at, to in blocks_of(rows_ref.shape[0], size):
+        upward = jnp.dot(rows_ref[at:to], up[...], preferred_element_type=FULL) + bias_ref[...]
+        for low, high in blocks_of(size, 32):
+            part = upward[low:high]
+            gate = 0.5 * (1.0 + lax.erf(part * ROOT_HALF))
+            active_ref[at + low : at + high] = (part * gate).astype(LOW)
+            slope_ref[at + low : at + high] = (
+                gate + part * jnp.exp(-0.5 * part * part) * INV_ROOT_TAU
+            )
+        got = contract(active_ref[at:to], down[...], 1, 1)
+        part_ref[at:to] = got.astype(part_ref.dtype)
+
+
+def feed_other_kernel(
+    rows_ref, blocks_ref, bias_ref, active_ref, slope_ref, part_ref, up_ref, down_ref
 ):
     count, rows, wide = blocks_ref.shape
     rows = rows // 2
@@ -452,25 +490,11 @@
             to = (lower * count + at) * rows
             up_ref[to : to + group * rows] = got[:, :hidden]
             down_ref[to : to + group * rows] = got[:, hidden:]
-    half = near_ref.shape[0]
-    size = half // 2
-    for base, rows_ref in ((half, other_ref), (0, near_ref)):
-        for at, to in blocks_of(half, size):
-            upward = (
-                jnp.dot(rows_ref[at:to], up_ref[...], preferred_element_type=FULL) + bias_ref[...]
-            )
-            for low, high in blocks_of(size, 32):
-                part = upward[low:high]
-                gate = 0.5 * (1.0 + lax.erf(part * ROOT_HALF))
-                active_ref[base + at + low : base + at + high] = (part * gate).astype(LOW)
-                slope_ref[base + at + low : base + at + high] = (
-                    gate + part * jnp.exp(-0.5 * part * part) * INV_ROOT_TAU
-                )
-            got = contract(active_ref[base + at : base + to], down_ref[...], 1, 1)
-            if base:
-                send_ref[at:to] = got.astype(LOW)
-            else:
-                keep_ref[at:to] = got
+    feed_rows(rows_ref, up_ref, down_ref, bias_ref, active_ref, slope_ref, part_ref)
+
+
+def feed_near_kernel(rows_ref, up_ref, down_ref, bias_ref, active_ref, slope_ref, part_ref):
+    feed_rows(rows_ref, up_ref, down_ref, bias_ref, active_ref, slope_ref, part_ref)
 
 
 def second_norm_kernel(
@@ -481,14 +505,13 @@
     cotangent_ref,
     cotangent_far_ref,
     output_ref,
-    grad_ref,
     low_ref,
     sums_ref,
 ):
     own = output_ref.shape[0]
     sums = [jnp.zeros((1, first_ref.shape[1]), FULL) for _ in range(3)]
     for at, to in blocks_of(first_ref.shape[0]):
-        values = first_ref[at:to] + (chip_ref[at:to] + far_ref[at:to].astype(FULL)) + rows_ref[3:4]
+        values = first_ref[at:to].astype(FULL) + (chip_ref[at:to] + far_ref[at:to].astype(FULL)) + rows_ref[3:4]
         output, normed, scale_inv = moments(values, rows_ref[6:7], rows_ref[7:8])
         if to <= own:
             upstream = cotangent_ref[at:to].astype(FULL)
@@ -496,7 +519,6 @@
         else:
             upstream = cotangent_far_ref[at - own : to - own].astype(FULL)
         grad = norm_backward(upstream, normed, scale_inv, rows_ref[6:7])
-        grad_ref[at:to] = grad
         low = grad.astype(LOW)
         low_ref[at:to] = low
         if to <= own:
@@ -505,51 +527,64 @@
     sums_ref[...] = jnp.concatenate(sums + [jnp.zeros((5, sums[0].shape[1]), FULL)], axis=0)
 
 
-def feed_backward_kernel(
-    near_ref, other_ref, up_ref, down_ref, slope_ref, grad_ref, keep_ref, send_ref, sum_ref
+def feed_backward_kernel(rows_ref, up_ref, down_ref, slope_ref, grad_ref, part_ref, sum_ref):
+    size = rows_ref.shape[0] // 2
+    total = jnp.zeros((1, up_ref.shape[1]), FULL)
+    for at, to in blocks_of(rows_ref.shape[0], size):
+        grad = jnp.dot(rows_ref[at:to], down_ref[...], preferred_element_type=FULL)
+        for low, high in blocks_of(size, 32):
+            place = slice(at + low, at + high)
+            part = (grad[low:high] * slope_ref[place]).astype(LOW)
+            grad_ref[place] = part
+            total += jnp.sum(part.astype(FULL), axis=0, keepdims=True)
+        got = contract(grad_ref[at:to], up_ref[...], 1, 1)
+        part_ref[at:to] = got.astype(part_ref.dtype)
+    sum_ref[...] = total
+
+
+def feed_weights_kernel(
+    hidden_near,
+    hidden_other,
+    branch_near,
+    branch_other,
+    active_near,
+    active_other,
+    grad_near,
+    grad_other,
+    out,
+    out_ref,
+    sems,
 ):
-    half = near_ref.shape[0]
-    size = half // 2
-    total = jnp.zeros((1, up_ref.shape[1]), FULL)
-    for base, rows_ref in ((half, other_ref), (0, near_ref)):
-        for at, to in blocks_of(half, size):
-            grad = jnp.dot(rows_ref[at:to], down_ref[...], preferred_element_type=FULL)
-            for low, high in blocks_of(size, 32):
-                place = slice(base + at + low, base + at + high)
-                part = (grad[low:high] * slope_ref[place]).astype(LOW)
-                grad_ref[place] = part
-                total += jnp.sum(part.astype(FULL), axis=0, keepdims=True)
-            got = contract(grad_ref[base + at : base + to], up_ref[...], 1, 1)
-            if base:
-                send_ref[at:to] = got.astype(LOW)
-            else:
-                keep_ref[at:to] = got
-    sum_ref[...] = total
-
-
-def feed_weights_kernel(
-    hidden_near, hidden_other, branch_near, branch_other, active_ref, grad_ref, out_ref
-):
-    half = hidden_near.shape[0]
     count, rows, wide = out_ref.shape
     rows = rows // 2
     hidden = wide // 2
-    for place, near, other, right in (
-        (0, hidden_near, hidden_other, grad_ref),
-        (hidden, branch_near, branch_other, active_ref),
+    copies = []
+    for place, near, other, right_near, right_other in (
+        (0, hidden_near, hidden_other, grad_near, grad_other),
+        (hidden, branch_near, branch_other, active_near, active_other),
     ):
-        got = contract(near[...], right[:half], 0, 0) + contract(other[...], right[half:], 0, 0)
+        got = contract(near[...], right_near[...], 0, 0) + contract(
+            other[...], right_other[...], 0, 0
+        )
         for at in range(count):
             out_ref[at, :, place : place + hidden] = jnp.concatenate(
                 [got[at * rows : (at + 1) * rows], got[(count + at) * rows :][:rows]], axis=0
             ).astype(LOW)
+        half = pl.ds(place, hidden)
+        copy = pltpu.make_async_copy(
+            out_ref.at[:, :, half], out.at[:, :, half], sems.at[place // hidden]
+        )
+        copy.start()
+        copies.append(copy)
+    for copy in copies:
+        copy.wait()
 
 
 def first_norm_backward_kernel(
     second_ref,
     chip_ref,
     far_ref,
-    normed_ref,
+    first_ref,
     scale_ref,
     rows_ref,
     second_sums_ref,
@@ -559,10 +594,14 @@
 ):
     own = grad_ref.shape[0]
     sums = [jnp.zeros((1, second_ref.shape[1]), FULL) for _ in range(3)]
-    for at, to in blocks_of(second_ref.shape[0]):
-        upstream = second_ref[at:to] + (chip_ref[at:to] + far_ref[at:to].astype(FULL))
-        normed = normed_ref[at:to]
-        grad = norm_backward(upstream, normed, scale_ref[at:to, :1], rows_ref[4:5])
+    inverse = 1.0 / rows_ref[4:5]
+    for at, to in blocks_of(second_ref.shape[0], TILE):
+        upstream = second_ref[at:to].astype(FULL) + (
+            chip_ref[at:to] + far_ref[at:to].astype(FULL)
+        )
+        normed = (first_ref[at:to].astype(FULL) - rows_ref[5:6]) * inverse
+        scale_inv = jnp.transpose(jnp.broadcast_to(scale_ref[:1, at:to], (TILE, TILE)))[:, :1]
+        grad = norm_backward(upstream, normed, scale_inv, rows_ref[4:5])
         low = grad.astype(LOW)
         low_ref[at:to] = low
         if to <= own:
@@ -590,7 +629,7 @@
         total += blocks_ref[at].astype(FULL)
     lower = index_ref[0] == 0
     keep_ref[...] = jnp.where(lower, total[:rows], total[rows:])
-    send_ref[...] = jnp.where(lower, total[rows:], total[:rows])
+    send_ref[...] = jnp.where(lower, total[rows:], total[:rows]).astype(send_ref.dtype)
 
 
 def last_sum_kernel(index_ref, blocks_ref, q_ref, k_ref, v_ref, out_ref, vector_ref):
@@ -657,9 +696,11 @@
 
     vector_rows = q_bias.shape[0]
     line_size = -(-12 * vector_rows // TILE) * TILE
+    first_own = jnp.concatenate([q_weight, k_weight, v_weight, out_weight], axis=1)
+    second_own = jnp.concatenate([up_weight, down_weight], axis=1)
     line = jnp.concatenate(
         [
-            q_bias,
+            after(q_bias, first_own, second_own),
             v_bias,
             out_bias,
             down_bias,
@@ -673,23 +714,21 @@
     )[None]
     lines = [line] + [swap(line, mask) for mask in (1, 2, 3)]
     tokens_far = swap(tokens, 2)
-    second_own = jnp.concatenate([up_weight, down_weight], axis=1)
     second_side = side(second_own)
+    first_own, tokens_far, second_side = lax.optimization_barrier(
+        (first_own, tokens_far, second_side)
+    )
     (first_block,) = call(
         first_block_kernel,
         [((dp_count, shard_rows, 3 * GROUP + TILE), LOW)],
         index,
         *lines,
-        q_weight,
-        k_weight,
-        v_weight,
-        out_weight,
+        first_own,
         smem=1,
     )
     first_full = spread(first_block).reshape(width, -1)
     tokens_pair = jnp.concatenate([tokens, tokens_far], axis=0)
     tokens_core = swap(tokens_pair, 1)
-    cotangent_far = swap(after(cotangent, tokens_far), 2)
     segment_row = ordered_segments(segments[0], my_index)[None]
     (second_block,) = call(
         second_block_kernel,
@@ -699,8 +738,8 @@
         second_side,
         smem=1,
     )
-    first_full, second_block, tokens_core, cotangent_far, segment_row = lax.optimization_barrier(
-        (first_full, second_block, tokens_core, cotangent_far, segment_row)
+    first_full, second_block, tokens_core, segment_row = lax.optimization_barrier(
+        (first_full, second_block, tokens_core, segment_row)
     )
     second_full = plane(second_block)
 
@@ -721,60 +760,67 @@
         first_full,
         segment_row,
         smem=1,
+        scratch=[pltpu.VMEM((length, 3 * GROUP), LOW), pltpu.SemaphoreType.DMA],
+        away=(0,),
     )
     attn_chip = attn_keep + swap(attn_send, 1).astype(FULL)
-    first, hidden_low, normed_first, inv_first = call(
+    attn_far = swap(far_pack(attn_chip), 2)
+    cotangent_far = swap(after(cotangent, attn_far), 2)
+    hidden_low, inv_first = call(
         first_norm_kernel,
-        [((half, width), FULL), ((half, width), LOW), ((half, width), FULL), ((half, TILE), FULL)],
+        [((half, width), LOW), ((8, half), FULL)],
         tokens_pair,
         attn_chip,
-        far_sum(attn_chip),
+        attn_far,
         rows,
     )
-    hidden_core = swap(hidden_low, 1)
-    active, slope, branch_keep, branch_send, up_full, down_full = call(
-        feed_kernel,
+    hidden_core = after(swap(hidden_low, 1), cotangent_far)
+    active_other, slope_other, branch_send, up_full, down_full = call(
+        feed_other_kernel,
         [
-            ((length, hidden_cols), LOW),
-            ((length, hidden_cols), FULL),
-            ((half, width), FULL),
+            ((half, hidden_cols), LOW),
+            ((half, hidden_cols), FULL),
             ((half, width), LOW),
             ((width, hidden_cols), LOW),
             ((width, hidden_cols), LOW),
         ],
-        hidden_low,
         hidden_core,
         second_full,
         bias_up,
     )
-    branch_chip = branch_keep + swap(branch_send, 1).astype(FULL)
-    layer_output, second_grad, branch_low, second_sums = call(
+    branch_got = swap(branch_send, 1)
+    active_near, slope_near, branch_keep = call(
+        feed_near_kernel,
+        [((half, hidden_cols), LOW), ((half, hidden_cols), FULL), ((half, width), FULL)],
+        hidden_low,
+        up_full,
+        down_full,
+        bias_up,
+    )
+    branch_chip = branch_keep + branch_got.astype(FULL)
+    layer_output, branch_low, second_sums = call(
         second_norm_kernel,
-        [((local_len, width), LOW), ((half, width), FULL), ((half, width), LOW), ((8, width), FULL)],
-        first,
+        [((local_len, width), LOW), ((half, width), LOW), ((8, width), FULL)],
+        hidden_low,
         branch_chip,
-        far_sum(branch_chip),
+        swap(far_pack(branch_chip), 2),
         rows,
         cotangent,
         cotangent_far,
     )
     branch_core = swap(branch_low, 1)
-    upward_grad, hidden_keep, hidden_send, up_sum = call(
-        feed_backward_kernel,
-        [
-            ((length, hidden_cols), LOW),
-            ((half, width), FULL),
-            ((half, width), LOW),
-            ((1, hidden_cols), FULL),
-        ],
-        branch_low,
-        branch_core,
-        up_full,
-        down_full,
-        slope,
-    )
-    hidden_chip = hidden_keep + swap(hidden_send, 1).astype(FULL)
-    hidden_far = far_sum(hidden_chip)
+    grad_shapes = [((half, hidden_cols), LOW), ((half, width), LOW), ((1, hidden_cols), FULL)]
+    upward_other, hidden_send, up_sum_other = call(
+        feed_backward_kernel, grad_shapes, branch_core, up_full, down_full, slope_other
+    )
+    hidden_got = swap(hidden_send, 1)
+    grad_shapes[1] = ((half, width), FULL)
+    upward_near, hidden_keep, up_sum_near = call(
+        feed_backward_kernel, grad_shapes, branch_low, up_full, down_full, slope_near
+    )
+    hidden_chip = hidden_keep + hidden_got.astype(FULL)
+    hidden_sent = far_pack(hidden_chip)
+    hidden_far = swap(hidden_sent, 2)
     (pair_block,) = call(
         feed_weights_kernel,
         [((dp_count // 2, 2 * shard_rows, 2 * hidden_cols), LOW)],
@@ -782,17 +828,24 @@
         hidden_core,
         branch_low,
         branch_core,
-        active,
-        upward_grad,
-    )
-    pair_blocks = plane(after(pair_block, hidden_chip))
+        active_near,
+        active_other,
+        upward_near,
+        upward_other,
+        scratch=[
+            pltpu.VMEM((dp_count // 2, 2 * shard_rows, 2 * hidden_cols), LOW),
+            pltpu.SemaphoreType.DMA((2,)),
+        ],
+        away=(0,),
+    )
+    pair_blocks = plane(pair_block)
     resid_grad, attended_low, given = call(
         first_norm_backward_kernel,
         [((local_len, width), FULL), ((half, width), LOW), ((8, width), FULL)],
-        second_grad,
+        branch_low,
         hidden_chip,
         hidden_far,
-        normed_first,
+        hidden_low,
         inv_first,
         rows,
         second_sums,
@@ -814,7 +867,8 @@
         first_full,
         segment_row,
         given,
-        up_sum,
+        up_sum_near,
+        up_sum_other,
         smem=1,
         scratch=[
             pltpu.VMEM((length, GROUP), LOW),
@@ -823,8 +877,10 @@
             pltpu.VMEM((width, TILE), FULL),
         ],
     )
+    input_chip = input_keep + swap(input_send, 1).astype(FULL)
+    input_sent = input_chip[local_len:].astype(LOW)
+    input_far = swap(input_sent, 2)
     vector_near = [swap(vector_sums, mask) for mask in (1, 2, 3)]
-    input_got = swap(input_send, 1)
     (last_block,) = call(
         weights_kernel,
         [((width, 3 * GROUP + TILE), LOW)],
@@ -834,27 +890,32 @@
         attended_core,
         qkv_grad,
         mixed_rows,
-    )
-    vector_sums = vector_sums + vector_near[0] + vector_near[1] + vector_near[2]
-    high, low = halves(vector_sums[:12].T)
-    last_block = lax.dynamic_update_slice(
-        last_block, jnp.concatenate([high, low], axis=1), (0, 3 * GROUP)
-    )
-    input_chip = input_keep + input_got.astype(FULL)
-    input_far = swap(input_chip[local_len:].astype(LOW), 2)
-    last_blocks = spread(
-        after(last_block, input_chip).reshape(dp_count, shard_rows, 3 * GROUP + TILE)
-    )
+        scratch=[pltpu.VMEM((width, 3 * GROUP), LOW), pltpu.SemaphoreType.DMA],
+        away=(0,),
+    )
+    (last_block,) = call(
+        vectors_kernel,
+        [((width, 3 * GROUP + TILE), LOW)],
+        last_block,
+        vector_sums,
+        *vector_near,
+        scratch=[pltpu.VMEM((width, TILE), LOW), pltpu.SemaphoreType.DMA],
+        away=(0,),
+        far=(0,),
+        aliases={0: 0},
+    )
+    last_block = after(last_block, input_far)
+    last_blocks = spread(last_block.reshape(dp_count, shard_rows, 3 * GROUP + TILE))
     input_grad = resid_grad + (input_chip[:local_len] + input_far.astype(FULL))
 
     pair_keep, pair_send = call(
         plane_sum_kernel,
-        [((shard_rows, 2 * hidden_cols), FULL)] * 2,
+        [((shard_rows, 2 * hidden_cols), FULL), ((shard_rows, 2 * hidden_cols), LOW)],
         side_index,
         pair_blocks,
         smem=1,
     )
-    pair_sum = pair_keep + side(pair_send)
+    pair_sum = pair_keep + side(pair_send).astype(FULL)
     q_grad, k_grad, v_grad, out_grad, line = call(
         last_sum_kernel,
         [((shard_rows, head_cols), FULL)] * 4 + [((1, line_size), FULL)],

time: 196 us -> 178 us (0.908)
  waiting for transfers between devices: 101 us -> 82.1 us
  local copies, waits for them, and re-layouts: 15 us -> 8.62 us
  starting transfers between devices: 49.7 us -> 55.1 us
  other arithmetic: 2.34 us -> 4.3 us
    ppermute x20, waiting for transfers between devices: 87.4 us -> 45.8 us  [swap(): return lax.ppermute(values, 'tensor', [(i, i ^ mask) for i in range(4)])]
    all_to_all x2, waiting for transfers between devices: 0.01 us -> 19.7 us  [spread(): return lax.all_to_all(stacked, 'dp', 0, 0, tiled=True)]
    ppermute x2, waiting for transfers between devices: 0.01 us -> 12 us  [side(): return lax.ppermute(values, 'dp', pairs)]
    all_to_all x2, waiting for transfers between devices: 14.1 us -> 4.61 us  [plane(): lax.all_to_all(stacked, 'dp', 0, 0, tiled=True, axis_index_groups=plane_g...]
    ppermute x20, starting transfers between devices: 19.5 us -> 27.6 us  [swap(): return lax.ppermute(values, 'tensor', [(i, i ^ mask) for i in range(4)])]
    unnamed x47 -> x35, local copies, waits for them, and re-layouts: 8.14 us -> 3.9 us
    dynamic_update_slice x1 -> x0, local copies, waits for them, and re-layouts: 2.7 us -> none  [shards(): lax.dynamic_update_slice(last_block, jnp.concatenate([high, low], axis=1)...]
    all_to_all x2, starting transfers between devices: 11.4 us -> 8.9 us  [plane(): lax.all_to_all(stacked, 'dp', 0, 0, tiled=True, axis_index_groups=plane_g...]
  transfers between devices with their start and end apart: 26 -> 26, of which waited for: 17 -> 17; matrix products, arithmetic and copies ran while one was open for 4% -> 5% of each run, Pallas kernels for 7% -> 10%
where the time goes in v5:
time: 178 us
  waiting for transfers between devices  82.1 us (46%)
  starting transfers between devices  55.1 us (31%)
  Pallas kernels  26.4 us (15%)
  local copies, waits for them, and re-layouts  8.62 us (5%)
  other arithmetic  4.3 us (2%)
    ppermute x20, waiting for transfers between devices, swap(): return lax.ppermute(values, 'tensor', [(i, i ^ mask) for i in range(4)])  45.8 us
    ppermute x20, starting transfers between devices, swap(): return lax.ppermute(values, 'tensor', [(i, i ^ mask) for i in range(4)])  27.6 us
    pallas_call x16, Pallas kernels, call(): pl.pallas_call(body, out_shape=[pltpu.HBM(shape, kind) if i in away else...  26.4 us
    all_to_all x2, waiting for transfers between devices, spread(): return lax.all_to_all(stacked, 'dp', 0, 0, tiled=True)  19.7 us
    all_to_all x2, starting transfers between devices, spread(): return lax.all_to_all(stacked, 'dp', 0, 0, tiled=True)  16 us
    ppermute x2, waiting for transfers between devices, side(): return lax.ppermute(values, 'dp', pairs)  12 us
    all_to_all x2, starting transfers between devices, plane(): lax.all_to_all(stacked, 'dp', 0, 0, tiled=True, axis_index_groups=plane_g...  8.9 us
    all_to_all x2, waiting for transfers between devices, plane(): lax.all_to_all(stacked, 'dp', 0, 0, tiled=True, axis_index_groups=plane_g...  4.61 us
  transfers between devices with their start and end apart: 26, of which 17 were waited for; matrix products, arithmetic and copies ran while one was open for 5% of the time, Pallas kernels for 10%

profile of v5, /device:TPU:0, one launch (start us, length us, event | category | flops | bytes accessed | tf_op | source)
XLA Modules:
  0.0 177.5 jit_solution(7338326785729724587)
XLA Ops:
  0.7 3.4 %collective-permute-start = (bf16[128,768]{1,0:T(8,128)(2,1)}, bf16[128,768]{1,0:T(8,128)(2,1)S(1)}, u32[]{:S(2)}, u32[]{:S(2)}) collective-permute-start(bf16[128,768]{1,0:T(8,128)(2,1)} %bitcast.49), channel_id=1, source_target_pairs={{0,2},{1,3},{2,0},{3,1},{4,6},{5,7},{6,4},{7,5},{8,10},{9,11},{10,... | collective-permute-start | bytes 589832 | tf_op jit(solution)/shard_map/ppermute | solution.py:31
  6.2 0.8 pad_maximum_fusion.4.weight_ref
  7.1 0.9 concatenate.27
  8.7 1.7 collective-permute-start.3
  10.4 1.0 collective-permute-start.2
  11.4 1.1 collective-permute-done.4.both_ref
  12.5 1.3 collective-permute-done.3.far_ref
  13.8 1.3 shard_map.323
  15.0 8.5 %all-to-all-start = ((bf16[32,24,896]{2,1,0:T(8,128)(2,1)}), bf16[32,24,896]{2,1,0:T(8,128)(2,1)S(1)}, u32[]{:S(2)}, u32[]{:S(2)}) async-start(bf16[32,24,896]{2,1,0:T(8,128)(2,1)} %shard_map.323), calls=%async_computation | async-start | bytes 2752512 | tf_op jit(solution)/shard_map/all_to_all | solution.py:39
  25.1 1.4 copy-done
  26.6 17.7 %all-to-all-done = bf16[32,24,896]{2,1,0:T(8,128)(2,1)S(1)} async-done(((bf16[32,24,896]{2,1,0:T(8,128)(2,1)}), bf16[32,24,896]{2,1,0:T(8,128)(2,1)S(1)}, u32[]{:S(2)}, u32[]{:S(2)}) %all-to-all-start) | async-done | bytes 1376288 | tf_op jit(solution)/shard_map/all_to_all | solution.py:39
  44.2 4.4 %all-to-all-start.1 = ((bf16[16,48,1536]{2,1,0:T(8,128)(2,1)}), bf16[16,48,1536]{2,1,0:T(8,128)(2,1)}, u32[]{:S(2)}, u32[]{:S(2)}) async-start(bf16[16,48,1536]{2,1,0:T(8,128)(2,1)} %copy-done), calls=%async_computation.1 | async-start | bytes 4718592 | tf_op jit(solution)/shard_map/all_to_all | solution.py:48
  48.7 2.8 %shard_map.325 = (bf16[512,768]{1,0:T(8,128)(2,1)}, bf16[512,256]{1,0:T(8,128)(2,1)S(1)}, f32[8,512]{1,0:T(8,128)S(1)}, bf16[256,768]{1,0:T(8,128)(2,1)S(1)}, f3...) custom-call(s32[1]{0:T(128)} %bitcast.1.index_ref, ...), custom_call_target="tpu_custom_call" | custom-call | flops 1000 | bytes 1000 | tf_op jit(solution)/shard_map/pallas_call | solution.py:83
  51.6 1.7 collective-permute-done.6
  53.5 3.1 %collective-permute-start.7 = (bf16[256,768]{1,0:T(8,128)(2,1)S(1)}, bf16[256,768]{1,0:T(8,128)(2,1)S(1)}, u32[]{:S(2)}, u32[]{:S(2)}) collective-permute-start(bf16[256,768]{1,0:T(8,128)(2,1)S(1)} %pad_maximum_fusion.1), channel_id=1, source_target_pairs={{0,2},{1,3},{2,0},{3,1},{4,6},{5,7},{6,4},{7,5},{8,10},{9,11},{10,... | collective-permute-start | bytes 1179656 | tf_op jit(solution)/shard_map/ppermute | solution.py:31
  56.6 9.6 %collective-permute-done.7.far_ref = bf16[256,768]{1,0:T(8,128)(2,1)S(1)} collective-permute-done((bf16[256,768]{1,0:T(8,128)(2,1)S(1)}, bf16[256,768]{1,0:T(8,128)(2,1)S(1)}, u32[]{:S(2)}, u32[]{:S(2)}) %collective-permute-start.7) | collective-permute-done | bytes 393248 | tf_op jit(solution)/shard_map/ppermute | solution.py:31
  66.7 3.1 %collective-permute-start.9 = (bf16[128,768]{1,0:T(8,128)(2,1)S(1)}, bf16[128,768]{1,0:T(8,128)(2,1)S(1)}, u32[]{:S(2)}, u32[]{:S(2)}) collective-permute-start(bf16[128,768]{1,0:T(8,128)(2,1)S(1)} %bitcast.40), channel_id=1, source_target_pairs={{0,2},{1,3},{2,0},{3,1},{4,6},{5,7},{6,4},{7,5},{8,10},{9,11},{10,... | collective-permute-start | bytes 589832 | tf_op jit(solution)/shard_map/ppermute | solution.py:31
  69.8 5.7 %collective-permute-done.9.cotangent_far_ref = bf16[128,768]{1,0:T(8,128)(2,1)S(1)} collective-permute-done((bf16[128,768]{1,0:T(8,128)(2,1)S(1)}, bf16[128,768]{1,0:T(8,128)(2,1)S(1)}, u32[]{:S(2)}, u32[]{:S(2)}) %collective-permute-start.9) | collective-permute-done | bytes 196640 | tf_op jit(solution)/shard_map/ppermute | solution.py:31
  75.5 4.6 %all-to-all-done.1.blocks_ref = bf16[16,48,1536]{2,1,0:T(8,128)(2,1)} async-done(((bf16[16,48,1536]{2,1,0:T(8,128)(2,1)}), bf16[16,48,1536]{2,1,0:T(8,128)(2,1)}, u32[]{:S(2)}, u32[]{:S(2)}) %all-to-all-start.1) | async-done | bytes 2359328 | tf_op jit(solution)/shard_map/all_to_all | solution.py:48
  80.2 3.1 %shard_map.327 = (bf16[256,768]{1,0:T(8,128)(2,1)S(1)}, f32[256,768]{1,0:T(8,128)S(1)}, bf16[256,768]{1,0:T(8,128)(2,1)S(1)}, bf16[768,768]{1,0:T(8,128)(2,1)S(1)}, bf16[768,768]{1,0:T(8,128)(2,1)S(1)}) custom-call(bf16[256,768]{1,0:T(8,128)(2,1)S(1)} %collective-permute-done.8.rows_ref.hidden_other, bf16[16,48,1536]{2,1,0:T(8,128)(2,1)} %all-to-all-done.1.blocks_ref, ...), custom_call_target="tpu_custom_call" | custom-call | flops 1000 | bytes 1000 | tf_op jit(solution)/shard_map/pallas_call | solution.py:83
  83.3 1.4 shard_map.328
  85.2 4.0 %collective-permute-start.11 = (bf16[256,768]{1,0:T(8,128)(2,1)S(1)}, bf16[256,768]{1,0:T(8,128)(2,1)S(1)}, u32[]{:S(2)}, u32[]{:S(2)}) collective-permute-start(bf16[256,768]{1,0:T(8,128)(2,1)S(1)} %pad_maximum_fusion.2), channel_id=1, source_target_pairs={{0,2},{1,3},{2,0},{3,1},{4,6},{5,7},{6,4},{7,5},{8,10},{9,11},{10,... | collective-permute-start | bytes 1179656 | tf_op jit(solution)/shard_map/ppermute | solution.py:31
  89.2 9.4 %collective-permute-done.11.far_ref = bf16[256,768]{1,0:T(8,128)(2,1)S(1)} collective-permute-done((bf16[256,768]{1,0:T(8,128)(2,1)S(1)}, bf16[256,768]{1,0:T(8,128)(2,1)S(1)}, u32[]{:S(2)}, u32[]{:S(2)}) %collective-permute-start.11) | collective-permute-done | bytes 393248 | tf_op jit(solution)/shard_map/ppermute | solution.py:31
  98.6 1.2 shard_map.329
  99.8 1.7 collective-permute-done.12.rows_ref.branch_other
  101.5 2.0 %shard_map.331 = (bf16[256,768]{1,0:T(8,128)(2,1)S(1)}, bf16[256,768]{1,0:T(8,128)(2,1)}, f32[1,768]{1,0:T(1,128)S(1)}) custom-call(bf16[256,768]{1,0:T(8,128)(2,1)S(1)} %collective-permute-done.12.rows_ref.branch_other, bf16[768,768]{1,0:T(8,128)(2,1)S(1)} %get-tuple-element.83.up_ref, bf16[768,768]{1,0:T(8,128)(2,1)S(1)} %get-tuple-element.84.down_ref, ...), custom_call_target="tpu_custom_call" | custom-call | flops 1000 | bytes 1000 | tf_op jit(solution)/shard_map/pallas_call | solution.py:83
  103.7 1.2 shard_map.330
  104.9 0.9 copy-done.2
  105.8 2.5 %shard_map.337 = bf16[16,48,1536]{2,1,0:T(8,128)(2,1)} custom-call(bf16[256,768]{1,0:T(8,128)(2,1)S(1)} %get-tuple-element.78.rows_ref.first_ref.hidden_near, bf16[256,768]{1,0:T(8,128)(2,1)S(1)} %collective-permute-done.8.rows_ref.hidden_other, bf16[256,768]{1,0:T(8,128)(2,1)S(1)} %get-tuple-element.88.rows_ref.second_ref.branch_near, ...), custom_call_target="tpu_custom_call" | custom-call | flops 1000 | bytes 1000 | tf_op jit(solution)/shard_map/pallas_call | solution.py:83
  108.4 4.5 %all-to-all-start.3 = ((bf16[16,48,1536]{2,1,0:T(8,128)(2,1)}), bf16[16,48,1536]{2,1,0:T(8,128)(2,1)}, u32[]{:S(2)}, u32[]{:S(2)}) async-start(bf16[16,48,1536]{2,1,0:T(8,128)(2,1)} %shard_map.337), calls=%async_computation.3 | async-start | bytes 4718592 | tf_op jit(solution)/shard_map/all_to_all | solution.py:48
  112.8 1.3 fusion.2
  114.3 3.3 %collective-permute-start.14 = (bf16[256,768]{1,0:T(8,128)(2,1)S(1)}, bf16[256,768]{1,0:T(8,128)(2,1)S(1)}, u32[]{:S(2)}, u32[]{:S(2)}) collective-permute-start(bf16[256,768]{1,0:T(8,128)(2,1)S(1)} %pad_maximum_fusion.3), channel_id=1, source_target_pairs={{0,2},{1,3},{2,0},{3,1},{4,6},{5,7},{6,4},{7,5},{8,10},{9,11},{10,... | collective-permute-start | bytes 1179656 | tf_op jit(solution)/shard_map/ppermute | solution.py:31
  117.6 9.6 %collective-permute-done.14.far_ref = bf16[256,768]{1,0:T(8,128)(2,1)S(1)} collective-permute-done((bf16[256,768]{1,0:T(8,128)(2,1)S(1)}, bf16[256,768]{1,0:T(8,128)(2,1)S(1)}, u32[]{:S(2)}, u32[]{:S(2)}) %collective-permute-start.14) | collective-permute-done | bytes 393248 | tf_op jit(solution)/shard_map/ppermute | solution.py:31
  128.6 1.7 collective-permute-done.15.other_ref
  130.3 3.8 %shard_map.333 = (bf16[512,768]{1,0:T(8,128)(2,1)S(1)}, bf16[256,768]{1,0:T(8,128)(2,1)S(1)}, f32[256,768]{1,0:T(8,128)S(1)}, f32[16,768]{1,0:T(8,128)S(1)}) custom-call(s32[1]{0:T(128)} %bitcast.1.index_ref, bf16[256,768]{1,0:T(8,128)(2,1)S(1)} %get-tuple-element.96.near_ref, bf16[256,768]{1,0:T(8,128)(2,1)S(1)} %collective-permute-done.15.other_ref, ...), custom_call_target="tpu_custom_call" | custom-call | flops 1000 | bytes 1000 | tf_op jit(solution)/shard_map/pallas_call | solution.py:83
  134.3 1.6 collective-permute-done.16
  136.0 3.3 %collective-permute-start.17 = (bf16[128,768]{1,0:T(8,128)(2,1)S(1)}, bf16[128,768]{1,0:T(8,128)(2,1)}, u32[]{:S(2)}, u32[]{:S(2)}) collective-permute-start(bf16[128,768]{1,0:T(8,128)(2,1)S(1)} %slice.162), channel_id=1, source_target_pairs={{0,2},{1,3},{2,0},{3,1},{4,6},{5,7},{6,4},{7,5},{8,10},{9,11},{10,... | collective-permute-start | bytes 589832 | tf_op jit(solution)/shard_map/ppermute | solution.py:31
  139.3 3.0 %collective-permute-start.19 = (f32[16,768]{1,0:T(8,128)S(1)}, f32[16,768]{1,0:T(8,128)S(1)}, u32[]{:S(2)}, u32[]{:S(2)}) collective-permute-start(f32[16,768]{1,0:T(8,128)S(1)} %get-tuple-element.106.own_ref), channel_id=1, source_target_pairs={{0,2},{1,3},{2,0},{3,1},{4,6},{5,7},{6,4},{7,5},{8,10},{9,11},{10,... | collective-permute-start | bytes 147464 | tf_op jit(solution)/shard_map/ppermute | solution.py:31
  142.7 2.1 %shard_map.334.block_ref = bf16[768,896]{1,0:T(8,128)(2,1)} custom-call(bf16[256,768]{1,0:T(8,128)(2,1)S(1)} %pad_maximum_fusion.near_ref.tokens_ref.tokens_near, bf16[256,768]{1,0:T(8,128)(2,1)S(1)} %collective-permute-done.5.other_ref.tokens_other, bf16[256,768]{1,0:T(8,128)(2,1)S(1)} %get-tuple-element.96.near_ref, ...), custom_call_target="tpu_custom_call" | custom-call | flops 1000 | bytes 1000 | tf_op jit(solution)/shard_map/pallas_call | solution.py:83
  145.4 1.3 collective-permute-done.19.far_ref
  146.7 0.8 shard_map.335
  147.5 7.6 %all-to-all-start.2 = ((bf16[32,24,896]{2,1,0:T(8,128)(2,1)}), bf16[32,24,896]{2,1,0:T(8,128)(2,1)S(1)}, u32[]{:S(2)}, u32[]{:S(2)}) async-start(bf16[32,24,896]{2,1,0:T(8,128)(2,1)} %bitcast.48), calls=%async_computation.2 | async-start | bytes 2752512 | tf_op jit(solution)/shard_map/all_to_all | solution.py:39
  155.1 2.1 %shard_map.338 = (f32[24,1536]{1,0:T(8,128)S(1)}, bf16[24,1536]{1,0:T(8,128)(2,1)S(1)}) custom-call(s32[1]{0:T(128)} %bitcast.4.index_ref, bf16[16,48,1536]{2,1,0:T(8,128)(2,1)} %all-to-all-done.3.blocks_ref), custom_call_target="tpu_custom_call" | custom-call | flops 1000 | bytes 1000 | tf_op jit(solution)/shard_map/pallas_call | solution.py:83
  157.2 1.9 %collective-permute-start.21 = (bf16[24,1536]{1,0:T(8,128)(2,1)S(1)}, bf16[24,1536]{1,0:T(8,128)(2,1)S(1)}, u32[]{:S(2)}, u32[]{:S(2)}) collective-permute-start(bf16[24,1536]{1,0:T(8,128)(2,1)S(1)} %get-tuple-element.116), channel_id=1, source_target_pairs={{0,64},{4,68},{8,72},{12,76},{16,80},{20,84},{24,88},{28,92},{32,9... | collective-permute-start | bytes 221192 | tf_op jit(solution)/shard_map/ppermute | solution.py:54
  159.1 1.7 fusion.1
  160.8 12.0 %collective-permute-done.21 = bf16[24,1536]{1,0:T(8,128)(2,1)S(1)} collective-permute-done((bf16[24,1536]{1,0:T(8,128)(2,1)S(1)}, bf16[24,1536]{1,0:T(8,128)(2,1)S(1)}, u32[]{:S(2)}, u32[]{:S(2)}) %collective-permute-start.21) | collective-permute-done | bytes 73760 | tf_op jit(solution)/shard_map/ppermute | solution.py:54
  173.5 2.0 %all-to-all-done.2.blocks_ref = bf16[32,24,896]{2,1,0:T(8,128)(2,1)S(1)} async-done(((bf16[32,24,896]{2,1,0:T(8,128)(2,1)}), bf16[32,24,896]{2,1,0:T(8,128)(2,1)S(1)}, u32[]{:S(2)}, u32[]{:S(2)}) %all-to-all-start.2) | async-done | bytes 1376288 | tf_op jit(solution)/shard_map/all_to_all | solution.py:39
  175.5 0.9 shard_map.336
  (83 shorter events, 10.5 us)
Async XLA Ops:
  0.7 10.7 %collective-permute-start = (bf16[128,768]{1,0:T(8,128)(2,1)}, bf16[128,768]{1,0:T(8,128)(2,1)S(1)}, u32[]{:S(2)}, u32[]{:S(2)}) collective-permute-start(bf16[128,768]{1,0:T(8,128)(2,1)} %bitcast.49), channel_id=1, source_target_pairs={{0,2},{1,3},{2,0},{3,1},{4,6},{5,7},{6,4},{7,5},{8,10},{9,11},{10,... | collective-permute-start | bytes 589832 | tf_op jit(solution)/shard_map/ppermute | solution.py:31
  5.6 5.8 %collective-permute-start.1 = (bf16[24,1536]{1,0:T(8,128)(2,1)S(1)}, bf16[24,1536]{1,0:T(8,128)(2,1)S(1)}, u32[]{:S(2)}, u32[]{:S(2)}) collective-permute-start(bf16[24,1536]{1,0:T(8,128)(2,1)S(1)} %constant_dynamic-update-slice_fusion.own_ref), channel_id=1, source_target_pairs={{0,64},{4,68},{8,72},{12,76},{16,80},{20,84},{24,88},{28,92},{32,9... | collective-permute-start | bytes 221192 | tf_op jit(solution)/shard_map/ppermute | solution.py:54
  8.0 4.5 %collective-permute-start.4 = (f32[1,128]{1,0:T(1,128)S(1)}, f32[1,128]{1,0:T(1,128)S(1)}, u32[]{:S(2)}, u32[]{:S(2)}) collective-permute-start(f32[1,128]{1,0:T(1,128)S(1)} %bitcast.44), channel_id=1, source_target_pairs={{0,3},{1,2},{2,1},{3,0},{4,7},{5,6},{6,5},{7,4},{8,11},{9,10},{10,... | collective-permute-start | bytes 1544 | tf_op jit(solution)/shard_map/ppermute | solution.py:31
  8.7 5.0 %collective-permute-start.3 = (f32[1,128]{1,0:T(1,128)S(1)}, f32[1,128]{1,0:T(1,128)S(1)}, u32[]{:S(2)}, u32[]{:S(2)}) collective-permute-start(f32[1,128]{1,0:T(1,128)S(1)} %bitcast.45), channel_id=1, source_target_pairs={{0,2},{1,3},{2,0},{3,1},{4,6},{5,7},{6,4},{7,5},{8,10},{9,11},{10,... | collective-permute-start | bytes 1544 | tf_op jit(solution)/shard_map/ppermute | solution.py:31
  10.4 3.4 %collective-permute-start.2 = (f32[1,128]{1,0:T(1,128)S(1)}, f32[1,128]{1,0:T(1,128)S(1)}, u32[]{:S(2)}, u32[]{:S(2)}) collective-permute-start(f32[1,128]{1,0:T(1,128)S(1)} %bitcast.46), channel_id=1, source_target_pairs={{0,1},{1,0},{2,3},{3,2},{4,5},{5,4},{6,7},{7,6},{8,9},{9,8},{10,11... | collective-permute-start | bytes 1544 | tf_op jit(solution)/shard_map/ppermute | solution.py:31
  15.0 8.5 %copy-start.15 = (s32[4]{0:T(128)S(1)}, s32[4]{0:T(128)}, u32[]{:S(2)}) copy-start(s32[4]{0:T(128)} %constant.82) | copy-start | bytes 52
  15.0 8.5 %copy-start.16 = (s32[4]{0:T(128)S(1)}, s32[4]{0:T(128)}, u32[]{:S(2)}) copy-start(s32[4]{0:T(128)} %constant.81) | copy-start | bytes 52
  15.0 8.5 %copy-start.14 = (s32[1,512]{1,0:T(1,128)S(1)}, s32[1,512]{1,0:T(1,128)}, u32[]{:S(2)}) copy-start(s32[1,512]{1,0:T(1,128)} %param.21) | copy-start | bytes 6148
  15.0 9.7 %copy-start.13 = (bf16[1,128,768]{2,1,0:T(8,128)(2,1)S(1)}, bf16[1,128,768]{2,1,0:T(8,128)(2,1)}, u32[]{:S(2)}) copy-start(bf16[1,128,768]{2,1,0:T(8,128)(2,1)} %param.20) | copy-start | bytes 589828
  15.0 29.2 %all-to-all-start = ((bf16[32,24,896]{2,1,0:T(8,128)(2,1)}), bf16[32,24,896]{2,1,0:T(8,128)(2,1)S(1)}, u32[]{:S(2)}, u32[]{:S(2)}) async-start(bf16[32,24,896]{2,1,0:T(8,128)(2,1)} %shard_map.323), calls=%async_computation | async-start | bytes 2752512 | tf_op jit(solution)/shard_map/all_to_all | solution.py:39
  24.8 1.8 %collective-permute-start.5 = (bf16[256,768]{1,0:T(8,128)(2,1)S(1)}, bf16[256,768]{1,0:T(8,128)(2,1)S(1)}, u32[]{:S(2)}, u32[]{:S(2)}) collective-permute-start(bf16[256,768]{1,0:T(8,128)(2,1)S(1)} %pad_maximum_fusion.near_ref.tokens_ref.tokens_near), channel_id=1, source_target_pairs={{0,1},{1,0},{2,3},{3,2},{4,5},{5,4},{6,7},{7,6},{8,9},{9,8},{10,11... | collective-permute-start | bytes 1179656 | tf_op jit(solution)/shard_map/ppermute | solution.py:31
  25.1 1.4 copy-start
  44.2 35.9 %all-to-all-start.1 = ((bf16[16,48,1536]{2,1,0:T(8,128)(2,1)}), bf16[16,48,1536]{2,1,0:T(8,128)(2,1)}, u32[]{:S(2)}, u32[]{:S(2)}) async-start(bf16[16,48,1536]{2,1,0:T(8,128)(2,1)} %copy-done), calls=%async_computation.1 | async-start | bytes 4718592 | tf_op jit(solution)/shard_map/all_to_all | solution.py:48
  51.5 1.9 %copy-start.5 = (bf16[512,256]{1,0:T(8,128)(2,1)}, bf16[512,256]{1,0:T(8,128)(2,1)S(1)}, u32[]{:S(2)}) copy-start(bf16[512,256]{1,0:T(8,128)(2,1)S(1)} %get-tuple-element.105.mixed_ref) | copy-start | bytes 786436
  51.5 1.8 %collective-permute-start.6 = (bf16[256,768]{1,0:T(8,128)(2,1)S(1)}, bf16[256,768]{1,0:T(8,128)(2,1)S(1)}, u32[]{:S(2)}, u32[]{:S(2)}) collective-permute-start(bf16[256,768]{1,0:T(8,128)(2,1)S(1)} %get-tuple-element.76), channel_id=1, source_target_pairs={{0,1},{1,0},{2,3},{3,2},{4,5},{5,4},{6,7},{7,6},{8,9},{9,8},{10,11... | collective-permute-start | bytes 1179656 | tf_op jit(solution)/shard_map/ppermute | solution.py:31
  53.5 13.3 %copy-start.7 = (bf16[1,128,768]{2,1,0:T(8,128)(2,1)S(1)}, bf16[1,128,768]{2,1,0:T(8,128)(2,1)}, u32[]{:S(2)}) copy-start(bf16[1,128,768]{2,1,0:T(8,128)(2,1)} %param.37) | copy-start | bytes 589828
  53.5 12.7 %collective-permute-start.7 = (bf16[256,768]{1,0:T(8,128)(2,1)S(1)}, bf16[256,768]{1,0:T(8,128)(2,1)S(1)}, u32[]{:S(2)}, u32[]{:S(2)}) collective-permute-start(bf16[256,768]{1,0:T(8,128)(2,1)S(1)} %pad_maximum_fusion.1), channel_id=1, source_target_pairs={{0,2},{1,3},{2,0},{3,1},{4,6},{5,7},{6,4},{7,5},{8,10},{9,11},{10,... | collective-permute-start | bytes 1179656 | tf_op jit(solution)/shard_map/ppermute | solution.py:31
  66.6 8.9 %collective-permute-start.8 = (bf16[256,768]{1,0:T(8,128)(2,1)S(1)}, bf16[256,768]{1,0:T(8,128)(2,1)S(1)}, u32[]{:S(2)}, u32[]{:S(2)}) collective-permute-start(bf16[256,768]{1,0:T(8,128)(2,1)S(1)} %get-tuple-element.78.rows_ref.first_ref.hidden_near), channel_id=1, source_target_pairs={{0,1},{1,0},{2,3},{3,2},{4,5},{5,4},{6,7},{7,6},{8,9},{9,8},{10,11... | collective-permute-start | bytes 1179656 | tf_op jit(solution)/shard_map/ppermute | solution.py:31
  66.7 8.8 %collective-permute-start.9 = (bf16[128,768]{1,0:T(8,128)(2,1)S(1)}, bf16[128,768]{1,0:T(8,128)(2,1)S(1)}, u32[]{:S(2)}, u32[]{:S(2)}) collective-permute-start(bf16[128,768]{1,0:T(8,128)(2,1)S(1)} %bitcast.40), channel_id=1, source_target_pairs={{0,2},{1,3},{2,0},{3,1},{4,6},{5,7},{6,4},{7,5},{8,10},{9,11},{10,... | collective-permute-start | bytes 589832 | tf_op jit(solution)/shard_map/ppermute | solution.py:31
  75.5 7.7 %copy-start.9 = (bf16[128,768]{1,0:T(8,128)(2,1)}, bf16[128,768]{1,0:T(8,128)(2,1)S(1)}, u32[]{:S(2)}) copy-start(bf16[128,768]{1,0:T(8,128)(2,1)S(1)} %collective-permute-done.9.cotangent_far_ref) | copy-start | bytes 589828
  83.3 1.8 %collective-permute-start.10 = (bf16[256,768]{1,0:T(8,128)(2,1)S(1)}, bf16[256,768]{1,0:T(8,128)(2,1)S(1)}, u32[]{:S(2)}, u32[]{:S(2)}) collective-permute-start(bf16[256,768]{1,0:T(8,128)(2,1)S(1)} %get-tuple-element.86), channel_id=1, source_target_pairs={{0,1},{1,0},{2,3},{3,2},{4,5},{5,4},{6,7},{7,6},{8,9},{9,8},{10,11... | collective-permute-start | bytes 1179656 | tf_op jit(solution)/shard_map/ppermute | solution.py:31
  85.1 13.5 %copy-start.8 = (bf16[1,128,768]{2,1,0:T(8,128)(2,1)S(1)}, bf16[1,128,768]{2,1,0:T(8,128)(2,1)}, u32[]{:S(2)}) copy-start(bf16[1,128,768]{2,1,0:T(8,128)(2,1)} %param.37) | copy-start | bytes 589828
  85.2 13.5 %copy-start.10 = (bf16[128,768]{1,0:T(8,128)(2,1)S(1)}, bf16[128,768]{1,0:T(8,128)(2,1)}, u32[]{:S(2)}) copy-start(bf16[128,768]{1,0:T(8,128)(2,1)} %copy-done.9) | copy-start | bytes 589828
  85.2 13.4 %collective-permute-start.11 = (bf16[256,768]{1,0:T(8,128)(2,1)S(1)}, bf16[256,768]{1,0:T(8,128)(2,1)S(1)}, u32[]{:S(2)}, u32[]{:S(2)}) collective-permute-start(bf16[256,768]{1,0:T(8,128)(2,1)S(1)} %pad_maximum_fusion.2), channel_id=1, source_target_pairs={{0,2},{1,3},{2,0},{3,1},{4,6},{5,7},{6,4},{7,5},{8,10},{9,11},{10,... | collective-permute-start | bytes 1179656 | tf_op jit(solution)/shard_map/ppermute | solution.py:31
  99.8 1.7 collective-permute-start.12
  103.5 9.3 %collective-permute-start.13 = (bf16[256,768]{1,0:T(8,128)(2,1)}, bf16[256,768]{1,0:T(8,128)(2,1)}, u32[]{:S(2)}, u32[]{:S(2)}) collective-permute-start(bf16[256,768]{1,0:T(8,128)(2,1)} %get-tuple-element.92), channel_id=1, source_target_pairs={{0,1},{1,0},{2,3},{3,2},{4,5},{5,4},{6,7},{7,6},{8,9},{9,8},{10,11... | collective-permute-start | bytes 1179656 | tf_op jit(solution)/shard_map/ppermute | solution.py:31
  104.9 0.9 copy-start.2
  108.4 39.2 %all-to-all-start.3 = ((bf16[16,48,1536]{2,1,0:T(8,128)(2,1)}), bf16[16,48,1536]{2,1,0:T(8,128)(2,1)}, u32[]{:S(2)}, u32[]{:S(2)}) async-start(bf16[16,48,1536]{2,1,0:T(8,128)(2,1)} %shard_map.337), calls=%async_computation.3 | async-start | bytes 4718592 | tf_op jit(solution)/shard_map/all_to_all | solution.py:48
  114.2 16.1 %copy-start.1 = (bf16[512,768]{1,0:T(8,128)(2,1)S(1)}, bf16[512,768]{1,0:T(8,128)(2,1)}, u32[]{:S(2)}) copy-start(bf16[512,768]{1,0:T(8,128)(2,1)} %get-tuple-element.97.qkv_ref) | copy-start | bytes 2359300
  114.3 13.0 %collective-permute-start.14 = (bf16[256,768]{1,0:T(8,128)(2,1)S(1)}, bf16[256,768]{1,0:T(8,128)(2,1)S(1)}, u32[]{:S(2)}, u32[]{:S(2)}) collective-permute-start(bf16[256,768]{1,0:T(8,128)(2,1)S(1)} %pad_maximum_fusion.3), channel_id=1, source_target_pairs={{0,2},{1,3},{2,0},{3,1},{4,6},{5,7},{6,4},{7,5},{8,10},{9,11},{10,... | collective-permute-start | bytes 1179656 | tf_op jit(solution)/shard_map/ppermute | solution.py:31
  127.8 0.7 copy-start.3
  128.6 1.7 collective-permute-start.15
  134.1 8.6 %copy-start.6 = (bf16[512,256]{1,0:T(8,128)(2,1)S(1)}, bf16[512,256]{1,0:T(8,128)(2,1)}, u32[]{:S(2)}) copy-start(bf16[512,256]{1,0:T(8,128)(2,1)} %copy-done.5) | copy-start | bytes 786436
  134.1 1.8 %collective-permute-start.16 = (bf16[256,768]{1,0:T(8,128)(2,1)S(1)}, bf16[256,768]{1,0:T(8,128)(2,1)S(1)}, u32[]{:S(2)}, u32[]{:S(2)}) collective-permute-start(bf16[256,768]{1,0:T(8,128)(2,1)S(1)} %get-tuple-element.103), channel_id=1, source_target_pairs={{0,1},{1,0},{2,3},{3,2},{4,5},{5,4},{6,7},{7,6},{8,9},{9,8},{10,11... | collective-permute-start | bytes 1179656 | tf_op jit(solution)/shard_map/ppermute | solution.py:31
  136.0 8.9 %copy-start.11 = (f32[256,768]{1,0:T(8,128)}, f32[256,768]{1,0:T(8,128)S(1)}, u32[]{:S(2)}) copy-start(f32[256,768]{1,0:T(8,128)S(1)} %convert_add_fusion) | copy-start | bytes 2359300
  136.0 11.5 %collective-permute-start.17 = (bf16[128,768]{1,0:T(8,128)(2,1)S(1)}, bf16[128,768]{1,0:T(8,128)(2,1)}, u32[]{:S(2)}, u32[]{:S(2)}) collective-permute-start(bf16[128,768]{1,0:T(8,128)(2,1)S(1)} %slice.162), channel_id=1, source_target_pairs={{0,2},{1,3},{2,0},{3,1},{4,6},{5,7},{6,4},{7,5},{8,10},{9,11},{10,... | collective-permute-start | bytes 589832 | tf_op jit(solution)/shard_map/ppermute | solution.py:31
  139.3 6.0 %collective-permute-start.20 = (f32[16,768]{1,0:T(8,128)S(1)}, f32[16,768]{1,0:T(8,128)S(1)}, u32[]{:S(2)}, u32[]{:S(2)}) collective-permute-start(f32[16,768]{1,0:T(8,128)S(1)} %get-tuple-element.106.own_ref), channel_id=1, source_target_pairs={{0,3},{1,2},{2,1},{3,0},{4,7},{5,6},{6,5},{7,4},{8,11},{9,10},{10,... | collective-permute-start | bytes 147464 | tf_op jit(solution)/shard_map/ppermute | solution.py:31
  139.3 7.3 %collective-permute-start.19 = (f32[16,768]{1,0:T(8,128)S(1)}, f32[16,768]{1,0:T(8,128)S(1)}, u32[]{:S(2)}, u32[]{:S(2)}) collective-permute-start(f32[16,768]{1,0:T(8,128)S(1)} %get-tuple-element.106.own_ref), channel_id=1, source_target_pairs={{0,2},{1,3},{2,0},{3,1},{4,6},{5,7},{6,4},{7,5},{8,10},{9,11},{10,... | collective-permute-start | bytes 147464 | tf_op jit(solution)/shard_map/ppermute | solution.py:31
  142.3 4.3 %collective-permute-start.18 = (f32[16,768]{1,0:T(8,128)S(1)}, f32[16,768]{1,0:T(8,128)S(1)}, u32[]{:S(2)}, u32[]{:S(2)}) collective-permute-start(f32[16,768]{1,0:T(8,128)S(1)} %get-tuple-element.106.own_ref), channel_id=1, source_target_pairs={{0,1},{1,0},{2,3},{3,2},{4,5},{5,4},{6,7},{7,6},{8,9},{9,8},{10,11... | collective-permute-start | bytes 147464 | tf_op jit(solution)/shard_map/ppermute | solution.py:31
  147.5 28.0 %all-to-all-start.2 = ((bf16[32,24,896]{2,1,0:T(8,128)(2,1)}), bf16[32,24,896]{2,1,0:T(8,128)(2,1)S(1)}, u32[]{:S(2)}, u32[]{:S(2)}) async-start(bf16[32,24,896]{2,1,0:T(8,128)(2,1)} %bitcast.48), calls=%async_computation.2 | async-start | bytes 2752512 | tf_op jit(solution)/shard_map/all_to_all | solution.py:39
  155.1 4.0 %copy-start.4 = (f32[128,768]{1,0:T(8,128)S(1)}, f32[128,768]{1,0:T(8,128)}, u32[]{:S(2)}) copy-start(f32[128,768]{1,0:T(8,128)} %copy-done.3) | copy-start | bytes 1179652
  155.1 4.0 %copy-start.12 = (f32[256,768]{1,0:T(8,128)S(1)}, f32[256,768]{1,0:T(8,128)}, u32[]{:S(2)}) copy-start(f32[256,768]{1,0:T(8,128)} %copy-done.11) | copy-start | bytes 2359300
  157.2 15.7 %collective-permute-start.21 = (bf16[24,1536]{1,0:T(8,128)(2,1)S(1)}, bf16[24,1536]{1,0:T(8,128)(2,1)S(1)}, u32[]{:S(2)}, u32[]{:S(2)}) collective-permute-start(bf16[24,1536]{1,0:T(8,128)(2,1)S(1)} %get-tuple-element.116), channel_id=1, source_target_pairs={{0,64},{4,68},{8,72},{12,76},{16,80},{20,84},{24,88},{28,92},{32,9... | collective-permute-start | bytes 221192 | tf_op jit(solution)/shard_map/ppermute | solution.py:54

commit v6 on v5

--- a/solution.py
+++ b/solution.py
@@ -140,12 +140,64 @@
     return jnp.where(lanes(shape) // 4 == lanes(shape, 0), 1.0, 0.0).astype(LOW)
 
 
+def unpack_lines(index, line_refs, vector_ref, columns, width):
+    devices, size = line_refs[0].shape[1:]
+    each = width // (4 * devices)
+    flipped = []
+    for part in range(2):
+        near = [ref[part].astype(FULL) for ref in line_refs]
+        ordered = []
+        for at in range(4):
+            row = near[3]
+            for mask in (2, 1, 0):
+                row = jnp.where((index ^ mask) == at, near[mask], row)
+            ordered.append(row)
+        flipped.append(jnp.transpose(jnp.concatenate(ordered, axis=0)).astype(LOW))
+
+    def spread_lines(place, valid):
+        shape = (4 * devices, place.shape[1])
+        row = lanes(shape, 0)
+        select = (row % devices == place // (4 * each)) & (
+            row // devices == place % (4 * each) // each
+        )
+        select = jnp.where(select & valid, 1.0, 0.0).astype(LOW)
+        return [jnp.dot(part, select, preferred_element_type=FULL) for part in flipped]
+
+    def vectors_at(place, valid):
+        line_at = lanes((size, place.shape[1]), 0)
+        keep = (line_at < 8 * each) & (line_at % each == place % each)
+        row = lanes((8, size), 0)
+        gather = jnp.where(lanes((8, size)) // each == row, 1.0, 0.0).astype(LOW)
+        total = jnp.zeros((8, place.shape[1]), FULL)
+        for part in spread_lines(place, valid):
+            part = jnp.where(keep, part, 0.0).astype(LOW)
+            total += jnp.dot(gather, part, preferred_element_type=FULL)
+        return total
+
+    place = lanes((1, width))
+    vector_ref[...] = vectors_at(place, place >= 0)
+    place = lanes((1, GROUP))
+    own = vectors_at(place + index * columns, place < columns)
+    bias = jnp.concatenate([own[0:1], jnp.zeros((1, GROUP), FULL), own[1:2]], axis=1)
+    place = lanes((1, 4 * columns)) + index * (4 * columns)
+    line_at = lanes((size, 4 * columns), 0)
+    keep = line_at == 8 * each + place % (4 * each)
+    up_bias = jnp.zeros((1, 4 * columns), FULL)
+    for part in spread_lines(place // 4, place >= 0):
+        up_bias += jnp.sum(jnp.where(keep, part, 0.0), axis=0, keepdims=True)
+    return (bias, up_bias)
+
+
 def forward_kernel(
     index_ref,
     near_ref,
     other_ref,
     weight_ref,
     segment_ref,
+    line_ref,
+    line_core_ref,
+    line_far_ref,
+    line_both_ref,
     qkv_out,
     mixed_ref,
     log_ref,
@@ -159,31 +211,11 @@
     index = index_ref[0]
     half = near_ref.shape[0]
     columns = 3 * HEAD_DIM
+    line_refs = (line_ref, line_core_ref, line_far_ref, line_both_ref)
     width = weight_ref.shape[0]
-    held = weight_ref[:, 3 * GROUP :].astype(FULL)
-    flat = jnp.transpose(held)
-    vector_ref[...] = flat[:8] + flat[12:20]
-    own = weight_ref[pl.ds(pl.multiple_of(index * columns, 64), columns), 3 * GROUP :].astype(FULL)
-    own = jnp.concatenate([own, jnp.zeros((GROUP - columns, TILE), FULL)], axis=0)
-    own = jnp.transpose(own)
-    expand = expand_matrix(columns)
-    wide = jnp.dot(own[:24, :].astype(LOW)[:, :GROUP], jnp.concatenate(
-        [expand, jnp.zeros((GROUP - columns, 4 * columns), LOW)], axis=0
-    ), preferred_element_type=FULL)
-    up_bias = jnp.zeros((1, 4 * columns), FULL)
-    place = lanes((1, 4 * columns)) % 4
-    for step in range(4):
-        row = wide[8 + step : 9 + step] + wide[20 + step : 21 + step]
-        up_bias = jnp.where(place == step, row, up_bias)
+    width = weight_ref.shape[0]
+    bias, up_bias = unpack_lines(index, line_refs, vector_ref, columns, width)
     up_bias_ref[...] = up_bias
-    bias = jnp.concatenate(
-        [
-            own[0:1] + own[12:13],
-            jnp.zeros((1, GROUP), FULL),
-            own[1:2] + own[13:14],
-        ],
-        axis=1,
-    )
     keep = lanes((1, 3 * GROUP)) % GROUP < columns
     for at, rows_ref in ((0, near_ref), (half, other_ref)):
         got = jnp.dot(rows_ref[...], weight_ref[:, : 3 * GROUP], preferred_element_type=FULL)
@@ -365,34 +397,17 @@
     return (row, jnp.where(place < many + 4 * vector_rows, column, 1000))
 
 
-def first_block_kernel(
-    index_ref, own_ref, core_ref, far_ref, both_ref, weight_ref, block_ref
-):
-    index = index_ref[0]
+def first_block_kernel(line_ref, weight_ref, block_ref):
     rows = weight_ref.shape[0]
     columns_each = weight_ref.shape[1] // 4
-    vector_rows = rows // 4
-    shape = (rows, own_ref.shape[1])
-    row_at = lanes(shape, 0)
-    near = [own_ref[...], core_ref[...], far_ref[...], both_ref[...]]
-    spread_rows = jnp.zeros(shape, FULL)
-    for at in range(4):
-        row = near[3]
-        for mask in (2, 1, 0):
-            row = jnp.where((index ^ mask) == at, near[mask], row)
-        spread_rows = jnp.where(row_at // vector_rows == at, row, spread_rows)
-    place_row, _ = place_of(vector_rows, shape, 1)
-    spread_rows = jnp.where(place_row == row_at % vector_rows, spread_rows, 0.0)
-    high = spread_rows.astype(LOW)
-    low = (spread_rows - high.astype(FULL)).astype(LOW)
-    shape = (shape[1], TILE)
-    _, place_column = place_of(vector_rows, shape, 0)
-    columns = lanes(shape)
-    first = jnp.where(place_column == columns, 1.0, 0.0).astype(LOW)
-    second = jnp.where(place_column + 12 == columns, 1.0, 0.0).astype(LOW)
-    packed = jnp.dot(high, first, preferred_element_type=FULL) + jnp.dot(
-        low, second, preferred_element_type=FULL
-    )
+    count = line_ref.shape[0]
+    row_at = lanes((rows, TILE), 0)
+    packed = jnp.zeros((rows, TILE), FULL)
+    for at in range(count):
+        line = line_ref[at : at + 1]
+        high = line.astype(LOW).astype(FULL)
+        packed = jnp.where(row_at == at, high, packed)
+        packed = jnp.where(row_at == count + at, line - high, packed)
     weight = weight_ref[...].astype(FULL)
     q_part, k_part, v_part, out = [
         weight[:, columns_each * i : columns_each * (i + 1)] for i in range(4)
@@ -466,7 +481,7 @@
             active_ref[at + low : at + high] = (part * gate).astype(LOW)
             slope_ref[at + low : at + high] = (
                 gate + part * jnp.exp(-0.5 * part * part) * INV_ROOT_TAU
-            )
+            ).astype(LOW)
         got = contract(active_ref[at:to], down[...], 1, 1)
         part_ref[at:to] = got.astype(part_ref.dtype)
 
@@ -534,7 +549,7 @@
         grad = jnp.dot(rows_ref[at:to], down_ref[...], preferred_element_type=FULL)
         for low, high in blocks_of(size, 32):
             place = slice(at + low, at + high)
-            part = (grad[low:high] * slope_ref[place]).astype(LOW)
+            part = (grad[low:high] * slope_ref[place].astype(FULL)).astype(LOW)
             grad_ref[place] = part
             total += jnp.sum(part.astype(FULL), axis=0, keepdims=True)
         got = contract(grad_ref[at:to], up_ref[...], 1, 1)
@@ -632,7 +647,7 @@
     send_ref[...] = jnp.where(lower, total[rows:], total[:rows]).astype(send_ref.dtype)
 
 
-def last_sum_kernel(index_ref, blocks_ref, q_ref, k_ref, v_ref, out_ref, vector_ref):
+def last_sum_kernel(index_ref, blocks_ref, q_ref, k_ref, v_ref, out_ref, *vector_refs):
     index = index_ref[0]
     rows = q_ref.shape[0]
     vector_rows = rows // 4
@@ -648,7 +663,7 @@
     )
     packed = total[:, 3 * GROUP :]
     packed = packed + pltpu.roll(packed, TILE - 12, 1)
-    wide = vector_ref.shape[1]
+    wide = -(-12 * vector_rows // TILE) * TILE
     _, place_column = place_of(vector_rows, (TILE, wide), 1)
     select = jnp.where(place_column == lanes((TILE, wide), 0), 1.0, 0.0).astype(LOW)
     line = jnp.zeros((rows, wide), FULL)
@@ -659,7 +674,11 @@
         line += jnp.dot(part, select, preferred_element_type=FULL)
     place_row, _ = place_of(vector_rows, (rows, wide), 1)
     keep = place_row + index * vector_rows == lanes((rows, wide), 0)
-    vector_ref[...] = jnp.sum(jnp.where(keep, line, 0.0), axis=0, keepdims=True)
+    line = jnp.sum(jnp.where(keep, line, 0.0), axis=0, keepdims=True)
+    for at, ref in enumerate(vector_refs):
+        size = ref.shape[1]
+        place = at * vector_rows
+        ref[...] = pltpu.roll(line, wide - place, 1)[:, :size] if place else line[:, :size]
 
 
 def shards(
@@ -696,11 +715,10 @@
 
     vector_rows = q_bias.shape[0]
     line_size = -(-12 * vector_rows // TILE) * TILE
-    first_own = jnp.concatenate([q_weight, k_weight, v_weight, out_weight], axis=1)
-    second_own = jnp.concatenate([up_weight, down_weight], axis=1)
+    line_count = line_size // TILE
     line = jnp.concatenate(
         [
-            after(q_bias, first_own, second_own),
+            q_bias,
             v_bias,
             out_bias,
             down_bias,
@@ -711,22 +729,18 @@
             up_bias,
             jnp.zeros((line_size - 12 * vector_rows,), FULL),
         ]
-    )[None]
-    lines = [line] + [swap(line, mask) for mask in (1, 2, 3)]
-    tokens_far = swap(tokens, 2)
-    second_side = side(second_own)
-    first_own, tokens_far, second_side = lax.optimization_barrier(
-        (first_own, tokens_far, second_side)
-    )
+    ).reshape(line_count, TILE)
+    first_own = jnp.concatenate([q_weight, k_weight, v_weight, out_weight], axis=1)
     (first_block,) = call(
         first_block_kernel,
         [((dp_count, shard_rows, 3 * GROUP + TILE), LOW)],
-        index,
-        *lines,
+        line,
         first_own,
-        smem=1,
-    )
-    first_full = spread(first_block).reshape(width, -1)
+    )
+    first_blocks = spread(first_block)
+    tokens_far = swap(tokens, 2)
+    second_own = jnp.concatenate([up_weight, down_weight], axis=1)
+    second_side = side(second_own)
     tokens_pair = jnp.concatenate([tokens, tokens_far], axis=0)
     tokens_core = swap(tokens_pair, 1)
     segment_row = ordered_segments(segments[0], my_index)[None]
@@ -738,9 +752,11 @@
         second_side,
         smem=1,
     )
-    first_full, second_block, tokens_core, segment_row = lax.optimization_barrier(
-        (first_full, second_block, tokens_core, segment_row)
-    )
+    first_blocks, second_block = lax.optimization_barrier((first_blocks, second_block))
+    first_full = first_blocks.reshape(width, -1)
+    lines = first_blocks[:, : 2 * line_count, 3 * GROUP :]
+    lines = lines.reshape(dp_count, 2, line_size).transpose(1, 0, 2)
+    lines = [lines] + [swap(lines, mask) for mask in (1, 2, 3)]
     second_full = plane(second_block)
 
     qkv_rows, mixed_rows, log_totals, attn_send, attn_keep, rows, bias_up = call(
@@ -759,19 +775,20 @@
         tokens_core,
         first_full,
         segment_row,
+        *lines,
         smem=1,
         scratch=[pltpu.VMEM((length, 3 * GROUP), LOW), pltpu.SemaphoreType.DMA],
         away=(0,),
     )
     attn_chip = attn_keep + swap(attn_send, 1).astype(FULL)
     attn_far = swap(far_pack(attn_chip), 2)
-    cotangent_far = swap(after(cotangent, attn_far), 2)
+    cotangent_far = swap(after(cotangent, attn_send), 2)
     hidden_low, inv_first = call(
         first_norm_kernel,
         [((half, width), LOW), ((8, half), FULL)],
         tokens_pair,
         attn_chip,
-        attn_far,
+        after(attn_far, cotangent_far),
         rows,
     )
     hidden_core = after(swap(hidden_low, 1), cotangent_far)
@@ -779,7 +796,7 @@
         feed_other_kernel,
         [
             ((half, hidden_cols), LOW),
-            ((half, hidden_cols), FULL),
+            ((half, hidden_cols), LOW),
             ((half, width), LOW),
             ((width, hidden_cols), LOW),
             ((width, hidden_cols), LOW),
@@ -791,7 +808,7 @@
     branch_got = swap(branch_send, 1)
     active_near, slope_near, branch_keep = call(
         feed_near_kernel,
-        [((half, hidden_cols), LOW), ((half, hidden_cols), FULL), ((half, width), FULL)],
+        [((half, hidden_cols), LOW), ((half, hidden_cols), LOW), ((half, width), FULL)],
         hidden_low,
         up_full,
         down_full,
@@ -809,15 +826,20 @@
         cotangent_far,
     )
     branch_core = swap(branch_low, 1)
-    grad_shapes = [((half, hidden_cols), LOW), ((half, width), LOW), ((1, hidden_cols), FULL)]
+    near_shapes = [((half, hidden_cols), LOW), ((half, width), FULL), ((1, hidden_cols), FULL)]
+    upward_near, hidden_keep, up_sum_near = call(
+        feed_backward_kernel, near_shapes, branch_low, up_full, down_full, slope_near
+    )
+    other_shapes = [near_shapes[0], ((half, width), LOW), near_shapes[2]]
     upward_other, hidden_send, up_sum_other = call(
-        feed_backward_kernel, grad_shapes, branch_core, up_full, down_full, slope_other
+        feed_backward_kernel,
+        other_shapes,
+        after(branch_core, upward_near),
+        up_full,
+        down_full,
+        slope_other,
     )
     hidden_got = swap(hidden_send, 1)
-    grad_shapes[1] = ((half, width), FULL)
-    upward_near, hidden_keep, up_sum_near = call(
-        feed_backward_kernel, grad_shapes, branch_low, up_full, down_full, slope_near
-    )
     hidden_chip = hidden_keep + hidden_got.astype(FULL)
     hidden_sent = far_pack(hidden_chip)
     hidden_far = swap(hidden_sent, 2)
@@ -916,15 +938,16 @@
         smem=1,
     )
     pair_sum = pair_keep + side(pair_send).astype(FULL)
-    q_grad, k_grad, v_grad, out_grad, line = call(
+    q_grad, k_grad, v_grad, out_grad, *vectors = call(
         last_sum_kernel,
-        [((shard_rows, head_cols), FULL)] * 4 + [((1, line_size), FULL)],
+        [((shard_rows, head_cols), FULL)] * 4
+        + [((1, vector_rows), FULL)] * 8
+        + [((1, 4 * vector_rows), FULL)],
         index,
         last_blocks,
         smem=1,
     )
-    line = line[0]
-    vectors = [line[vector_rows * i : vector_rows * (i + 1)] for i in range(8)]
+    vectors = [vector.reshape(-1) for vector in vectors]
     return (
         layer_output[None],
         input_grad[None],
@@ -937,7 +960,7 @@
         vectors[6],
         vectors[7],
         vectors[0],
-        line[8 * vector_rows : 12 * vector_rows],
+        vectors[8],
         vectors[1],
         vectors[2],
         vectors[3],

time: 178 us -> 173 us (0.972)
  starting transfers between devices: 55.1 us -> 50.1 us
  waiting for transfers between devices: 82.1 us -> 84.7 us
  local copies, waits for them, and re-layouts: 8.62 us -> 6.36 us
    all_to_all x2, waiting for transfers between devices: 19.7 us -> 1.86 us  [spread(): return lax.all_to_all(stacked, 'dp', 0, 0, tiled=True)]
    ppermute x2, waiting for transfers between devices: 12 us -> 26.5 us  [side(): return lax.ppermute(values, 'dp', pairs)]
    ppermute x20, starting transfers between devices: 27.6 us -> 16.5 us  [swap(): return lax.ppermute(values, 'tensor', [(i, i ^ mask) for i in range(4)])]
    ppermute x20, waiting for transfers between devices: 45.8 us -> 53.1 us  [swap(): return lax.ppermute(values, 'tensor', [(i, i ^ mask) for i in range(4)])]
    all_to_all x2, starting transfers between devices: 8.9 us -> 13.1 us  [plane(): lax.all_to_all(stacked, 'dp', 0, 0, tiled=True, axis_index_groups=plane_g...]
    unnamed x35 -> x39, local copies, waits for them, and re-layouts: 3.9 us -> 3.43 us
  transfers between devices with their start and end apart: 26 -> 26, of which waited for: 17 -> 18; matrix products, arithmetic and copies ran while one was open for 5% -> 3% of each run, Pallas kernels for 10% -> 11%
where the time goes in v6:
time: 173 us
  waiting for transfers between devices  84.7 us (49%)
  starting transfers between devices  50.1 us (29%)
  Pallas kernels  26.8 us (15%)
  local copies, waits for them, and re-layouts  6.36 us (4%)
  other arithmetic  3.41 us (2%)
    ppermute x20, waiting for transfers between devices, swap(): return lax.ppermute(values, 'tensor', [(i, i ^ mask) for i in range(4)])  53.1 us
    pallas_call x16, Pallas kernels, call(): pl.pallas_call(body, out_shape=[pltpu.HBM(shape, kind) if i in away else...  26.8 us
    ppermute x2, waiting for transfers between devices, side(): return lax.ppermute(values, 'dp', pairs)  26.5 us
    all_to_all x2, starting transfers between devices, spread(): return lax.all_to_all(stacked, 'dp', 0, 0, tiled=True)  16.8 us
    ppermute x20, starting transfers between devices, swap(): return lax.ppermute(values, 'tensor', [(i, i ^ mask) for i in range(4)])  16.5 us
    all_to_all x2, starting transfers between devices, plane(): lax.all_to_all(stacked, 'dp', 0, 0, tiled=True, axis_index_groups=plane_g...  13.1 us
    ppermute x2, starting transfers between devices, side(): return lax.ppermute(values, 'dp', pairs)  3.75 us
  transfers between devices with their start and end apart: 26, of which 18 were waited for; matrix products, arithmetic and copies ran while one was open for 3% of the time, Pallas kernels for 11%

profile of v6, /device:TPU:0, one launch (start us, length us, event | category | flops | bytes accessed | tf_op | source)
XLA Modules:
  0.0 172.7 jit_solution(15086107008154392090)
XLA Ops:
  0.7 0.8 pad_maximum_fusion.4.weight_ref
  1.5 0.9 concatenate.25
  2.4 1.2 shard_map.323
  3.6 9.4 %all-to-all-start = ((bf16[32,24,896]{2,1,0:T(8,128)(2,1)}), bf16[32,24,896]{2,1,0:T(8,128)(2,1)S(1)}, u32[]{:S(2)}, u32[]{:S(2)}) async-start(bf16[32,24,896]{2,1,0:T(8,128)(2,1)} %shard_map.323), calls=%async_computation | async-start | bytes 2752512 | tf_op jit(solution)/shard_map/all_to_all | solution.py:39
  13.1 1.9 %collective-permute-start.2 = (bf16[24,1536]{1,0:T(8,128)(2,1)S(1)}, bf16[24,1536]{1,0:T(8,128)(2,1)S(1)}, u32[]{:S(2)}, u32[]{:S(2)}) collective-permute-start(bf16[24,1536]{1,0:T(8,128)(2,1)S(1)} %constant_dynamic-update-slice_fusion.own_ref), channel_id=1, source_target_pairs={{0,64},{4,68},{8,72},{12,76},{16,80},{20,84},{24,88},{28,92},{32,9... | collective-permute-start | bytes 221192 | tf_op jit(solution)/shard_map/ppermute | solution.py:54
  15.0 2.9 %collective-permute-start = (bf16[128,768]{1,0:T(8,128)(2,1)S(1)}, bf16[128,768]{1,0:T(8,128)(2,1)S(1)}, u32[]{:S(2)}, u32[]{:S(2)}) collective-permute-start(bf16[128,768]{1,0:T(8,128)(2,1)S(1)} %bitcast.39), channel_id=1, source_target_pairs={{0,2},{1,3},{2,0},{3,1},{4,6},{5,7},{6,4},{7,5},{8,10},{9,11},{10,... | collective-permute-start | bytes 589832 | tf_op jit(solution)/shard_map/ppermute | solution.py:31
  19.0 13.8 %collective-permute-done.2.other_ref = bf16[24,1536]{1,0:T(8,128)(2,1)S(1)} collective-permute-done((bf16[24,1536]{1,0:T(8,128)(2,1)S(1)}, bf16[24,1536]{1,0:T(8,128)(2,1)S(1)}, u32[]{:S(2)}, u32[]{:S(2)}) %collective-permute-start.2) | collective-permute-done | bytes 73760 | tf_op jit(solution)/shard_map/ppermute | solution.py:54
  33.1 1.4 copy-done
  34.5 2.4 %collective-permute-done = bf16[128,768]{1,0:T(8,128)(2,1)S(1)} collective-permute-done((bf16[128,768]{1,0:T(8,128)(2,1)S(1)}, bf16[128,768]{1,0:T(8,128)(2,1)S(1)}, u32[]{:S(2)}, u32[]{:S(2)}) %collective-permute-start) | collective-permute-done | bytes 196640 | tf_op jit(solution)/shard_map/ppermute | solution.py:31
  37.0 7.0 %all-to-all-start.1 = ((bf16[16,48,1536]{2,1,0:T(8,128)(2,1)}), bf16[16,48,1536]{2,1,0:T(8,128)(2,1)}, u32[]{:S(2)}, u32[]{:S(2)}) async-start(bf16[16,48,1536]{2,1,0:T(8,128)(2,1)} %copy-done), calls=%async_computation.1 | async-start | bytes 4718592 | tf_op jit(solution)/shard_map/all_to_all | solution.py:48
  44.7 2.9 %collective-permute-start.4 = (bf16[2,32,128]{2,1,0:T(8,128)(2,1)S(1)}, bf16[2,32,128]{2,1,0:T(8,128)(2,1)S(1)}, u32[]{:S(2)}, u32[]{:S(2)}) collective-permute-start(bf16[2,32,128]{2,1,0:T(8,128)(2,1)S(1)} %slice_bitcast_fusion.line_ref), channel_id=1, source_target_pairs={{0,2},{1,3},{2,0},{3,1},{4,6},{5,7},{6,4},{7,5},{8,10},{9,11},{10,... | collective-permute-start | bytes 49160 | tf_op jit(solution)/shard_map/ppermute | solution.py:31
  47.6 1.3 collective-permute-done.5.line_both_ref
  48.9 1.0 collective-permute-done.4.line_far_ref
  49.9 3.2 %shard_map.325 = (bf16[512,768]{1,0:T(8,128)(2,1)}, bf16[512,256]{1,0:T(8,128)(2,1)S(1)}, f32[8,512]{1,0:T(8,128)S(1)}, bf16[256,768]{1,0:T(8,128)(2,1)S(1)}, f3...) custom-call(s32[1]{0:T(128)} %bitcast.1.index_ref, ...), custom_call_target="tpu_custom_call" | custom-call | flops 1000 | bytes 1000 | tf_op jit(solution)/shard_map/pallas_call | solution.py:83
  53.2 1.7 collective-permute-done.6
  55.1 3.0 %collective-permute-start.7 = (bf16[256,768]{1,0:T(8,128)(2,1)S(1)}, bf16[256,768]{1,0:T(8,128)(2,1)S(1)}, u32[]{:S(2)}, u32[]{:S(2)}) collective-permute-start(bf16[256,768]{1,0:T(8,128)(2,1)S(1)} %pad_maximum_fusion.1), channel_id=1, source_target_pairs={{0,2},{1,3},{2,0},{3,1},{4,6},{5,7},{6,4},{7,5},{8,10},{9,11},{10,... | collective-permute-start | bytes 1179656 | tf_op jit(solution)/shard_map/ppermute | solution.py:31
  58.1 0.8 collective-permute-start.8
  58.9 13.2 %collective-permute-done.8.cotangent_far_ref = bf16[128,768]{1,0:T(8,128)(2,1)S(1)} collective-permute-done((bf16[128,768]{1,0:T(8,128)(2,1)S(1)}, bf16[128,768]{1,0:T(8,128)(2,1)S(1)}, u32[]{:S(2)}, u32[]{:S(2)}) %collective-permute-start.8) | collective-permute-done | bytes 196640 | tf_op jit(solution)/shard_map/ppermute | solution.py:31
  72.8 1.7 collective-permute-done.9.rows_ref.hidden_other
  74.5 3.2 %all-to-all-done.1.blocks_ref = bf16[16,48,1536]{2,1,0:T(8,128)(2,1)} async-done(((bf16[16,48,1536]{2,1,0:T(8,128)(2,1)}), bf16[16,48,1536]{2,1,0:T(8,128)(2,1)}, u32[]{:S(2)}, u32[]{:S(2)}) %all-to-all-start.1) | async-done | bytes 2359328 | tf_op jit(solution)/shard_map/all_to_all | solution.py:48
  77.6 3.1 %shard_map.327 = (bf16[256,768]{1,0:T(8,128)(2,1)S(1)}, bf16[256,768]{1,0:T(8,128)(2,1)S(1)}, bf16[256,768]{1,0:T(8,128)(2,1)S(1)}, bf16[768,768]{1,0:T(8,128)(2,1)S(1)}, bf16[768,768]{1,0:T(8,128)(2,1)S(1)}) custom-call(bf16[256,768]{1,0:T(8,128)(2,1)S(1)} %collective-permute-done.9.rows_ref.hidden_other, bf16[16,48,1536]{2,1,0:T(8,128)(2,1)} %all-to-all-done.1.blocks_ref, ...), custom_call_target="tpu_custom_call" | custom-call | flops 1000 | bytes 1000 | tf_op jit(solution)/shard_map/pallas_call | solution.py:83
  80.8 1.4 shard_map.328
  82.7 0.7 collective-permute-start.11
  83.4 12.0 %collective-permute-done.11.far_ref = bf16[256,768]{1,0:T(8,128)(2,1)S(1)} collective-permute-done((bf16[256,768]{1,0:T(8,128)(2,1)S(1)}, bf16[256,768]{1,0:T(8,128)(2,1)S(1)}, u32[]{:S(2)}, u32[]{:S(2)}) %collective-permute-start.11) | collective-permute-done | bytes 393248 | tf_op jit(solution)/shard_map/ppermute | solution.py:31
  95.5 1.2 shard_map.329
  96.7 1.2 shard_map.330
  97.9 0.9 copy-done.2
  98.8 2.0 %shard_map.331 = (bf16[256,768]{1,0:T(8,128)(2,1)S(1)}, bf16[256,768]{1,0:T(8,128)(2,1)}, f32[1,768]{1,0:T(1,128)S(1)}) custom-call(bf16[256,768]{1,0:T(8,128)(2,1)S(1)} %collective-permute-done.12.rows_ref.branch_other, bf16[768,768]{1,0:T(8,128)(2,1)S(1)} %get-tuple-element.82.up_ref, bf16[768,768]{1,0:T(8,128)(2,1)S(1)} %get-tuple-element.83.down_ref, ...), custom_call_target="tpu_custom_call" | custom-call | flops 1000 | bytes 1000 | tf_op jit(solution)/shard_map/pallas_call | solution.py:83
  101.3 2.5 %shard_map.337 = bf16[16,48,1536]{2,1,0:T(8,128)(2,1)} custom-call(bf16[256,768]{1,0:T(8,128)(2,1)S(1)} %get-tuple-element.78.rows_ref.first_ref.hidden_near, bf16[256,768]{1,0:T(8,128)(2,1)S(1)} %collective-permute-done.9.rows_ref.hidden_other, bf16[256,768]{1,0:T(8,128)(2,1)S(1)} %get-tuple-element.87.rows_ref.second_ref.branch_near, ...), custom_call_target="tpu_custom_call" | custom-call | flops 1000 | bytes 1000 | tf_op jit(solution)/shard_map/pallas_call | solution.py:83
  103.9 6.1 %all-to-all-start.3 = ((bf16[16,48,1536]{2,1,0:T(8,128)(2,1)}), bf16[16,48,1536]{2,1,0:T(8,128)(2,1)}, u32[]{:S(2)}, u32[]{:S(2)}) async-start(bf16[16,48,1536]{2,1,0:T(8,128)(2,1)} %shard_map.337), calls=%async_computation.3 | async-start | bytes 4718592 | tf_op jit(solution)/shard_map/all_to_all | solution.py:48
  110.0 1.3 fusion.2
  112.1 11.6 %collective-permute-done.14.far_ref = bf16[256,768]{1,0:T(8,128)(2,1)S(1)} collective-permute-done((bf16[256,768]{1,0:T(8,128)(2,1)S(1)}, bf16[256,768]{1,0:T(8,128)(2,1)S(1)}, u32[]{:S(2)}, u32[]{:S(2)}) %collective-permute-start.14) | collective-permute-done | bytes 393248 | tf_op jit(solution)/shard_map/ppermute | solution.py:31
  124.3 0.7 copy-done.3
  125.1 1.7 collective-permute-done.15.other_ref
  126.8 3.8 %shard_map.333 = (bf16[512,768]{1,0:T(8,128)(2,1)S(1)}, bf16[256,768]{1,0:T(8,128)(2,1)S(1)}, f32[256,768]{1,0:T(8,128)S(1)}, f32[16,768]{1,0:T(8,128)S(1)}) custom-call(s32[1]{0:T(128)} %bitcast.1.index_ref, bf16[256,768]{1,0:T(8,128)(2,1)S(1)} %get-tuple-element.97.near_ref, bf16[256,768]{1,0:T(8,128)(2,1)S(1)} %collective-permute-done.15.other_ref, ...), custom_call_target="tpu_custom_call" | custom-call | flops 1000 | bytes 1000 | tf_op jit(solution)/shard_map/pallas_call | solution.py:83
  130.8 1.6 collective-permute-done.16
  133.2 2.4 %collective-permute-start.20 = (f32[16,768]{1,0:T(8,128)S(1)}, f32[16,768]{1,0:T(8,128)S(1)}, u32[]{:S(2)}, u32[]{:S(2)}) collective-permute-start(f32[16,768]{1,0:T(8,128)S(1)} %get-tuple-element.107.own_ref), channel_id=1, source_target_pairs={{0,3},{1,2},{2,1},{3,0},{4,7},{5,6},{6,5},{7,4},{8,11},{9,10},{10,... | collective-permute-start | bytes 147464 | tf_op jit(solution)/shard_map/ppermute | solution.py:31
  136.6 2.1 %shard_map.334.block_ref = bf16[768,896]{1,0:T(8,128)(2,1)} custom-call(bf16[256,768]{1,0:T(8,128)(2,1)S(1)} %pad_maximum_fusion.near_ref.tokens_ref.tokens_near, bf16[256,768]{1,0:T(8,128)(2,1)S(1)} %collective-permute-done.1.other_ref.tokens_other, bf16[256,768]{1,0:T(8,128)(2,1)S(1)} %get-tuple-element.97.near_ref, ...), custom_call_target="tpu_custom_call" | custom-call | flops 1000 | bytes 1000 | tf_op jit(solution)/shard_map/pallas_call | solution.py:83
  138.8 2.5 %collective-permute-done.20.both_ref = f32[16,768]{1,0:T(8,128)S(1)} collective-permute-done((f32[16,768]{1,0:T(8,128)S(1)}, f32[16,768]{1,0:T(8,128)S(1)}, u32[]{:S(2)}, u32[]{:S(2)}) %collective-permute-start.20) | collective-permute-done | bytes 49184 | tf_op jit(solution)/shard_map/ppermute | solution.py:31
  141.3 1.9 %collective-permute-done.19.far_ref = f32[16,768]{1,0:T(8,128)S(1)} collective-permute-done((f32[16,768]{1,0:T(8,128)S(1)}, f32[16,768]{1,0:T(8,128)S(1)}, u32[]{:S(2)}, u32[]{:S(2)}) %collective-permute-start.19) | collective-permute-done | bytes 49184 | tf_op jit(solution)/shard_map/ppermute | solution.py:31
  143.2 0.9 shard_map.335
  144.2 7.4 %all-to-all-start.2 = ((bf16[32,24,896]{2,1,0:T(8,128)(2,1)}), bf16[32,24,896]{2,1,0:T(8,128)(2,1)S(1)}, u32[]{:S(2)}, u32[]{:S(2)}) async-start(bf16[32,24,896]{2,1,0:T(8,128)(2,1)} %bitcast.38), calls=%async_computation.2 | async-start | bytes 2752512 | tf_op jit(solution)/shard_map/all_to_all | solution.py:39
  151.6 2.1 %shard_map.338 = (f32[24,1536]{1,0:T(8,128)S(1)}, bf16[24,1536]{1,0:T(8,128)(2,1)S(1)}) custom-call(s32[1]{0:T(128)} %bitcast.3.index_ref, bf16[16,48,1536]{2,1,0:T(8,128)(2,1)} %all-to-all-done.3.blocks_ref), custom_call_target="tpu_custom_call" | custom-call | flops 1000 | bytes 1000 | tf_op jit(solution)/shard_map/pallas_call | solution.py:83
  153.7 1.9 %collective-permute-start.21 = (bf16[24,1536]{1,0:T(8,128)(2,1)S(1)}, bf16[24,1536]{1,0:T(8,128)(2,1)S(1)}, u32[]{:S(2)}, u32[]{:S(2)}) collective-permute-start(bf16[24,1536]{1,0:T(8,128)(2,1)S(1)} %get-tuple-element.116), channel_id=1, source_target_pairs={{0,64},{4,68},{8,72},{12,76},{16,80},{20,84},{24,88},{28,92},{32,9... | collective-permute-start | bytes 221192 | tf_op jit(solution)/shard_map/ppermute | solution.py:54
  155.5 0.8 fusion.1
  156.4 12.7 %collective-permute-done.21 = bf16[24,1536]{1,0:T(8,128)(2,1)S(1)} collective-permute-done((bf16[24,1536]{1,0:T(8,128)(2,1)S(1)}, bf16[24,1536]{1,0:T(8,128)(2,1)S(1)}, u32[]{:S(2)}, u32[]{:S(2)}) %collective-permute-start.21) | collective-permute-done | bytes 73760 | tf_op jit(solution)/shard_map/ppermute | solution.py:54
  169.7 1.9 %all-to-all-done.2.blocks_ref = bf16[32,24,896]{2,1,0:T(8,128)(2,1)S(1)} async-done(((bf16[32,24,896]{2,1,0:T(8,128)(2,1)}), bf16[32,24,896]{2,1,0:T(8,128)(2,1)S(1)}, u32[]{:S(2)}, u32[]{:S(2)}) %all-to-all-start.2) | async-done | bytes 1376288 | tf_op jit(solution)/shard_map/all_to_all | solution.py:39
  171.6 1.0 shard_map.336
  (87 shorter events, 8.5 us)
Async XLA Ops:
  3.6 9.4 %copy-start.15 = (bf16[24,768]{1,0:T(8,128)(2,1)S(1)}, bf16[24,768]{1,0:T(8,128)(2,1)}, u32[]{:S(2)}) copy-start(bf16[24,768]{1,0:T(8,128)(2,1)} %param.25) | copy-start | bytes 110596
  3.6 9.5 %copy-start.16 = (bf16[24,768]{1,0:T(8,128)(2,1)S(1)}, bf16[24,768]{1,0:T(8,128)(2,1)}, u32[]{:S(2)}) copy-start(bf16[24,768]{1,0:T(8,128)(2,1)} %param.27) | copy-start | bytes 110596
  3.6 11.4 %copy-start.13 = (bf16[1,128,768]{2,1,0:T(8,128)(2,1)S(1)}, bf16[1,128,768]{2,1,0:T(8,128)(2,1)}, u32[]{:S(2)}) copy-start(bf16[1,128,768]{2,1,0:T(8,128)(2,1)} %param.20) | copy-start | bytes 589828
  3.6 14.3 %copy-start.17 = (s32[4]{0:T(128)S(1)}, s32[4]{0:T(128)}, u32[]{:S(2)}) copy-start(s32[4]{0:T(128)} %constant.82) | copy-start | bytes 52
  3.6 14.3 %copy-start.18 = (s32[4]{0:T(128)S(1)}, s32[4]{0:T(128)}, u32[]{:S(2)}) copy-start(s32[4]{0:T(128)} %constant.81) | copy-start | bytes 52
  3.6 14.3 %copy-start.14 = (s32[1,512]{1,0:T(1,128)S(1)}, s32[1,512]{1,0:T(1,128)}, u32[]{:S(2)}) copy-start(s32[1,512]{1,0:T(1,128)} %param.21) | copy-start | bytes 6148
  3.6 33.4 %all-to-all-start = ((bf16[32,24,896]{2,1,0:T(8,128)(2,1)}), bf16[32,24,896]{2,1,0:T(8,128)(2,1)S(1)}, u32[]{:S(2)}, u32[]{:S(2)}) async-start(bf16[32,24,896]{2,1,0:T(8,128)(2,1)} %shard_map.323), calls=%async_computation | async-start | bytes 2752512 | tf_op jit(solution)/shard_map/all_to_all | solution.py:39
  13.1 19.8 %collective-permute-start.2 = (bf16[24,1536]{1,0:T(8,128)(2,1)S(1)}, bf16[24,1536]{1,0:T(8,128)(2,1)S(1)}, u32[]{:S(2)}, u32[]{:S(2)}) collective-permute-start(bf16[24,1536]{1,0:T(8,128)(2,1)S(1)} %constant_dynamic-update-slice_fusion.own_ref), channel_id=1, source_target_pairs={{0,64},{4,68},{8,72},{12,76},{16,80},{20,84},{24,88},{28,92},{32,9... | collective-permute-start | bytes 221192 | tf_op jit(solution)/shard_map/ppermute | solution.py:54
  15.0 21.9 %collective-permute-start = (bf16[128,768]{1,0:T(8,128)(2,1)S(1)}, bf16[128,768]{1,0:T(8,128)(2,1)S(1)}, u32[]{:S(2)}, u32[]{:S(2)}) collective-permute-start(bf16[128,768]{1,0:T(8,128)(2,1)S(1)} %bitcast.39), channel_id=1, source_target_pairs={{0,2},{1,3},{2,0},{3,1},{4,6},{5,7},{6,4},{7,5},{8,10},{9,11},{10,... | collective-permute-start | bytes 589832 | tf_op jit(solution)/shard_map/ppermute | solution.py:31
  33.1 1.4 copy-start
  36.9 10.7 %collective-permute-start.1 = (bf16[256,768]{1,0:T(8,128)(2,1)S(1)}, bf16[256,768]{1,0:T(8,128)(2,1)S(1)}, u32[]{:S(2)}, u32[]{:S(2)}) collective-permute-start(bf16[256,768]{1,0:T(8,128)(2,1)S(1)} %pad_maximum_fusion.near_ref.tokens_ref.tokens_near), channel_id=1, source_target_pairs={{0,1},{1,0},{2,3},{3,2},{4,5},{5,4},{6,7},{7,6},{8,9},{9,8},{10,11... | collective-permute-start | bytes 1179656 | tf_op jit(solution)/shard_map/ppermute | solution.py:31
  37.0 40.6 %all-to-all-start.1 = ((bf16[16,48,1536]{2,1,0:T(8,128)(2,1)}), bf16[16,48,1536]{2,1,0:T(8,128)(2,1)}, u32[]{:S(2)}, u32[]{:S(2)}) async-start(bf16[16,48,1536]{2,1,0:T(8,128)(2,1)} %copy-done), calls=%async_computation.1 | async-start | bytes 4718592 | tf_op jit(solution)/shard_map/all_to_all | solution.py:48
  44.2 4.7 %collective-permute-start.5 = (bf16[2,32,128]{2,1,0:T(8,128)(2,1)S(1)}, bf16[2,32,128]{2,1,0:T(8,128)(2,1)S(1)}, u32[]{:S(2)}, u32[]{:S(2)}) collective-permute-start(bf16[2,32,128]{2,1,0:T(8,128)(2,1)S(1)} %slice_bitcast_fusion.line_ref), channel_id=1, source_target_pairs={{0,3},{1,2},{2,1},{3,0},{4,7},{5,6},{6,5},{7,4},{8,11},{9,10},{10,... | collective-permute-start | bytes 49160 | tf_op jit(solution)/shard_map/ppermute | solution.py:31
  44.7 5.2 %collective-permute-start.4 = (bf16[2,32,128]{2,1,0:T(8,128)(2,1)S(1)}, bf16[2,32,128]{2,1,0:T(8,128)(2,1)S(1)}, u32[]{:S(2)}, u32[]{:S(2)}) collective-permute-start(bf16[2,32,128]{2,1,0:T(8,128)(2,1)S(1)} %slice_bitcast_fusion.line_ref), channel_id=1, source_target_pairs={{0,2},{1,3},{2,0},{3,1},{4,6},{5,7},{6,4},{7,5},{8,10},{9,11},{10,... | collective-permute-start | bytes 49160 | tf_op jit(solution)/shard_map/ppermute | solution.py:31
  47.6 2.3 %collective-permute-start.3 = (bf16[2,32,128]{2,1,0:T(8,128)(2,1)S(1)}, bf16[2,32,128]{2,1,0:T(8,128)(2,1)S(1)}, u32[]{:S(2)}, u32[]{:S(2)}) collective-permute-start(bf16[2,32,128]{2,1,0:T(8,128)(2,1)S(1)} %slice_bitcast_fusion.line_ref), channel_id=1, source_target_pairs={{0,1},{1,0},{2,3},{3,2},{4,5},{5,4},{6,7},{7,6},{8,9},{9,8},{10,11... | collective-permute-start | bytes 49160 | tf_op jit(solution)/shard_map/ppermute | solution.py:31
  53.1 2.0 %copy-start.5 = (bf16[512,256]{1,0:T(8,128)(2,1)}, bf16[512,256]{1,0:T(8,128)(2,1)S(1)}, u32[]{:S(2)}) copy-start(bf16[512,256]{1,0:T(8,128)(2,1)S(1)} %get-tuple-element.106.mixed_ref) | copy-start | bytes 786436
  53.1 1.8 %collective-permute-start.6 = (bf16[256,768]{1,0:T(8,128)(2,1)S(1)}, bf16[256,768]{1,0:T(8,128)(2,1)S(1)}, u32[]{:S(2)}, u32[]{:S(2)}) collective-permute-start(bf16[256,768]{1,0:T(8,128)(2,1)S(1)} %get-tuple-element.74), channel_id=1, source_target_pairs={{0,1},{1,0},{2,3},{3,2},{4,5},{5,4},{6,7},{7,6},{8,9},{9,8},{10,11... | collective-permute-start | bytes 1179656 | tf_op jit(solution)/shard_map/ppermute | solution.py:31
  55.0 3.1 %copy-start.7 = (bf16[1,128,768]{2,1,0:T(8,128)(2,1)S(1)}, bf16[1,128,768]{2,1,0:T(8,128)(2,1)}, u32[]{:S(2)}) copy-start(bf16[1,128,768]{2,1,0:T(8,128)(2,1)} %param.37) | copy-start | bytes 589828
  55.1 17.0 %collective-permute-start.7 = (bf16[256,768]{1,0:T(8,128)(2,1)S(1)}, bf16[256,768]{1,0:T(8,128)(2,1)S(1)}, u32[]{:S(2)}, u32[]{:S(2)}) collective-permute-start(bf16[256,768]{1,0:T(8,128)(2,1)S(1)} %pad_maximum_fusion.1), channel_id=1, source_target_pairs={{0,2},{1,3},{2,0},{3,1},{4,6},{5,7},{6,4},{7,5},{8,10},{9,11},{10,... | collective-permute-start | bytes 1179656 | tf_op jit(solution)/shard_map/ppermute | solution.py:31
  58.1 14.0 %collective-permute-start.8 = (bf16[128,768]{1,0:T(8,128)(2,1)S(1)}, bf16[128,768]{1,0:T(8,128)(2,1)S(1)}, u32[]{:S(2)}, u32[]{:S(2)}) collective-permute-start(bf16[128,768]{1,0:T(8,128)(2,1)S(1)} %bitcast.33), channel_id=1, source_target_pairs={{0,2},{1,3},{2,0},{3,1},{4,6},{5,7},{6,4},{7,5},{8,10},{9,11},{10,... | collective-permute-start | bytes 589832 | tf_op jit(solution)/shard_map/ppermute | solution.py:31
  72.1 0.7 copy-start.9
  72.8 1.7 collective-permute-start.9
  80.7 1.8 %collective-permute-start.10 = (bf16[256,768]{1,0:T(8,128)(2,1)S(1)}, bf16[256,768]{1,0:T(8,128)(2,1)S(1)}, u32[]{:S(2)}, u32[]{:S(2)}) collective-permute-start(bf16[256,768]{1,0:T(8,128)(2,1)S(1)} %get-tuple-element.85), channel_id=1, source_target_pairs={{0,1},{1,0},{2,3},{3,2},{4,5},{5,4},{6,7},{7,6},{8,9},{9,8},{10,11... | collective-permute-start | bytes 1179656 | tf_op jit(solution)/shard_map/ppermute | solution.py:31
  82.6 12.9 %copy-start.8 = (bf16[1,128,768]{2,1,0:T(8,128)(2,1)S(1)}, bf16[1,128,768]{2,1,0:T(8,128)(2,1)}, u32[]{:S(2)}) copy-start(bf16[1,128,768]{2,1,0:T(8,128)(2,1)} %param.37) | copy-start | bytes 589828
  82.6 12.9 %copy-start.10 = (bf16[128,768]{1,0:T(8,128)(2,1)S(1)}, bf16[128,768]{1,0:T(8,128)(2,1)}, u32[]{:S(2)}) copy-start(bf16[128,768]{1,0:T(8,128)(2,1)} %copy-done.9) | copy-start | bytes 589828
  82.7 12.8 %collective-permute-start.11 = (bf16[256,768]{1,0:T(8,128)(2,1)S(1)}, bf16[256,768]{1,0:T(8,128)(2,1)S(1)}, u32[]{:S(2)}, u32[]{:S(2)}) collective-permute-start(bf16[256,768]{1,0:T(8,128)(2,1)S(1)} %pad_maximum_fusion.2), channel_id=1, source_target_pairs={{0,2},{1,3},{2,0},{3,1},{4,6},{5,7},{6,4},{7,5},{8,10},{9,11},{10,... | collective-permute-start | bytes 1179656 | tf_op jit(solution)/shard_map/ppermute | solution.py:31
  96.7 2.2 %collective-permute-start.12 = (bf16[256,768]{1,0:T(8,128)(2,1)S(1)}, bf16[256,768]{1,0:T(8,128)(2,1)S(1)}, u32[]{:S(2)}, u32[]{:S(2)}) collective-permute-start(bf16[256,768]{1,0:T(8,128)(2,1)S(1)} %get-tuple-element.87.rows_ref.second_ref.branch_near), channel_id=1, source_target_pairs={{0,1},{1,0},{2,3},{3,2},{4,5},{5,4},{6,7},{7,6},{8,9},{9,8},{10,11... | collective-permute-start | bytes 1179656 | tf_op jit(solution)/shard_map/ppermute | solution.py:31
  97.9 0.9 copy-start.2
  100.8 9.2 %collective-permute-start.13 = (bf16[256,768]{1,0:T(8,128)(2,1)}, bf16[256,768]{1,0:T(8,128)(2,1)}, u32[]{:S(2)}, u32[]{:S(2)}) collective-permute-start(bf16[256,768]{1,0:T(8,128)(2,1)} %get-tuple-element.93), channel_id=1, source_target_pairs={{0,1},{1,0},{2,3},{3,2},{4,5},{5,4},{6,7},{7,6},{8,9},{9,8},{10,11... | collective-permute-start | bytes 1179656 | tf_op jit(solution)/shard_map/ppermute | solution.py:31
  103.9 40.3 %all-to-all-start.3 = ((bf16[16,48,1536]{2,1,0:T(8,128)(2,1)}), bf16[16,48,1536]{2,1,0:T(8,128)(2,1)}, u32[]{:S(2)}, u32[]{:S(2)}) async-start(bf16[16,48,1536]{2,1,0:T(8,128)(2,1)} %shard_map.337), calls=%async_computation.3 | async-start | bytes 4718592 | tf_op jit(solution)/shard_map/all_to_all | solution.py:48
  111.4 15.5 %copy-start.1 = (bf16[512,768]{1,0:T(8,128)(2,1)S(1)}, bf16[512,768]{1,0:T(8,128)(2,1)}, u32[]{:S(2)}) copy-start(bf16[512,768]{1,0:T(8,128)(2,1)} %get-tuple-element.98.qkv_ref) | copy-start | bytes 2359300
  111.4 12.3 %collective-permute-start.14 = (bf16[256,768]{1,0:T(8,128)(2,1)S(1)}, bf16[256,768]{1,0:T(8,128)(2,1)S(1)}, u32[]{:S(2)}, u32[]{:S(2)}) collective-permute-start(bf16[256,768]{1,0:T(8,128)(2,1)S(1)} %pad_maximum_fusion.3), channel_id=1, source_target_pairs={{0,2},{1,3},{2,0},{3,1},{4,6},{5,7},{6,4},{7,5},{8,10},{9,11},{10,... | collective-permute-start | bytes 1179656 | tf_op jit(solution)/shard_map/ppermute | solution.py:31
  124.3 0.7 copy-start.3
  125.1 1.7 collective-permute-start.15
  130.6 6.0 %copy-start.6 = (bf16[512,256]{1,0:T(8,128)(2,1)S(1)}, bf16[512,256]{1,0:T(8,128)(2,1)}, u32[]{:S(2)}) copy-start(bf16[512,256]{1,0:T(8,128)(2,1)} %copy-done.5) | copy-start | bytes 786436
  130.6 1.8 %collective-permute-start.16 = (bf16[256,768]{1,0:T(8,128)(2,1)S(1)}, bf16[256,768]{1,0:T(8,128)(2,1)S(1)}, u32[]{:S(2)}, u32[]{:S(2)}) collective-permute-start(bf16[256,768]{1,0:T(8,128)(2,1)S(1)} %get-tuple-element.104), channel_id=1, source_target_pairs={{0,1},{1,0},{2,3},{3,2},{4,5},{5,4},{6,7},{7,6},{8,9},{9,8},{10,11... | collective-permute-start | bytes 1179656 | tf_op jit(solution)/shard_map/ppermute | solution.py:31
  132.5 6.3 %copy-start.11 = (f32[256,768]{1,0:T(8,128)}, f32[256,768]{1,0:T(8,128)S(1)}, u32[]{:S(2)}) copy-start(f32[256,768]{1,0:T(8,128)S(1)} %convert_add_fusion) | copy-start | bytes 2359300
  132.5 11.5 %collective-permute-start.17 = (bf16[128,768]{1,0:T(8,128)(2,1)S(1)}, bf16[128,768]{1,0:T(8,128)(2,1)S(1)}, u32[]{:S(2)}, u32[]{:S(2)}) collective-permute-start(bf16[128,768]{1,0:T(8,128)(2,1)S(1)} %slice.87), channel_id=1, source_target_pairs={{0,2},{1,3},{2,0},{3,1},{4,6},{5,7},{6,4},{7,5},{8,10},{9,11},{10,... | collective-permute-start | bytes 589832 | tf_op jit(solution)/shard_map/ppermute | solution.py:31
  133.2 8.1 %collective-permute-start.20 = (f32[16,768]{1,0:T(8,128)S(1)}, f32[16,768]{1,0:T(8,128)S(1)}, u32[]{:S(2)}, u32[]{:S(2)}) collective-permute-start(f32[16,768]{1,0:T(8,128)S(1)} %get-tuple-element.107.own_ref), channel_id=1, source_target_pairs={{0,3},{1,2},{2,1},{3,0},{4,7},{5,6},{6,5},{7,4},{8,11},{9,10},{10,... | collective-permute-start | bytes 147464 | tf_op jit(solution)/shard_map/ppermute | solution.py:31
  135.6 7.6 %collective-permute-start.19 = (f32[16,768]{1,0:T(8,128)S(1)}, f32[16,768]{1,0:T(8,128)S(1)}, u32[]{:S(2)}, u32[]{:S(2)}) collective-permute-start(f32[16,768]{1,0:T(8,128)S(1)} %get-tuple-element.107.own_ref), channel_id=1, source_target_pairs={{0,2},{1,3},{2,0},{3,1},{4,6},{5,7},{6,4},{7,5},{8,10},{9,11},{10,... | collective-permute-start | bytes 147464 | tf_op jit(solution)/shard_map/ppermute | solution.py:31
  136.2 6.9 %collective-permute-start.18 = (f32[16,768]{1,0:T(8,128)S(1)}, f32[16,768]{1,0:T(8,128)S(1)}, u32[]{:S(2)}, u32[]{:S(2)}) collective-permute-start(f32[16,768]{1,0:T(8,128)S(1)} %get-tuple-element.107.own_ref), channel_id=1, source_target_pairs={{0,1},{1,0},{2,3},{3,2},{4,5},{5,4},{6,7},{7,6},{8,9},{9,8},{10,11... | collective-permute-start | bytes 147464 | tf_op jit(solution)/shard_map/ppermute | solution.py:31
  144.2 27.4 %all-to-all-start.2 = ((bf16[32,24,896]{2,1,0:T(8,128)(2,1)}), bf16[32,24,896]{2,1,0:T(8,128)(2,1)S(1)}, u32[]{:S(2)}, u32[]{:S(2)}) async-start(bf16[32,24,896]{2,1,0:T(8,128)(2,1)} %bitcast.38), calls=%async_computation.2 | async-start | bytes 2752512 | tf_op jit(solution)/shard_map/all_to_all | solution.py:39
  151.6 4.0 %copy-start.4 = (f32[128,768]{1,0:T(8,128)S(1)}, f32[128,768]{1,0:T(8,128)}, u32[]{:S(2)}) copy-start(f32[128,768]{1,0:T(8,128)} %copy-done.3) | copy-start | bytes 1179652
  151.6 4.0 %copy-start.12 = (f32[256,768]{1,0:T(8,128)S(1)}, f32[256,768]{1,0:T(8,128)}, u32[]{:S(2)}) copy-start(f32[256,768]{1,0:T(8,128)} %copy-done.11) | copy-start | bytes 2359300
  153.7 15.4 %collective-permute-start.21 = (bf16[24,1536]{1,0:T(8,128)(2,1)S(1)}, bf16[24,1536]{1,0:T(8,128)(2,1)S(1)}, u32[]{:S(2)}, u32[]{:S(2)}) collective-permute-start(bf16[24,1536]{1,0:T(8,128)(2,1)S(1)} %get-tuple-element.116), channel_id=1, source_target_pairs={{0,64},{4,68},{8,72},{12,76},{16,80},{20,84},{24,88},{28,92},{32,9... | collective-permute-start | bytes 221192 | tf_op jit(solution)/shard_map/ppermute | solution.py:54

commit v7 on v6

--- a/solution.py
+++ b/solution.py
@@ -48,10 +48,14 @@
     return lax.all_to_all(stacked, "dp", 0, 0, tiled=True, axis_index_groups=plane_groups())
 
 
-def side(values):
+def side(values, mask=0):
     count = lax.axis_size("dp")
-    pairs = [(i, (i + count // 2) % count) for i in range(count)]
-    return lax.ppermute(values, "dp", pairs)
+    pairs = [
+        (4 * i + j, 4 * ((i + count // 2) % count) + (j ^ mask))
+        for i in range(count)
+        for j in range(4)
+    ]
+    return lax.ppermute(values, ("dp", "tensor"), pairs)
 
 
 def halves(values):
@@ -140,17 +144,18 @@
     return jnp.where(lanes(shape) // 4 == lanes(shape, 0), 1.0, 0.0).astype(LOW)
 
 
-def unpack_lines(index, line_refs, vector_ref, columns, width):
+def unpack_lines(index, lower, line_refs, vector_ref, columns, width):
     devices, size = line_refs[0].shape[1:]
+    devices = 2 * devices
     each = width // (4 * devices)
     flipped = []
     for part in range(2):
         near = [ref[part].astype(FULL) for ref in line_refs]
         ordered = []
-        for at in range(4):
-            row = near[3]
-            for mask in (2, 1, 0):
-                row = jnp.where((index ^ mask) == at, near[mask], row)
+        for at in range(8):
+            row = near[7]
+            for mask in range(7):
+                row = jnp.where((2 * index + lower) ^ (mask % 4 * 2 + mask // 4) == at, near[mask], row)
             ordered.append(row)
         flipped.append(jnp.transpose(jnp.concatenate(ordered, axis=0)).astype(LOW))
 
@@ -192,29 +197,34 @@
     index_ref,
     near_ref,
     other_ref,
-    weight_ref,
+    half_ref,
+    half_other_ref,
     segment_ref,
-    line_ref,
-    line_core_ref,
-    line_far_ref,
-    line_both_ref,
-    qkv_out,
-    mixed_ref,
-    log_ref,
-    send_ref,
-    keep_ref,
-    vector_ref,
-    up_bias_ref,
-    qkv_ref,
-    qkv_sem,
+    *refs,
 ):
-    index = index_ref[0]
+    line_refs = refs[:8]
+    (
+        qkv_out,
+        mixed_ref,
+        log_ref,
+        send_ref,
+        keep_ref,
+        vector_ref,
+        up_bias_ref,
+        weight_ref,
+        qkv_ref,
+        qkv_sem,
+    ) = refs[8:]
+    index, lower = index_ref[0], index_ref[1]
     half = near_ref.shape[0]
     columns = 3 * HEAD_DIM
-    line_refs = (line_ref, line_core_ref, line_far_ref, line_both_ref)
     width = weight_ref.shape[0]
-    width = weight_ref.shape[0]
-    bias, up_bias = unpack_lines(index, line_refs, vector_ref, columns, width)
+    part = width // 2
+    weight_ref[pl.ds(pl.multiple_of(lower * part, 16), part), :] = half_ref[:, : 3 * GROUP]
+    weight_ref[pl.ds(pl.multiple_of((1 - lower) * part, 16), part), :] = half_other_ref[
+        :, : 3 * GROUP
+    ]
+    bias, up_bias = unpack_lines(index, lower, line_refs, vector_ref, columns, width)
     up_bias_ref[...] = up_bias
     keep = lanes((1, 3 * GROUP)) % GROUP < columns
     for at, rows_ref in ((0, near_ref), (half, other_ref)):
@@ -377,7 +387,9 @@
 
 
 def vectors_kernel(block_ref, own_ref, core_ref, far_ref, both_ref, out_ref, held, sem):
-    total = own_ref[...] + core_ref[...] + (far_ref[...] + both_ref[...])
+    total = own_ref[...]
+    for ref in (core_ref, far_ref, both_ref):
+        total += ref[...].astype(FULL)
     total = total[:12]
     high = total.astype(LOW).astype(FULL)
     rows = jnp.concatenate(
@@ -733,16 +745,17 @@
     first_own = jnp.concatenate([q_weight, k_weight, v_weight, out_weight], axis=1)
     (first_block,) = call(
         first_block_kernel,
-        [((dp_count, shard_rows, 3 * GROUP + TILE), LOW)],
+        [((dp_count // 2, shard_rows, 3 * GROUP + TILE), LOW)],
         line,
         first_own,
     )
-    first_blocks = spread(first_block)
+    first_half = plane(first_block)
     tokens_far = swap(tokens, 2)
     second_own = jnp.concatenate([up_weight, down_weight], axis=1)
     second_side = side(second_own)
     tokens_pair = jnp.concatenate([tokens, tokens_far], axis=0)
-    tokens_core = swap(tokens_pair, 1)
+    cotangent_far = swap(cotangent, 2)
+    tokens_core = swap(after(tokens_pair, cotangent_far), 1)
     segment_row = ordered_segments(segments[0], my_index)[None]
     (second_block,) = call(
         second_block_kernel,
@@ -752,14 +765,14 @@
         second_side,
         smem=1,
     )
-    first_blocks, second_block = lax.optimization_barrier((first_blocks, second_block))
-    first_full = first_blocks.reshape(width, -1)
-    lines = first_blocks[:, : 2 * line_count, 3 * GROUP :]
-    lines = lines.reshape(dp_count, 2, line_size).transpose(1, 0, 2)
-    lines = [lines] + [swap(lines, mask) for mask in (1, 2, 3)]
+    first_half, second_block = lax.optimization_barrier((first_half, second_block))
+    first_other = side(first_half)
+    lines = first_half[:, : 2 * line_count, 3 * GROUP :]
+    lines = lines.reshape(dp_count // 2, 2, line_size).transpose(1, 0, 2)
+    lines = [lines] + [swap(lines, mask) for mask in (1, 2, 3)] + [side(lines, m) for m in range(4)]
     second_full = plane(second_block)
 
-    qkv_rows, mixed_rows, log_totals, attn_send, attn_keep, rows, bias_up = call(
+    qkv_rows, mixed_rows, log_totals, attn_send, attn_keep, rows, bias_up, first_full = call(
         forward_kernel,
         [
             ((length, 3 * GROUP), LOW),
@@ -769,11 +782,13 @@
             ((half, width), FULL),
             ((8, width), FULL),
             ((1, hidden_cols), FULL),
+            ((width, 3 * GROUP), LOW),
         ],
-        index,
+        jnp.concatenate([index, side_index]),
         tokens_pair,
         tokens_core,
-        first_full,
+        first_half.reshape(width // 2, -1),
+        first_other.reshape(width // 2, -1),
         segment_row,
         *lines,
         smem=1,
@@ -782,16 +797,15 @@
     )
     attn_chip = attn_keep + swap(attn_send, 1).astype(FULL)
     attn_far = swap(far_pack(attn_chip), 2)
-    cotangent_far = swap(after(cotangent, attn_send), 2)
     hidden_low, inv_first = call(
         first_norm_kernel,
         [((half, width), LOW), ((8, half), FULL)],
         tokens_pair,
         attn_chip,
-        after(attn_far, cotangent_far),
+        attn_far,
         rows,
     )
-    hidden_core = after(swap(hidden_low, 1), cotangent_far)
+    hidden_core = swap(hidden_low, 1)
     active_other, slope_other, branch_send, up_full, down_full = call(
         feed_other_kernel,
         [
@@ -902,7 +916,7 @@
     input_chip = input_keep + swap(input_send, 1).astype(FULL)
     input_sent = input_chip[local_len:].astype(LOW)
     input_far = swap(input_sent, 2)
-    vector_near = [swap(vector_sums, mask) for mask in (1, 2, 3)]
+    vector_near = [swap(vector_sums.astype(LOW), mask) for mask in (1, 2, 3)]
     (last_block,) = call(
         weights_kernel,
         [((width, 3 * GROUP + TILE), LOW)],

time: 173 us -> 165 us (0.954)
  waiting for transfers between devices: 84.7 us -> 67.1 us
  starting transfers between devices: 50.1 us -> 59 us
    ppermute x2 -> x7, waiting for transfers between devices: 26.5 us -> 14.8 us  [side(): return lax.ppermute(values, ('dp', 'tensor'), pairs)]
    all_to_all x2 -> x1, starting transfers between devices: 16.8 us -> 6.25 us  [spread(): return lax.all_to_all(stacked, 'dp', 0, 0, tiled=True)]
    ppermute x20, waiting for transfers between devices: 53.1 us -> 42.8 us  [swap(): return lax.ppermute(values, 'tensor', [(i, i ^ mask) for i in range(4)])]
    all_to_all x2 -> x3, starting transfers between devices: 13.1 us -> 22.1 us  [plane(): lax.all_to_all(stacked, 'dp', 0, 0, tiled=True, axis_index_groups=plane_g...]
    ppermute x2 -> x7, starting transfers between devices: 3.75 us -> 9.9 us  [side(): return lax.ppermute(values, ('dp', 'tensor'), pairs)]
    ppermute x20, starting transfers between devices: 16.5 us -> 20.7 us  [swap(): return lax.ppermute(values, 'tensor', [(i, i ^ mask) for i in range(4)])]
    all_to_all x2 -> x3, waiting for transfers between devices: 3.28 us -> 7.43 us  [plane(): lax.all_to_all(stacked, 'dp', 0, 0, tiled=True, axis_index_groups=plane_g...]
  transfers between devices with their start and end apart: 26 -> 31, of which waited for: 18 -> 18; matrix products, arithmetic and copies ran while one was open for 3% -> 3% of each run, Pallas kernels for 11% -> 11%
where the time goes in v7:
time: 165 us
  waiting for transfers between devices  67.1 us (41%)
  starting transfers between devices  59 us (36%)
  Pallas kernels  28 us (17%)
  local copies, waits for them, and re-layouts  5.85 us (4%)
  other arithmetic  3.52 us (2%)
    ppermute x20, waiting for transfers between devices, swap(): return lax.ppermute(values, 'tensor', [(i, i ^ mask) for i in range(4)])  42.8 us
    pallas_call x16, Pallas kernels, call(): pl.pallas_call(body, out_shape=[pltpu.HBM(shape, kind) if i in away else...  28 us
    all_to_all x3, starting transfers between devices, plane(): lax.all_to_all(stacked, 'dp', 0, 0, tiled=True, axis_index_groups=plane_g...  22.1 us
    ppermute x20, starting transfers between devices, swap(): return lax.ppermute(values, 'tensor', [(i, i ^ mask) for i in range(4)])  20.7 us
    ppermute x7, waiting for transfers between devices, side(): return lax.ppermute(values, ('dp', 'tensor'), pairs)  14.8 us
    ppermute x7, starting transfers between devices, side(): return lax.ppermute(values, ('dp', 'tensor'), pairs)  9.9 us
    all_to_all x3, waiting for transfers between devices, plane(): lax.all_to_all(stacked, 'dp', 0, 0, tiled=True, axis_index_groups=plane_g...  7.43 us
    all_to_all x1, starting transfers between devices, spread(): return lax.all_to_all(stacked, 'dp', 0, 0, tiled=True)  6.25 us
  transfers between devices with their start and end apart: 31, of which 18 were waited for; matrix products, arithmetic and copies ran while one was open for 3% of the time, Pallas kernels for 11%

profile of v7, /device:TPU:0, one launch (start us, length us, event | category | flops | bytes accessed | tf_op | source)
XLA Modules:
  0.0 165.0 jit_solution(17848649707342413727)
XLA Ops:
  0.7 0.9 pad_maximum_fusion.4.weight_ref
  1.7 0.9 concatenate.29
  2.5 0.9 shard_map.323
  3.5 8.0 %all-to-all-start = ((bf16[16,24,896]{2,1,0:T(8,128)(2,1)}), bf16[16,24,896]{2,1,0:T(8,128)(2,1)S(1)}, u32[]{:S(2)}, u32[]{:S(2)}) async-start(bf16[16,24,896]{2,1,0:T(8,128)(2,1)} %shard_map.323), calls=%async_computation | async-start | bytes 1376256 | tf_op jit(solution)/shard_map/all_to_all | solution.py:48
  11.5 1.7 %collective-permute-start.3 = (bf16[24,1536]{1,0:T(8,128)(2,1)S(1)}, bf16[24,1536]{1,0:T(8,128)(2,1)S(1)}, u32[]{:S(2)}, u32[]{:S(2)}) collective-permute-start(bf16[24,1536]{1,0:T(8,128)(2,1)S(1)} %constant_dynamic-update-slice_fusion.own_ref), channel_id=1, source_target_pairs={{0,64},{1,65},{2,66},{3,67},{4,68},{5,69},{6,70},{7,71},{8,72},{9,... | collective-permute-start | bytes 221192 | tf_op jit(solution)/shard_map/ppermute | solution.py:58
  13.1 2.9 %collective-permute-start = (bf16[128,768]{1,0:T(8,128)(2,1)S(1)}, bf16[128,768]{1,0:T(8,128)(2,1)S(1)}, u32[]{:S(2)}, u32[]{:S(2)}) collective-permute-start(bf16[128,768]{1,0:T(8,128)(2,1)S(1)} %bitcast.40), channel_id=1, source_target_pairs={{0,2},{1,3},{2,0},{3,1},{4,6},{5,7},{6,4},{7,5},{8,10},{9,11},{10,... | collective-permute-start | bytes 589832 | tf_op jit(solution)/shard_map/ppermute | solution.py:31
  17.9 1.6 shard_map.324
  19.5 5.2 %all-to-all-done = bf16[16,24,896]{2,1,0:T(8,128)(2,1)S(1)} async-done(((bf16[16,24,896]{2,1,0:T(8,128)(2,1)}), bf16[16,24,896]{2,1,0:T(8,128)(2,1)S(1)}, u32[]{:S(2)}, u32[]{:S(2)}) %all-to-all-start) | async-done | bytes 688160 | tf_op jit(solution)/shard_map/all_to_all | solution.py:48
  24.7 1.6 collective-permute-start.4
  27.1 8.0 %all-to-all-start.1 = ((bf16[16,48,1536]{2,1,0:T(8,128)(2,1)}), bf16[16,48,1536]{2,1,0:T(8,128)(2,1)}, u32[]{:S(2)}, u32[]{:S(2)}) async-start(bf16[16,48,1536]{2,1,0:T(8,128)(2,1)} %shard_map.324), calls=%async_computation.1 | async-start | bytes 4718592 | tf_op jit(solution)/shard_map/all_to_all | solution.py:48
  35.1 1.7 %collective-permute-start.11 = (bf16[2,16,128]{2,1,0:T(8,128)(2,1)S(1)}, bf16[2,16,128]{2,1,0:T(8,128)(2,1)S(1)}, u32[]{:S(2)}, u32[]{:S(2)}) collective-permute-start(bf16[2,16,128]{2,1,0:T(8,128)(2,1)S(1)} %slice_bitcast_fusion.refs_0_), channel_id=1, source_target_pairs={{0,67},{1,66},{2,65},{3,64},{4,71},{5,70},{6,69},{7,68},{8,75},{9,... | collective-permute-start | bytes 24584 | tf_op jit(solution)/shard_map/ppermute | solution.py:58
  36.8 1.4 collective-permute-start.10
  38.3 1.7 %collective-permute-start.8 = (bf16[2,16,128]{2,1,0:T(8,128)(2,1)S(1)}, bf16[2,16,128]{2,1,0:T(8,128)(2,1)S(1)}, u32[]{:S(2)}, u32[]{:S(2)}) collective-permute-start(bf16[2,16,128]{2,1,0:T(8,128)(2,1)S(1)} %slice_bitcast_fusion.refs_0_), channel_id=1, source_target_pairs={{0,64},{1,65},{2,66},{3,67},{4,68},{5,69},{6,70},{7,71},{8,72},{9,... | collective-permute-start | bytes 24584 | tf_op jit(solution)/shard_map/ppermute | solution.py:58
  40.0 1.5 collective-permute-start.7
  41.7 1.7 %collective-permute-start.6 = (bf16[2,16,128]{2,1,0:T(8,128)(2,1)S(1)}, bf16[2,16,128]{2,1,0:T(8,128)(2,1)S(1)}, u32[]{:S(2)}, u32[]{:S(2)}) collective-permute-start(bf16[2,16,128]{2,1,0:T(8,128)(2,1)S(1)} %slice_bitcast_fusion.refs_0_), channel_id=1, source_target_pairs={{0,2},{1,3},{2,0},{3,1},{4,6},{5,7},{6,4},{7,5},{8,10},{9,11},{10,... | collective-permute-start | bytes 24584 | tf_op jit(solution)/shard_map/ppermute | solution.py:31
  43.5 1.1 collective-permute-done.7.refs_3_
  44.6 2.3 %collective-permute-done.6.refs_2_ = bf16[2,16,128]{2,1,0:T(8,128)(2,1)S(1)} collective-permute-done((bf16[2,16,128]{2,1,0:T(8,128)(2,1)S(1)}, bf16[2,16,128]{2,1,0:T(8,128)(2,1)S(1)}, u32[]{:S(2)}, u32[]{:S(2)}) %collective-permute-start.6) | collective-permute-done | bytes 8224 | tf_op jit(solution)/shard_map/ppermute | solution.py:31
  46.9 3.8 %shard_map.325 = (bf16[512,768]{1,0:T(8,128)(2,1)}, bf16[512,256]{1,0:T(8,128)(2,1)S(1)}, f32[8,512]{1,0:T(8,128)S(1)}, bf16[256,768]{1,0:T(8,128)(2,1)S(1)}, f3...) custom-call(s32[2]{0:T(128)S(1)} %pad_add_fusion.1.index_ref, ...), custom_call_target="tpu_custom_call" | custom-call | flops 1000 | bytes 1000 | tf_op jit(solution)/shard_map/pallas_call | solution.py:87
  50.8 1.7 %collective-permute-done.12 = bf16[256,768]{1,0:T(8,128)(2,1)S(1)} collective-permute-done((bf16[256,768]{1,0:T(8,128)(2,1)S(1)}, bf16[256,768]{1,0:T(8,128)(2,1)S(1)}, u32[]{:S(2)}, u32[]{:S(2)}) %collective-permute-start.12) | collective-permute-done | bytes 393248 | tf_op jit(solution)/shard_map/ppermute | solution.py:31
  52.7 1.8 %collective-permute-start.13 = (bf16[256,768]{1,0:T(8,128)(2,1)S(1)}, bf16[256,768]{1,0:T(8,128)(2,1)S(1)}, u32[]{:S(2)}, u32[]{:S(2)}) collective-permute-start(bf16[256,768]{1,0:T(8,128)(2,1)S(1)} %pad_maximum_fusion.1), channel_id=1, source_target_pairs={{0,2},{1,3},{2,0},{3,1},{4,6},{5,7},{6,4},{7,5},{8,10},{9,11},{10,... | collective-permute-start | bytes 1179656 | tf_op jit(solution)/shard_map/ppermute | solution.py:31
  54.5 11.0 %collective-permute-done.13.far_ref = bf16[256,768]{1,0:T(8,128)(2,1)S(1)} collective-permute-done((bf16[256,768]{1,0:T(8,128)(2,1)S(1)}, bf16[256,768]{1,0:T(8,128)(2,1)S(1)}, u32[]{:S(2)}, u32[]{:S(2)}) %collective-permute-start.13) | collective-permute-done | bytes 393248 | tf_op jit(solution)/shard_map/ppermute | solution.py:31
  65.9 1.7 %collective-permute-done.14.rows_ref.hidden_other = bf16[256,768]{1,0:T(8,128)(2,1)S(1)} collective-permute-done((bf16[256,768]{1,0:T(8,128)(2,1)S(1)}, bf16[256,768]{1,0:T(8,128)(2,1)S(1)}, u32[]{:S(2)}, u32[]{:S(2)}) %collective-permute-start.14) | collective-permute-done | bytes 393248 | tf_op jit(solution)/shard_map/ppermute | solution.py:31
  67.6 1.2 all-to-all-done.1.blocks_ref
  68.8 3.1 %shard_map.327 = (bf16[256,768]{1,0:T(8,128)(2,1)S(1)}, bf16[256,768]{1,0:T(8,128)(2,1)S(1)}, bf16[256,768]{1,0:T(8,128)(2,1)S(1)}, bf16[768,768]{1,0:T(8,128)(2,1)S(1)}, bf16[768,768]{1,0:T(8,128)(2,1)S(1)}) custom-call(bf16[256,768]{1,0:T(8,128)(2,1)S(1)} %collective-permute-done.14.rows_ref.hidden_other, bf16[16,48,1536]{2,1,0:T(8,128)(2,1)} %all-to-all-done.1.blocks_ref, ...), custom_call_target="tpu_custom_call" | custom-call | flops 1000 | bytes 1000 | tf_op jit(solution)/shard_map/pallas_call | solution.py:87
  72.0 1.3 shard_map.328
  73.9 2.8 %collective-permute-start.16 = (bf16[256,768]{1,0:T(8,128)(2,1)S(1)}, bf16[256,768]{1,0:T(8,128)(2,1)S(1)}, u32[]{:S(2)}, u32[]{:S(2)}) collective-permute-start(bf16[256,768]{1,0:T(8,128)(2,1)S(1)} %pad_maximum_fusion.2), channel_id=1, source_target_pairs={{0,2},{1,3},{2,0},{3,1},{4,6},{5,7},{6,4},{7,5},{8,10},{9,11},{10,... | collective-permute-start | bytes 1179656 | tf_op jit(solution)/shard_map/ppermute | solution.py:31
  76.7 10.1 %collective-permute-done.16.far_ref = bf16[256,768]{1,0:T(8,128)(2,1)S(1)} collective-permute-done((bf16[256,768]{1,0:T(8,128)(2,1)S(1)}, bf16[256,768]{1,0:T(8,128)(2,1)S(1)}, u32[]{:S(2)}, u32[]{:S(2)}) %collective-permute-start.16) | collective-permute-done | bytes 393248 | tf_op jit(solution)/shard_map/ppermute | solution.py:31
  86.8 1.2 shard_map.329
  88.0 1.2 shard_map.330
  90.1 2.0 %shard_map.331 = (bf16[256,768]{1,0:T(8,128)(2,1)S(1)}, bf16[256,768]{1,0:T(8,128)(2,1)}, f32[1,768]{1,0:T(1,128)S(1)}) custom-call(bf16[256,768]{1,0:T(8,128)(2,1)S(1)} %collective-permute-done.17.rows_ref.branch_other, bf16[768,768]{1,0:T(8,128)(2,1)S(1)} %get-tuple-element.79.up_ref, bf16[768,768]{1,0:T(8,128)(2,1)S(1)} %get-tuple-element.80.down_ref, ...), custom_call_target="tpu_custom_call" | custom-call | flops 1000 | bytes 1000 | tf_op jit(solution)/shard_map/pallas_call | solution.py:87
  93.2 2.5 %shard_map.337 = bf16[16,48,1536]{2,1,0:T(8,128)(2,1)} custom-call(bf16[256,768]{1,0:T(8,128)(2,1)S(1)} %get-tuple-element.76.rows_ref.first_ref.hidden_near, bf16[256,768]{1,0:T(8,128)(2,1)S(1)} %collective-permute-done.14.rows_ref.hidden_other, bf16[256,768]{1,0:T(8,128)(2,1)S(1)} %get-tuple-element.84.rows_ref.second_ref.branch_near, ...), custom_call_target="tpu_custom_call" | custom-call | flops 1000 | bytes 1000 | tf_op jit(solution)/shard_map/pallas_call | solution.py:87
  95.7 6.1 %all-to-all-start.3 = ((bf16[16,48,1536]{2,1,0:T(8,128)(2,1)}), bf16[16,48,1536]{2,1,0:T(8,128)(2,1)S(1)}, u32[]{:S(2)}, u32[]{:S(2)}) async-start(bf16[16,48,1536]{2,1,0:T(8,128)(2,1)} %shard_map.337), calls=%async_computation.3 | async-start | bytes 4718592 | tf_op jit(solution)/shard_map/all_to_all | solution.py:48
  101.8 1.3 fusion.2
  103.3 2.6 %collective-permute-start.19 = (bf16[256,768]{1,0:T(8,128)(2,1)S(1)}, bf16[256,768]{1,0:T(8,128)(2,1)S(1)}, u32[]{:S(2)}, u32[]{:S(2)}) collective-permute-start(bf16[256,768]{1,0:T(8,128)(2,1)S(1)} %pad_maximum_fusion.3), channel_id=1, source_target_pairs={{0,2},{1,3},{2,0},{3,1},{4,6},{5,7},{6,4},{7,5},{8,10},{9,11},{10,... | collective-permute-start | bytes 1179656 | tf_op jit(solution)/shard_map/ppermute | solution.py:31
  105.9 9.7 %collective-permute-done.19.far_ref = bf16[256,768]{1,0:T(8,128)(2,1)S(1)} collective-permute-done((bf16[256,768]{1,0:T(8,128)(2,1)S(1)}, bf16[256,768]{1,0:T(8,128)(2,1)S(1)}, u32[]{:S(2)}, u32[]{:S(2)}) %collective-permute-start.19) | collective-permute-done | bytes 393248 | tf_op jit(solution)/shard_map/ppermute | solution.py:31
  117.0 1.7 %collective-permute-done.20.other_ref = bf16[256,768]{1,0:T(8,128)(2,1)S(1)} collective-permute-done((bf16[256,768]{1,0:T(8,128)(2,1)S(1)}, bf16[256,768]{1,0:T(8,128)(2,1)S(1)}, u32[]{:S(2)}, u32[]{:S(2)}) %collective-permute-start.20) | collective-permute-done | bytes 393248 | tf_op jit(solution)/shard_map/ppermute | solution.py:31
  118.7 3.8 %shard_map.333 = (bf16[512,768]{1,0:T(8,128)(2,1)S(1)}, bf16[256,768]{1,0:T(8,128)(2,1)S(1)}, f32[256,768]{1,0:T(8,128)S(1)}, f32[16,768]{1,0:T(8,128)S(1)}) custom-call(s32[1]{0:T(128)} %bitcast.1.index_ref, bf16[256,768]{1,0:T(8,128)(2,1)S(1)} %get-tuple-element.94.near_ref, bf16[256,768]{1,0:T(8,128)(2,1)S(1)} %collective-permute-done.20.other_ref, ...), custom_call_target="tpu_custom_call" | custom-call | flops 1000 | bytes 1000 | tf_op jit(solution)/shard_map/pallas_call | solution.py:87
  122.7 1.6 collective-permute-done.21
  124.4 2.6 %collective-permute-start.22 = (bf16[128,768]{1,0:T(8,128)(2,1)S(1)}, bf16[128,768]{1,0:T(8,128)(2,1)S(1)}, u32[]{:S(2)}, u32[]{:S(2)}) collective-permute-start(bf16[128,768]{1,0:T(8,128)(2,1)S(1)} %slice.87), channel_id=1, source_target_pairs={{0,2},{1,3},{2,0},{3,1},{4,6},{5,7},{6,4},{7,5},{8,10},{9,11},{10,... | collective-permute-start | bytes 589832 | tf_op jit(solution)/shard_map/ppermute | solution.py:31
  127.5 2.5 %collective-permute-start.24 = (bf16[16,768]{1,0:T(8,128)(2,1)S(1)}, bf16[16,768]{1,0:T(8,128)(2,1)S(1)}, u32[]{:S(2)}, u32[]{:S(2)}) collective-permute-start(bf16[16,768]{1,0:T(8,128)(2,1)S(1)} %convert_element_type.41), channel_id=1, source_target_pairs={{0,2},{1,3},{2,0},{3,1},{4,6},{5,7},{6,4},{7,5},{8,10},{9,11},{10,... | collective-permute-start | bytes 73736 | tf_op jit(solution)/shard_map/ppermute | solution.py:31
  130.4 2.1 %shard_map.334.block_ref = bf16[768,896]{1,0:T(8,128)(2,1)} custom-call(bf16[256,768]{1,0:T(8,128)(2,1)S(1)} %pad_maximum_fusion.near_ref.tokens_ref.tokens_near, bf16[256,768]{1,0:T(8,128)(2,1)S(1)} %copy-done.1, bf16[256,768]{1,0:T(8,128)(2,1)S(1)} %get-tuple-element.94.near_ref, bf16[256,768]{1,0:T(8,128)(2,1)S(1)} %collective-permute-done.20.other_ref, ...), custom_call_target="tpu_custom_call" | custom-call | flops 1000 | bytes 1000 | tf_op jit(solution)/shard_map/pallas_call | solution.py:87
  132.7 1.3 collective-permute-done.24.far_ref
  134.9 1.1 all-to-all-done.3.blocks_ref
  136.0 6.3 %all-to-all-start.2 = ((bf16[32,24,896]{2,1,0:T(8,128)(2,1)}), bf16[32,24,896]{2,1,0:T(8,128)(2,1)}, u32[]{:S(2)}, u32[]{:S(2)}) async-start(bf16[32,24,896]{2,1,0:T(8,128)(2,1)} %bitcast.39), calls=%async_computation.2 | async-start | bytes 2752512 | tf_op jit(solution)/shard_map/all_to_all | solution.py:39
  142.6 1.8 %collective-permute-start.26 = (bf16[24,1536]{1,0:T(8,128)(2,1)S(1)}, bf16[24,1536]{1,0:T(8,128)(2,1)S(1)}, u32[]{:S(2)}, u32[]{:S(2)}) collective-permute-start(bf16[24,1536]{1,0:T(8,128)(2,1)S(1)} %get-tuple-element.114), channel_id=1, source_target_pairs={{0,64},{1,65},{2,66},{3,67},{4,68},{5,69},{6,70},{7,71},{8,72},{9,... | collective-permute-start | bytes 221192 | tf_op jit(solution)/shard_map/ppermute | solution.py:58
  145.2 14.6 %collective-permute-done.26 = bf16[24,1536]{1,0:T(8,128)(2,1)S(1)} collective-permute-done((bf16[24,1536]{1,0:T(8,128)(2,1)S(1)}, bf16[24,1536]{1,0:T(8,128)(2,1)S(1)}, u32[]{:S(2)}, u32[]{:S(2)}) %collective-permute-start.26) | collective-permute-done | bytes 73760 | tf_op jit(solution)/shard_map/ppermute | solution.py:58
  160.4 2.1 %all-to-all-done.2.blocks_ref = bf16[32,24,896]{2,1,0:T(8,128)(2,1)} async-done(((bf16[32,24,896]{2,1,0:T(8,128)(2,1)}), bf16[32,24,896]{2,1,0:T(8,128)(2,1)}, u32[]{:S(2)}, u32[]{:S(2)}) %all-to-all-start.2) | async-done | bytes 1376288 | tf_op jit(solution)/shard_map/all_to_all | solution.py:39
  162.5 2.3 %shard_map.336 = (f32[24,192]{1,0:T(8,128)}, f32[24,192]{1,0:T(8,128)}, f32[24,192]{1,0:T(8,128)}, f32[24,192]{1,0:T(8,128)}, f32[1,6]{1,0:T(1,128)}, /*index=5*...) custom-call(s32[1]{0:T(128)} %bitcast.1.index_ref, ...), custom_call_target="tpu_custom_call" | custom-call | flops 1000 | bytes 1000 | tf_op jit(solution)/shard_map/pallas_call | solution.py:87
  (123 shorter events, 11.5 us)
Async XLA Ops:
  0.7 16.0 %copy-start.29 = (s32[4]{0:T(128)S(1)}, s32[4]{0:T(128)}, u32[]{:S(2)}) copy-start(s32[4]{0:T(128)} %constant.82) | copy-start | bytes 52
  0.7 16.0 %copy-start.30 = (s32[4]{0:T(128)S(1)}, s32[4]{0:T(128)}, u32[]{:S(2)}) copy-start(s32[4]{0:T(128)} %constant.81) | copy-start | bytes 52
  0.7 10.8 %copy-start.28 = (bf16[24,768]{1,0:T(8,128)(2,1)S(1)}, bf16[24,768]{1,0:T(8,128)(2,1)}, u32[]{:S(2)}) copy-start(bf16[24,768]{1,0:T(8,128)(2,1)} %param.27) | copy-start | bytes 110596
  0.7 12.4 %copy-start.25 = (bf16[1,128,768]{2,1,0:T(8,128)(2,1)S(1)}, bf16[1,128,768]{2,1,0:T(8,128)(2,1)}, u32[]{:S(2)}) copy-start(bf16[1,128,768]{2,1,0:T(8,128)(2,1)} %param.20) | copy-start | bytes 589828
  0.7 15.3 %copy-start.13 = (bf16[1,128,768]{2,1,0:T(8,128)(2,1)S(1)}, bf16[1,128,768]{2,1,0:T(8,128)(2,1)}, u32[]{:S(2)}) copy-start(bf16[1,128,768]{2,1,0:T(8,128)(2,1)} %param.37) | copy-start | bytes 589828
  0.7 16.0 %copy-start.26 = (s32[1,512]{1,0:T(1,128)S(1)}, s32[1,512]{1,0:T(1,128)}, u32[]{:S(2)}) copy-start(s32[1,512]{1,0:T(1,128)} %param.21) | copy-start | bytes 6148
  3.5 21.2 %all-to-all-start = ((bf16[16,24,896]{2,1,0:T(8,128)(2,1)}), bf16[16,24,896]{2,1,0:T(8,128)(2,1)S(1)}, u32[]{:S(2)}, u32[]{:S(2)}) async-start(bf16[16,24,896]{2,1,0:T(8,128)(2,1)} %shard_map.323), calls=%async_computation | async-start | bytes 1376256 | tf_op jit(solution)/shard_map/all_to_all | solution.py:48
  11.5 6.4 %collective-permute-start.3 = (bf16[24,1536]{1,0:T(8,128)(2,1)S(1)}, bf16[24,1536]{1,0:T(8,128)(2,1)S(1)}, u32[]{:S(2)}, u32[]{:S(2)}) collective-permute-start(bf16[24,1536]{1,0:T(8,128)(2,1)S(1)} %constant_dynamic-update-slice_fusion.own_ref), channel_id=1, source_target_pairs={{0,64},{1,65},{2,66},{3,67},{4,68},{5,69},{6,70},{7,71},{8,72},{9,... | collective-permute-start | bytes 221192 | tf_op jit(solution)/shard_map/ppermute | solution.py:58
  13.1 13.1 %collective-permute-start = (bf16[128,768]{1,0:T(8,128)(2,1)S(1)}, bf16[128,768]{1,0:T(8,128)(2,1)S(1)}, u32[]{:S(2)}, u32[]{:S(2)}) collective-permute-start(bf16[128,768]{1,0:T(8,128)(2,1)S(1)} %bitcast.40), channel_id=1, source_target_pairs={{0,2},{1,3},{2,0},{3,1},{4,6},{5,7},{6,4},{7,5},{8,10},{9,11},{10,... | collective-permute-start | bytes 589832 | tf_op jit(solution)/shard_map/ppermute | solution.py:31
  16.0 10.2 %collective-permute-start.1 = (bf16[128,768]{1,0:T(8,128)(2,1)S(1)}, bf16[128,768]{1,0:T(8,128)(2,1)S(1)}, u32[]{:S(2)}, u32[]{:S(2)}) collective-permute-start(bf16[128,768]{1,0:T(8,128)(2,1)S(1)} %bitcast.34), channel_id=1, source_target_pairs={{0,2},{1,3},{2,0},{3,1},{4,6},{5,7},{6,4},{7,5},{8,10},{9,11},{10,... | collective-permute-start | bytes 589832 | tf_op jit(solution)/shard_map/ppermute | solution.py:31
  24.7 22.2 %collective-permute-start.4 = (bf16[16,24,896]{2,1,0:T(8,128)(2,1)S(1)}, bf16[16,24,896]{2,1,0:T(8,128)(2,1)S(1)}, u32[]{:S(2)}, u32[]{:S(2)}) collective-permute-start(bf16[16,24,896]{2,1,0:T(8,128)(2,1)S(1)} %all-to-all-done), channel_id=1, source_target_pairs={{0,64},{1,65},{2,66},{3,67},{4,68},{5,69},{6,70},{7,71},{8,72},{9,... | collective-permute-start | bytes 2064392 | tf_op jit(solution)/shard_map/ppermute | solution.py:58
  27.0 11.3 %collective-permute-start.2 = (bf16[256,768]{1,0:T(8,128)(2,1)S(1)}, bf16[256,768]{1,0:T(8,128)(2,1)S(1)}, u32[]{:S(2)}, u32[]{:S(2)}) collective-permute-start(bf16[256,768]{1,0:T(8,128)(2,1)S(1)} %pad_maximum_fusion.near_ref.tokens_ref.tokens_near), channel_id=1, source_target_pairs={{0,1},{1,0},{2,3},{3,2},{4,5},{5,4},{6,7},{7,6},{8,9},{9,8},{10,11... | collective-permute-start | bytes 1179656 | tf_op jit(solution)/shard_map/ppermute | solution.py:31
  27.1 41.7 %all-to-all-start.1 = ((bf16[16,48,1536]{2,1,0:T(8,128)(2,1)}), bf16[16,48,1536]{2,1,0:T(8,128)(2,1)}, u32[]{:S(2)}, u32[]{:S(2)}) async-start(bf16[16,48,1536]{2,1,0:T(8,128)(2,1)} %shard_map.324), calls=%async_computation.1 | async-start | bytes 4718592 | tf_op jit(solution)/shard_map/all_to_all | solution.py:48
  35.1 4.9 %collective-permute-start.11 = (bf16[2,16,128]{2,1,0:T(8,128)(2,1)S(1)}, bf16[2,16,128]{2,1,0:T(8,128)(2,1)S(1)}, u32[]{:S(2)}, u32[]{:S(2)}) collective-permute-start(bf16[2,16,128]{2,1,0:T(8,128)(2,1)S(1)} %slice_bitcast_fusion.refs_0_), channel_id=1, source_target_pairs={{0,67},{1,66},{2,65},{3,64},{4,71},{5,70},{6,69},{7,68},{8,75},{9,... | collective-permute-start | bytes 24584 | tf_op jit(solution)/shard_map/ppermute | solution.py:58
  36.8 4.9 %collective-permute-start.10 = (bf16[2,16,128]{2,1,0:T(8,128)(2,1)S(1)}, bf16[2,16,128]{2,1,0:T(8,128)(2,1)S(1)}, u32[]{:S(2)}, u32[]{:S(2)}) collective-permute-start(bf16[2,16,128]{2,1,0:T(8,128)(2,1)S(1)} %slice_bitcast_fusion.refs_0_), channel_id=1, source_target_pairs={{0,66},{1,67},{2,64},{3,65},{4,70},{5,71},{6,68},{7,69},{8,74},{9,... | collective-permute-start | bytes 24584 | tf_op jit(solution)/shard_map/ppermute | solution.py:58
  38.3 5.1 %collective-permute-start.9 = (bf16[2,16,128]{2,1,0:T(8,128)(2,1)S(1)}, bf16[2,16,128]{2,1,0:T(8,128)(2,1)S(1)}, u32[]{:S(2)}, u32[]{:S(2)}) collective-permute-start(bf16[2,16,128]{2,1,0:T(8,128)(2,1)S(1)} %slice_bitcast_fusion.refs_0_), channel_id=1, source_target_pairs={{0,65},{1,64},{2,67},{3,66},{4,69},{5,68},{6,71},{7,70},{8,73},{9,... | collective-permute-start | bytes 24584 | tf_op jit(solution)/shard_map/ppermute | solution.py:58
  38.3 14.3 %copy-start = (bf16[256,768]{1,0:T(8,128)(2,1)}, bf16[256,768]{1,0:T(8,128)(2,1)S(1)}, u32[]{:S(2)}) copy-start(bf16[256,768]{1,0:T(8,128)(2,1)S(1)} %collective-permute-done.2.other_ref.tokens_other) | copy-start | bytes 1179652
  38.3 5.2 %collective-permute-start.8 = (bf16[2,16,128]{2,1,0:T(8,128)(2,1)S(1)}, bf16[2,16,128]{2,1,0:T(8,128)(2,1)S(1)}, u32[]{:S(2)}, u32[]{:S(2)}) collective-permute-start(bf16[2,16,128]{2,1,0:T(8,128)(2,1)S(1)} %slice_bitcast_fusion.refs_0_), channel_id=1, source_target_pairs={{0,64},{1,65},{2,66},{3,67},{4,68},{5,69},{6,70},{7,71},{8,72},{9,... | collective-permute-start | bytes 24584 | tf_op jit(solution)/shard_map/ppermute | solution.py:58
  40.0 4.6 %collective-permute-start.7 = (bf16[2,16,128]{2,1,0:T(8,128)(2,1)S(1)}, bf16[2,16,128]{2,1,0:T(8,128)(2,1)S(1)}, u32[]{:S(2)}, u32[]{:S(2)}) collective-permute-start(bf16[2,16,128]{2,1,0:T(8,128)(2,1)S(1)} %slice_bitcast_fusion.refs_0_), channel_id=1, source_target_pairs={{0,3},{1,2},{2,1},{3,0},{4,7},{5,6},{6,5},{7,4},{8,11},{9,10},{10,... | collective-permute-start | bytes 24584 | tf_op jit(solution)/shard_map/ppermute | solution.py:31
  41.7 5.2 %collective-permute-start.6 = (bf16[2,16,128]{2,1,0:T(8,128)(2,1)S(1)}, bf16[2,16,128]{2,1,0:T(8,128)(2,1)S(1)}, u32[]{:S(2)}, u32[]{:S(2)}) collective-permute-start(bf16[2,16,128]{2,1,0:T(8,128)(2,1)S(1)} %slice_bitcast_fusion.refs_0_), channel_id=1, source_target_pairs={{0,2},{1,3},{2,0},{3,1},{4,6},{5,7},{6,4},{7,5},{8,10},{9,11},{10,... | collective-permute-start | bytes 24584 | tf_op jit(solution)/shard_map/ppermute | solution.py:31
  43.4 3.5 %collective-permute-start.5 = (bf16[2,16,128]{2,1,0:T(8,128)(2,1)S(1)}, bf16[2,16,128]{2,1,0:T(8,128)(2,1)S(1)}, u32[]{:S(2)}, u32[]{:S(2)}) collective-permute-start(bf16[2,16,128]{2,1,0:T(8,128)(2,1)S(1)} %slice_bitcast_fusion.refs_0_), channel_id=1, source_target_pairs={{0,1},{1,0},{2,3},{3,2},{4,5},{5,4},{6,7},{7,6},{8,9},{9,8},{10,11... | collective-permute-start | bytes 24584 | tf_op jit(solution)/shard_map/ppermute | solution.py:31
  50.7 14.8 %copy-start.10 = (f32[8,768]{1,0:T(8,128)}, f32[8,768]{1,0:T(8,128)S(1)}, u32[]{:S(2)}) copy-start(f32[8,768]{1,0:T(8,128)S(1)} %get-tuple-element.75.rows_ref) | copy-start | bytes 73732
  50.7 1.8 %collective-permute-start.12 = (bf16[256,768]{1,0:T(8,128)(2,1)S(1)}, bf16[256,768]{1,0:T(8,128)(2,1)S(1)}, u32[]{:S(2)}, u32[]{:S(2)}) collective-permute-start(bf16[256,768]{1,0:T(8,128)(2,1)S(1)} %get-tuple-element.74), channel_id=1, source_target_pairs={{0,1},{1,0},{2,3},{3,2},{4,5},{5,4},{6,7},{7,6},{8,9},{9,8},{10,11... | collective-permute-start | bytes 1179656 | tf_op jit(solution)/shard_map/ppermute | solution.py:31
  52.7 12.7 %collective-permute-start.13 = (bf16[256,768]{1,0:T(8,128)(2,1)S(1)}, bf16[256,768]{1,0:T(8,128)(2,1)S(1)}, u32[]{:S(2)}, u32[]{:S(2)}) collective-permute-start(bf16[256,768]{1,0:T(8,128)(2,1)S(1)} %pad_maximum_fusion.1), channel_id=1, source_target_pairs={{0,2},{1,3},{2,0},{3,1},{4,6},{5,7},{6,4},{7,5},{8,10},{9,11},{10,... | collective-permute-start | bytes 1179656 | tf_op jit(solution)/shard_map/ppermute | solution.py:31
  65.9 1.8 %collective-permute-start.14 = (bf16[256,768]{1,0:T(8,128)(2,1)S(1)}, bf16[256,768]{1,0:T(8,128)(2,1)S(1)}, u32[]{:S(2)}, u32[]{:S(2)}) collective-permute-start(bf16[256,768]{1,0:T(8,128)(2,1)S(1)} %get-tuple-element.76.rows_ref.first_ref.hidden_near), channel_id=1, source_target_pairs={{0,1},{1,0},{2,3},{3,2},{4,5},{5,4},{6,7},{7,6},{8,9},{9,8},{10,11... | collective-permute-start | bytes 1179656 | tf_op jit(solution)/shard_map/ppermute | solution.py:31
  71.9 1.8 %collective-permute-start.15 = (bf16[256,768]{1,0:T(8,128)(2,1)S(1)}, bf16[256,768]{1,0:T(8,128)(2,1)S(1)}, u32[]{:S(2)}, u32[]{:S(2)}) collective-permute-start(bf16[256,768]{1,0:T(8,128)(2,1)S(1)} %get-tuple-element.82), channel_id=1, source_target_pairs={{0,1},{1,0},{2,3},{3,2},{4,5},{5,4},{6,7},{7,6},{8,9},{9,8},{10,11... | collective-permute-start | bytes 1179656 | tf_op jit(solution)/shard_map/ppermute | solution.py:31
  73.8 13.0 %copy-start.11 = (f32[8,768]{1,0:T(8,128)S(1)}, f32[8,768]{1,0:T(8,128)}, u32[]{:S(2)}) copy-start(f32[8,768]{1,0:T(8,128)} %copy-done.10) | copy-start | bytes 73732
  73.8 13.0 %copy-start.14 = (bf16[1,128,768]{2,1,0:T(8,128)(2,1)S(1)}, bf16[1,128,768]{2,1,0:T(8,128)(2,1)}, u32[]{:S(2)}) copy-start(bf16[1,128,768]{2,1,0:T(8,128)(2,1)} %param.37) | copy-start | bytes 589828
  73.8 13.0 %copy-start.16 = (bf16[128,768]{1,0:T(8,128)(2,1)S(1)}, bf16[128,768]{1,0:T(8,128)(2,1)}, u32[]{:S(2)}) copy-start(bf16[128,768]{1,0:T(8,128)(2,1)} %copy-done.15) | copy-start | bytes 589828
  73.9 12.9 %collective-permute-start.16 = (bf16[256,768]{1,0:T(8,128)(2,1)S(1)}, bf16[256,768]{1,0:T(8,128)(2,1)S(1)}, u32[]{:S(2)}, u32[]{:S(2)}) collective-permute-start(bf16[256,768]{1,0:T(8,128)(2,1)S(1)} %pad_maximum_fusion.2), channel_id=1, source_target_pairs={{0,2},{1,3},{2,0},{3,1},{4,6},{5,7},{6,4},{7,5},{8,10},{9,11},{10,... | collective-permute-start | bytes 1179656 | tf_op jit(solution)/shard_map/ppermute | solution.py:31
  88.0 2.1 %collective-permute-start.17 = (bf16[256,768]{1,0:T(8,128)(2,1)S(1)}, bf16[256,768]{1,0:T(8,128)(2,1)S(1)}, u32[]{:S(2)}, u32[]{:S(2)}) collective-permute-start(bf16[256,768]{1,0:T(8,128)(2,1)S(1)} %get-tuple-element.84.rows_ref.second_ref.branch_near), channel_id=1, source_target_pairs={{0,1},{1,0},{2,3},{3,2},{4,5},{5,4},{6,7},{7,6},{8,9},{9,8},{10,11... | collective-permute-start | bytes 1179656 | tf_op jit(solution)/shard_map/ppermute | solution.py:31
  92.7 9.1 %collective-permute-start.18 = (bf16[256,768]{1,0:T(8,128)(2,1)}, bf16[256,768]{1,0:T(8,128)(2,1)}, u32[]{:S(2)}, u32[]{:S(2)}) collective-permute-start(bf16[256,768]{1,0:T(8,128)(2,1)} %get-tuple-element.90), channel_id=1, source_target_pairs={{0,1},{1,0},{2,3},{3,2},{4,5},{5,4},{6,7},{7,6},{8,9},{9,8},{10,11... | collective-permute-start | bytes 1179656 | tf_op jit(solution)/shard_map/ppermute | solution.py:31
  95.7 40.3 %all-to-all-start.3 = ((bf16[16,48,1536]{2,1,0:T(8,128)(2,1)}), bf16[16,48,1536]{2,1,0:T(8,128)(2,1)S(1)}, u32[]{:S(2)}, u32[]{:S(2)}) async-start(bf16[16,48,1536]{2,1,0:T(8,128)(2,1)} %shard_map.337), calls=%async_computation.3 | async-start | bytes 4718592 | tf_op jit(solution)/shard_map/all_to_all | solution.py:48
  103.2 12.5 %copy-start.12 = (f32[8,768]{1,0:T(8,128)S(1)}, f32[8,768]{1,0:T(8,128)}, u32[]{:S(2)}) copy-start(f32[8,768]{1,0:T(8,128)} %copy-done.10) | copy-start | bytes 73732
  103.2 12.5 %copy-start.18 = (f32[8,768]{1,0:T(8,128)S(1)}, f32[8,768]{1,0:T(8,128)}, u32[]{:S(2)}) copy-start(f32[8,768]{1,0:T(8,128)} %copy-done.17) | copy-start | bytes 73732
  103.2 15.5 %copy-start.3 = (bf16[768,768]{1,0:T(8,128)(2,1)S(1)}, bf16[768,768]{1,0:T(8,128)(2,1)}, u32[]{:S(2)}) copy-start(bf16[768,768]{1,0:T(8,128)(2,1)} %copy-done.2) | copy-start | bytes 3538948
  103.2 15.5 %copy-start.4 = (bf16[512,768]{1,0:T(8,128)(2,1)S(1)}, bf16[512,768]{1,0:T(8,128)(2,1)}, u32[]{:S(2)}) copy-start(bf16[512,768]{1,0:T(8,128)(2,1)} %get-tuple-element.95.qkv_ref) | copy-start | bytes 2359300
  103.2 15.5 %copy-start.20 = (f32[8,512]{1,0:T(8,128)S(1)}, f32[8,512]{1,0:T(8,128)}, u32[]{:S(2)}) copy-start(f32[8,512]{1,0:T(8,128)} %copy-done.19) | copy-start | bytes 49156
  103.3 15.4 %copy-start.22 = (f32[1,768]{1,0:T(1,128)S(1)}, f32[1,768]{1,0:T(1,128)}, u32[]{:S(2)}) copy-start(f32[1,768]{1,0:T(1,128)} %copy-done.21) | copy-start | bytes 9220
  103.3 12.3 %collective-permute-start.19 = (bf16[256,768]{1,0:T(8,128)(2,1)S(1)}, bf16[256,768]{1,0:T(8,128)(2,1)S(1)}, u32[]{:S(2)}, u32[]{:S(2)}) collective-permute-start(bf16[256,768]{1,0:T(8,128)(2,1)S(1)} %pad_maximum_fusion.3), channel_id=1, source_target_pairs={{0,2},{1,3},{2,0},{3,1},{4,6},{5,7},{6,4},{7,5},{8,10},{9,11},{10,... | collective-permute-start | bytes 1179656 | tf_op jit(solution)/shard_map/ppermute | solution.py:31
  117.0 1.7 %collective-permute-start.20 = (bf16[256,768]{1,0:T(8,128)(2,1)S(1)}, bf16[256,768]{1,0:T(8,128)(2,1)S(1)}, u32[]{:S(2)}, u32[]{:S(2)}) collective-permute-start(bf16[256,768]{1,0:T(8,128)(2,1)S(1)} %get-tuple-element.94.near_ref), channel_id=1, source_target_pairs={{0,1},{1,0},{2,3},{3,2},{4,5},{5,4},{6,7},{7,6},{8,9},{9,8},{10,11... | collective-permute-start | bytes 1179656 | tf_op jit(solution)/shard_map/ppermute | solution.py:31
  122.5 1.8 %collective-permute-start.21 = (bf16[256,768]{1,0:T(8,128)(2,1)S(1)}, bf16[256,768]{1,0:T(8,128)(2,1)S(1)}, u32[]{:S(2)}, u32[]{:S(2)}) collective-permute-start(bf16[256,768]{1,0:T(8,128)(2,1)S(1)} %get-tuple-element.102), channel_id=1, source_target_pairs={{0,1},{1,0},{2,3},{3,2},{4,5},{5,4},{6,7},{7,6},{8,9},{9,8},{10,11... | collective-permute-start | bytes 1179656 | tf_op jit(solution)/shard_map/ppermute | solution.py:31
  124.4 10.4 %collective-permute-start.22 = (bf16[128,768]{1,0:T(8,128)(2,1)S(1)}, bf16[128,768]{1,0:T(8,128)(2,1)S(1)}, u32[]{:S(2)}, u32[]{:S(2)}) collective-permute-start(bf16[128,768]{1,0:T(8,128)(2,1)S(1)} %slice.87), channel_id=1, source_target_pairs={{0,2},{1,3},{2,0},{3,1},{4,6},{5,7},{6,4},{7,5},{8,10},{9,11},{10,... | collective-permute-start | bytes 589832 | tf_op jit(solution)/shard_map/ppermute | solution.py:31
  127.0 5.6 %collective-permute-start.25 = (bf16[16,768]{1,0:T(8,128)(2,1)S(1)}, bf16[16,768]{1,0:T(8,128)(2,1)S(1)}, u32[]{:S(2)}, u32[]{:S(2)}) collective-permute-start(bf16[16,768]{1,0:T(8,128)(2,1)S(1)} %convert_element_type.41), channel_id=1, source_target_pairs={{0,3},{1,2},{2,1},{3,0},{4,7},{5,6},{6,5},{7,4},{8,11},{9,10},{10,... | collective-permute-start | bytes 73736 | tf_op jit(solution)/shard_map/ppermute | solution.py:31
  127.5 6.5 %collective-permute-start.24 = (bf16[16,768]{1,0:T(8,128)(2,1)S(1)}, bf16[16,768]{1,0:T(8,128)(2,1)S(1)}, u32[]{:S(2)}, u32[]{:S(2)}) collective-permute-start(bf16[16,768]{1,0:T(8,128)(2,1)S(1)} %convert_element_type.41), channel_id=1, source_target_pairs={{0,2},{1,3},{2,0},{3,1},{4,6},{5,7},{6,4},{7,5},{8,10},{9,11},{10,... | collective-permute-start | bytes 73736 | tf_op jit(solution)/shard_map/ppermute | solution.py:31
  130.0 4.0 %collective-permute-start.23 = (bf16[16,768]{1,0:T(8,128)(2,1)S(1)}, bf16[16,768]{1,0:T(8,128)(2,1)S(1)}, u32[]{:S(2)}, u32[]{:S(2)}) collective-permute-start(bf16[16,768]{1,0:T(8,128)(2,1)S(1)} %convert_element_type.41), channel_id=1, source_target_pairs={{0,1},{1,0},{2,3},{3,2},{4,5},{5,4},{6,7},{7,6},{8,9},{9,8},{10,11... | collective-permute-start | bytes 73736 | tf_op jit(solution)/shard_map/ppermute | solution.py:31
  136.0 26.5 %all-to-all-start.2 = ((bf16[32,24,896]{2,1,0:T(8,128)(2,1)}), bf16[32,24,896]{2,1,0:T(8,128)(2,1)}, u32[]{:S(2)}, u32[]{:S(2)}) async-start(bf16[32,24,896]{2,1,0:T(8,128)(2,1)} %bitcast.39), calls=%async_computation.2 | async-start | bytes 2752512 | tf_op jit(solution)/shard_map/all_to_all | solution.py:39
  142.6 17.2 %collective-permute-start.26 = (bf16[24,1536]{1,0:T(8,128)(2,1)S(1)}, bf16[24,1536]{1,0:T(8,128)(2,1)S(1)}, u32[]{:S(2)}, u32[]{:S(2)}) collective-permute-start(bf16[24,1536]{1,0:T(8,128)(2,1)S(1)} %get-tuple-element.114), channel_id=1, source_target_pairs={{0,64},{1,65},{2,66},{3,67},{4,68},{5,69},{6,70},{7,71},{8,72},{9,... | collective-permute-start | bytes 221192 | tf_op jit(solution)/shard_map/ppermute | solution.py:58
  (14 other events, 49.2 us)

commit v8 on v7

--- a/solution.py
+++ b/solution.py
@@ -145,12 +145,12 @@
 
 
 def unpack_lines(index, lower, line_refs, vector_ref, columns, width):
-    devices, size = line_refs[0].shape[1:]
+    devices, size = line_refs[0].shape[2:]
     devices = 2 * devices
     each = width // (4 * devices)
     flipped = []
     for part in range(2):
-        near = [ref[part].astype(FULL) for ref in line_refs]
+        near = [ref[far, part].astype(FULL) for far in range(2) for ref in line_refs]
         ordered = []
         for at in range(8):
             row = near[7]
@@ -202,7 +202,7 @@
     segment_ref,
     *refs,
 ):
-    line_refs = refs[:8]
+    line_refs = refs[:4]
     (
         qkv_out,
         mixed_ref,
@@ -214,7 +214,7 @@
         weight_ref,
         qkv_ref,
         qkv_sem,
-    ) = refs[8:]
+    ) = refs[4:]
     index, lower = index_ref[0], index_ref[1]
     half = near_ref.shape[0]
     columns = 3 * HEAD_DIM
@@ -755,7 +755,7 @@
     second_side = side(second_own)
     tokens_pair = jnp.concatenate([tokens, tokens_far], axis=0)
     cotangent_far = swap(cotangent, 2)
-    tokens_core = swap(after(tokens_pair, cotangent_far), 1)
+    tokens_core = swap(tokens_pair, 1)
     segment_row = ordered_segments(segments[0], my_index)[None]
     (second_block,) = call(
         second_block_kernel,
@@ -767,9 +767,12 @@
     )
     first_half, second_block = lax.optimization_barrier((first_half, second_block))
     first_other = side(first_half)
-    lines = first_half[:, : 2 * line_count, 3 * GROUP :]
-    lines = lines.reshape(dp_count // 2, 2, line_size).transpose(1, 0, 2)
-    lines = [lines] + [swap(lines, mask) for mask in (1, 2, 3)] + [side(lines, m) for m in range(4)]
+    lines = jnp.stack(
+        [half_rows[:, : 2 * line_count, 3 * GROUP :] for half_rows in (first_half, first_other)]
+    )
+    lines = lines.reshape(2, dp_count // 2, 2, line_size).transpose(0, 2, 1, 3)
+    lines = [lines] + [swap(lines, mask) for mask in (1, 2, 3)]
+    segment_row = after(segment_row, cotangent_far)
     second_full = plane(second_block)
 
     qkv_rows, mixed_rows, log_totals, attn_send, attn_keep, rows, bias_up, first_full = call(

time: 165 us -> 165 us (level)
  starting transfers between devices: 59 us -> 47.6 us
  waiting for transfers between devices: 67.1 us -> 78 us
    ppermute x7 -> x3, waiting for transfers between devices: 14.8 us -> 23.9 us  [side(): return lax.ppermute(values, ('dp', 'tensor'), pairs)]
    ppermute x7 -> x3, starting transfers between devices: 9.9 us -> 5.12 us  [side(): return lax.ppermute(values, ('dp', 'tensor'), pairs)]
    all_to_all x3, starting transfers between devices: 22.1 us -> 17.4 us  [plane(): lax.all_to_all(stacked, 'dp', 0, 0, tiled=True, axis_index_groups=plane_g...]
    ppermute x20, waiting for transfers between devices: 42.8 us -> 45.8 us  [swap(): return lax.ppermute(values, 'tensor', [(i, i ^ mask) for i in range(4)])]
    ppermute x20, starting transfers between devices: 20.7 us -> 18.6 us  [swap(): return lax.ppermute(values, 'tensor', [(i, i ^ mask) for i in range(4)])]
  transfers between devices with their start and end apart: 31 -> 27, of which waited for: 18 -> 17; matrix products, arithmetic and copies ran while one was open for 3% -> 3% of each run, Pallas kernels for 11% -> 11%
where the time goes in v8:
time: 165 us; the launch traced here: 164 us
  waiting for transfers between devices  78 us (47%)
  starting transfers between devices  47.6 us (29%)
  Pallas kernels  28.1 us (17%)
  local copies, waits for them, and re-layouts  5.32 us (3%)
  other arithmetic  3.54 us (2%)
    ppermute x20, waiting for transfers between devices, swap(): return lax.ppermute(values, 'tensor', [(i, i ^ mask) for i in range(4)])  45.8 us
    pallas_call x16, Pallas kernels, call(): pl.pallas_call(body, out_shape=[pltpu.HBM(shape, kind) if i in away else...  28.1 us
    ppermute x3, waiting for transfers between devices, side(): return lax.ppermute(values, ('dp', 'tensor'), pairs)  23.9 us
    ppermute x20, starting transfers between devices, swap(): return lax.ppermute(values, 'tensor', [(i, i ^ mask) for i in range(4)])  18.6 us
    all_to_all x3, starting transfers between devices, plane(): lax.all_to_all(stacked, 'dp', 0, 0, tiled=True, axis_index_groups=plane_g...  17.4 us
    all_to_all x1, starting transfers between devices, spread(): return lax.all_to_all(stacked, 'dp', 0, 0, tiled=True)  6.43 us
    all_to_all x3, waiting for transfers between devices, plane(): lax.all_to_all(stacked, 'dp', 0, 0, tiled=True, axis_index_groups=plane_g...  6.23 us
    ppermute x3, starting transfers between devices, side(): return lax.ppermute(values, ('dp', 'tensor'), pairs)  5.12 us
  transfers between devices with their start and end apart: 27, of which 17 were waited for; matrix products, arithmetic and copies ran while one was open for 3% of the time, Pallas kernels for 11%

profile of v8, /device:TPU:0, one launch (start us, length us, event | category | flops | bytes accessed | tf_op | source)
XLA Modules:
  0.0 164.0 jit_solution(701806445919360830)
XLA Ops:
  0.7 0.9 pad_maximum_fusion.4.weight_ref
  1.7 0.9 concatenate.29
  2.5 0.9 shard_map.323
  3.5 8.0 %all-to-all-start = ((bf16[16,24,896]{2,1,0:T(8,128)(2,1)}), bf16[16,24,896]{2,1,0:T(8,128)(2,1)S(1)}, u32[]{:S(2)}, u32[]{:S(2)}) async-start(bf16[16,24,896]{2,1,0:T(8,128)(2,1)} %shard_map.323), calls=%async_computation | async-start | bytes 1376256 | tf_op jit(solution)/shard_map/all_to_all | solution.py:48
  11.5 1.7 %collective-permute-start.2 = (bf16[24,1536]{1,0:T(8,128)(2,1)S(1)}, bf16[24,1536]{1,0:T(8,128)(2,1)S(1)}, u32[]{:S(2)}, u32[]{:S(2)}) collective-permute-start(bf16[24,1536]{1,0:T(8,128)(2,1)S(1)} %constant_dynamic-update-slice_fusion.own_ref), channel_id=1, source_target_pairs={{0,64},{1,65},{2,66},{3,67},{4,68},{5,69},{6,70},{7,71},{8,72},{9,... | collective-permute-start | bytes 221192 | tf_op jit(solution)/shard_map/ppermute | solution.py:58
  13.1 2.9 %collective-permute-start = (bf16[128,768]{1,0:T(8,128)(2,1)S(1)}, bf16[128,768]{1,0:T(8,128)(2,1)S(1)}, u32[]{:S(2)}, u32[]{:S(2)}) collective-permute-start(bf16[128,768]{1,0:T(8,128)(2,1)S(1)} %bitcast.44), channel_id=1, source_target_pairs={{0,2},{1,3},{2,0},{3,1},{4,6},{5,7},{6,4},{7,5},{8,10},{9,11},{10,... | collective-permute-start | bytes 589832 | tf_op jit(solution)/shard_map/ppermute | solution.py:31
  17.9 1.6 shard_map.324
  19.5 5.2 %all-to-all-done = bf16[16,24,896]{2,1,0:T(8,128)(2,1)S(1)} async-done(((bf16[16,24,896]{2,1,0:T(8,128)(2,1)}), bf16[16,24,896]{2,1,0:T(8,128)(2,1)S(1)}, u32[]{:S(2)}, u32[]{:S(2)}) %all-to-all-start) | async-done | bytes 688160 | tf_op jit(solution)/shard_map/all_to_all | solution.py:48
  24.8 1.7 %collective-permute-start.3 = (bf16[16,24,896]{2,0,1:T(8,128)(2,1)S(1)}, bf16[16,24,896]{2,0,1:T(8,128)(2,1)S(1)}, u32[]{:S(2)}, u32[]{:S(2)}) collective-permute-start(bf16[16,24,896]{2,0,1:T(8,128)(2,1)S(1)} %copy.42), channel_id=1, source_target_pairs={{0,64},{1,65},{2,66},{3,67},{4,68},{5,69},{6,70},{7,71},{8,72},{9,... | collective-permute-start | bytes 2064392 | tf_op jit(solution)/shard_map/ppermute | solution.py:58
  26.6 4.5 %all-to-all-start.1 = ((bf16[16,48,1536]{2,1,0:T(8,128)(2,1)}), bf16[16,48,1536]{2,1,0:T(8,128)(2,1)}, u32[]{:S(2)}, u32[]{:S(2)}) async-start(bf16[16,48,1536]{2,1,0:T(8,128)(2,1)} %shard_map.324), calls=%async_computation.1 | async-start | bytes 4718592 | tf_op jit(solution)/shard_map/all_to_all | solution.py:48
  31.1 9.3 %collective-permute-done.3 = bf16[16,24,896]{2,0,1:T(8,128)(2,1)S(1)} collective-permute-done((bf16[16,24,896]{2,0,1:T(8,128)(2,1)S(1)}, bf16[16,24,896]{2,0,1:T(8,128)(2,1)S(1)}, u32[]{:S(2)}, u32[]{:S(2)}) %collective-permute-start.3) | collective-permute-done | bytes 688160 | tf_op jit(solution)/shard_map/ppermute | solution.py:58
  40.6 3.1 %collective-permute-start.6 = (bf16[2,2,16,128]{3,2,1,0:T(8,128)(2,1)S(1)}, bf16[2,2,16,128]{3,2,1,0:T(8,128)(2,1)S(1)}, u32[]{:S(2)}, u32[]{:S(2)}) collective-permute-start(bf16[2,2,16,128]{3,2,1,0:T(8,128)(2,1)S(1)} %maximum_bitcast_fusion.refs_0_), channel_id=1, source_target_pairs={{0,2},{1,3},{2,0},{3,1},{4,6},{5,7},{6,4},{7,5},{8,10},{9,11},{10,... | collective-permute-start | bytes 49160 | tf_op jit(solution)/shard_map/ppermute | solution.py:31
  44.0 1.1 collective-permute-done.7.refs_3_
  45.8 3.8 %shard_map.325 = (bf16[512,768]{1,0:T(8,128)(2,1)}, bf16[512,256]{1,0:T(8,128)(2,1)S(1)}, f32[8,512]{1,0:T(8,128)S(1)}, bf16[256,768]{1,0:T(8,128)(2,1)S(1)}, f3...) custom-call(s32[2]{0:T(128)S(1)} %pad_add_fusion.1.index_ref, ...), custom_call_target="tpu_custom_call" | custom-call | flops 1000 | bytes 1000 | tf_op jit(solution)/shard_map/pallas_call | solution.py:87
  49.7 2.5 %collective-permute-start.8 = (bf16[256,768]{1,0:T(8,128)(2,1)S(1)}, bf16[256,768]{1,0:T(8,128)(2,1)S(1)}, u32[]{:S(2)}, u32[]{:S(2)}) collective-permute-start(bf16[256,768]{1,0:T(8,128)(2,1)S(1)} %get-tuple-element.74), channel_id=1, source_target_pairs={{0,1},{1,0},{2,3},{3,2},{4,5},{5,4},{6,7},{7,6},{8,9},{9,8},{10,11... | collective-permute-start | bytes 1179656 | tf_op jit(solution)/shard_map/ppermute | solution.py:31
  52.1 1.3 collective-permute-done.8
  53.7 1.2 collective-permute-start.9
  54.9 11.8 %collective-permute-done.9.far_ref = bf16[256,768]{1,0:T(8,128)(2,1)S(1)} collective-permute-done((bf16[256,768]{1,0:T(8,128)(2,1)S(1)}, bf16[256,768]{1,0:T(8,128)(2,1)S(1)}, u32[]{:S(2)}, u32[]{:S(2)}) %collective-permute-start.9) | collective-permute-done | bytes 393248 | tf_op jit(solution)/shard_map/ppermute | solution.py:31
  67.1 1.7 %collective-permute-done.10.rows_ref.hidden_other = bf16[256,768]{1,0:T(8,128)(2,1)S(1)} collective-permute-done((bf16[256,768]{1,0:T(8,128)(2,1)S(1)}, bf16[256,768]{1,0:T(8,128)(2,1)S(1)}, u32[]{:S(2)}, u32[]{:S(2)}) %collective-permute-start.10) | collective-permute-done | bytes 393248 | tf_op jit(solution)/shard_map/ppermute | solution.py:31
  68.9 3.1 %shard_map.327 = (bf16[256,768]{1,0:T(8,128)(2,1)S(1)}, bf16[256,768]{1,0:T(8,128)(2,1)S(1)}, bf16[256,768]{1,0:T(8,128)(2,1)S(1)}, bf16[768,768]{1,0:T(8,128)(2,1)S(1)}, bf16[768,768]{1,0:T(8,128)(2,1)S(1)}) custom-call(bf16[256,768]{1,0:T(8,128)(2,1)S(1)} %collective-permute-done.10.rows_ref.hidden_other, bf16[16,48,1536]{2,1,0:T(8,128)(2,1)} %all-to-all-done.1.blocks_ref, ...), custom_call_target="tpu_custom_call" | custom-call | flops 1000 | bytes 1000 | tf_op jit(solution)/shard_map/pallas_call | solution.py:87
  72.2 1.3 shard_map.328
  74.0 0.9 collective-permute-start.12
  74.9 11.8 %collective-permute-done.12.far_ref = bf16[256,768]{1,0:T(8,128)(2,1)S(1)} collective-permute-done((bf16[256,768]{1,0:T(8,128)(2,1)S(1)}, bf16[256,768]{1,0:T(8,128)(2,1)S(1)}, u32[]{:S(2)}, u32[]{:S(2)}) %collective-permute-start.12) | collective-permute-done | bytes 393248 | tf_op jit(solution)/shard_map/ppermute | solution.py:31
  86.7 1.2 shard_map.329
  87.9 1.2 shard_map.330
  89.2 0.9 copy-done.5
  90.0 2.0 %shard_map.331 = (bf16[256,768]{1,0:T(8,128)(2,1)S(1)}, bf16[256,768]{1,0:T(8,128)(2,1)}, f32[1,768]{1,0:T(1,128)S(1)}) custom-call(bf16[256,768]{1,0:T(8,128)(2,1)S(1)} %collective-permute-done.13.rows_ref.branch_other, bf16[768,768]{1,0:T(8,128)(2,1)S(1)} %get-tuple-element.79.up_ref, bf16[768,768]{1,0:T(8,128)(2,1)S(1)} %get-tuple-element.80.down_ref, ...), custom_call_target="tpu_custom_call" | custom-call | flops 1000 | bytes 1000 | tf_op jit(solution)/shard_map/pallas_call | solution.py:87
  93.1 2.5 %shard_map.337 = bf16[16,48,1536]{2,1,0:T(8,128)(2,1)} custom-call(bf16[256,768]{1,0:T(8,128)(2,1)S(1)} %get-tuple-element.76.rows_ref.first_ref.hidden_near, bf16[256,768]{1,0:T(8,128)(2,1)S(1)} %collective-permute-done.10.rows_ref.hidden_other, bf16[256,768]{1,0:T(8,128)(2,1)S(1)} %get-tuple-element.84.rows_ref.second_ref.branch_near, ...), custom_call_target="tpu_custom_call" | custom-call | flops 1000 | bytes 1000 | tf_op jit(solution)/shard_map/pallas_call | solution.py:87
  95.6 5.0 %all-to-all-start.3 = ((bf16[16,48,1536]{2,1,0:T(8,128)(2,1)}), bf16[16,48,1536]{2,1,0:T(8,128)(2,1)S(1)}, u32[]{:S(2)}, u32[]{:S(2)}) async-start(bf16[16,48,1536]{2,1,0:T(8,128)(2,1)} %shard_map.337), calls=%async_computation.3 | async-start | bytes 4718592 | tf_op jit(solution)/shard_map/all_to_all | solution.py:48
  100.7 1.3 fusion.2
  102.1 1.3 collective-permute-start.15
  103.5 11.0 %collective-permute-done.15.far_ref = bf16[256,768]{1,0:T(8,128)(2,1)S(1)} collective-permute-done((bf16[256,768]{1,0:T(8,128)(2,1)S(1)}, bf16[256,768]{1,0:T(8,128)(2,1)S(1)}, u32[]{:S(2)}, u32[]{:S(2)}) %collective-permute-start.15) | collective-permute-done | bytes 393248 | tf_op jit(solution)/shard_map/ppermute | solution.py:31
  115.8 1.7 %collective-permute-done.16.other_ref = bf16[256,768]{1,0:T(8,128)(2,1)S(1)} collective-permute-done((bf16[256,768]{1,0:T(8,128)(2,1)S(1)}, bf16[256,768]{1,0:T(8,128)(2,1)S(1)}, u32[]{:S(2)}, u32[]{:S(2)}) %collective-permute-start.16) | collective-permute-done | bytes 393248 | tf_op jit(solution)/shard_map/ppermute | solution.py:31
  117.6 3.8 %shard_map.333 = (bf16[512,768]{1,0:T(8,128)(2,1)S(1)}, bf16[256,768]{1,0:T(8,128)(2,1)S(1)}, f32[256,768]{1,0:T(8,128)S(1)}, f32[16,768]{1,0:T(8,128)S(1)}) custom-call(s32[1]{0:T(128)} %bitcast.1.index_ref, bf16[256,768]{1,0:T(8,128)(2,1)S(1)} %get-tuple-element.94.near_ref, bf16[256,768]{1,0:T(8,128)(2,1)S(1)} %collective-permute-done.16.other_ref, ...), custom_call_target="tpu_custom_call" | custom-call | flops 1000 | bytes 1000 | tf_op jit(solution)/shard_map/pallas_call | solution.py:87
  121.6 1.6 collective-permute-done.17
  123.3 1.3 collective-permute-start.18
  124.6 1.8 %collective-permute-start.21 = (bf16[16,768]{1,0:T(8,128)(2,1)S(1)}, bf16[16,768]{1,0:T(8,128)(2,1)S(1)}, u32[]{:S(2)}, u32[]{:S(2)}) collective-permute-start(bf16[16,768]{1,0:T(8,128)(2,1)S(1)} %convert_element_type.41), channel_id=1, source_target_pairs={{0,3},{1,2},{2,1},{3,0},{4,7},{5,6},{6,5},{7,4},{8,11},{9,10},{10,... | collective-permute-start | bytes 73736 | tf_op jit(solution)/shard_map/ppermute | solution.py:31
  126.4 1.2 collective-permute-start.20
  128.0 2.1 %shard_map.334.block_ref = bf16[768,896]{1,0:T(8,128)(2,1)} custom-call(bf16[256,768]{1,0:T(8,128)(2,1)S(1)} %pad_maximum_fusion.near_ref.tokens_ref.tokens_near, bf16[256,768]{1,0:T(8,128)(2,1)S(1)} %copy-done.1, bf16[256,768]{1,0:T(8,128)(2,1)S(1)} %get-tuple-element.94.near_ref, bf16[256,768]{1,0:T(8,128)(2,1)S(1)} %collective-permute-done.16.other_ref, ...), custom_call_target="tpu_custom_call" | custom-call | flops 1000 | bytes 1000 | tf_op jit(solution)/shard_map/pallas_call | solution.py:87
  130.2 1.4 collective-permute-done.21.both_ref
  131.6 1.3 collective-permute-done.20.far_ref
  132.9 0.9 shard_map.335
  133.8 1.0 all-to-all-done.3.blocks_ref
  134.8 6.4 %all-to-all-start.2 = ((bf16[32,24,896]{2,1,0:T(8,128)(2,1)}), bf16[32,24,896]{2,1,0:T(8,128)(2,1)}, u32[]{:S(2)}, u32[]{:S(2)}) async-start(bf16[32,24,896]{2,1,0:T(8,128)(2,1)} %bitcast.43), calls=%async_computation.2 | async-start | bytes 2752512 | tf_op jit(solution)/shard_map/all_to_all | solution.py:39
  141.6 1.8 %collective-permute-start.22 = (bf16[24,1536]{1,0:T(8,128)(2,1)S(1)}, bf16[24,1536]{1,0:T(8,128)(2,1)S(1)}, u32[]{:S(2)}, u32[]{:S(2)}) collective-permute-start(bf16[24,1536]{1,0:T(8,128)(2,1)S(1)} %get-tuple-element.114), channel_id=1, source_target_pairs={{0,64},{1,65},{2,66},{3,67},{4,68},{5,69},{6,70},{7,71},{8,72},{9,... | collective-permute-start | bytes 221192 | tf_op jit(solution)/shard_map/ppermute | solution.py:58
  144.2 14.6 %collective-permute-done.22 = bf16[24,1536]{1,0:T(8,128)(2,1)S(1)} collective-permute-done((bf16[24,1536]{1,0:T(8,128)(2,1)S(1)}, bf16[24,1536]{1,0:T(8,128)(2,1)S(1)}, u32[]{:S(2)}, u32[]{:S(2)}) %collective-permute-start.22) | collective-permute-done | bytes 73760 | tf_op jit(solution)/shard_map/ppermute | solution.py:58
  159.5 2.1 %all-to-all-done.2.blocks_ref = bf16[32,24,896]{2,1,0:T(8,128)(2,1)} async-done(((bf16[32,24,896]{2,1,0:T(8,128)(2,1)}), bf16[32,24,896]{2,1,0:T(8,128)(2,1)}, u32[]{:S(2)}, u32[]{:S(2)}) %all-to-all-start.2) | async-done | bytes 1376288 | tf_op jit(solution)/shard_map/all_to_all | solution.py:39
  161.5 2.3 %shard_map.336 = (f32[24,192]{1,0:T(8,128)}, f32[24,192]{1,0:T(8,128)}, f32[24,192]{1,0:T(8,128)}, f32[24,192]{1,0:T(8,128)}, f32[1,6]{1,0:T(1,128)}, /*index=5*...) custom-call(s32[1]{0:T(128)} %bitcast.1.index_ref, ...), custom_call_target="tpu_custom_call" | custom-call | flops 1000 | bytes 1000 | tf_op jit(solution)/shard_map/pallas_call | solution.py:87
  (118 shorter events, 9.5 us)
Async XLA Ops:
  0.7 16.0 %copy-start.29 = (s32[4]{0:T(128)S(1)}, s32[4]{0:T(128)}, u32[]{:S(2)}) copy-start(s32[4]{0:T(128)} %constant.82) | copy-start | bytes 52
  0.7 16.0 %copy-start.30 = (s32[4]{0:T(128)S(1)}, s32[4]{0:T(128)}, u32[]{:S(2)}) copy-start(s32[4]{0:T(128)} %constant.81) | copy-start | bytes 52
  0.7 10.8 %copy-start.27 = (bf16[24,768]{1,0:T(8,128)(2,1)S(1)}, bf16[24,768]{1,0:T(8,128)(2,1)}, u32[]{:S(2)}) copy-start(bf16[24,768]{1,0:T(8,128)(2,1)} %param.25) | copy-start | bytes 110596
  0.7 10.8 %copy-start.28 = (bf16[24,768]{1,0:T(8,128)(2,1)S(1)}, bf16[24,768]{1,0:T(8,128)(2,1)}, u32[]{:S(2)}) copy-start(bf16[24,768]{1,0:T(8,128)(2,1)} %param.27) | copy-start | bytes 110596
  0.7 12.4 %copy-start.25 = (bf16[1,128,768]{2,1,0:T(8,128)(2,1)S(1)}, bf16[1,128,768]{2,1,0:T(8,128)(2,1)}, u32[]{:S(2)}) copy-start(bf16[1,128,768]{2,1,0:T(8,128)(2,1)} %param.20) | copy-start | bytes 589828
  0.7 15.3 %copy-start.13 = (bf16[1,128,768]{2,1,0:T(8,128)(2,1)S(1)}, bf16[1,128,768]{2,1,0:T(8,128)(2,1)}, u32[]{:S(2)}) copy-start(bf16[1,128,768]{2,1,0:T(8,128)(2,1)} %param.37) | copy-start | bytes 589828
  0.7 16.0 %copy-start.26 = (s32[1,512]{1,0:T(1,128)S(1)}, s32[1,512]{1,0:T(1,128)}, u32[]{:S(2)}) copy-start(s32[1,512]{1,0:T(1,128)} %param.21) | copy-start | bytes 6148
  3.5 21.2 %all-to-all-start = ((bf16[16,24,896]{2,1,0:T(8,128)(2,1)}), bf16[16,24,896]{2,1,0:T(8,128)(2,1)S(1)}, u32[]{:S(2)}, u32[]{:S(2)}) async-start(bf16[16,24,896]{2,1,0:T(8,128)(2,1)} %shard_map.323), calls=%async_computation | async-start | bytes 1376256 | tf_op jit(solution)/shard_map/all_to_all | solution.py:48
  11.5 6.4 %collective-permute-start.2 = (bf16[24,1536]{1,0:T(8,128)(2,1)S(1)}, bf16[24,1536]{1,0:T(8,128)(2,1)S(1)}, u32[]{:S(2)}, u32[]{:S(2)}) collective-permute-start(bf16[24,1536]{1,0:T(8,128)(2,1)S(1)} %constant_dynamic-update-slice_fusion.own_ref), channel_id=1, source_target_pairs={{0,64},{1,65},{2,66},{3,67},{4,68},{5,69},{6,70},{7,71},{8,72},{9,... | collective-permute-start | bytes 221192 | tf_op jit(solution)/shard_map/ppermute | solution.py:58
  13.1 13.3 %collective-permute-start = (bf16[128,768]{1,0:T(8,128)(2,1)S(1)}, bf16[128,768]{1,0:T(8,128)(2,1)S(1)}, u32[]{:S(2)}, u32[]{:S(2)}) collective-permute-start(bf16[128,768]{1,0:T(8,128)(2,1)S(1)} %bitcast.44), channel_id=1, source_target_pairs={{0,2},{1,3},{2,0},{3,1},{4,6},{5,7},{6,4},{7,5},{8,10},{9,11},{10,... | collective-permute-start | bytes 589832 | tf_op jit(solution)/shard_map/ppermute | solution.py:31
  16.0 27.8 %collective-permute-start.4 = (bf16[128,768]{1,0:T(8,128)(2,1)S(1)}, bf16[128,768]{1,0:T(8,128)(2,1)S(1)}, u32[]{:S(2)}, u32[]{:S(2)}) collective-permute-start(bf16[128,768]{1,0:T(8,128)(2,1)S(1)} %bitcast.38), channel_id=1, source_target_pairs={{0,2},{1,3},{2,0},{3,1},{4,6},{5,7},{6,4},{7,5},{8,10},{9,11},{10,... | collective-permute-start | bytes 589832 | tf_op jit(solution)/shard_map/ppermute | solution.py:31
  24.8 15.6 %collective-permute-start.3 = (bf16[16,24,896]{2,0,1:T(8,128)(2,1)S(1)}, bf16[16,24,896]{2,0,1:T(8,128)(2,1)S(1)}, u32[]{:S(2)}, u32[]{:S(2)}) collective-permute-start(bf16[16,24,896]{2,0,1:T(8,128)(2,1)S(1)} %copy.42), channel_id=1, source_target_pairs={{0,64},{1,65},{2,66},{3,67},{4,68},{5,69},{6,70},{7,71},{8,72},{9,... | collective-permute-start | bytes 2064392 | tf_op jit(solution)/shard_map/ppermute | solution.py:58
  26.5 17.5 %collective-permute-start.1 = (bf16[256,768]{1,0:T(8,128)(2,1)S(1)}, bf16[256,768]{1,0:T(8,128)(2,1)S(1)}, u32[]{:S(2)}, u32[]{:S(2)}) collective-permute-start(bf16[256,768]{1,0:T(8,128)(2,1)S(1)} %pad_maximum_fusion.near_ref.tokens_ref.tokens_near), channel_id=1, source_target_pairs={{0,1},{1,0},{2,3},{3,2},{4,5},{5,4},{6,7},{7,6},{8,9},{9,8},{10,11... | collective-permute-start | bytes 1179656 | tf_op jit(solution)/shard_map/ppermute | solution.py:31
  26.6 42.3 %all-to-all-start.1 = ((bf16[16,48,1536]{2,1,0:T(8,128)(2,1)}), bf16[16,48,1536]{2,1,0:T(8,128)(2,1)}, u32[]{:S(2)}, u32[]{:S(2)}) async-start(bf16[16,48,1536]{2,1,0:T(8,128)(2,1)} %shard_map.324), calls=%async_computation.1 | async-start | bytes 4718592 | tf_op jit(solution)/shard_map/all_to_all | solution.py:48
  40.4 4.7 %collective-permute-start.7 = (bf16[2,2,16,128]{3,2,1,0:T(8,128)(2,1)S(1)}, bf16[2,2,16,128]{3,2,1,0:T(8,128)(2,1)S(1)}, u32[]{:S(2)}, u32[]{:S(2)}) collective-permute-start(bf16[2,2,16,128]{3,2,1,0:T(8,128)(2,1)S(1)} %maximum_bitcast_fusion.refs_0_), channel_id=1, source_target_pairs={{0,3},{1,2},{2,1},{3,0},{4,7},{5,6},{6,5},{7,4},{8,11},{9,10},{10,... | collective-permute-start | bytes 49160 | tf_op jit(solution)/shard_map/ppermute | solution.py:31
  40.6 5.2 %collective-permute-start.6 = (bf16[2,2,16,128]{3,2,1,0:T(8,128)(2,1)S(1)}, bf16[2,2,16,128]{3,2,1,0:T(8,128)(2,1)S(1)}, u32[]{:S(2)}, u32[]{:S(2)}) collective-permute-start(bf16[2,2,16,128]{3,2,1,0:T(8,128)(2,1)S(1)} %maximum_bitcast_fusion.refs_0_), channel_id=1, source_target_pairs={{0,2},{1,3},{2,0},{3,1},{4,6},{5,7},{6,4},{7,5},{8,10},{9,11},{10,... | collective-permute-start | bytes 49160 | tf_op jit(solution)/shard_map/ppermute | solution.py:31
  43.7 2.1 %collective-permute-start.5 = (bf16[2,2,16,128]{3,2,1,0:T(8,128)(2,1)S(1)}, bf16[2,2,16,128]{3,2,1,0:T(8,128)(2,1)S(1)}, u32[]{:S(2)}, u32[]{:S(2)}) collective-permute-start(bf16[2,2,16,128]{3,2,1,0:T(8,128)(2,1)S(1)} %maximum_bitcast_fusion.refs_0_), channel_id=1, source_target_pairs={{0,1},{1,0},{2,3},{3,2},{4,5},{5,4},{6,7},{7,6},{8,9},{9,8},{10,11... | collective-permute-start | bytes 49160 | tf_op jit(solution)/shard_map/ppermute | solution.py:31
  43.8 5.8 %copy-start.15 = (bf16[128,768]{1,0:T(8,128)(2,1)}, bf16[128,768]{1,0:T(8,128)(2,1)S(1)}, u32[]{:S(2)}) copy-start(bf16[128,768]{1,0:T(8,128)(2,1)S(1)} %collective-permute-done.4.cotangent_far_ref) | copy-start | bytes 589828
  44.0 9.6 %copy-start = (bf16[256,768]{1,0:T(8,128)(2,1)}, bf16[256,768]{1,0:T(8,128)(2,1)S(1)}, u32[]{:S(2)}) copy-start(bf16[256,768]{1,0:T(8,128)(2,1)S(1)} %collective-permute-done.1.other_ref.tokens_other) | copy-start | bytes 1179652
  49.6 17.0 %copy-start.10 = (f32[8,768]{1,0:T(8,128)}, f32[8,768]{1,0:T(8,128)S(1)}, u32[]{:S(2)}) copy-start(f32[8,768]{1,0:T(8,128)S(1)} %get-tuple-element.75.rows_ref) | copy-start | bytes 73732
  49.7 3.8 %collective-permute-start.8 = (bf16[256,768]{1,0:T(8,128)(2,1)S(1)}, bf16[256,768]{1,0:T(8,128)(2,1)S(1)}, u32[]{:S(2)}, u32[]{:S(2)}) collective-permute-start(bf16[256,768]{1,0:T(8,128)(2,1)S(1)} %get-tuple-element.74), channel_id=1, source_target_pairs={{0,1},{1,0},{2,3},{3,2},{4,5},{5,4},{6,7},{7,6},{8,9},{9,8},{10,11... | collective-permute-start | bytes 1179656 | tf_op jit(solution)/shard_map/ppermute | solution.py:31
  53.7 13.0 %collective-permute-start.9 = (bf16[256,768]{1,0:T(8,128)(2,1)S(1)}, bf16[256,768]{1,0:T(8,128)(2,1)S(1)}, u32[]{:S(2)}, u32[]{:S(2)}) collective-permute-start(bf16[256,768]{1,0:T(8,128)(2,1)S(1)} %pad_maximum_fusion.1), channel_id=1, source_target_pairs={{0,2},{1,3},{2,0},{3,1},{4,6},{5,7},{6,4},{7,5},{8,10},{9,11},{10,... | collective-permute-start | bytes 1179656 | tf_op jit(solution)/shard_map/ppermute | solution.py:31
  67.1 1.8 %collective-permute-start.10 = (bf16[256,768]{1,0:T(8,128)(2,1)S(1)}, bf16[256,768]{1,0:T(8,128)(2,1)S(1)}, u32[]{:S(2)}, u32[]{:S(2)}) collective-permute-start(bf16[256,768]{1,0:T(8,128)(2,1)S(1)} %get-tuple-element.76.rows_ref.first_ref.hidden_near), channel_id=1, source_target_pairs={{0,1},{1,0},{2,3},{3,2},{4,5},{5,4},{6,7},{7,6},{8,9},{9,8},{10,11... | collective-permute-start | bytes 1179656 | tf_op jit(solution)/shard_map/ppermute | solution.py:31
  71.9 1.8 %collective-permute-start.11 = (bf16[256,768]{1,0:T(8,128)(2,1)S(1)}, bf16[256,768]{1,0:T(8,128)(2,1)S(1)}, u32[]{:S(2)}, u32[]{:S(2)}) collective-permute-start(bf16[256,768]{1,0:T(8,128)(2,1)S(1)} %get-tuple-element.82), channel_id=1, source_target_pairs={{0,1},{1,0},{2,3},{3,2},{4,5},{5,4},{6,7},{7,6},{8,9},{9,8},{10,11... | collective-permute-start | bytes 1179656 | tf_op jit(solution)/shard_map/ppermute | solution.py:31
  73.8 12.9 %copy-start.11 = (f32[8,768]{1,0:T(8,128)S(1)}, f32[8,768]{1,0:T(8,128)}, u32[]{:S(2)}) copy-start(f32[8,768]{1,0:T(8,128)} %copy-done.10) | copy-start | bytes 73732
  73.9 12.9 %copy-start.14 = (bf16[1,128,768]{2,1,0:T(8,128)(2,1)S(1)}, bf16[1,128,768]{2,1,0:T(8,128)(2,1)}, u32[]{:S(2)}) copy-start(bf16[1,128,768]{2,1,0:T(8,128)(2,1)} %param.37) | copy-start | bytes 589828
  73.9 12.9 %copy-start.16 = (bf16[128,768]{1,0:T(8,128)(2,1)S(1)}, bf16[128,768]{1,0:T(8,128)(2,1)}, u32[]{:S(2)}) copy-start(bf16[128,768]{1,0:T(8,128)(2,1)} %copy-done.15) | copy-start | bytes 589828
  74.0 12.8 %collective-permute-start.12 = (bf16[256,768]{1,0:T(8,128)(2,1)S(1)}, bf16[256,768]{1,0:T(8,128)(2,1)S(1)}, u32[]{:S(2)}, u32[]{:S(2)}) collective-permute-start(bf16[256,768]{1,0:T(8,128)(2,1)S(1)} %pad_maximum_fusion.2), channel_id=1, source_target_pairs={{0,2},{1,3},{2,0},{3,1},{4,6},{5,7},{6,4},{7,5},{8,10},{9,11},{10,... | collective-permute-start | bytes 1179656 | tf_op jit(solution)/shard_map/ppermute | solution.py:31
  87.9 2.1 %collective-permute-start.13 = (bf16[256,768]{1,0:T(8,128)(2,1)S(1)}, bf16[256,768]{1,0:T(8,128)(2,1)S(1)}, u32[]{:S(2)}, u32[]{:S(2)}) collective-permute-start(bf16[256,768]{1,0:T(8,128)(2,1)S(1)} %get-tuple-element.84.rows_ref.second_ref.branch_near), channel_id=1, source_target_pairs={{0,1},{1,0},{2,3},{3,2},{4,5},{5,4},{6,7},{7,6},{8,9},{9,8},{10,11... | collective-permute-start | bytes 1179656 | tf_op jit(solution)/shard_map/ppermute | solution.py:31
  92.6 8.1 %collective-permute-start.14 = (bf16[256,768]{1,0:T(8,128)(2,1)}, bf16[256,768]{1,0:T(8,128)(2,1)}, u32[]{:S(2)}, u32[]{:S(2)}) collective-permute-start(bf16[256,768]{1,0:T(8,128)(2,1)} %get-tuple-element.90), channel_id=1, source_target_pairs={{0,1},{1,0},{2,3},{3,2},{4,5},{5,4},{6,7},{7,6},{8,9},{9,8},{10,11... | collective-permute-start | bytes 1179656 | tf_op jit(solution)/shard_map/ppermute | solution.py:31
  95.6 39.2 %all-to-all-start.3 = ((bf16[16,48,1536]{2,1,0:T(8,128)(2,1)}), bf16[16,48,1536]{2,1,0:T(8,128)(2,1)S(1)}, u32[]{:S(2)}, u32[]{:S(2)}) async-start(bf16[16,48,1536]{2,1,0:T(8,128)(2,1)} %shard_map.337), calls=%async_computation.3 | async-start | bytes 4718592 | tf_op jit(solution)/shard_map/all_to_all | solution.py:48
  102.0 12.5 %copy-start.12 = (f32[8,768]{1,0:T(8,128)S(1)}, f32[8,768]{1,0:T(8,128)}, u32[]{:S(2)}) copy-start(f32[8,768]{1,0:T(8,128)} %copy-done.10) | copy-start | bytes 73732
  102.0 12.5 %copy-start.18 = (f32[8,768]{1,0:T(8,128)S(1)}, f32[8,768]{1,0:T(8,128)}, u32[]{:S(2)}) copy-start(f32[8,768]{1,0:T(8,128)} %copy-done.17) | copy-start | bytes 73732
  102.1 15.5 %copy-start.3 = (bf16[768,768]{1,0:T(8,128)(2,1)S(1)}, bf16[768,768]{1,0:T(8,128)(2,1)}, u32[]{:S(2)}) copy-start(bf16[768,768]{1,0:T(8,128)(2,1)} %copy-done.2) | copy-start | bytes 3538948
  102.1 15.5 %copy-start.4 = (bf16[512,768]{1,0:T(8,128)(2,1)S(1)}, bf16[512,768]{1,0:T(8,128)(2,1)}, u32[]{:S(2)}) copy-start(bf16[512,768]{1,0:T(8,128)(2,1)} %get-tuple-element.95.qkv_ref) | copy-start | bytes 2359300
  102.1 15.5 %copy-start.20 = (f32[8,512]{1,0:T(8,128)S(1)}, f32[8,512]{1,0:T(8,128)}, u32[]{:S(2)}) copy-start(f32[8,512]{1,0:T(8,128)} %copy-done.19) | copy-start | bytes 49156
  102.1 15.5 %copy-start.22 = (f32[1,768]{1,0:T(1,128)S(1)}, f32[1,768]{1,0:T(1,128)}, u32[]{:S(2)}) copy-start(f32[1,768]{1,0:T(1,128)} %copy-done.21) | copy-start | bytes 9220
  102.1 12.3 %collective-permute-start.15 = (bf16[256,768]{1,0:T(8,128)(2,1)S(1)}, bf16[256,768]{1,0:T(8,128)(2,1)S(1)}, u32[]{:S(2)}, u32[]{:S(2)}) collective-permute-start(bf16[256,768]{1,0:T(8,128)(2,1)S(1)} %pad_maximum_fusion.3), channel_id=1, source_target_pairs={{0,2},{1,3},{2,0},{3,1},{4,6},{5,7},{6,4},{7,5},{8,10},{9,11},{10,... | collective-permute-start | bytes 1179656 | tf_op jit(solution)/shard_map/ppermute | solution.py:31
  115.8 1.7 %collective-permute-start.16 = (bf16[256,768]{1,0:T(8,128)(2,1)S(1)}, bf16[256,768]{1,0:T(8,128)(2,1)S(1)}, u32[]{:S(2)}, u32[]{:S(2)}) collective-permute-start(bf16[256,768]{1,0:T(8,128)(2,1)S(1)} %get-tuple-element.94.near_ref), channel_id=1, source_target_pairs={{0,1},{1,0},{2,3},{3,2},{4,5},{5,4},{6,7},{7,6},{8,9},{9,8},{10,11... | collective-permute-start | bytes 1179656 | tf_op jit(solution)/shard_map/ppermute | solution.py:31
  121.4 6.6 %copy-start.1 = (bf16[256,768]{1,0:T(8,128)(2,1)S(1)}, bf16[256,768]{1,0:T(8,128)(2,1)}, u32[]{:S(2)}) copy-start(bf16[256,768]{1,0:T(8,128)(2,1)} %copy-done) | copy-start | bytes 1179652
  121.4 6.6 %copy-start.9 = (bf16[512,256]{1,0:T(8,128)(2,1)S(1)}, bf16[512,256]{1,0:T(8,128)(2,1)}, u32[]{:S(2)}) copy-start(bf16[512,256]{1,0:T(8,128)(2,1)} %copy-done.8) | copy-start | bytes 786436
  121.4 1.8 %collective-permute-start.17 = (bf16[256,768]{1,0:T(8,128)(2,1)S(1)}, bf16[256,768]{1,0:T(8,128)(2,1)S(1)}, u32[]{:S(2)}, u32[]{:S(2)}) collective-permute-start(bf16[256,768]{1,0:T(8,128)(2,1)S(1)} %get-tuple-element.102), channel_id=1, source_target_pairs={{0,1},{1,0},{2,3},{3,2},{4,5},{5,4},{6,7},{7,6},{8,9},{9,8},{10,11... | collective-permute-start | bytes 1179656 | tf_op jit(solution)/shard_map/ppermute | solution.py:31
  123.3 10.5 %collective-permute-start.18 = (bf16[128,768]{1,0:T(8,128)(2,1)S(1)}, bf16[128,768]{1,0:T(8,128)(2,1)S(1)}, u32[]{:S(2)}, u32[]{:S(2)}) collective-permute-start(bf16[128,768]{1,0:T(8,128)(2,1)S(1)} %slice.93), channel_id=1, source_target_pairs={{0,2},{1,3},{2,0},{3,1},{4,6},{5,7},{6,4},{7,5},{8,10},{9,11},{10,... | collective-permute-start | bytes 589832 | tf_op jit(solution)/shard_map/ppermute | solution.py:31
  124.6 6.9 %collective-permute-start.21 = (bf16[16,768]{1,0:T(8,128)(2,1)S(1)}, bf16[16,768]{1,0:T(8,128)(2,1)S(1)}, u32[]{:S(2)}, u32[]{:S(2)}) collective-permute-start(bf16[16,768]{1,0:T(8,128)(2,1)S(1)} %convert_element_type.41), channel_id=1, source_target_pairs={{0,3},{1,2},{2,1},{3,0},{4,7},{5,6},{6,5},{7,4},{8,11},{9,10},{10,... | collective-permute-start | bytes 73736 | tf_op jit(solution)/shard_map/ppermute | solution.py:31
  126.4 6.5 %collective-permute-start.20 = (bf16[16,768]{1,0:T(8,128)(2,1)S(1)}, bf16[16,768]{1,0:T(8,128)(2,1)S(1)}, u32[]{:S(2)}, u32[]{:S(2)}) collective-permute-start(bf16[16,768]{1,0:T(8,128)(2,1)S(1)} %convert_element_type.41), channel_id=1, source_target_pairs={{0,2},{1,3},{2,0},{3,1},{4,6},{5,7},{6,4},{7,5},{8,10},{9,11},{10,... | collective-permute-start | bytes 73736 | tf_op jit(solution)/shard_map/ppermute | solution.py:31
  127.6 5.3 %collective-permute-start.19 = (bf16[16,768]{1,0:T(8,128)(2,1)S(1)}, bf16[16,768]{1,0:T(8,128)(2,1)S(1)}, u32[]{:S(2)}, u32[]{:S(2)}) collective-permute-start(bf16[16,768]{1,0:T(8,128)(2,1)S(1)} %convert_element_type.41), channel_id=1, source_target_pairs={{0,1},{1,0},{2,3},{3,2},{4,5},{5,4},{6,7},{7,6},{8,9},{9,8},{10,11... | collective-permute-start | bytes 73736 | tf_op jit(solution)/shard_map/ppermute | solution.py:31
  134.8 26.7 %all-to-all-start.2 = ((bf16[32,24,896]{2,1,0:T(8,128)(2,1)}), bf16[32,24,896]{2,1,0:T(8,128)(2,1)}, u32[]{:S(2)}, u32[]{:S(2)}) async-start(bf16[32,24,896]{2,1,0:T(8,128)(2,1)} %bitcast.43), calls=%async_computation.2 | async-start | bytes 2752512 | tf_op jit(solution)/shard_map/all_to_all | solution.py:39
  141.6 17.2 %collective-permute-start.22 = (bf16[24,1536]{1,0:T(8,128)(2,1)S(1)}, bf16[24,1536]{1,0:T(8,128)(2,1)S(1)}, u32[]{:S(2)}, u32[]{:S(2)}) collective-permute-start(bf16[24,1536]{1,0:T(8,128)(2,1)S(1)} %get-tuple-element.114), channel_id=1, source_target_pairs={{0,64},{1,65},{2,66},{3,67},{4,68},{5,69},{6,70},{7,71},{8,72},{9,... | collective-permute-start | bytes 221192 | tf_op jit(solution)/shard_map/ppermute | solution.py:58
  (10 other events, 21.1 us)
